TPU v7x, 32 devices: a whole 2x2x4 slice. The times are simulated.
32 devices in a mesh: expert: 16 (over z, y, x), tensor: 1, dp: 2 (over core).
Axes of the slice: x: 2, y: 2, z: 4, core: 2. Of those that a mesh axis runs over, the one named last changes fastest.
Arguments:
- tokens: bfloat16 [2048, 7168], P(('expert', 'dp'), 'tensor'), may hold values from -6 to 6
- gate_weight: bfloat16 [16, 7168, 1024], P('expert', 'tensor', 'dp'), may hold values from -0.25 to 0.25
- up_weight: bfloat16 [16, 7168, 1024], P('expert', 'tensor', 'dp'), may hold values from -0.25 to 0.25
- down_weight: bfloat16 [16, 1024, 7168], P('expert', 'dp', 'tensor'), may hold values from -0.1875 to 0.1875
- sketch: bfloat16 [16, 2, 1024, 512], P('expert', None, 'dp'), may hold values from -6 to 6
- clusters: int32 [16], replicated, may hold values from 0 to 5, never falling along the last dimension, each value on 1 to 4 neighbouring positions
- routes: int32 [2048, 8], P(('expert', 'dp')), may hold values from 0 to 15, all different within a row; in each aligned block of 64 rows (0 to 63, 64 to 127, ...) at most 48 rows name the same one
- route_weights: float32 [2048, 8], P(('expert', 'dp')), may hold values from 0.05 to 0.3
Outputs:
- mixed: bfloat16 [2048, 7168], P(('expert', 'dp'), 'tensor')
Inputs may be any that keep to these rules, and one draw needn't show every extreme that they name: `clusters`: the experts of one cluster are consecutive; a cluster holds 1 to 4 experts, and one holds exactly 4. `routes`: A row names 8 different experts. In each aligned block of 64 rows (the rows of one device) no expert is named by more than 48 rows, a bound that some block reaches.
All inputs are finite; a program needn't handle non-finite values.
Results may differ from a plain program's by a relative error of at most 0.023.
Values may be sent and summed in bfloat16 or wider, within the bound.
No kernel may reach another device: no remote copies, remote signals or barrier semaphores. Data moves between devices by JAX's collectives and lax.ppermute only.
A program may use at most 128 MiB of HBM per device.

v0:
```python
import jax
import jax.numpy as jnp
from jax import lax
from jax.sharding import PartitionSpec as P

MOST = 4


HIGHEST = lax.Precision.HIGHEST


def shifted(value, axis, steps):
    count = lax.axis_size(axis)
    initial, last = (max(0, -steps), min(count, count - steps))
    return lax.ppermute(value, axis, [(source, source + steps) for source in range(initial, last)])


def activate(projected, coefficients):
    gate_part = jnp.dot(projected, coefficients[0], preferred_element_type=jnp.float32)
    up_part = jnp.dot(projected, coefficients[1], preferred_element_type=jnp.float32)
    return (jax.nn.silu(gate_part) * up_part).astype(jnp.bfloat16)


def on_device(tokens, gate_weight, up_weight, down_weight, sketch, clusters, routes, route_weights):
    gate_rows = gate_weight[0]
    up_rows = up_weight[0]
    sketched = jnp.dot(gate_rows, sketch[0, 0], preferred_element_type=jnp.float32) + jnp.dot(
        up_rows, sketch[0, 1], preferred_element_type=jnp.float32
    )
    own_sketch = lax.psum_scatter(sketched, "dp", scatter_dimension=0, tiled=True)
    experts = lax.axis_size("expert")
    position = lax.axis_index("expert")
    my_cluster = clusters[position]
    summed = own_sketch
    for offset in range(1, MOST):
        below = shifted(own_sketch, "expert", offset)
        above = shifted(own_sketch, "expert", -offset)
        below_same = jnp.logical_and(
            position - offset >= 0, clusters[jnp.maximum(position - offset, 0)] == my_cluster
        )
        above_same = jnp.logical_and(
            position + offset < experts,
            clusters[jnp.minimum(position + offset, experts - 1)] == my_cluster,
        )
        summed = summed + jnp.where(below_same, below, 0.0) + jnp.where(above_same, above, 0.0)
    local_gram = lax.dot_general(summed, summed, (((0,), (0,)), ((), ())), precision=HIGHEST)
    gram = lax.psum(local_gram, ("tensor", "dp"))
    factor = jnp.linalg.cholesky(gram)
    basis_part = jax.scipy.linalg.solve_triangular(factor, summed.T, lower=True).T.astype(
        jnp.bfloat16
    )
    basis = lax.all_gather(basis_part, "dp", axis=0, tiled=True)
    gate_coeff = lax.dot_general(
        basis, gate_rows, (((0,), (0,)), ((), ())), preferred_element_type=jnp.float32
    )
    up_coeff = lax.dot_general(
        basis, up_rows, (((0,), (0,)), ((), ())), preferred_element_type=jnp.float32
    )
    partials = jnp.stack([gate_coeff, up_coeff]).astype(jnp.bfloat16)
    coeff_half = lax.psum(partials, "tensor").astype(jnp.float32).astype(jnp.bfloat16)
    coefficients, down_rows = (
        lax.all_gather(coeff_half, "dp", axis=2, tiled=True),
        lax.all_gather(down_weight[0], "dp", axis=0, tiled=True),
    )
    tok_rows = tokens.shape[0]
    top_count = routes.shape[1]
    capacity = tok_rows * top_count * 3 // (2 * experts)
    targets = routes.reshape(-1)
    assignments = targets.shape[0]
    onehot = (targets[:, None] == jnp.arange(experts, dtype=jnp.int32)[None, :]).astype(jnp.int32)
    place = jnp.sum((jnp.cumsum(onehot, axis=0) - 1) * onehot, axis=1)
    slot_index = targets * capacity + place
    owners = jnp.full((experts * capacity,), tok_rows, jnp.int32)
    owners = owners.at[slot_index].set(jnp.arange(assignments, dtype=jnp.int32) // top_count)
    padded = jnp.concatenate([tokens, jnp.zeros((1, tokens.shape[1]), tokens.dtype)], axis=0)
    outgoing = padded[owners].reshape(experts, capacity, tokens.shape[1])
    arrived = lax.all_to_all(outgoing, "expert", split_axis=0, concat_axis=0, tiled=True)
    arrived_rows = arrived.reshape(experts * capacity, tokens.shape[1])
    proj_part = jnp.dot(arrived_rows, basis, preferred_element_type=jnp.float32)
    projected = lax.psum(proj_part, "tensor").astype(jnp.bfloat16)
    hidden = activate(projected, coefficients)
    answers = jnp.dot(hidden, down_rows, preferred_element_type=jnp.float32).astype(jnp.bfloat16)
    returned = lax.all_to_all(
        answers.reshape(experts, capacity, tokens.shape[1]),
        "expert",
        split_axis=0,
        concat_axis=0,
        tiled=True,
    )
    picked = returned.reshape(experts * capacity, tokens.shape[1])[slot_index].astype(jnp.float32)
    weighted = picked * route_weights.reshape(-1)[:, None]
    return jnp.sum(weighted.reshape(tok_rows, top_count, tokens.shape[1]), axis=1).astype(
        jnp.bfloat16
    )


def solution(mesh):
    return jax.shard_map(
        on_device,
        mesh=mesh,
        in_specs=(
            P(("expert", "dp"), "tensor"),
            P("expert", "tensor", "dp"),
            P("expert", "tensor", "dp"),
            P("expert", "dp", "tensor"),
            P("expert", None, "dp", None),
            P(),
            P(("expert", "dp"), None),
            P(("expert", "dp"), None),
        ),
        out_specs=P(("expert", "dp"), "tensor"),
        check_vma=False,
    )
```

profile of v0, /device:TPU:28, one launch (start us, length us, event | category | flops | bytes accessed | tf_op | source)
XLA Modules:
  0.0 1667.0 jit_solution(1404134176902049348)
XLA Ops:
  6.5 7.3 fusion.11
  13.9 10.6 convolution_add_fusion
  24.6 25.3 %reduce-scatter.2.cloned.1.call-done = f32[3584,512]{1,0:T(8,128)} async-done(((f32[7168,512]{1,0:T(8,128)}), f32[3584,512]{1,0:T(8,128)}) %reduce-scatter.2.cloned.1.call-update) | async-done | bytes 7340048 | tf_op jit(solution)/shard_map/reduce_scatter | solution.py:30
  49.9 3.4 collective-permute-start
  53.2 3.4 collective-permute-start.1
  56.6 1.3 collective-permute-start.2
  57.9 7.5 collective-permute-start.3
  65.5 1.3 collective-permute-start.4
  66.7 304.4 %collective-permute-done = f32[3584,512]{1,0:T(8,128)} collective-permute-done((f32[3584,512]{1,0:T(8,128)}, f32[3584,512]{1,0:T(8,128)}, u32[]{:S(2)}, u32[]{:S(2)}) %collective-permute-start) | collective-permute-done | bytes 7340064 | tf_op jit(solution)/shard_map/ppermute | solution.py:15
  371.1 4.5 collective-permute-start.5
  383.9 299.2 %collective-permute-done.1 = f32[3584,512]{1,0:T(8,128)} collective-permute-done((f32[3584,512]{1,0:T(8,128)}, f32[3584,512]{1,0:T(8,128)}, u32[]{:S(2)}, u32[]{:S(2)}) %collective-permute-start.1) | collective-permute-done | bytes 7340064 | tf_op jit(solution)/shard_map/ppermute | solution.py:15
  683.2 0.9 collective-permute-done.3
  684.1 150.3 %collective-permute-done.4 = f32[3584,512]{1,0:T(8,128)} collective-permute-done((f32[3584,512]{1,0:T(8,128)}, f32[3584,512]{1,0:T(8,128)}, u32[]{:S(2)}, u32[]{:S(2)}) %collective-permute-start.4) | collective-permute-done | bytes 7340064 | tf_op jit(solution)/shard_map/ppermute | solution.py:15
  834.4 11.8 select_add_fusion
  846.2 17.9 %fusion.75 = f32[512,512]{0,1:T(8,128)} fusion(f32[3584,512]{1,0:T(8,128)} %select_add_fusion), kind=kOutput, calls=%fused_computation.127 | convolution fusion | flops 11274289152 | bytes 8388608 | tf_op jit(solution)/shard_map/dot_general | solution.py:46
  864.4 20.7 %all-reduce.4.cloned.1.call-done = f32[512,512]{0,1:T(8,128)} async-done(((f32[512,512]{0,1:T(8,128)}), f32[512,512]{0,1:T(8,128)}) %all-reduce.4.cloned.1.call-update) | async-done | bytes 1048592 | tf_op jit(solution)/shard_map/psum | solution.py:47
  885.0 1.6 copy.17
  886.6 1.4 fusion.40
  888.1 1.0 copy-done
  889.1 11.7 cholesky.104
  900.8 1.2 cholesky.224
  902.0 9.8 custom-call.31
  911.8 2.1 constant_dynamic-update-slice_fusion.3
  913.9 1.3 convolution_subtract_fusion
  915.2 11.7 cholesky.217
  927.5 10.2 custom-call.32
  937.8 0.9 convolution_dynamic-update-slice_fusion
  938.7 1.4 convolution_subtract_fusion.1
  940.2 11.7 cholesky.238
  952.5 0.7 compare_reduce_fusion.1
  953.2 9.8 custom-call.33
  963.1 0.8 convolution_dynamic-update-slice_fusion.1
  963.9 1.4 convolution_subtract_fusion.2
  965.3 11.7 cholesky.255
  981.6 2.5 select_select_fusion
  984.1 13.6 while.1
  984.7 2.8 bitcast_dynamic-update-slice_fusion.2
  988.2 2.8 bitcast_dynamic-update-slice_fusion.2
  991.6 2.8 bitcast_dynamic-update-slice_fusion.2
  995.0 2.8 bitcast_dynamic-update-slice_fusion.2
  997.8 40.1 %custom-call.34 = f32[4,128,128]{1,2,0:T(8,128)S(1)} custom-call(f32[4,128,128]{2,1,0:T(8,128)} %get-tuple-element.12), custom_call_target="InvertDiagBlocksLowerTriangular" | custom-call | tf_op jit(solution)/shard_map/jit(_solve_triangular)/triangular_solve | solution.py:49
  1037.9 3.4 fusion.74
  1041.3 3.9 fusion.53
  1045.2 1.8 fusion.73
  1047.1 7.0 fusion.19
  1054.1 1.8 fusion.72
  1055.9 9.7 fusion.13
  1065.6 2.2 convolution_convert_fusion
  1067.9 2.0 maximum_bitcast_fusion
  1070.1 1.2 reduce-window.6
  1071.9 2.4 scatter_custom_fusion
  1074.4 9.3 gather_fusion
  1083.8 6.9 all-to-all-start
  1090.7 9.3 fusion.33
  1100.0 6.3 fusion.36
  1106.4 1.1 pad_maximum_fusion
  1108.0 233.6 %all-to-all-done = bf16[16,48,7168]{2,1,0:T(8,128)(2,1)} async-done(((bf16[16,48,7168]{2,1,0:T(8,128)(2,1)}), bf16[16,48,7168]{2,1,0:T(8,128)(2,1)}, u32[]{:S(2)}, u32[]{:S(2)}) %all-to-all-start) | async-done | bytes 11010080 | tf_op jit(solution)/shard_map/all_to_all | solution.py:77
  1341.6 12.3 convolution_convert_fusion.1
  1353.9 2.4 fusion.39
  1356.3 19.6 %fusion.3 = bf16[768,7168]{1,0:T(8,128)(2,1)} fusion(bf16[1,1024,7168]{2,1,0:T(8,128)(2,1)} %all-gather.9.cloned.1.call-done, f32[768,1024]{1,0:T(8,128)S(1)} %fusion.39, bf16[768,512]{1,0:T(8,128)(2,1)} %convolution_convert_fusion.1, bf16[2,512,1024]{2,1,0:T(8,128)(2,1)} %all-gather.7.cloned.1.call-done), kind=kOutput, calls=%fused_computation.9 | convolution fusion | flops 12089819136 | bytes 30670848 | tf_op jit(solution)/shard_map/dot_general | solution.py:82
  1376.0 6.5 all-to-all-start.1
  1382.6 248.2 %all-to-all-done.1 = bf16[16,48,7168]{2,1,0:T(8,128)(2,1)} async-done(((bf16[16,48,7168]{2,1,0:T(8,128)(2,1)}), bf16[16,48,7168]{2,1,0:T(8,128)(2,1)}, u32[]{:S(2)}, u32[]{:S(2)}) %all-to-all-start.1) | async-done | bytes 11010080 | tf_op jit(solution)/shard_map/all_to_all | solution.py:83
  1630.8 19.5 %gather_fusion.1 = bf16[512,7168]{1,0:T(8,128)(2,1)} fusion(bf16[768,7168]{1,0:T(8,128)(2,1)} %bitcast.34, s32[1024]{0:T(1024)S(1)} %pad_clamp_fusion), kind=kCustom, calls=%fused_computation.1 | custom fusion | bytes 14682112 | tf_op jit(solution)/shard_map/gather | solution.py:90
  1650.3 9.8 fusion
  (72 shorter events, 8.5 us)
Async XLA Ops:
  6.5 7.4 copy-start.1
  6.5 43.3 %reduce-scatter.2.cloned.1.call-start = ((), (), s32[]{:S(2)}) async-start(), calls=%async_computation.3 | async-start | bytes 22020096 | tf_op jit(solution)/shard_map/reduce_scatter | solution.py:30
  24.5 351.1 %copy-start.3 = (s32[16]{0:T(128)S(1)}, s32[16]{0:T(128)}, u32[]{:S(2)}) copy-start(s32[16]{0:T(128)} %param.13) | copy-start | bytes 196
  24.5 860.5 %all-reduce.4.cloned.1.call-start = ((), (), s32[]{:S(2)}) async-start(), calls=%async_computation.4 | async-start | bytes 2097152 | tf_op jit(solution)/shard_map/psum | solution.py:47
  49.9 321.2 %collective-permute-start = (f32[3584,512]{1,0:T(8,128)}, f32[3584,512]{1,0:T(8,128)}, u32[]{:S(2)}, u32[]{:S(2)}) collective-permute-start(f32[3584,512]{1,0:T(8,128)} %reduce-scatter.2.cloned.1.call-done), channel_id=1, source_target_pairs={{0,2},{2,4},{4,6},{6,8},{8,10},{10,12},{12,14},{14,16},{16,18},{18... | collective-permute-start | bytes 22020104 | tf_op jit(solution)/shard_map/ppermute | solution.py:15
  53.2 629.9 %collective-permute-start.1 = (f32[3584,512]{1,0:T(8,128)}, f32[3584,512]{1,0:T(8,128)}, u32[]{:S(2)}, u32[]{:S(2)}) collective-permute-start(f32[3584,512]{1,0:T(8,128)} %reduce-scatter.2.cloned.1.call-done), channel_id=1, source_target_pairs={{2,0},{4,2},{6,4},{8,6},{10,8},{12,10},{14,12},{16,14},{18,16},{20... | collective-permute-start | bytes 22020104 | tf_op jit(solution)/shard_map/ppermute | solution.py:15
  56.6 626.6 %collective-permute-start.2 = (f32[3584,512]{1,0:T(8,128)}, f32[3584,512]{1,0:T(8,128)}, u32[]{:S(2)}, u32[]{:S(2)}) collective-permute-start(f32[3584,512]{1,0:T(8,128)} %reduce-scatter.2.cloned.1.call-done), channel_id=1, source_target_pairs={{0,4},{2,6},{4,8},{6,10},{8,12},{10,14},{12,16},{14,18},{16,20},{1... | collective-permute-start | bytes 22020104 | tf_op jit(solution)/shard_map/ppermute | solution.py:15
  57.9 626.2 %collective-permute-start.3 = (f32[3584,512]{1,0:T(8,128)}, f32[3584,512]{1,0:T(8,128)}, u32[]{:S(2)}, u32[]{:S(2)}) collective-permute-start(f32[3584,512]{1,0:T(8,128)} %reduce-scatter.2.cloned.1.call-done), channel_id=1, source_target_pairs={{4,0},{6,2},{8,4},{10,6},{12,8},{14,10},{16,12},{18,14},{20,16},{2... | collective-permute-start | bytes 22020104 | tf_op jit(solution)/shard_map/ppermute | solution.py:15
  65.5 768.9 %collective-permute-start.4 = (f32[3584,512]{1,0:T(8,128)}, f32[3584,512]{1,0:T(8,128)}, u32[]{:S(2)}, u32[]{:S(2)}) collective-permute-start(f32[3584,512]{1,0:T(8,128)} %reduce-scatter.2.cloned.1.call-done), channel_id=1, source_target_pairs={{0,6},{2,8},{4,10},{6,12},{8,14},{10,16},{12,18},{14,20},{16,22},{... | collective-permute-start | bytes 22020104 | tf_op jit(solution)/shard_map/ppermute | solution.py:15
  371.1 463.3 %collective-permute-start.5 = (f32[3584,512]{1,0:T(8,128)}, f32[3584,512]{1,0:T(8,128)}, u32[]{:S(2)}, u32[]{:S(2)}) collective-permute-start(f32[3584,512]{1,0:T(8,128)} %reduce-scatter.2.cloned.1.call-done), channel_id=1, source_target_pairs={{6,0},{8,2},{10,4},{12,6},{14,8},{16,10},{18,12},{20,14},{22,16},{... | collective-permute-start | bytes 22020104 | tf_op jit(solution)/shard_map/ppermute | solution.py:15
  864.1 226.6 %all-gather.5.cloned.1.call-start = ((), (), s32[]{:S(2)}) async-start(), calls=%async_computation.5 | async-start | bytes 11010048 | tf_op jit(solution)/shard_map/all_gather | solution.py:52
  888.1 1.0 copy-start
  911.8 133.4 %slice-start = ((s8[7340032]{0:T(1024)(128)(4,1)}), s8[3145728]{0:T(1024)(128)(4,1)S(1)}, s32[]{:S(2)}) async-start(s8[7340032]{0:T(1024)(128)(4,1)} %bitcast.141), calls=%async_computation.8 | async-start | bytes 6291456
  1037.9 7.3 slice-start.1
  1065.6 4.2 copy-start.4
  1067.8 3.9 copy-start.2
  1083.8 257.9 %all-to-all-start = ((bf16[16,48,7168]{2,1,0:T(8,128)(2,1)}), bf16[16,48,7168]{2,1,0:T(8,128)(2,1)}, u32[]{:S(2)}, u32[]{:S(2)}) async-start(bf16[16,48,7168]{2,1,0:T(8,128)(2,1)} %bitcast.146), calls=%async_computation | async-start | bytes 22020096 | tf_op jit(solution)/shard_map/all_to_all | solution.py:77
  1090.7 263.2 %all-gather.7.cloned.1.call-start = ((), (), s32[]{:S(2)}) async-start(), calls=%async_computation.6 | async-start | bytes 3145728 | tf_op jit(solution)/shard_map/all_gather | solution.py:62
  1090.7 9.3 copy-start.6
  1107.4 248.9 %all-gather.9.cloned.1.call-start = ((), (), s32[]{:S(2)}) async-start(), calls=%async_computation.7 | async-start | bytes 22020096 | tf_op jit(solution)/shard_map/all_gather | solution.py:63
  1376.0 6.5 copy-start.5
  1376.0 254.8 %all-to-all-start.1 = ((bf16[16,48,7168]{2,1,0:T(8,128)(2,1)}), bf16[16,48,7168]{2,1,0:T(8,128)(2,1)}, u32[]{:S(2)}, u32[]{:S(2)}) async-start(bf16[16,48,7168]{2,1,0:T(8,128)(2,1)} %bitcast.147), calls=%async_computation.2 | async-start | bytes 22020096 | tf_op jit(solution)/shard_map/all_to_all | solution.py:83
Sparse Core Ops, SparseCore 0:
  24.6 25.1 reduce-scatter.1
  864.2 20.7 all-reduce.3
  1070.0 19.4 all-gather.4
  1107.6 11.7 all-gather.6
  1120.8 28.1 all-gather.8
where the time goes:
time: 1670 us
  waiting for transfers between devices  1280 us (77%)
  other arithmetic  151 us (9%)
  matrix products  124 us (7%)
  local copies, waits for them, and re-layouts  50.2 us (3%)
  starting transfers between devices  35.1 us (2%)
  between operations  24.1 us (1%)
    ppermute x6, waiting for transfers between devices, shifted(): lax.ppermute(value, axis, [(source, source + steps) for source in range(i...  755 us
    all_to_all x1, waiting for transfers between devices, on_device(): lax.all_to_all(answers.reshape(experts, capacity, tokens.shape[1]), 'expe...  248 us
    all_to_all x1, waiting for transfers between devices, on_device(): lax.all_to_all(outgoing, 'expert', split_axis=0, concat_axis=0, tiled=True)  234 us
    another operation x14, other arithmetic, on_device(): factor = jnp.linalg.cholesky(gram)  80.7 us
    another operation x3, other arithmetic, on_device(): jax.scipy.linalg.solve_triangular(factor, summed.T, lower=True)  42.6 us
  transfers between devices with their start and end apart: 13, of which 8 were waited for; matrix products, arithmetic and copies ran while one was open for 3% of the time, Pallas kernels for 0%

commit v1 on v0

v1 whole, which is shorter than its diff:
```python
import jax
import jax.numpy as jnp
from jax import lax
from jax.sharding import PartitionSpec as P

MOST = 4


HIGHEST = lax.Precision.HIGHEST


def swap_in_group(value, mask):
    count = lax.axis_size("expert")
    return lax.ppermute(value, "expert", [(source, source ^ mask) for source in range(count)])


def shift_groups(value, steps):
    count = lax.axis_size("expert")
    moves = [(s, s + steps) for s in range(count) if 0 <= s + steps < count]
    return lax.ppermute(value, "expert", moves)


def cluster_rows(own, clusters):
    experts = lax.axis_size("expert")
    position = lax.axis_index("expert")
    place = position % MOST
    first = position - place
    got = [lax.dynamic_index_in_dim(own, place, 0, keepdims=False)]
    for mask in range(1, MOST):
        block = lax.dynamic_index_in_dim(own, place ^ mask, 0, keepdims=False)
        got.append(swap_in_group(block, mask))
    wide = [value.astype(jnp.float32) for value in got]
    names = [clusters[first + (place ^ mask)] for mask in range(MOST)]
    head_name, tail_name = clusters[first], clusters[first + MOST - 1]

    def chosen(name):
        return sum(jnp.where(names[k] == name, wide[k], 0.0) for k in range(MOST))

    from_below = shift_groups(chosen(tail_name).astype(jnp.bfloat16), MOST).astype(jnp.float32)
    from_above = shift_groups(chosen(head_name).astype(jnp.bfloat16), -MOST).astype(jnp.float32)
    below_name = jnp.where(first > 0, clusters[jnp.maximum(first - 1, 0)], -1)
    above_name = jnp.where(
        first + MOST < experts, clusters[jnp.minimum(first + MOST, experts - 1)], -1
    )
    back = []
    for mask in range(MOST):
        total = chosen(names[mask])
        total = total + jnp.where(names[mask] == below_name, from_below, 0.0)
        total = total + jnp.where(names[mask] == above_name, from_above, 0.0)
        total = total.astype(jnp.bfloat16)
        back.append(total if mask == 0 else swap_in_group(total, mask))
    stacked = jnp.stack(back)
    order = jnp.arange(MOST, dtype=jnp.int32) ^ place
    return stacked[order]


def on_device(tokens, gate_weight, up_weight, down_weight, sketch, clusters, routes, route_weights):
    experts = lax.axis_size("expert")
    position = lax.axis_index("expert")
    half = lax.axis_index("dp")
    dps = lax.axis_size("dp")
    gate_rows = gate_weight[0]
    up_rows = up_weight[0]
    depth, rank = gate_rows.shape[0], sketch.shape[-1]
    gathered = lax.all_gather(tokens, "expert", axis=0, tiled=True)
    down_rows = lax.all_gather(down_weight[0], "dp", axis=0, tiled=True)
    names = jnp.arange(experts, dtype=jnp.int32)
    shares = jnp.sum(
        jnp.where(routes[:, :, None] == names, route_weights[:, :, None], 0.0), axis=1
    )
    all_shares = lax.all_gather(shares, "expert", axis=0, tiled=True)
    share = lax.dynamic_slice_in_dim(all_shares, position, 1, axis=1)

    sketched = jnp.dot(gate_rows, sketch[0, 0], preferred_element_type=jnp.float32) + jnp.dot(
        up_rows, sketch[0, 1], preferred_element_type=jnp.float32
    )
    own_sketch = lax.psum_scatter(
        sketched.astype(jnp.bfloat16), "dp", scatter_dimension=0, tiled=True
    )
    blocks = own_sketch.reshape(MOST, depth // dps // MOST, rank)
    summed_half = cluster_rows(blocks, clusters).reshape(depth // dps, rank)
    summed = lax.all_gather(summed_half, "dp", axis=0, tiled=True)

    def crossed(right):
        return lax.dot_general(
            summed, right, (((0,), (0,)), ((), ())), preferred_element_type=jnp.float32
        )

    gram = lax.psum(crossed(summed), "tensor")
    raw = lax.psum(jnp.stack([crossed(gate_rows), crossed(up_rows)]), "tensor")
    raw_projected = lax.psum(
        jnp.dot(gathered, summed, preferred_element_type=jnp.float32), "tensor"
    )
    factor = jnp.linalg.cholesky(gram)
    inverse = jax.scipy.linalg.solve_triangular(
        factor, jnp.eye(rank, dtype=jnp.float32), lower=True
    )
    coeff_half = jnp.einsum("rs,gsh->grh", inverse, raw, precision=HIGHEST).astype(jnp.bfloat16)
    coefficients = lax.all_gather(coeff_half, "dp", axis=2, tiled=True)
    projected = lax.dot_general(
        raw_projected, inverse, (((1,), (1,)), ((), ())), precision=HIGHEST
    ).astype(jnp.bfloat16)
    gate_part = jnp.dot(projected, coefficients[0], preferred_element_type=jnp.float32)
    up_part = jnp.dot(projected, coefficients[1], preferred_element_type=jnp.float32)
    hidden = (jax.nn.silu(gate_part) * up_part).astype(jnp.bfloat16)
    answers = jnp.dot(hidden, down_rows, preferred_element_type=jnp.float32)
    weighted = (answers * share).astype(jnp.bfloat16)
    return lax.psum_scatter(weighted, "expert", scatter_dimension=0, tiled=True)


def solution(mesh):
    return jax.shard_map(
        on_device,
        mesh=mesh,
        in_specs=(
            P(("expert", "dp"), "tensor"),
            P("expert", "tensor", "dp"),
            P("expert", "tensor", "dp"),
            P("expert", "dp", "tensor"),
            P("expert", None, "dp", None),
            P(),
            P(("expert", "dp"), None),
            P(("expert", "dp"), None),
        ),
        out_specs=P(("expert", "dp"), "tensor"),
        check_vma=False,
    )
```

time: 1670 us -> 792 us (0.47)
  the two profiles are of different devices: /device:TPU:28 before, /device:TPU:0 now
where the time goes in v1:
time: 792 us; the launch traced here: 783 us
  waiting for transfers between devices  407 us (51%)
  other arithmetic  140 us (18%)
  matrix products  113 us (14%)
  between operations  47.8 us (6%)
  blocking collectives  41.5 us (5%)
  local copies, waits for them, and re-layouts  20.5 us (3%)
  starting transfers between devices  13 us (2%)
    reduce_scatter x1, waiting for transfers between devices, on_device(): return lax.psum_scatter(weighted, 'expert', scatter_dimension=0, tiled=True)  300 us
    another operation x14, other arithmetic, on_device(): factor = jnp.linalg.cholesky(gram)  87.1 us
    ppermute x6, waiting for transfers between devices, swap_in_group(): lax.ppermute(value, 'expert', [(source, source ^ mask) for source in rang...  67.8 us
    all_gather x1, blocking collectives, on_device(): all_shares = lax.all_gather(shares, 'expert', axis=0, tiled=True)  41.5 us
    another operation x3, other arithmetic, on_device(): jax.scipy.linalg.solve_triangular(factor, jnp.eye(rank, dtype=jnp.float32...  40.3 us
    dot_general x1, matrix products, on_device(): answers = jnp.dot(hidden, down_rows, preferred_element_type=jnp.float32)  25.9 us
    dot_general x3, matrix products, crossed(): lax.dot_general(summed, right, (((0,), (0,)), ((), ())), preferred_elemen...  22.6 us
    reduce_scatter x1, waiting for transfers between devices, on_device(): lax.psum_scatter(sketched.astype(jnp.bfloat16), 'dp', scatter_dimension=0...  18.5 us
  transfers between devices with their start and end apart: 14, of which 8 were waited for; matrix products, arithmetic and copies ran while one was open for 27% of the time, Pallas kernels for 0%

profile of v1, /device:TPU:0, one launch (start us, length us, event | category | flops | bytes accessed | tf_op | source)
XLA Modules:
  0.0 783.0 jit_solution(13528425324193972722)
XLA Ops:
  6.5 12.5 %fusion.6 = f32[7168,512]{1,0:T(8,128)} fusion(bf16[1,7168,512]{2,1,0:T(8,128)(2,1)} %param.9, bf16[1,2,512,512]{3,2,1,0:T(8,128)(2,1)} %param.12), kind=kOutput, calls=%fused_computation.11 | convolution fusion | flops 3758096384 | bytes 22544384 | tf_op jit(solution)/shard_map/dot_general | solution.py:74
  19.0 9.2 %add_convert_fusion = bf16[7168,512]{1,0:T(8,128)(2,1)} fusion(f32[7168,512]{1,0:T(8,128)} %fusion.6, bf16[1,7168,512]{2,1,0:T(8,128)(2,1)S(1)} %copy-done, bf16[1,2,512,512]{3,2,1,0:T(8,128)(2,1)S(1)} %copy-done.2), kind=kOutput, calls=%fused_computation.5 | convolution fusion | flops 3765436416 | bytes 29884416 | tf_op jit(solution)/shard_map/dot_general | solution.py:74
  28.4 18.5 %reduce-scatter.3.cloned.1.call-done = bf16[3584,512]{1,0:T(8,128)(2,1)} async-done(((bf16[7168,512]{1,0:T(8,128)(2,1)}), bf16[3584,512]{1,0:T(8,128)(2,1)}) %reduce-scatter.3.cloned.1.call-update) | async-done | bytes 3670032 | tf_op jit(solution)/shard_map/reduce_scatter | solution.py:77
  46.9 3.4 dynamic-slice_bitcast_fusion
  50.2 1.7 collective-permute-start
  51.9 1.5 collective-permute-start.1
  53.7 0.7 fusion.95
  64.4 9.2 %collective-permute-done = bf16[896,512]{1,0:T(8,128)(2,1)S(1)} collective-permute-done((bf16[896,512]{1,0:T(8,128)(2,1)}, bf16[896,512]{1,0:T(8,128)(2,1)S(1)}, u32[]{:S(2)}, u32[]{:S(2)}) %collective-permute-start) | collective-permute-done | bytes 917536 | tf_op jit(solution)/shard_map/ppermute | solution.py:14
  73.6 20.6 %collective-permute-done.1 = bf16[896,512]{1,0:T(8,128)(2,1)S(1)} collective-permute-done((bf16[896,512]{1,0:T(8,128)(2,1)}, bf16[896,512]{1,0:T(8,128)(2,1)S(1)}, u32[]{:S(2)}, u32[]{:S(2)}) %collective-permute-start.1) | collective-permute-done | bytes 917536 | tf_op jit(solution)/shard_map/ppermute | solution.py:14
  94.2 3.6 fusion.31
  97.8 4.2 collective-permute-start.3
  102.0 1.3 collective-permute-start.4
  124.5 1.3 collective-permute-done.4
  125.7 3.3 fusion.55
  129.1 1.5 collective-permute-start.5
  130.5 3.3 fusion.20
  134.1 1.9 collective-permute-start.7
  136.1 16.4 %collective-permute-done.5 = bf16[896,512]{1,0:T(8,128)(2,1)S(1)} collective-permute-done((bf16[896,512]{1,0:T(8,128)(2,1)S(1)}, bf16[896,512]{1,0:T(8,128)(2,1)S(1)}, u32[]{:S(2)}, u32[]{:S(2)}) %collective-permute-start.5) | collective-permute-done | bytes 917536 | tf_op jit(solution)/shard_map/ppermute | solution.py:14
  152.4 21.6 %collective-permute-done.6 = bf16[896,512]{1,0:T(8,128)(2,1)S(1)} collective-permute-done((bf16[896,512]{1,0:T(8,128)(2,1)S(1)}, bf16[896,512]{1,0:T(8,128)(2,1)S(1)}, u32[]{:S(2)}, u32[]{:S(2)}) %collective-permute-start.6) | collective-permute-done | bytes 917536 | tf_op jit(solution)/shard_map/ppermute | solution.py:14
  174.0 2.0 pad_maximum_fusion
  176.0 4.6 gather_fusion
  181.0 0.4 all-gather.9.cloned.1.call-update
  181.7 17.8 %all-gather.7.cloned.1.call-done = bf16[7168,512]{1,0:T(8,128)(2,1)} async-done(((bf16[3584,512]{1,0:T(8,128)(2,1)}), bf16[7168,512]{1,0:T(8,128)(2,1)}) %all-gather.7.cloned.1.call-update) | async-done | bytes 7340048 | tf_op jit(solution)/shard_map/all_gather | solution.py:82
  199.4 8.7 %fusion.97 = f32[512,512]{1,0:T(8,128)S(1)} fusion(bf16[7168,512]{1,0:T(8,128)(2,1)} %all-gather.7.cloned.1.call-done), kind=kOutput, calls=%fused_computation.174 | convolution fusion | flops 3758096384 | bytes 8388608 | tf_op jit(solution)/shard_map/dot_general | solution.py:85
  208.7 1.0 copy-done.1
  209.7 11.7 %cholesky.104 = f32[128,128]{1,0:T(8,128)S(1)} custom-call(f32[128,128]{1,0:T(8,128)S(1)} %cholesky.266), custom_call_target="Cholesky" | custom-call | tf_op jit(solution)/shard_map/jit(cholesky)/cholesky | solution.py:94
  221.6 9.8 %custom-call.31 = f32[1,128,128]{1,2,0:T(8,128)S(1)} custom-call(f32[1,128,128]{2,1,0:T(8,128)S(1)} %get-tuple-element.41), custom_call_target="InvertDiagBlocksLowerTriangular" | custom-call | tf_op jit(solution)/shard_map/jit(cholesky)/cholesky | solution.py:94
  231.4 1.2 constant_dynamic-update-slice_fusion
  232.7 1.3 convolution_subtract_fusion.3
  233.9 11.7 %cholesky.217 = f32[128,128]{1,0:T(8,128)S(1)} custom-call(f32[128,128]{1,0:T(8,128)S(1)} %cholesky.270), custom_call_target="Cholesky" | custom-call | tf_op jit(solution)/shard_map/jit(cholesky)/cholesky | solution.py:94
  245.7 18.5 %custom-call.32 = f32[1,128,128]{1,2,0:T(8,128)S(1)} custom-call(f32[1,128,128]{2,1,0:T(8,128)S(1)} %get-tuple-element.38), custom_call_target="InvertDiagBlocksLowerTriangular" | custom-call | tf_op jit(solution)/shard_map/jit(cholesky)/cholesky | solution.py:94
  264.5 1.3 convolution_subtract_fusion.4
  265.8 11.7 %cholesky.238 = f32[128,128]{1,0:T(8,128)S(1)} custom-call(f32[128,128]{1,0:T(8,128)S(1)} %cholesky.275), custom_call_target="Cholesky" | custom-call | tf_op jit(solution)/shard_map/jit(cholesky)/cholesky | solution.py:94
  277.5 9.8 %custom-call.33 = f32[1,128,128]{1,2,0:T(8,128)S(1)} custom-call(f32[1,128,128]{2,1,0:T(8,128)S(1)} %get-tuple-element.35), custom_call_target="InvertDiagBlocksLowerTriangular" | custom-call | tf_op jit(solution)/shard_map/jit(cholesky)/cholesky | solution.py:94
  287.6 1.2 convolution_subtract_fusion.5
  288.8 11.7 %cholesky.255 = f32[128,128]{1,0:T(8,128)S(1)} custom-call(f32[128,128]{1,0:T(8,128)S(1)} %convolution_subtract_fusion.5), custom_call_target="Cholesky" | custom-call | tf_op jit(solution)/shard_map/jit(cholesky)/cholesky | solution.py:94
  300.5 0.7 compare_reduce_fusion.2
  302.4 0.7 compare_reduce_fusion.1
  303.7 0.7 compare_reduce_fusion
  305.2 10.4 %while.1 = (s32[]{:T(128)}, f32[512,512]{1,0:T(8,128)S(1)}, s32[4,2]{0,1:T(2,128)S(1)}, f32[4,128,128]{2,1,0:T(8,128)}, s32[]{:T(128)}) while((s32[]{:T(128)}, f32[512,512]{1,0:T(8,128)S(1)}, s32[4,2]{0,1:T(2,128)S(1)}, f32[4,128,128]{2,1,0:T(8,128)}, s32[]{:T(128)}) %tuple.39), condition=%wide.while_cond, body=%wide.while_body.sunk | while | flops 2 | bytes 132705 | solution.py:95
  305.5 0.6 fusion.113
  306.0 1.9 bitcast_dynamic-update-slice_fusion.2
  308.0 0.6 fusion.113
  308.6 1.9 bitcast_dynamic-update-slice_fusion.2
  310.5 0.6 fusion.113
  311.1 1.9 bitcast_dynamic-update-slice_fusion.2
  313.1 0.6 fusion.113
  313.6 1.9 bitcast_dynamic-update-slice_fusion.2
  315.5 40.1 %custom-call.34 = f32[4,128,128]{1,2,0:T(8,128)S(1)} custom-call(f32[4,128,128]{2,1,0:T(8,128)} %get-tuple-element.12), custom_call_target="InvertDiagBlocksLowerTriangular" | custom-call | tf_op jit(solution)/shard_map/jit(_solve_triangular)/triangular_solve | solution.py:95
  356.4 0.4 fusion.82
  356.8 0.4 convolution_subtract_fusion
  357.3 1.3 fusion.80
  358.6 0.6 convolution_subtract_fusion.2
  359.2 1.6 fusion.79
  360.8 9.9 %fusion.46 = f32[1,512,512]{2,1,0:T(8,128)S(1)} fusion(bf16[7168,512]{1,0:T(8,128)(2,1)} %all-gather.7.cloned.1.call-done, bf16[1,7168,512]{2,1,0:T(8,128)(2,1)} %param.9), kind=kOutput, calls=%fused_computation.82 | convolution fusion | flops 3758096384 | bytes 15728640 | tf_op jit(solution)/shard_map/dot_general | solution.py:85
  370.8 4.0 fusion.49
  374.7 7.9 %fusion.43 = bf16[2,512,512]{1,2,0:T(8,128)(2,1)} fusion(f32[1,512,512]{2,1,0:T(8,128)S(1)} %fusion.49, f32[1,512,512]{2,1,0:T(8,128)S(1)} %fusion.46, f32[128,512]{1,0:T(8,128)S(1)} %fusion.79, f32[128,512]{1,0:T(8,128)S(1)} %fusion.80, f32[128,512]{1,0:T(8,128)S(1)} %fusion.82, f32[128,512]{1,0:T(8,128)S(1)} %fusion.70), kind=kOutput, calls=%fused_computation.81 | convolution fusion | flops 3223060480 | bytes 4194304 | tf_op jit(solution)/shard_map/rs,gsh->grh/dot_general | solution.py:98
  382.7 0.5 all-gather.13.cloned.1.call-update
  383.3 41.5 %all-gather.1 = f32[16,64,16]{1,2,0:T(8,128)S(1)} all-gather(f32[1,64,16]{1,2,0:T(8,128)S(1)} %bitcast.143), channel_id=1, replica_groups=mesh['expert'=16,'tensor'=1,'dp'=2] {'expert'}, dimensions={0}, use_global_device_ids=true | all-gather | bytes 69632 | tf_op jit(solution)/shard_map/all_gather | solution.py:71
  425.1 13.4 %fusion.96 = f32[512,1024]{1,0:T(8,128)S(1)} fusion(bf16[7168,512]{1,0:T(8,128)(2,1)} %all-gather.7.cloned.1.call-done, bf16[1024,7168]{1,0:T(8,128)(2,1)} %all-gather.9.cloned.1.call-done), kind=kOutput, calls=%fused_computation.173 | convolution fusion | flops 7516192768 | bytes 24117248 | tf_op jit(solution)/shard_map/dot_general | solution.py:92
  438.4 6.9 convolution_convert_fusion
  445.4 4.4 fusion.52
  449.8 25.9 %multiply_convert_fusion = bf16[1024,7168]{1,0:T(8,128)(2,1)} fusion(bf16[1,1024,7168]{2,1,0:T(8,128)(2,1)} %all-gather.13.cloned.1.call-done, f32[1024]{0:T(1024)S(1)} %bitcast.144, f32[1024,1024]{1,0:T(8,128)} %fusion.52, bf16[1024,512]{1,0:T(8,128)(2,1)S(1)} %convolution_convert_fusion, bf16[2,512,1024]{1,2,0:T(8,128)(2,1)} %all-gather.11.cloned.1.call-done), kind=kOutput, calls=%fused_computation.3 | convolution fusion | flops 16127098880 | bytes 35655680 | tf_op jit(solution)/shard_map/dot_general | solution.py:106
  475.8 300.2 %reduce-scatter.5.cloned.1.call-done = bf16[64,7168]{1,0:T(8,128)(2,1)} async-done(((bf16[1024,7168]{1,0:T(8,128)(2,1)}), bf16[64,7168]{1,0:T(8,128)(2,1)}) %reduce-scatter.5.cloned.1.call-update) | async-done | bytes 917520 | tf_op jit(solution)/shard_map/reduce_scatter | solution.py:108
  (71 shorter events, 4.0 us)
Async XLA Ops:
  6.5 12.5 %copy-start.2 = (bf16[1,2,512,512]{3,2,1,0:T(8,128)(2,1)S(1)}, bf16[1,2,512,512]{3,2,1,0:T(8,128)(2,1)}, u32[]{:S(2)}) copy-start(bf16[1,2,512,512]{3,2,1,0:T(8,128)(2,1)} %param.12) | copy-start | bytes 3145732
  6.5 40.3 %reduce-scatter.3.cloned.1.call-start = ((), (), s32[]{:S(2)}) async-start(), calls=%async_computation.2 | async-start | bytes 11010048 | tf_op jit(solution)/shard_map/reduce_scatter | solution.py:77
  6.5 12.5 %copy-start = (bf16[1,7168,512]{2,1,0:T(8,128)(2,1)S(1)}, bf16[1,7168,512]{2,1,0:T(8,128)(2,1)}, u32[]{:S(2)}) copy-start(bf16[1,7168,512]{2,1,0:T(8,128)(2,1)} %param.10) | copy-start | bytes 22020100
  28.3 171.2 %all-gather.7.cloned.1.call-start = ((), (), s32[]{:S(2)}) async-start(), calls=%async_computation.3 | async-start | bytes 11010048 | tf_op jit(solution)/shard_map/all_gather | solution.py:82
  46.9 6.9 copy-start.4
  50.2 23.4 %collective-permute-start = (bf16[896,512]{1,0:T(8,128)(2,1)}, bf16[896,512]{1,0:T(8,128)(2,1)S(1)}, u32[]{:S(2)}, u32[]{:S(2)}) collective-permute-start(bf16[896,512]{1,0:T(8,128)(2,1)} %get-tuple-element.31), channel_id=1, source_target_pairs={{0,2},{2,0},{4,6},{6,4},{8,10},{10,8},{12,14},{14,12},{16,18},{18,... | collective-permute-start | bytes 2752520 | tf_op jit(solution)/shard_map/ppermute | solution.py:14
  51.9 42.3 %collective-permute-start.1 = (bf16[896,512]{1,0:T(8,128)(2,1)}, bf16[896,512]{1,0:T(8,128)(2,1)S(1)}, u32[]{:S(2)}, u32[]{:S(2)}) collective-permute-start(bf16[896,512]{1,0:T(8,128)(2,1)} %get-tuple-element.30), channel_id=1, source_target_pairs={{0,4},{2,6},{4,0},{6,2},{8,12},{10,14},{12,8},{14,10},{16,20},{18,... | collective-permute-start | bytes 2752520 | tf_op jit(solution)/shard_map/ppermute | solution.py:14
  53.4 40.8 %collective-permute-start.2 = (bf16[896,512]{1,0:T(8,128)(2,1)}, bf16[896,512]{1,0:T(8,128)(2,1)S(1)}, u32[]{:S(2)}, u32[]{:S(2)}) collective-permute-start(bf16[896,512]{1,0:T(8,128)(2,1)} %get-tuple-element.29), channel_id=1, source_target_pairs={{0,6},{2,4},{4,2},{6,0},{8,14},{10,12},{12,10},{14,8},{16,22},{18,... | collective-permute-start | bytes 2752520 | tf_op jit(solution)/shard_map/ppermute | solution.py:14
  97.8 26.6 %collective-permute-start.3 = (bf16[896,512]{1,0:T(8,128)(2,1)}, bf16[896,512]{1,0:T(8,128)(2,1)}, u32[]{:S(2)}, u32[]{:S(2)}) collective-permute-start(bf16[896,512]{1,0:T(8,128)(2,1)} %get-tuple-element.28), channel_id=1, source_target_pairs={{0,8},{2,10},{4,12},{6,14},{8,16},{10,18},{12,20},{14,22},{16,24},... | collective-permute-start | bytes 2752520 | tf_op jit(solution)/shard_map/ppermute | solution.py:20
  102.0 23.8 %collective-permute-start.4 = (bf16[896,512]{1,0:T(8,128)(2,1)}, bf16[896,512]{1,0:T(8,128)(2,1)}, u32[]{:S(2)}, u32[]{:S(2)}) collective-permute-start(bf16[896,512]{1,0:T(8,128)(2,1)} %get-tuple-element.27), channel_id=1, source_target_pairs={{8,0},{10,2},{12,4},{14,6},{16,8},{18,10},{20,12},{22,14},{24,16},... | collective-permute-start | bytes 2752520 | tf_op jit(solution)/shard_map/ppermute | solution.py:20
  129.1 23.4 %collective-permute-start.5 = (bf16[896,512]{1,0:T(8,128)(2,1)S(1)}, bf16[896,512]{1,0:T(8,128)(2,1)S(1)}, u32[]{:S(2)}, u32[]{:S(2)}) collective-permute-start(bf16[896,512]{1,0:T(8,128)(2,1)S(1)} %get-tuple-element.24), channel_id=1, source_target_pairs={{0,2},{2,0},{4,6},{6,4},{8,10},{10,8},{12,14},{14,12},{16,18},{18,... | collective-permute-start | bytes 2752520 | tf_op jit(solution)/shard_map/ppermute | solution.py:14
  133.9 40.1 %collective-permute-start.6 = (bf16[896,512]{1,0:T(8,128)(2,1)S(1)}, bf16[896,512]{1,0:T(8,128)(2,1)S(1)}, u32[]{:S(2)}, u32[]{:S(2)}) collective-permute-start(bf16[896,512]{1,0:T(8,128)(2,1)S(1)} %get-tuple-element.25), channel_id=1, source_target_pairs={{0,4},{2,6},{4,0},{6,2},{8,12},{10,14},{12,8},{14,10},{16,20},{18,... | collective-permute-start | bytes 2752520 | tf_op jit(solution)/shard_map/ppermute | solution.py:14
  134.1 39.9 %collective-permute-start.7 = (bf16[896,512]{1,0:T(8,128)(2,1)S(1)}, bf16[896,512]{1,0:T(8,128)(2,1)S(1)}, u32[]{:S(2)}, u32[]{:S(2)}) collective-permute-start(bf16[896,512]{1,0:T(8,128)(2,1)S(1)} %get-tuple-element.26), channel_id=1, source_target_pairs={{0,6},{2,4},{4,2},{6,0},{8,14},{10,12},{12,10},{14,8},{16,22},{18,... | collective-permute-start | bytes 2752520 | tf_op jit(solution)/shard_map/ppermute | solution.py:14
  180.7 244.4 %all-gather.9.cloned.1.call-start = ((), (), s32[]{:S(2)}) async-start(), calls=%async_computation.4 | async-start | bytes 15597568 | tf_op jit(solution)/shard_map/all_gather | solution.py:65
  181.4 263.9 %all-gather.11.cloned.1.call-start = ((), (), s32[]{:S(2)}) async-start(), calls=%async_computation.5 | async-start | bytes 3145728 | tf_op jit(solution)/shard_map/all_gather | solution.py:99
  208.7 1.0 copy-start.1
  355.7 0.7 copy-start.3
  358.5 12.2 %slice-start = ((s8[7340032]{0:T(1024)(128)(4,1)}), s8[4194304]{0:T(1024)(128)(4,1)S(1)}, s32[]{:S(2)}) async-start(s8[7340032]{0:T(1024)(128)(4,1)} %bitcast.133), calls=%async_computation.8 | async-start | bytes 8388608
  358.5 12.2 %slice-start.2 = ((s8[7340032]{0:T(1024)(128)(4,1)}), s8[4194304]{0:T(1024)(128)(4,1)S(1)}, s32[]{:S(2)}) async-start(s8[7340032]{0:T(1024)(128)(4,1)} %bitcast.145), calls=%async_computation.10 | async-start | bytes 8388608
  360.8 10.0 %slice-start.1 = ((s8[7340032]{0:T(1024)(128)(4,1)}), s8[3145728]{0:T(1024)(128)(4,1)S(1)}, s32[]{:S(2)}) async-start(s8[7340032]{0:T(1024)(128)(4,1)} %bitcast.133), calls=%async_computation.9 | async-start | bytes 6291456
  360.8 10.0 %slice-start.3 = ((s8[7340032]{0:T(1024)(128)(4,1)}), s8[3145728]{0:T(1024)(128)(4,1)S(1)}, s32[]{:S(2)}) async-start(s8[7340032]{0:T(1024)(128)(4,1)} %bitcast.145), calls=%async_computation.11 | async-start | bytes 6291456
  382.6 0.7 copy-start.5
  382.6 0.7 copy-start.6
  382.6 67.2 %all-gather.13.cloned.1.call-start = ((), (), s32[]{:S(2)}) async-start(), calls=%async_computation.7 | async-start | bytes 22020096 | tf_op jit(solution)/shard_map/all_gather | solution.py:66
  383.2 392.7 %reduce-scatter.5.cloned.1.call-start = ((), (), s32[]{:S(2)}) async-start(), calls=%async_computation.6 | async-start | bytes 15597568 | tf_op jit(solution)/shard_map/reduce_scatter | solution.py:108
Sparse Core Ops, SparseCore 0:
  28.4 18.4 reduce-scatter.2
  180.8 18.6 all-gather.6
  202.6 173.3 all-gather.8
  382.7 11.7 all-gather.10
  396.0 28.1 all-gather.12
  475.9 300.0 reduce-scatter.4

commit v2 on v1

v2 whole, which is shorter than its diff:
```python
import jax
import jax.numpy as jnp
from jax import lax
from jax.sharding import PartitionSpec as P

MOST = 4
CLUSTER_CHUNKS = 2
OUT_CHUNKS = 4

HIGHEST = lax.Precision.HIGHEST
HIGH = lax.Precision.HIGH


def swap_expert(value, mask):
    count = lax.axis_size("expert")
    return lax.ppermute(value, "expert", [(source, source ^ mask) for source in range(count)])


def swap_dp(value):
    count = lax.axis_size("dp")
    return lax.ppermute(value, "dp", [(source, count - 1 - source) for source in range(count)])


def shift_groups(value, steps):
    count = lax.axis_size("expert")
    moves = [(s, s + steps) for s in range(count) if 0 <= s + steps < count]
    return lax.ppermute(value, "expert", moves)


def cluster_rows(own, clusters):
    experts = lax.axis_size("expert")
    position = lax.axis_index("expert")
    place = position % MOST
    first = position - place
    wide = [own[0]]
    for mask in range(1, MOST):
        wide.append(swap_expert(own[mask], mask))
    wide = [value.astype(jnp.float32) for value in wide]
    names = [clusters[first + (place ^ mask)] for mask in range(MOST)]
    head_name, tail_name = clusters[first], clusters[first + MOST - 1]

    def chosen(name):
        return sum(jnp.where(names[k] == name, wide[k], 0.0) for k in range(MOST))

    from_below = shift_groups(chosen(tail_name).astype(jnp.bfloat16), MOST).astype(jnp.float32)
    from_above = shift_groups(chosen(head_name).astype(jnp.bfloat16), -MOST).astype(jnp.float32)
    below_name = jnp.where(first > 0, clusters[jnp.maximum(first - 1, 0)], -1)
    above_name = jnp.where(
        first + MOST < experts, clusters[jnp.minimum(first + MOST, experts - 1)], -1
    )
    totals = []
    for mask in range(MOST):
        total = chosen(names[mask])
        total = total + jnp.where(names[mask] == below_name, from_below, 0.0)
        total = total + jnp.where(names[mask] == above_name, from_above, 0.0)
        totals.append(total.astype(jnp.bfloat16))
    return totals


def relative(array, axis, size, index):
    return [
        lax.dynamic_index_in_dim(array, index ^ step, axis, keepdims=False) for step in range(size)
    ]


def on_device(tokens, gate_weight, up_weight, down_weight, sketch, clusters, routes, route_weights):
    experts = lax.axis_size("expert")
    position = lax.axis_index("expert")
    place = position % MOST
    groups = experts // MOST
    half = lax.axis_index("dp")
    dps = lax.axis_size("dp")
    gate_rows = gate_weight[0]
    up_rows = up_weight[0]
    depth, rank = gate_rows.shape[0], sketch.shape[-1]
    rows = depth // dps // MOST
    toks = tokens.shape[0]

    names = jnp.arange(experts, dtype=jnp.int32)
    shares = jnp.sum(
        jnp.where(routes[:, :, None] == names, route_weights[:, :, None], 0.0), axis=1
    )
    all_shares = lax.all_gather(shares, "expert", axis=0, tiled=False)
    share = lax.dynamic_index_in_dim(all_shares, position, 2, keepdims=False)
    share = share[names ^ position]

    down_rows = lax.all_gather(down_weight[0], "dp", axis=0, tiled=True)

    halves = jnp.stack(relative(tokens.reshape(toks, dps, MOST, rows), 1, dps, half), axis=1)
    token_blocks = relative(halves, 2, MOST, place)
    plane = [token_blocks[0]]
    for mask in range(1, MOST):
        plane.append(swap_expert(token_blocks[mask], mask))
    plane = jnp.stack(plane)
    spread = [plane]
    for step in range(1, groups):
        spread.append(swap_expert(plane, step * MOST))
    gathered = jnp.stack(spread).reshape(experts * toks, dps * rows)

    sketched = jnp.dot(gate_rows, sketch[0, 0], preferred_element_type=jnp.float32) + jnp.dot(
        up_rows, sketch[0, 1], preferred_element_type=jnp.float32
    )
    sketched = sketched.reshape(dps, MOST, rows, rank)
    own_half, other_half = relative(sketched, 0, dps, half)
    own_half = (own_half + swap_dp(other_half.astype(jnp.bfloat16)).astype(jnp.float32)).astype(
        jnp.bfloat16
    )
    own_blocks = relative(own_half, 0, MOST, place)
    chunk = rows // CLUSTER_CHUNKS
    pieces = [
        cluster_rows([block[c * chunk : (c + 1) * chunk] for block in own_blocks], clusters)
        for c in range(CLUSTER_CHUNKS)
    ]
    wide_pieces, own_pieces = [], []
    for piece in pieces:
        stacked = jnp.stack(piece)
        wide_pieces.append((stacked, swap_dp(stacked)))
        back = jnp.stack(
            [piece[0]] + [swap_expert(piece[mask], mask) for mask in range(1, MOST)]
        )
        own_pieces.append(jnp.stack([back, swap_dp(back)]))
    summed = jnp.concatenate(own_pieces, axis=2)
    group_sums = jnp.concatenate(
        [jnp.stack([own, other], axis=1) for own, other in wide_pieces], axis=2
    ).reshape(MOST, dps * rows, rank)

    parts = [
        jnp.dot(gathered, group_sums[k], preferred_element_type=jnp.float32) for k in range(MOST)
    ]
    raw_projected = parts[0].reshape(groups, MOST, toks, rank)
    for mask in range(1, MOST):
        arrived = swap_expert(parts[mask].astype(jnp.bfloat16), mask)
        arrived = arrived.reshape(groups, MOST, toks, rank).astype(jnp.float32)
        raw_projected = raw_projected + jnp.stack(
            [arrived[:, k ^ mask] for k in range(MOST)], axis=1
        )
    raw_projected = lax.psum(raw_projected.reshape(experts * toks, rank), "tensor")

    summed = jnp.stack(
        relative(jnp.stack(relative(summed, 1, MOST, place), axis=1), 0, dps, half)
    ).reshape(depth, rank)

    def crossed(right):
        return lax.dot_general(
            summed, right, (((0,), (0,)), ((), ())), preferred_element_type=jnp.float32
        )

    gram = lax.psum(crossed(summed), "tensor")
    raw = lax.psum(jnp.stack([crossed(gate_rows), crossed(up_rows)]), "tensor")
    factor = jnp.linalg.cholesky(gram)
    inverse = jax.scipy.linalg.solve_triangular(
        factor, jnp.eye(rank, dtype=jnp.float32), lower=True
    )
    coeff_half = jnp.einsum("rs,gsh->grh", inverse, raw, precision=HIGH).astype(jnp.bfloat16)
    both = jnp.stack([coeff_half, swap_dp(coeff_half)])
    both = relative(both, 0, dps, half)
    coefficients = jnp.concatenate(both, axis=2)
    projected = lax.dot_general(
        raw_projected, inverse, (((1,), (1,)), ((), ())), precision=HIGH
    ).astype(jnp.bfloat16)
    gate_part = jnp.dot(projected, coefficients[0], preferred_element_type=jnp.float32)
    up_part = jnp.dot(projected, coefficients[1], preferred_element_type=jnp.float32)
    hidden = (jax.nn.silu(gate_part) * up_part).astype(jnp.bfloat16)

    width = hidden.shape[1]
    hidden = hidden.reshape(groups, 2, 2, toks, width)
    share = share.reshape(groups, 2, 2, toks)
    chunks = OUT_CHUNKS if depth % (OUT_CHUNKS * 128) == 0 else 1
    cols = depth // chunks
    by_axis = []
    for axis in (2, 1):
        sides = []
        for side in (0, 1):
            picked = lax.index_in_dim(hidden, side, axis, keepdims=False).reshape(-1, width)
            weight = lax.index_in_dim(share, side, axis, keepdims=False).reshape(-1, 1)
            sides.append((picked, weight))
        by_axis.append(sides)

    def answered(side, c):
        picked, weight = side
        value = jnp.dot(
            picked, down_rows[:, c * cols : (c + 1) * cols], preferred_element_type=jnp.float32
        )
        return value * weight

    sent = []
    for c in range(chunks):
        order = c % 2
        outgoing = answered(by_axis[order][1], c).astype(jnp.bfloat16)
        sent.append(swap_expert(outgoing, 1 << order))
    outs = []
    for c in range(chunks):
        order = c % 2
        value = answered(by_axis[order][0], c) + sent[c].astype(jnp.float32)
        value = value.astype(jnp.bfloat16).reshape(groups, 2, toks, cols)
        kept = value[:, 0].astype(jnp.float32) + swap_expert(value[:, 1], 2 >> order).astype(
            jnp.float32
        )
        kept = kept.astype(jnp.bfloat16)
        total = kept[0].astype(jnp.float32)
        for step in range(1, groups):
            total = total + swap_expert(kept[step], step * MOST).astype(jnp.float32)
        outs.append(total.astype(jnp.bfloat16))
    return jnp.concatenate(outs, axis=1)


def solution(mesh):
    return jax.shard_map(
        on_device,
        mesh=mesh,
        in_specs=(
            P(("expert", "dp"), "tensor"),
            P("expert", "tensor", "dp"),
            P("expert", "tensor", "dp"),
            P("expert", "dp", "tensor"),
            P("expert", None, "dp", None),
            P(),
            P(("expert", "dp"), None),
            P(("expert", "dp"), None),
        ),
        out_specs=P(("expert", "dp"), "tensor"),
        check_vma=False,
    )
```

time: 792 us -> 745 us (0.941)
  waiting for transfers between devices: 407 us -> 206 us
  starting transfers between devices: 13 us -> 101 us
  local copies, waits for them, and re-layouts: 20.5 us -> 64.2 us
  other arithmetic: 140 us -> 178 us
  matrix products: 113 us -> 88.1 us
  blocking collectives: 41.5 us -> 49.9 us
    reduce_scatter x2 -> x0, waiting for transfers between devices: 319 us -> none  [the longest x1 300 us: on_device(): return lax.psum_scatter(weighted, 'expert', scatter_dimension=0, tiled=True)]
    ppermute x6 -> x47, waiting for transfers between devices: 67.8 us -> 200 us  [the longest x41 193 us: swap_expert(): lax.ppermute(value, 'expert', [(source, source ^ mask) for source in rang...]
    ppermute x6 -> x47, starting transfers between devices: 7.11 us -> 92.3 us  [the longest x41 90.8 us: swap_expert(): lax.ppermute(value, 'expert', [(source, source ^ mask) for source in rang...]
    another operation x2 -> x8, other arithmetic: 5.33 us -> 29.4 us  [the longest x2 10.4 us: on_device(): gathered = jnp.stack(spread).reshape(experts * toks, dps * rows)]
    another operation x12 -> x19, local copies, waits for them, and re-layouts: 10.2 us -> 31 us
    all_gather x3 -> x0, waiting for transfers between devices: 17.8 us -> none  [the longest x1 17.8 us: on_device(): summed = lax.all_gather(summed_half, 'dp', axis=0, tiled=True)]
    unnamed x23 -> x97, local copies, waits for them, and re-layouts: 1.17 us -> 13.5 us
    dot_general x3 -> x14, matrix products: 47.1 us -> 36.7 us  [the longest x8 19.3 us: answered(): jnp.dot(picked, down_rows[:, c * cols:(c + 1) * cols], preferred_element_...]
  transfers between devices with their start and end apart: 14 -> 52, of which waited for: 8 -> 23; matrix products, arithmetic and copies ran while one was open for 27% -> 39% of each run, Pallas kernels for 0% -> 0%
where the time goes in v2:
time: 745 us; the launch traced here: 736 us
  waiting for transfers between devices  206 us (28%)
  other arithmetic  178 us (24%)
  starting transfers between devices  101 us (14%)
  matrix products  88.1 us (12%)
  local copies, waits for them, and re-layouts  64.2 us (9%)
  blocking collectives  49.9 us (7%)
  between operations  48.4 us (6%)
    ppermute x41, waiting for transfers between devices, swap_expert(): lax.ppermute(value, 'expert', [(source, source ^ mask) for source in rang...  193 us
    ppermute x41, starting transfers between devices, swap_expert(): lax.ppermute(value, 'expert', [(source, source ^ mask) for source in rang...  90.8 us
    another operation x14, other arithmetic, on_device(): factor = jnp.linalg.cholesky(gram)  78.9 us
    all_gather x1, blocking collectives, on_device(): all_shares = lax.all_gather(shares, 'expert', axis=0, tiled=False)  49.9 us
    another operation x3, other arithmetic, on_device(): jax.scipy.linalg.solve_triangular(factor, jnp.eye(rank, dtype=jnp.float32...  41.2 us
    dot_general x8, matrix products, answered(): jnp.dot(picked, down_rows[:, c * cols:(c + 1) * cols], preferred_element_...  19.3 us
    dot_general x3, matrix products, crossed(): lax.dot_general(summed, right, (((0,), (0,)), ((), ())), preferred_elemen...  16.9 us
  transfers between devices with their start and end apart: 52, of which 23 were waited for; matrix products, arithmetic and copies ran while one was open for 39% of the time, Pallas kernels for 0%

profile of v2, /device:TPU:0, one launch (start us, length us, event | category | flops | bytes accessed | tf_op | source)
XLA Modules:
  0.0 735.5 jit_solution(12148188429326411025)
XLA Ops:
  6.5 7.3 fusion.6
  13.8 10.6 %convolution_add_fusion = f32[7168,512]{1,0:T(8,128)} fusion(f32[7168,512]{1,0:T(8,128)S(1)} %fusion.6, bf16[1,7168,512]{2,1,0:T(8,128)(2,1)} %param.10, bf16[1,2,512,512]{3,2,1,0:T(8,128)(2,1)S(1)} %copy-done.27), kind=kOutput, calls=%fused_computation.3 | convolution fusion | flops 3761766400 | bytes 37224448 | tf_op jit(solution)/shard_map/dot_general | solution.py:100
  24.4 5.4 fusion.8
  30.3 6.4 collective-permute-done.6
  36.6 5.5 fusion
  45.3 2.9 collective-permute-start.13
  54.0 5.4 collective-permute-done.13
  59.5 3.0 collective-permute-start.9
  97.9 49.9 %all-gather.2 = f32[16,64,16]{1,2,0:T(8,128)S(1)} all-gather(f32[1,64,16]{1,2,0:T(8,128)S(1)} %bitcast.397), channel_id=3, replica_groups=mesh['expert'=16,'tensor'=1,'dp'=2] {'expert'}, dimensions={0}, use_global_device_ids=true | all-gather | bytes 69632 | tf_op jit(solution)/shard_map/all_gather | solution.py:83
  150.1 2.9 fusion.100
  157.1 4.6 collective-permute-start.16
  163.5 3.4 collective-permute-done.11
  169.4 2.6 collective-permute-done.17
  174.8 3.4 collective-permute-start.24
  184.0 3.7 collective-permute-start.28
  190.2 8.5 %collective-permute-done.23 = bf16[448,512]{1,0:T(8,128)(2,1)S(1)} collective-permute-done((bf16[448,512]{1,0:T(8,128)(2,1)S(1)}, bf16[448,512]{1,0:T(8,128)(2,1)S(1)}, u32[]{:S(2)}, u32[]{:S(2)}) %collective-permute-start.23) | collective-permute-done | bytes 458784 | tf_op jit(solution)/shard_map/ppermute | solution.py:16
  203.6 2.7 fusion.184
  206.3 4.8 collective-permute-done.27
  211.0 3.3 fusion.186
  218.1 2.6 fusion.222
  220.7 10.0 %collective-permute-done.3 = bf16[4,64,2,896]{3,2,1,0:T(2,128)(2,1)S(1)} collective-permute-done((bf16[4,64,2,896]{3,2,1,0:T(2,128)(2,1)}, bf16[4,64,2,896]{3,2,1,0:T(2,128)(2,1)S(1)}, u32[]{:S(2)}, u32[]{:S(2)}) %collective-permute-start.3) | collective-permute-done | bytes 917536 | tf_op jit(solution)/shard_map/ppermute | solution.py:16
  230.6 25.0 %collective-permute-done.4 = bf16[4,64,2,896]{3,2,1,0:T(2,128)(2,1)} collective-permute-done((bf16[4,64,2,896]{3,2,1,0:T(2,128)(2,1)}, bf16[4,64,2,896]{3,2,1,0:T(2,128)(2,1)}, u32[]{:S(2)}, u32[]{:S(2)}) %collective-permute-start.4) | collective-permute-done | bytes 917536 | tf_op jit(solution)/shard_map/ppermute | solution.py:16
  255.6 7.8 %pad_maximum_fusion.2 = bf16[4,4,64,2,896]{4,3,2,1,0:T(2,128)(2,1)S(1)} fusion(bf16[1,4,64,2,896]{4,3,2,1,0:T(2,128)(2,1)} %bitcast.50, bf16[1,4,64,2,896]{4,3,2,1,0:T(2,128)(2,1)} %bitcast.49, bf16[1,4,64,2,896]{4,3,2,1,0:T(2,128)(2,1)S(1)} %bitcast.351, bf16[1,4,64,2,896]{4,3,2,1,0:T(2,128)(2,1)S(1)} %fusion.222), kind=kLoop, calls=%fused_computation.34 | loop fusion | flops 5505024 | bytes 7340032 | tf_op jit(solution)/shard_map/stack | solution.py:98
  266.5 2.9 maximum_maximum_fusion.1
  271.2 3.2 pad_maximum_fusion
  278.0 4.0 convolution_bitcast_fusion
  285.7 11.7 %cholesky.104 = f32[128,128]{1,0:T(8,128)S(1)} custom-call(f32[128,128]{1,0:T(8,128)S(1)} %cholesky.266), custom_call_target="Cholesky" | custom-call | tf_op jit(solution)/shard_map/jit(cholesky)/cholesky | solution.py:150
  297.6 9.8 %custom-call.31 = f32[1,128,128]{1,2,0:T(8,128)S(1)} custom-call(f32[1,128,128]{2,1,0:T(8,128)S(1)} %get-tuple-element.109), custom_call_target="InvertDiagBlocksLowerTriangular" | custom-call | tf_op jit(solution)/shard_map/jit(cholesky)/cholesky | solution.py:150
  309.9 11.9 %cholesky.217 = f32[128,128]{1,0:T(8,128)S(1)} custom-call(f32[128,128]{1,0:T(8,128)S(1)} %cholesky.270), custom_call_target="Cholesky" | custom-call | tf_op jit(solution)/shard_map/jit(cholesky)/cholesky | solution.py:150
  321.9 9.8 %custom-call.32 = f32[1,128,128]{1,2,0:T(8,128)S(1)} custom-call(f32[1,128,128]{2,1,0:T(8,128)S(1)} %get-tuple-element.106), custom_call_target="InvertDiagBlocksLowerTriangular" | custom-call | tf_op jit(solution)/shard_map/jit(cholesky)/cholesky | solution.py:150
  333.2 11.7 %cholesky.238 = f32[128,128]{1,0:T(8,128)S(1)} custom-call(f32[128,128]{1,0:T(8,128)S(1)} %cholesky.275), custom_call_target="Cholesky" | custom-call | tf_op jit(solution)/shard_map/jit(cholesky)/cholesky | solution.py:150
  345.0 9.8 %custom-call.33 = f32[1,128,128]{1,2,0:T(8,128)S(1)} custom-call(f32[1,128,128]{2,1,0:T(8,128)S(1)} %get-tuple-element.103), custom_call_target="InvertDiagBlocksLowerTriangular" | custom-call | tf_op jit(solution)/shard_map/jit(cholesky)/cholesky | solution.py:150
  356.2 12.1 %cholesky.255 = f32[128,128]{1,0:T(8,128)S(1)} custom-call(f32[128,128]{1,0:T(8,128)S(1)} %convolution_subtract_fusion.5), custom_call_target="Cholesky" | custom-call | tf_op jit(solution)/shard_map/jit(cholesky)/cholesky | solution.py:150
  373.9 14.2 %while.1 = (s32[]{:T(128)}, f32[512,512]{1,0:T(8,128)}, s32[4,2]{0,1:T(2,128)S(1)}, f32[4,128,128]{2,1,0:T(8,128)}, s32[]{:T(128)}) while((s32[]{:T(128)}, f32[512,512]{1,0:T(8,128)}, s32[4,2]{0,1:T(2,128)S(1)}, f32[4,128,128]{2,1,0:T(8,128)}, s32[]{:T(128)}) %tuple.85), condition=%wide.while_cond, body=%wide.while_body.sunk | while | flops 2 | bytes 132705 | solution.py:151
  374.6 2.9 bitcast_dynamic-update-slice_fusion.2
  378.2 2.9 bitcast_dynamic-update-slice_fusion.2
  381.7 2.9 bitcast_dynamic-update-slice_fusion.2
  385.3 2.8 bitcast_dynamic-update-slice_fusion.2
  388.1 40.1 %custom-call.34 = f32[4,128,128]{1,2,0:T(8,128)S(1)} custom-call(f32[4,128,128]{2,1,0:T(8,128)} %get-tuple-element.12), custom_call_target="InvertDiagBlocksLowerTriangular" | custom-call | tf_op jit(solution)/shard_map/jit(_solve_triangular)/triangular_solve | solution.py:151
  436.4 5.8 pad_maximum_fusion.1
  442.2 6.4 fusion.54
  448.6 6.6 fusion.57
  455.3 4.5 fusion.51
  459.9 2.9 maximum_maximum_fusion
  465.5 3.0 convolution_convert_fusion.1
  469.5 3.0 convolution_convert_fusion.3
  473.3 3.1 convolution_convert_fusion.2
  483.8 3.4 stack.196
  487.3 3.4 stack.197
  490.7 3.8 stack.198
  497.1 19.5 %collective-permute-done.19 = bf16[1024,512]{1,0:T(8,128)(2,1)S(1)} collective-permute-done((bf16[1024,512]{1,0:T(8,128)(2,1)}, bf16[1024,512]{1,0:T(8,128)(2,1)S(1)}, u32[]{:S(2)}, u32[]{:S(2)}) %collective-permute-start.19) | collective-permute-done | bytes 1048608 | tf_op jit(solution)/shard_map/ppermute | solution.py:16
  527.2 4.6 multiply_convert_fusion.4
  543.7 31.1 %collective-permute-done.31 = bf16[512,1792]{1,0:T(8,128)(2,1)S(1)} collective-permute-done((bf16[512,1792]{1,0:T(8,128)(2,1)S(1)}, bf16[512,1792]{1,0:T(8,128)(2,1)S(1)}, u32[]{:S(2)}, u32[]{:S(2)}) %collective-permute-start.31) | collective-permute-done | bytes 1835040 | tf_op jit(solution)/shard_map/ppermute | solution.py:16
  582.3 31.8 %collective-permute-done.41 = bf16[512,1792]{1,0:T(8,128)(2,1)S(1)} collective-permute-done((bf16[512,1792]{1,0:T(8,128)(2,1)S(1)}, bf16[512,1792]{1,0:T(8,128)(2,1)S(1)}, u32[]{:S(2)}, u32[]{:S(2)}) %collective-permute-start.41) | collective-permute-done | bytes 1835040 | tf_op jit(solution)/shard_map/ppermute | solution.py:16
  621.6 16.3 %collective-permute-done.32 = bf16[4,64,1792]{2,1,0:T(8,128)(2,1)S(1)} collective-permute-done((bf16[4,64,1792]{2,1,0:T(8,128)(2,1)S(1)}, bf16[4,64,1792]{2,1,0:T(8,128)(2,1)S(1)}, u32[]{:S(2)}, u32[]{:S(2)}) %collective-permute-start.32) | collective-permute-done | bytes 917536 | tf_op jit(solution)/shard_map/ppermute | solution.py:16
  638.1 12.7 %collective-permute-start.33 = (bf16[64,1792]{1,0:T(8,128)(2,1)S(1)}, bf16[64,1792]{1,0:T(8,128)(2,1)S(1)}, u32[]{:S(2)}, u32[]{:S(2)}) collective-permute-start(bf16[64,1792]{1,0:T(8,128)(2,1)S(1)} %get-tuple-element.82), channel_id=1, source_target_pairs={{0,8},{2,10},{4,12},{6,14},{8,0},{10,2},{12,4},{14,6},{16,24},{18,... | collective-permute-start | bytes 688136 | tf_op jit(solution)/shard_map/ppermute | solution.py:16
  653.6 2.7 collective-permute-done.42
  656.2 13.0 %collective-permute-start.38 = (bf16[64,1792]{1,0:T(8,128)(2,1)S(1)}, bf16[64,1792]{1,0:T(8,128)(2,1)S(1)}, u32[]{:S(2)}, u32[]{:S(2)}) collective-permute-start(bf16[64,1792]{1,0:T(8,128)(2,1)S(1)} %get-tuple-element.85), channel_id=1, source_target_pairs={{0,8},{2,10},{4,12},{6,14},{8,0},{10,2},{12,4},{14,6},{16,24},{18,... | collective-permute-start | bytes 688136 | tf_op jit(solution)/shard_map/ppermute | solution.py:16
  674.4 4.6 collective-permute-done.38
  680.2 8.7 %collective-permute-done.39 = bf16[64,1792]{1,0:T(8,128)(2,1)S(1)} collective-permute-done((bf16[64,1792]{1,0:T(8,128)(2,1)S(1)}, bf16[64,1792]{1,0:T(8,128)(2,1)S(1)}, u32[]{:S(2)}, u32[]{:S(2)}) %collective-permute-start.39) | collective-permute-done | bytes 229408 | tf_op jit(solution)/shard_map/ppermute | solution.py:16
  688.9 14.1 %collective-permute-start.49 = (bf16[64,1792]{1,0:T(8,128)(2,1)S(1)}, bf16[64,1792]{1,0:T(8,128)(2,1)S(1)}, u32[]{:S(2)}, u32[]{:S(2)}) collective-permute-start(bf16[64,1792]{1,0:T(8,128)(2,1)S(1)} %get-tuple-element.93), channel_id=1, source_target_pairs={{0,16},{2,18},{4,20},{6,22},{8,24},{10,26},{12,28},{14,30},{16,0},... | collective-permute-start | bytes 688136 | tf_op jit(solution)/shard_map/ppermute | solution.py:16
  703.1 2.8 collective-permute-start.50
  705.9 11.6 %collective-permute-done.44 = bf16[64,1792]{1,0:T(8,128)(2,1)S(1)} collective-permute-done((bf16[64,1792]{1,0:T(8,128)(2,1)S(1)}, bf16[64,1792]{1,0:T(8,128)(2,1)S(1)}, u32[]{:S(2)}, u32[]{:S(2)}) %collective-permute-start.44) | collective-permute-done | bytes 229408 | tf_op jit(solution)/shard_map/ppermute | solution.py:16
  717.7 9.7 %collective-permute-done.49 = bf16[64,1792]{1,0:T(8,128)(2,1)S(1)} collective-permute-done((bf16[64,1792]{1,0:T(8,128)(2,1)S(1)}, bf16[64,1792]{1,0:T(8,128)(2,1)S(1)}, u32[]{:S(2)}, u32[]{:S(2)}) %collective-permute-start.49) | collective-permute-done | bytes 229408 | tf_op jit(solution)/shard_map/ppermute | solution.py:16
  (280 shorter events, 138.1 us)
Async XLA Ops:
  6.5 520.7 %all-gather.5.cloned.1.call-start = ((), (), s32[]{:S(2)}) async-start(), calls=%async_computation | async-start | bytes 22020096 | tf_op jit(solution)/shard_map/all_gather | solution.py:87
  29.8 6.8 collective-permute-start.6
  45.3 14.2 %collective-permute-start.13 = (bf16[448,512]{1,0:T(8,128)(2,1)S(1)}, bf16[448,512]{1,0:T(8,128)(2,1)S(1)}, u32[]{:S(2)}, u32[]{:S(2)}) collective-permute-start(bf16[448,512]{1,0:T(8,128)(2,1)S(1)} %get-tuple-element.54), channel_id=1, source_target_pairs={{0,2},{2,0},{4,6},{6,4},{8,10},{10,8},{12,14},{14,12},{16,18},{18,... | collective-permute-start | bytes 1376264 | tf_op jit(solution)/shard_map/ppermute | solution.py:16
  48.2 15.4 %copy-start.41 = (s32[16]{0:T(128)S(1)}, s32[16]{0:T(128)}, u32[]{:S(2)}) copy-start(s32[16]{0:T(128)} %param.13) | copy-start | bytes 196
  48.2 49.7 %copy-start.42 = (f32[64,8]{0,1:T(8,128)S(1)}, f32[64,8]{0,1:T(8,128)}, u32[]{:S(2)}) copy-start(f32[64,8]{0,1:T(8,128)} %param.15) | copy-start | bytes 6148
  48.2 49.7 %copy-start.43 = (s32[64,8]{0,1:T(8,128)S(1)}, s32[64,8]{0,1:T(8,128)}, u32[]{:S(2)}) copy-start(s32[64,8]{0,1:T(8,128)} %param.14) | copy-start | bytes 6148
  49.0 101.0 %collective-permute-start.14 = (bf16[448,512]{1,0:T(8,128)(2,1)}, bf16[448,512]{1,0:T(8,128)(2,1)}, u32[]{:S(2)}, u32[]{:S(2)}) collective-permute-start(bf16[448,512]{1,0:T(8,128)(2,1)} %get-tuple-element.53), channel_id=1, source_target_pairs={{0,4},{2,6},{4,0},{6,2},{8,12},{10,14},{12,8},{14,10},{16,20},{18,... | collective-permute-start | bytes 1376264 | tf_op jit(solution)/shard_map/ppermute | solution.py:16
  50.5 99.5 %collective-permute-start.15 = (bf16[448,512]{1,0:T(8,128)(2,1)}, bf16[448,512]{1,0:T(8,128)(2,1)}, u32[]{:S(2)}, u32[]{:S(2)}) collective-permute-start(bf16[448,512]{1,0:T(8,128)(2,1)} %get-tuple-element.52), channel_id=1, source_target_pairs={{0,6},{2,4},{4,2},{6,0},{8,14},{10,12},{12,10},{14,8},{16,22},{18,... | collective-permute-start | bytes 1376264 | tf_op jit(solution)/shard_map/ppermute | solution.py:16
  51.6 98.5 %collective-permute-start.7 = (bf16[448,512]{1,0:T(8,128)(2,1)}, bf16[448,512]{1,0:T(8,128)(2,1)S(1)}, u32[]{:S(2)}, u32[]{:S(2)}) collective-permute-start(bf16[448,512]{1,0:T(8,128)(2,1)} %get-tuple-element.51), channel_id=1, source_target_pairs={{0,2},{2,0},{4,6},{6,4},{8,10},{10,8},{12,14},{14,12},{16,18},{18,... | collective-permute-start | bytes 1376264 | tf_op jit(solution)/shard_map/ppermute | solution.py:16
  52.5 97.6 %collective-permute-start.8 = (bf16[448,512]{1,0:T(8,128)(2,1)}, bf16[448,512]{1,0:T(8,128)(2,1)S(1)}, u32[]{:S(2)}, u32[]{:S(2)}) collective-permute-start(bf16[448,512]{1,0:T(8,128)(2,1)} %get-tuple-element.50), channel_id=1, source_target_pairs={{0,4},{2,6},{4,0},{6,2},{8,12},{10,14},{12,8},{14,10},{16,20},{18,... | collective-permute-start | bytes 1376264 | tf_op jit(solution)/shard_map/ppermute | solution.py:16
  59.5 35.9 %copy-start.14 = (bf16[448,512]{1,0:T(8,128)(2,1)}, bf16[448,512]{1,0:T(8,128)(2,1)S(1)}, u32[]{:S(2)}) copy-start(bf16[448,512]{1,0:T(8,128)(2,1)S(1)} %collective-permute-done.13) | copy-start | bytes 1376260
  59.5 90.6 %collective-permute-start.9 = (bf16[448,512]{1,0:T(8,128)(2,1)}, bf16[448,512]{1,0:T(8,128)(2,1)S(1)}, u32[]{:S(2)}, u32[]{:S(2)}) collective-permute-start(bf16[448,512]{1,0:T(8,128)(2,1)} %get-tuple-element.49), channel_id=1, source_target_pairs={{0,6},{2,4},{4,2},{6,0},{8,14},{10,12},{12,10},{14,8},{16,22},{18,... | collective-permute-start | bytes 1376264 | tf_op jit(solution)/shard_map/ppermute | solution.py:16
  150.0 17.0 %copy-start.1 = (bf16[4,896,512]{2,1,0:T(8,128)(2,1)S(1)}, bf16[4,896,512]{2,1,0:T(8,128)(2,1)}, u32[]{:S(2)}) copy-start(bf16[4,896,512]{2,1,0:T(8,128)(2,1)} %copy-done) | copy-start | bytes 11010052
  150.0 24.8 %collective-permute-start = (bf16[64,2,896]{2,1,0:T(2,128)(2,1)S(1)}, bf16[64,2,896]{2,1,0:T(2,128)(2,1)S(1)}, u32[]{:S(2)}, u32[]{:S(2)}) collective-permute-start(bf16[64,2,896]{2,1,0:T(2,128)(2,1)S(1)} %get-tuple-element.70), channel_id=1, source_target_pairs={{0,2},{2,0},{4,6},{6,4},{8,10},{10,8},{12,14},{14,12},{16,18},{18,... | collective-permute-start | bytes 688136 | tf_op jit(solution)/shard_map/ppermute | solution.py:16
  153.0 19.1 %copy-start.15 = (bf16[448,512]{1,0:T(8,128)(2,1)S(1)}, bf16[448,512]{1,0:T(8,128)(2,1)}, u32[]{:S(2)}) copy-start(bf16[448,512]{1,0:T(8,128)(2,1)} %copy-done.14) | copy-start | bytes 1376260
  153.0 10.6 %collective-permute-start.10 = (bf16[448,512]{1,0:T(8,128)(2,1)S(1)}, bf16[448,512]{1,0:T(8,128)(2,1)S(1)}, u32[]{:S(2)}, u32[]{:S(2)}) collective-permute-start(bf16[448,512]{1,0:T(8,128)(2,1)S(1)} %get-tuple-element.43), channel_id=1, source_target_pairs={{0,8},{2,10},{4,12},{6,14},{8,16},{10,18},{12,20},{14,22},{16,24},... | collective-permute-start | bytes 1376264 | tf_op jit(solution)/shard_map/ppermute | solution.py:27
  154.4 12.5 %collective-permute-start.11 = (bf16[448,512]{1,0:T(8,128)(2,1)S(1)}, bf16[448,512]{1,0:T(8,128)(2,1)S(1)}, u32[]{:S(2)}, u32[]{:S(2)}) collective-permute-start(bf16[448,512]{1,0:T(8,128)(2,1)S(1)} %get-tuple-element.44), channel_id=1, source_target_pairs={{8,0},{10,2},{12,4},{14,6},{16,8},{18,10},{20,12},{22,14},{24,16},... | collective-permute-start | bytes 1376264 | tf_op jit(solution)/shard_map/ppermute | solution.py:27
  157.1 10.7 %collective-permute-start.16 = (bf16[448,512]{1,0:T(8,128)(2,1)S(1)}, bf16[448,512]{1,0:T(8,128)(2,1)S(1)}, u32[]{:S(2)}, u32[]{:S(2)}) collective-permute-start(bf16[448,512]{1,0:T(8,128)(2,1)S(1)} %get-tuple-element.48), channel_id=1, source_target_pairs={{0,8},{2,10},{4,12},{6,14},{8,16},{10,18},{12,20},{14,22},{16,24},... | collective-permute-start | bytes 1376264 | tf_op jit(solution)/shard_map/ppermute | solution.py:27
  161.6 10.4 %collective-permute-start.17 = (bf16[448,512]{1,0:T(8,128)(2,1)S(1)}, bf16[448,512]{1,0:T(8,128)(2,1)S(1)}, u32[]{:S(2)}, u32[]{:S(2)}) collective-permute-start(bf16[448,512]{1,0:T(8,128)(2,1)S(1)} %get-tuple-element.47), channel_id=1, source_target_pairs={{8,0},{10,2},{12,4},{14,6},{16,8},{18,10},{20,12},{22,14},{24,16},... | collective-permute-start | bytes 1376264 | tf_op jit(solution)/shard_map/ppermute | solution.py:27
  163.5 15.6 %collective-permute-start.1 = (bf16[64,2,896]{2,1,0:T(2,128)(2,1)S(1)}, bf16[64,2,896]{2,1,0:T(2,128)(2,1)S(1)}, u32[]{:S(2)}, u32[]{:S(2)}) collective-permute-start(bf16[64,2,896]{2,1,0:T(2,128)(2,1)S(1)} %get-tuple-element.71), channel_id=1, source_target_pairs={{0,4},{2,6},{4,0},{6,2},{8,12},{10,14},{12,8},{14,10},{16,20},{18,... | collective-permute-start | bytes 688136 | tf_op jit(solution)/shard_map/ppermute | solution.py:16
  166.9 16.3 %collective-permute-start.2 = (bf16[64,2,896]{2,1,0:T(2,128)(2,1)S(1)}, bf16[64,2,896]{2,1,0:T(2,128)(2,1)S(1)}, u32[]{:S(2)}, u32[]{:S(2)}) collective-permute-start(bf16[64,2,896]{2,1,0:T(2,128)(2,1)S(1)} %fusion.159), channel_id=1, source_target_pairs={{0,6},{2,4},{4,2},{6,0},{8,14},{10,12},{12,10},{14,8},{16,22},{18,... | collective-permute-start | bytes 688136 | tf_op jit(solution)/shard_map/ppermute | solution.py:16
  167.7 16.3 %collective-permute-start.22 = (bf16[448,512]{1,0:T(8,128)(2,1)S(1)}, bf16[448,512]{1,0:T(8,128)(2,1)S(1)}, u32[]{:S(2)}, u32[]{:S(2)}) collective-permute-start(bf16[448,512]{1,0:T(8,128)(2,1)S(1)} %get-tuple-element.35), channel_id=1, source_target_pairs={{0,2},{2,0},{4,6},{6,4},{8,10},{10,8},{12,14},{14,12},{16,18},{18,... | collective-permute-start | bytes 1376264 | tf_op jit(solution)/shard_map/ppermute | solution.py:16
  172.0 26.7 %collective-permute-start.23 = (bf16[448,512]{1,0:T(8,128)(2,1)S(1)}, bf16[448,512]{1,0:T(8,128)(2,1)S(1)}, u32[]{:S(2)}, u32[]{:S(2)}) collective-permute-start(bf16[448,512]{1,0:T(8,128)(2,1)S(1)} %get-tuple-element.36), channel_id=1, source_target_pairs={{0,4},{2,6},{4,0},{6,2},{8,12},{10,14},{12,8},{14,10},{16,20},{18,... | collective-permute-start | bytes 1376264 | tf_op jit(solution)/shard_map/ppermute | solution.py:16
  174.8 31.4 %copy-start.22 = (bf16[64,2,896]{2,1,0:T(2,128)(2,1)}, bf16[64,2,896]{2,1,0:T(2,128)(2,1)S(1)}, u32[]{:S(2)}) copy-start(bf16[64,2,896]{2,1,0:T(2,128)(2,1)S(1)} %collective-permute-done) | copy-start | bytes 688132
  174.8 26.4 %collective-permute-start.24 = (bf16[448,512]{1,0:T(8,128)(2,1)S(1)}, bf16[448,512]{1,0:T(8,128)(2,1)S(1)}, u32[]{:S(2)}, u32[]{:S(2)}) collective-permute-start(bf16[448,512]{1,0:T(8,128)(2,1)S(1)} %get-tuple-element.37), channel_id=1, source_target_pairs={{0,6},{2,4},{4,2},{6,0},{8,14},{10,12},{12,10},{14,8},{16,22},{18,... | collective-permute-start | bytes 1376264 | tf_op jit(solution)/shard_map/ppermute | solution.py:16
  179.1 39.0 %copy-start.24 = (bf16[64,2,896]{2,1,0:T(2,128)(2,1)}, bf16[64,2,896]{2,1,0:T(2,128)(2,1)S(1)}, u32[]{:S(2)}) copy-start(bf16[64,2,896]{2,1,0:T(2,128)(2,1)S(1)} %collective-permute-done.1) | copy-start | bytes 688132
  179.1 23.0 %collective-permute-start.26 = (bf16[448,512]{1,0:T(8,128)(2,1)S(1)}, bf16[448,512]{1,0:T(8,128)(2,1)S(1)}, u32[]{:S(2)}, u32[]{:S(2)}) collective-permute-start(bf16[448,512]{1,0:T(8,128)(2,1)S(1)} %get-tuple-element.39), channel_id=1, source_target_pairs={{0,2},{2,0},{4,6},{6,4},{8,10},{10,8},{12,14},{14,12},{16,18},{18,... | collective-permute-start | bytes 1376264 | tf_op jit(solution)/shard_map/ppermute | solution.py:16
  183.2 20.4 %copy-start.25 = (bf16[64,2,896]{2,1,0:T(2,128)(2,1)}, bf16[64,2,896]{2,1,0:T(2,128)(2,1)S(1)}, u32[]{:S(2)}) copy-start(bf16[64,2,896]{2,1,0:T(2,128)(2,1)S(1)} %collective-permute-done.2) | copy-start | bytes 688132
  183.2 27.8 %collective-permute-start.27 = (bf16[448,512]{1,0:T(8,128)(2,1)S(1)}, bf16[448,512]{1,0:T(8,128)(2,1)S(1)}, u32[]{:S(2)}, u32[]{:S(2)}) collective-permute-start(bf16[448,512]{1,0:T(8,128)(2,1)S(1)} %get-tuple-element.40), channel_id=1, source_target_pairs={{0,4},{2,6},{4,0},{6,2},{8,12},{10,14},{12,8},{14,10},{16,20},{18,... | collective-permute-start | bytes 1376264 | tf_op jit(solution)/shard_map/ppermute | solution.py:16
  184.0 27.0 %collective-permute-start.28 = (bf16[448,512]{1,0:T(8,128)(2,1)S(1)}, bf16[448,512]{1,0:T(8,128)(2,1)S(1)}, u32[]{:S(2)}, u32[]{:S(2)}) collective-permute-start(bf16[448,512]{1,0:T(8,128)(2,1)S(1)} %get-tuple-element.41), channel_id=1, source_target_pairs={{0,6},{2,4},{4,2},{6,0},{8,14},{10,12},{12,10},{14,8},{16,22},{18,... | collective-permute-start | bytes 1376264 | tf_op jit(solution)/shard_map/ppermute | solution.py:16
  198.7 31.9 %collective-permute-start.3 = (bf16[4,64,2,896]{3,2,1,0:T(2,128)(2,1)}, bf16[4,64,2,896]{3,2,1,0:T(2,128)(2,1)S(1)}, u32[]{:S(2)}, u32[]{:S(2)}) collective-permute-start(bf16[4,64,2,896]{3,2,1,0:T(2,128)(2,1)} %pad_maximum_fusion.9), channel_id=1, source_target_pairs={{0,8},{2,10},{4,12},{6,14},{8,0},{10,2},{12,4},{14,6},{16,24},{18,... | collective-permute-start | bytes 2752520 | tf_op jit(solution)/shard_map/ppermute | solution.py:16
  201.2 54.4 %collective-permute-start.4 = (bf16[4,64,2,896]{3,2,1,0:T(2,128)(2,1)}, bf16[4,64,2,896]{3,2,1,0:T(2,128)(2,1)}, u32[]{:S(2)}, u32[]{:S(2)}) collective-permute-start(bf16[4,64,2,896]{3,2,1,0:T(2,128)(2,1)} %pad_maximum_fusion.9), channel_id=1, source_target_pairs={{0,16},{2,18},{4,20},{6,22},{8,24},{10,26},{12,28},{14,30},{16,0},... | collective-permute-start | bytes 2752520 | tf_op jit(solution)/shard_map/ppermute | solution.py:16
  202.1 53.5 %collective-permute-start.5 = (bf16[4,64,2,896]{3,2,1,0:T(2,128)(2,1)}, bf16[4,64,2,896]{3,2,1,0:T(2,128)(2,1)}, u32[]{:S(2)}, u32[]{:S(2)}) collective-permute-start(bf16[4,64,2,896]{3,2,1,0:T(2,128)(2,1)} %pad_maximum_fusion.9), channel_id=1, source_target_pairs={{0,24},{2,26},{4,28},{6,30},{8,16},{10,18},{12,20},{14,22},{16,8},... | collective-permute-start | bytes 2752520 | tf_op jit(solution)/shard_map/ppermute | solution.py:16
  211.0 55.5 %collective-permute-start.25 = (bf16[4,448,512]{2,1,0:T(8,128)(2,1)}, bf16[4,448,512]{2,1,0:T(8,128)(2,1)}, u32[]{:S(2)}, u32[]{:S(2)}) collective-permute-start(bf16[4,448,512]{2,1,0:T(8,128)(2,1)} %get-tuple-element.62), channel_id=1, source_target_pairs={{0,1},{1,0},{2,3},{3,2},{4,5},{5,4},{6,7},{7,6},{8,9},{9,8},{10,11... | collective-permute-start | bytes 5505032 | tf_op jit(solution)/shard_map/ppermute | solution.py:21
  214.4 52.1 %collective-permute-start.29 = (bf16[4,448,512]{2,1,0:T(8,128)(2,1)}, bf16[4,448,512]{2,1,0:T(8,128)(2,1)}, u32[]{:S(2)}, u32[]{:S(2)}) collective-permute-start(bf16[4,448,512]{2,1,0:T(8,128)(2,1)} %get-tuple-element.64), channel_id=1, source_target_pairs={{0,1},{1,0},{2,3},{3,2},{4,5},{5,4},{6,7},{7,6},{8,9},{9,8},{10,11... | collective-permute-start | bytes 5505032 | tf_op jit(solution)/shard_map/ppermute | solution.py:21
  230.6 32.8 %copy-start.16 = (bf16[4,64,2,896]{3,2,1,0:T(2,128)(2,1)}, bf16[4,64,2,896]{3,2,1,0:T(2,128)(2,1)S(1)}, u32[]{:S(2)}) copy-start(bf16[4,64,2,896]{3,2,1,0:T(2,128)(2,1)S(1)} %collective-permute-done.3) | copy-start | bytes 2752516
  266.0 193.9 %collective-permute-start.12 = (bf16[4,448,512]{2,1,0:T(8,128)(2,1)}, bf16[4,448,512]{2,1,0:T(8,128)(2,1)}, u32[]{:S(2)}, u32[]{:S(2)}) collective-permute-start(bf16[4,448,512]{2,1,0:T(8,128)(2,1)} %get-tuple-element.96), channel_id=1, source_target_pairs={{0,1},{1,0},{2,3},{3,2},{4,5},{5,4},{6,7},{7,6},{8,9},{9,8},{10,11... | collective-permute-start | bytes 5505032 | tf_op jit(solution)/shard_map/ppermute | solution.py:21
  266.0 193.9 %collective-permute-start.18 = (bf16[4,448,512]{2,1,0:T(8,128)(2,1)}, bf16[4,448,512]{2,1,0:T(8,128)(2,1)}, u32[]{:S(2)}, u32[]{:S(2)}) collective-permute-start(bf16[4,448,512]{2,1,0:T(8,128)(2,1)} %get-tuple-element.98), channel_id=1, source_target_pairs={{0,1},{1,0},{2,3},{3,2},{4,5},{5,4},{6,7},{7,6},{8,9},{9,8},{10,11... | collective-permute-start | bytes 5505032 | tf_op jit(solution)/shard_map/ppermute | solution.py:21
  428.3 8.1 %copy-start.3 = (bf16[1,4,896,512]{3,2,1,0:T(8,128)(2,1)S(1)}, bf16[1,4,896,512]{3,2,1,0:T(8,128)(2,1)}, u32[]{:S(2)}) copy-start(bf16[1,4,896,512]{3,2,1,0:T(8,128)(2,1)} %copy-done.2) | copy-start | bytes 11010052
  431.4 10.8 %slice-start = ((s8[7340032]{0:T(1024)(128)(4,1)}), s8[4194304]{0:T(1024)(128)(4,1)S(1)}, s32[]{:S(2)}) async-start(s8[7340032]{0:T(1024)(128)(4,1)} %bitcast.340), calls=%async_computation.1 | async-start | bytes 8388608
  459.8 34.6 %collective-permute-start.30 = (bf16[2,512,512]{1,2,0:T(8,128)(2,1)}, bf16[2,512,512]{1,2,0:T(8,128)(2,1)}, u32[]{:S(2)}, u32[]{:S(2)}) collective-permute-start(bf16[2,512,512]{1,2,0:T(8,128)(2,1)} %bitcast.89), channel_id=1, source_target_pairs={{0,1},{1,0},{2,3},{3,2},{4,5},{5,4},{6,7},{7,6},{8,9},{9,8},{10,11... | collective-permute-start | bytes 3145736 | tf_op jit(solution)/shard_map/ppermute | solution.py:21
  468.5 28.2 %collective-permute-start.21 = (bf16[1024,512]{1,0:T(8,128)(2,1)}, bf16[1024,512]{1,0:T(8,128)(2,1)S(1)}, u32[]{:S(2)}, u32[]{:S(2)}) collective-permute-start(bf16[1024,512]{1,0:T(8,128)(2,1)} %convolution_convert_fusion.1), channel_id=1, source_target_pairs={{0,6},{2,4},{4,2},{6,0},{8,14},{10,12},{12,10},{14,8},{16,22},{18,... | collective-permute-start | bytes 3145736 | tf_op jit(solution)/shard_map/ppermute | solution.py:16
  472.5 44.1 %collective-permute-start.19 = (bf16[1024,512]{1,0:T(8,128)(2,1)}, bf16[1024,512]{1,0:T(8,128)(2,1)S(1)}, u32[]{:S(2)}, u32[]{:S(2)}) collective-permute-start(bf16[1024,512]{1,0:T(8,128)(2,1)} %convolution_convert_fusion.3), channel_id=1, source_target_pairs={{0,2},{2,0},{4,6},{6,4},{8,10},{10,8},{12,14},{14,12},{16,18},{18,... | collective-permute-start | bytes 3145736 | tf_op jit(solution)/shard_map/ppermute | solution.py:16
  476.4 41.3 %collective-permute-start.20 = (bf16[1024,512]{1,0:T(8,128)(2,1)}, bf16[1024,512]{1,0:T(8,128)(2,1)S(1)}, u32[]{:S(2)}, u32[]{:S(2)}) collective-permute-start(bf16[1024,512]{1,0:T(8,128)(2,1)} %convolution_convert_fusion.2), channel_id=1, source_target_pairs={{0,4},{2,6},{4,0},{6,2},{8,12},{10,14},{12,8},{14,10},{16,20},{18,... | collective-permute-start | bytes 3145736 | tf_op jit(solution)/shard_map/ppermute | solution.py:16
  531.8 43.0 %collective-permute-start.31 = (bf16[512,1792]{1,0:T(8,128)(2,1)S(1)}, bf16[512,1792]{1,0:T(8,128)(2,1)S(1)}, u32[]{:S(2)}, u32[]{:S(2)}) collective-permute-start(bf16[512,1792]{1,0:T(8,128)(2,1)S(1)} %multiply_convert_fusion.4), channel_id=1, source_target_pairs={{0,2},{2,0},{4,6},{6,4},{8,10},{10,8},{12,14},{14,12},{16,18},{18,... | collective-permute-start | bytes 5505032 | tf_op jit(solution)/shard_map/ppermute | solution.py:16
  535.9 43.0 %collective-permute-start.36 = (bf16[512,1792]{1,0:T(8,128)(2,1)S(1)}, bf16[512,1792]{1,0:T(8,128)(2,1)S(1)}, u32[]{:S(2)}, u32[]{:S(2)}) collective-permute-start(bf16[512,1792]{1,0:T(8,128)(2,1)S(1)} %multiply_convert_fusion.3), channel_id=1, source_target_pairs={{0,4},{2,6},{4,0},{6,2},{8,12},{10,14},{12,8},{14,10},{16,20},{18,... | collective-permute-start | bytes 5505032 | tf_op jit(solution)/shard_map/ppermute | solution.py:16
  540.0 74.1 %collective-permute-start.41 = (bf16[512,1792]{1,0:T(8,128)(2,1)S(1)}, bf16[512,1792]{1,0:T(8,128)(2,1)S(1)}, u32[]{:S(2)}, u32[]{:S(2)}) collective-permute-start(bf16[512,1792]{1,0:T(8,128)(2,1)S(1)} %multiply_convert_fusion.2), channel_id=1, source_target_pairs={{0,2},{2,0},{4,6},{6,4},{8,10},{10,8},{12,14},{14,12},{16,18},{18,... | collective-permute-start | bytes 5505032 | tf_op jit(solution)/shard_map/ppermute | solution.py:16
  543.1 75.1 %collective-permute-start.46 = (bf16[512,1792]{1,0:T(8,128)(2,1)S(1)}, bf16[512,1792]{1,0:T(8,128)(2,1)S(1)}, u32[]{:S(2)}, u32[]{:S(2)}) collective-permute-start(bf16[512,1792]{1,0:T(8,128)(2,1)S(1)} %multiply_convert_fusion.1), channel_id=1, source_target_pairs={{0,4},{2,6},{4,0},{6,2},{8,12},{10,14},{12,8},{14,10},{16,20},{18,... | collective-permute-start | bytes 5505032 | tf_op jit(solution)/shard_map/ppermute | solution.py:16
  576.9 60.9 %collective-permute-start.32 = (bf16[4,64,1792]{2,1,0:T(8,128)(2,1)S(1)}, bf16[4,64,1792]{2,1,0:T(8,128)(2,1)S(1)}, u32[]{:S(2)}, u32[]{:S(2)}) collective-permute-start(bf16[4,64,1792]{2,1,0:T(8,128)(2,1)S(1)} %slice_bitcast_fusion.6), channel_id=1, source_target_pairs={{0,4},{2,6},{4,0},{6,2},{8,12},{10,14},{12,8},{14,10},{16,20},{18,... | collective-permute-start | bytes 2752520 | tf_op jit(solution)/shard_map/ppermute | solution.py:16
  581.0 69.8 %collective-permute-start.37 = (bf16[4,64,1792]{2,1,0:T(8,128)(2,1)S(1)}, bf16[4,64,1792]{2,1,0:T(8,128)(2,1)S(1)}, u32[]{:S(2)}, u32[]{:S(2)}) collective-permute-start(bf16[4,64,1792]{2,1,0:T(8,128)(2,1)S(1)} %slice_bitcast_fusion.4), channel_id=1, source_target_pairs={{0,2},{2,0},{4,6},{6,4},{8,10},{10,8},{12,14},{14,12},{16,18},{18,... | collective-permute-start | bytes 2752520 | tf_op jit(solution)/shard_map/ppermute | solution.py:16
  616.3 40.0 %collective-permute-start.42 = (bf16[4,64,1792]{2,1,0:T(8,128)(2,1)S(1)}, bf16[4,64,1792]{2,1,0:T(8,128)(2,1)S(1)}, u32[]{:S(2)}, u32[]{:S(2)}) collective-permute-start(bf16[4,64,1792]{2,1,0:T(8,128)(2,1)S(1)} %slice_bitcast_fusion.2), channel_id=1, source_target_pairs={{0,4},{2,6},{4,0},{6,2},{8,12},{10,14},{12,8},{14,10},{16,20},{18,... | collective-permute-start | bytes 2752520 | tf_op jit(solution)/shard_map/ppermute | solution.py:16
  620.4 49.1 %collective-permute-start.47 = (bf16[4,64,1792]{2,1,0:T(8,128)(2,1)S(1)}, bf16[4,64,1792]{2,1,0:T(8,128)(2,1)S(1)}, u32[]{:S(2)}, u32[]{:S(2)}) collective-permute-start(bf16[4,64,1792]{2,1,0:T(8,128)(2,1)S(1)} %slice_bitcast_fusion), channel_id=1, source_target_pairs={{0,2},{2,0},{4,6},{6,4},{8,10},{10,8},{12,14},{14,12},{16,18},{18,... | collective-permute-start | bytes 2752520 | tf_op jit(solution)/shard_map/ppermute | solution.py:16
  638.1 31.7 %collective-permute-start.33 = (bf16[64,1792]{1,0:T(8,128)(2,1)S(1)}, bf16[64,1792]{1,0:T(8,128)(2,1)S(1)}, u32[]{:S(2)}, u32[]{:S(2)}) collective-permute-start(bf16[64,1792]{1,0:T(8,128)(2,1)S(1)} %get-tuple-element.82), channel_id=1, source_target_pairs={{0,8},{2,10},{4,12},{6,14},{8,0},{10,2},{12,4},{14,6},{16,24},{18,... | collective-permute-start | bytes 688136 | tf_op jit(solution)/shard_map/ppermute | solution.py:16
  650.8 21.4 %collective-permute-start.34 = (bf16[64,1792]{1,0:T(8,128)(2,1)S(1)}, bf16[64,1792]{1,0:T(8,128)(2,1)S(1)}, u32[]{:S(2)}, u32[]{:S(2)}) collective-permute-start(bf16[64,1792]{1,0:T(8,128)(2,1)S(1)} %get-tuple-element.84), channel_id=1, source_target_pairs={{0,16},{2,18},{4,20},{6,22},{8,24},{10,26},{12,28},{14,30},{16,0},... | collective-permute-start | bytes 688136 | tf_op jit(solution)/shard_map/ppermute | solution.py:16
  650.8 22.5 %collective-permute-start.35 = (bf16[64,1792]{1,0:T(8,128)(2,1)S(1)}, bf16[64,1792]{1,0:T(8,128)(2,1)S(1)}, u32[]{:S(2)}, u32[]{:S(2)}) collective-permute-start(bf16[64,1792]{1,0:T(8,128)(2,1)S(1)} %get-tuple-element.83), channel_id=1, source_target_pairs={{0,24},{2,26},{4,28},{6,30},{8,16},{10,18},{12,20},{14,22},{16,8},... | collective-permute-start | bytes 688136 | tf_op jit(solution)/shard_map/ppermute | solution.py:16
  656.2 22.7 %collective-permute-start.38 = (bf16[64,1792]{1,0:T(8,128)(2,1)S(1)}, bf16[64,1792]{1,0:T(8,128)(2,1)S(1)}, u32[]{:S(2)}, u32[]{:S(2)}) collective-permute-start(bf16[64,1792]{1,0:T(8,128)(2,1)S(1)} %get-tuple-element.85), channel_id=1, source_target_pairs={{0,8},{2,10},{4,12},{6,14},{8,0},{10,2},{12,4},{14,6},{16,24},{18,... | collective-permute-start | bytes 688136 | tf_op jit(solution)/shard_map/ppermute | solution.py:16
  669.5 19.4 %collective-permute-start.39 = (bf16[64,1792]{1,0:T(8,128)(2,1)S(1)}, bf16[64,1792]{1,0:T(8,128)(2,1)S(1)}, u32[]{:S(2)}, u32[]{:S(2)}) collective-permute-start(bf16[64,1792]{1,0:T(8,128)(2,1)S(1)} %get-tuple-element.87), channel_id=1, source_target_pairs={{0,16},{2,18},{4,20},{6,22},{8,24},{10,26},{12,28},{14,30},{16,0},... | collective-permute-start | bytes 688136 | tf_op jit(solution)/shard_map/ppermute | solution.py:16
  669.8 19.1 %collective-permute-start.40 = (bf16[64,1792]{1,0:T(8,128)(2,1)S(1)}, bf16[64,1792]{1,0:T(8,128)(2,1)S(1)}, u32[]{:S(2)}, u32[]{:S(2)}) collective-permute-start(bf16[64,1792]{1,0:T(8,128)(2,1)S(1)} %get-tuple-element.86), channel_id=1, source_target_pairs={{0,24},{2,26},{4,28},{6,30},{8,16},{10,18},{12,20},{14,22},{16,8},... | collective-permute-start | bytes 688136 | tf_op jit(solution)/shard_map/ppermute | solution.py:16
  672.3 30.8 %collective-permute-start.43 = (bf16[64,1792]{1,0:T(8,128)(2,1)S(1)}, bf16[64,1792]{1,0:T(8,128)(2,1)S(1)}, u32[]{:S(2)}, u32[]{:S(2)}) collective-permute-start(bf16[64,1792]{1,0:T(8,128)(2,1)S(1)} %get-tuple-element.88), channel_id=1, source_target_pairs={{0,8},{2,10},{4,12},{6,14},{8,0},{10,2},{12,4},{14,6},{16,24},{18,... | collective-permute-start | bytes 688136 | tf_op jit(solution)/shard_map/ppermute | solution.py:16
  673.4 44.2 %collective-permute-start.44 = (bf16[64,1792]{1,0:T(8,128)(2,1)S(1)}, bf16[64,1792]{1,0:T(8,128)(2,1)S(1)}, u32[]{:S(2)}, u32[]{:S(2)}) collective-permute-start(bf16[64,1792]{1,0:T(8,128)(2,1)S(1)} %get-tuple-element.90), channel_id=1, source_target_pairs={{0,16},{2,18},{4,20},{6,22},{8,24},{10,26},{12,28},{14,30},{16,0},... | collective-permute-start | bytes 688136 | tf_op jit(solution)/shard_map/ppermute | solution.py:16
  679.0 38.6 %collective-permute-start.45 = (bf16[64,1792]{1,0:T(8,128)(2,1)S(1)}, bf16[64,1792]{1,0:T(8,128)(2,1)S(1)}, u32[]{:S(2)}, u32[]{:S(2)}) collective-permute-start(bf16[64,1792]{1,0:T(8,128)(2,1)S(1)} %get-tuple-element.89), channel_id=1, source_target_pairs={{0,24},{2,26},{4,28},{6,30},{8,16},{10,18},{12,20},{14,22},{16,8},... | collective-permute-start | bytes 688136 | tf_op jit(solution)/shard_map/ppermute | solution.py:16
  688.9 28.8 %collective-permute-start.48 = (bf16[64,1792]{1,0:T(8,128)(2,1)S(1)}, bf16[64,1792]{1,0:T(8,128)(2,1)S(1)}, u32[]{:S(2)}, u32[]{:S(2)}) collective-permute-start(bf16[64,1792]{1,0:T(8,128)(2,1)S(1)} %get-tuple-element.91), channel_id=1, source_target_pairs={{0,8},{2,10},{4,12},{6,14},{8,0},{10,2},{12,4},{14,6},{16,24},{18,... | collective-permute-start | bytes 688136 | tf_op jit(solution)/shard_map/ppermute | solution.py:16
  688.9 38.4 %collective-permute-start.49 = (bf16[64,1792]{1,0:T(8,128)(2,1)S(1)}, bf16[64,1792]{1,0:T(8,128)(2,1)S(1)}, u32[]{:S(2)}, u32[]{:S(2)}) collective-permute-start(bf16[64,1792]{1,0:T(8,128)(2,1)S(1)} %get-tuple-element.93), channel_id=1, source_target_pairs={{0,16},{2,18},{4,20},{6,22},{8,24},{10,26},{12,28},{14,30},{16,0},... | collective-permute-start | bytes 688136 | tf_op jit(solution)/shard_map/ppermute | solution.py:16
  703.1 24.3 %collective-permute-start.50 = (bf16[64,1792]{1,0:T(8,128)(2,1)S(1)}, bf16[64,1792]{1,0:T(8,128)(2,1)S(1)}, u32[]{:S(2)}, u32[]{:S(2)}) collective-permute-start(bf16[64,1792]{1,0:T(8,128)(2,1)S(1)} %get-tuple-element.92), channel_id=1, source_target_pairs={{0,24},{2,26},{4,28},{6,30},{8,16},{10,18},{12,20},{14,22},{16,8},... | collective-permute-start | bytes 688136 | tf_op jit(solution)/shard_map/ppermute | solution.py:16
  (35 other events, 130.0 us)
Sparse Core Ops, SparseCore 0:
  48.3 27.3 all-gather.4

commit v3 on v1

v3 whole, which is shorter than its diff:
```python
import functools

import jax
import jax.numpy as jnp
from jax import lax
from jax.experimental import pallas as pl
from jax.experimental.pallas import tpu as pltpu
from jax.sharding import PartitionSpec as P

MOST = 4
LANES = 128
VMEM_BYTES = 56 * 1024 * 1024

HIGHEST = lax.Precision.HIGHEST
F32 = jnp.float32
BF16 = jnp.bfloat16


def swap_expert(value, mask):
    count = lax.axis_size("expert")
    return lax.ppermute(value, "expert", [(source, source ^ mask) for source in range(count)])


def swap_dp(value):
    count = lax.axis_size("dp")
    return lax.ppermute(value, "dp", [(source, count - 1 - source) for source in range(count)])


def shift_groups(value, steps):
    count = lax.axis_size("expert")
    moves = [(s, s + steps) for s in range(count) if 0 <= s + steps < count]
    return lax.ppermute(value, "expert", moves)


def whole():
    return pl.BlockSpec(memory_space=pltpu.VMEM)


def scalars():
    return pl.BlockSpec(memory_space=pltpu.SMEM)


def params(**more):
    return pltpu.CompilerParams(vmem_limit_bytes=VMEM_BYTES, **more)


def cost(flops, moved):
    return pl.CostEstimate(flops=int(flops), bytes_accessed=int(moved), transcendentals=0)


def mul(a, b, dims=((1,), (0,))):
    return lax.dot_general(a, b, (dims, ((), ())), preferred_element_type=F32)


def exact(a, b, dims):
    return lax.dot_general(a, b, (dims, ((), ())), precision=HIGHEST, preferred_element_type=F32)


def parts_of(value):
    high = value.astype(BF16)
    return high, (value - high.astype(F32)).astype(BF16)


def mul3(a, b, dims):
    (a0, a1), (b0, b1) = parts_of(a), parts_of(b)
    return mul(a0, b0, dims) + (mul(a0, b1, dims) + mul(a1, b0, dims))


def token_kernel(groups, rows, meta, tokens, routes, weights, *pieces):
    place = lax.rem(meta[2 * MOST], MOST)
    toks = tokens.shape[0]
    lane = lax.broadcasted_iota(jnp.int32, (toks, LANES), 1)
    group = lax.rem(lane, groups)
    for k in range(MOST):
        expert = group * MOST + (place ^ k)
        share = jnp.zeros((toks, LANES), F32)
        for t in range(routes.shape[1]):
            share += jnp.where(routes[:, t : t + 1] == expert, weights[:, t : t + 1], 0.0)
        high, low = parts_of(share)
        pieces[k][:, :LANES] = jnp.where(
            lane < groups, high.astype(F32), low.astype(F32)
        ).astype(BF16)
        for d in range(2):
            start = pl.multiple_of(meta[d * MOST + k] * rows, LANES)
            pieces[k][:, LANES + d * rows : LANES + (d + 1) * rows] = tokens[:, pl.ds(start, rows)]


def token_pieces(meta, tokens, routes, weights, groups, rows, place):
    toks = tokens.shape[0]
    if rows % LANES == 0:
        return pl.pallas_call(
            functools.partial(token_kernel, groups, rows),
            out_shape=[jax.ShapeDtypeStruct((toks, LANES + 2 * rows), BF16)] * MOST,
            in_specs=[scalars(), whole(), whole(), whole()],
            out_specs=[whole()] * MOST,
            compiler_params=params(),
            name="token_pieces",
        )(meta, tokens, routes, weights)
    lane = jnp.arange(LANES, dtype=jnp.int32)
    pieces = []
    for k in range(MOST):
        expert = (lane % groups) * MOST + (place ^ k)
        share = jnp.sum(jnp.where(routes[:, :, None] == expert, weights[:, :, None], 0.0), axis=1)
        high, low = parts_of(share)
        columns = [
            lax.dynamic_slice_in_dim(tokens, meta[d * MOST + k] * rows, rows, axis=1)
            for d in range(2)
        ]
        pieces.append(jnp.concatenate([jnp.where(lane < groups, high, low)] + columns, axis=1))
    return pieces


def sketch_kernel(meta, gate, up, sketch, out):
    value = mul(gate[...], sketch[0]) + mul(up[...], sketch[1])
    out[0] = value.astype(out.dtype)


def sketch_half(meta, gate, up, sketch, side, dtype, rows):
    hid, rank = sketch.shape[1:]
    row_block = pl.BlockSpec((rows, hid), lambda k, meta: (meta[side * MOST + k], 0))
    return pl.pallas_call(
        sketch_kernel,
        grid_spec=pltpu.PrefetchScalarGridSpec(
            num_scalar_prefetch=1,
            grid=(MOST,),
            in_specs=[row_block, row_block, pl.BlockSpec((2, hid, rank), lambda k, meta: (0, 0, 0))],
            out_specs=pl.BlockSpec((1, rows, rank), lambda k, meta: (k, 0, 0)),
        ),
        out_shape=jax.ShapeDtypeStruct((MOST, rows, rank), dtype),
        compiler_params=params(),
        cost_estimate=cost(4 * MOST * rows * hid * rank, 4 * MOST * rows * hid),
        name="sketch_half",
    )(meta, gate, up, sketch)


def chosen(values, names, name):
    total = jnp.zeros(values[0].shape, F32)
    for value, own in zip(values, names):
        total += jnp.where(own == name, value, 0.0)
    return total


def ends_kernel(meta, *refs):
    values = [ref[...].astype(F32) for ref in refs[:MOST]]
    tail, head = refs[MOST:]
    position = meta[2 * MOST]
    place = lax.rem(position, MOST)
    first = position - place
    base = 2 * MOST + 1
    names = [meta[base + first + (place ^ k)] for k in range(MOST)]
    tail[...] = chosen(values, names, meta[base + first + MOST - 1]).astype(BF16)
    head[...] = chosen(values, names, meta[base + first]).astype(BF16)


def totals_kernel(experts, meta, *refs):
    values = [ref[...].astype(F32) for ref in refs[:MOST]]
    below, above = (ref[...].astype(F32) for ref in refs[MOST : MOST + 2])
    stacked, sends = refs[MOST + 2], refs[MOST + 3 :]
    position = meta[2 * MOST]
    place = lax.rem(position, MOST)
    first = position - place
    base = 2 * MOST + 1
    names = [meta[base + first + (place ^ k)] for k in range(MOST)]
    below_name = jnp.where(first > 0, meta[base + jnp.maximum(first - 1, 0)], -1)
    above_name = jnp.where(
        first + MOST < experts, meta[base + jnp.minimum(first + MOST, experts - 1)], -1
    )
    for k in range(MOST):
        total = chosen(values, names, names[k])
        total += jnp.where(names[k] == below_name, below, 0.0)
        total += jnp.where(names[k] == above_name, above, 0.0)
        total = total.astype(BF16)
        stacked[k] = total
        if k:
            sends[k - 1][...] = total


def stack_kernel(*refs):
    for k in range(MOST):
        refs[MOST][k] = refs[k][...]


def cluster_rows(meta, own):
    shape = own[0].shape
    experts = lax.axis_size("expert")
    got = [own[0]] + [swap_expert(own[k], k) for k in range(1, MOST)]
    piece = jax.ShapeDtypeStruct(shape, BF16)
    stacked = jax.ShapeDtypeStruct((MOST,) + shape, BF16)
    tail, head = pl.pallas_call(
        ends_kernel,
        out_shape=[piece, piece],
        in_specs=[scalars()] + [whole()] * MOST,
        out_specs=[whole()] * 2,
        compiler_params=params(),
        name="end_sums",
    )(meta, *got)
    below = shift_groups(tail, MOST)
    above = shift_groups(head, -MOST)
    sums, *sends = pl.pallas_call(
        functools.partial(totals_kernel, experts),
        out_shape=[stacked] + [piece] * (MOST - 1),
        in_specs=[scalars()] + [whole()] * (MOST + 2),
        out_specs=[whole()] * MOST,
        compiler_params=params(),
        name="cluster_sums",
    )(meta, *got, below, above)
    back = [sums[0]] + [swap_expert(sends[k - 1], k) for k in range(1, MOST)]
    mine = pl.pallas_call(
        stack_kernel,
        out_shape=stacked,
        in_specs=[whole()] * MOST,
        out_specs=whole(),
        compiler_params=params(),
        name="own_sums",
    )(*back)
    return sums, mine


def cross_kernel(started, meta, own, other, gate, up, *refs):
    if started:
        old_gram, old_raw, gram, raw, current = refs
    else:
        gram, raw, current = refs
    step = pl.program_id(0)

    @pl.when(step == 0)
    def _():
        gram[...] = old_gram[...] if started else jnp.zeros(gram.shape, F32)
        raw[...] = old_raw[...] if started else jnp.zeros(raw.shape, F32)

    @pl.when(step < MOST)
    def _():
        current[...] = own[0]

    @pl.when(step >= MOST)
    def _():
        current[...] = other[0]

    rows = current[...]
    turned = rows.T
    gram[...] += mul(turned, rows)
    raw[0] += mul(turned, gate[...])
    raw[1] += mul(turned, up[...])


def crossed(meta, own, other, gate, up, chunk, chunks, before):
    _, rows, rank = own.shape
    hid = gate.shape[1]
    row_block = pl.BlockSpec((rows, hid), lambda i, meta: (meta[i] * chunks + chunk, 0))
    gram_spec = pl.BlockSpec((rank, rank), lambda i, meta: (0, 0))
    raw_spec = pl.BlockSpec((2, rank, hid), lambda i, meta: (0, 0, 0))
    return pl.pallas_call(
        functools.partial(cross_kernel, bool(before)),
        grid_spec=pltpu.PrefetchScalarGridSpec(
            num_scalar_prefetch=1,
            grid=(2 * MOST,),
            in_specs=[
                pl.BlockSpec((1, rows, rank), lambda i, meta: (jnp.minimum(i, MOST - 1), 0, 0)),
                pl.BlockSpec((1, rows, rank), lambda i, meta: (jnp.maximum(i - MOST, 0), 0, 0)),
                row_block,
                row_block,
            ]
            + ([gram_spec, raw_spec] if before else []),
            out_specs=[gram_spec, raw_spec],
            scratch_shapes=[pltpu.VMEM((rows, rank), BF16)],
        ),
        out_shape=[
            jax.ShapeDtypeStruct((rank, rank), F32),
            jax.ShapeDtypeStruct((2, rank, hid), F32),
        ],
        compiler_params=params(),
        cost_estimate=cost(4 * MOST * rows * rank * (rank + 2 * hid), 8 * MOST * rows * rank * 3),
        name="crossed",
    )(meta, own, other, gate, up, *before)


def project_kernel(chunks, *refs):
    tokens, refs = refs[: -2 * chunks - 2], refs[-2 * chunks - 2 :]
    sums, out, basis = refs[: 2 * chunks], refs[-2], refs[-1]
    rows = sums[0].shape[1]
    for i, ref in enumerate(sums):
        basis[i * rows : (i + 1) * rows, :] = ref[0]
    toks = tokens[0].shape[0]
    for i, ref in enumerate(tokens):
        out[0, i * toks : (i + 1) * toks] = mul(ref[:, LANES:], basis[...]).astype(BF16)


def project(tokens, sums):
    rank = sums[0].shape[-1]
    toks, width = tokens[0].shape
    depth = width - LANES
    total = len(tokens) * toks
    return pl.pallas_call(
        functools.partial(project_kernel, len(sums) // 2),
        grid=(MOST,),
        in_specs=[pl.BlockSpec((toks, width), lambda k: (0, 0))] * len(tokens)
        + [pl.BlockSpec((1,) + value.shape[1:], lambda k: (k, 0, 0)) for value in sums],
        out_specs=pl.BlockSpec((1, total, rank), lambda k: (k, 0, 0)),
        out_shape=jax.ShapeDtypeStruct((MOST, total, rank), BF16),
        scratch_shapes=[pltpu.VMEM((depth, rank), BF16)],
        compiler_params=params(),
        cost_estimate=cost(2 * MOST * total * depth * rank, 4 * MOST * total * rank),
        name="project",
    )(*tokens, *sums)


def factor_kernel(tile, gram_ref, raw_ref, inverse_ref, coeff_ref, work_ref):
    rank = gram_ref.shape[0]
    steps = rank // tile
    work_ref[...] = gram_ref[...]
    row_of = lax.broadcasted_iota(jnp.int32, (tile, tile), 0)
    col_of = lax.broadcasted_iota(jnp.int32, (tile, tile), 1)
    lane = lax.broadcasted_iota(jnp.int32, (8, tile), 1)
    sub = lax.broadcasted_iota(jnp.int32, (8, tile), 0)
    lane_row = lane[:1]

    def step(index, carry):
        base = pl.multiple_of(index * tile, tile)
        here = pl.ds(base, tile)
        strips = [
            work_ref[pl.ds(pl.multiple_of(base + 8 * s, 8), 8), here] for s in range(tile // 8)
        ]
        for j in range(tile):
            first, inner = divmod(j, 8)
            row = strips[first][inner : inner + 1, :]
            pivot = 1.0 / row[:, j : j + 1]
            scaled = jnp.where(lane_row == j, 1.0, row) * pivot
            for s in range(first, tile // 8):
                strip = strips[s]
                column = strip[:, j : j + 1]
                new = jnp.where(lane == j, 0.0, strip) - column * scaled
                strips[s] = jnp.where(sub > inner, new, strip) if s == first else new
        block = jnp.concatenate(strips, axis=0)
        pivots = jnp.sum(jnp.where(row_of == col_of, block, 0.0), axis=1, keepdims=True)
        unit = jnp.where(row_of == col_of, 1.0, 0.0)
        own = jnp.where(col_of < row_of, block, unit) / jnp.sqrt(pivots)
        work_ref[here, here] = unit
        right = exact(own, work_ref[here, :], ((1,), (0,)))
        columns = lax.broadcasted_iota(jnp.int32, (tile, rank), 1)
        inverse_ref[here, :] = jnp.where(columns < base + tile, right, 0.0)
        for s in range(steps - 1):

            @pl.when(index == s)
            def _():
                below = slice((s + 1) * tile, rank)
                mine = slice(s * tile, (s + 1) * tile)
                left = exact(work_ref[below, mine], own, ((1,), (1,)))
                work_ref[below, mine] = jnp.zeros((rank - (s + 1) * tile, tile), F32)
                work_ref[below, :] = work_ref[below, :] - exact(left, right, ((1,), (0,)))

        return carry

    lax.fori_loop(0, steps, step, 0)
    inverse = inverse_ref[...]
    for side in range(2):
        coeff_ref[side] = mul3(inverse, raw_ref[side], ((1,), (0,))).astype(BF16)


def factored(gram, raw):
    rank = gram.shape[0]
    return pl.pallas_call(
        functools.partial(factor_kernel, min(LANES, rank)),
        out_shape=[
            jax.ShapeDtypeStruct((rank, rank), F32),
            jax.ShapeDtypeStruct(raw.shape, BF16),
        ],
        in_specs=[whole()] * 2,
        out_specs=[whole()] * 2,
        scratch_shapes=[pltpu.VMEM((rank, rank), F32)],
        compiler_params=params(),
        cost_estimate=cost(4e10, 8 * rank * rank),
        name="factored",
    )(gram, raw)


def hidden_kernel(toks, groups, meta, inverse, mine, others, tokens, *refs):
    arrived, outs = refs[:MOST], refs[MOST:]
    group = meta[2 * MOST] // MOST
    lane = lax.broadcasted_iota(jnp.int32, tokens.shape, 1)
    picked = (lane == group) | (lane == group + groups)
    share = jnp.sum(jnp.where(picked, tokens[...].astype(F32), 0.0), axis=1, keepdims=True)
    raw = []
    for k in range(MOST):
        total = jnp.zeros((toks, inverse.shape[0]), F32)
        for mask in range(MOST):
            source = (k ^ mask) * toks
            total += arrived[mask][source : source + toks, :].astype(F32)
        raw.append(total)
    projected = mul3(jnp.concatenate(raw, axis=0), inverse[...], ((1,), (1,))).astype(BF16)
    hid = mine.shape[2]
    for d, side in enumerate((mine, others)):
        gate = mul(projected, side[0])
        hidden = gate / (1.0 + jnp.exp(-gate)) * mul(projected, side[1]) * share
        hidden = hidden.astype(BF16)
        block = pl.ds(pl.multiple_of(meta[d * MOST] // MOST * hid, LANES), hid)
        for k in range(MOST):
            x, y = k % 2, k // 2
            rows = hidden[k * toks : (k + 1) * toks]
            outs[x][0, y * toks : (y + 1) * toks, block] = rows
            outs[2 + y][0, x * toks : (x + 1) * toks, block] = rows


def hidden_rows(meta, inverse, coeff, other_coeff, tokens, arrived, toks):
    rank, hid = coeff.shape[1:]
    groups = tokens.shape[0] // (MOST * toks)
    block = MOST * toks
    out = jax.ShapeDtypeStruct((groups, block // 2, 2 * hid), BF16)
    coeff_spec = pl.BlockSpec((2, rank, hid), lambda g: (0, 0, 0))
    return pl.pallas_call(
        functools.partial(hidden_kernel, toks, groups),
        grid=(groups,),
        in_specs=[
            scalars(),
            pl.BlockSpec((rank, rank), lambda g: (0, 0)),
            coeff_spec,
            coeff_spec,
            pl.BlockSpec((block, LANES), lambda g: (g, 0)),
        ]
        + [pl.BlockSpec((block, rank), lambda g: (g, 0))] * MOST,
        out_specs=[pl.BlockSpec((1, block // 2, 2 * hid), lambda g: (g, 0, 0))] * 4,
        out_shape=[out] * 4,
        compiler_params=params(),
        cost_estimate=cost(groups * block * rank * (6 * rank + 8 * hid), 16 * groups * block * hid),
        name="hidden_rows",
    )(meta, inverse, coeff, other_coeff, tokens, *arrived)


def column_chunks(depth):
    units = depth // LANES
    if units % 2 or units < 6:
        return [(0, depth, 0)]
    left = units // 2
    sizes = [left * 12 // 28, left * 10 // 28]
    sizes.append(left - sum(sizes))
    chunks, start = [], 0
    for size in sizes:
        for order in range(2):
            chunks.append((start, size * LANES, order))
            start += size * LANES
    return chunks


def scattered_answers(sides, down, toks):
    depth = down.shape[1]
    experts = lax.axis_size("expert")
    chunks = column_chunks(depth)

    def answered(rows, start, width):
        return mul(rows.reshape(-1, rows.shape[-1]), down[:, start : start + width])

    first = [answered(sides[2 * order + 1], start, width).astype(BF16) for start, width, order in chunks]
    pairs = [list(range(i, min(i + 2, len(chunks)))) for i in range(0, len(chunks), 2)]
    outs = []
    held = None
    for pair in pairs:
        outgoing = [first[i] for i in pair]
        if held is not None:
            tied = lax.optimization_barrier(tuple(outgoing) + tuple(held))
            outgoing, held = list(tied[: len(pair)]), list(tied[len(pair) :])
            finish(held_kept, held, outs, toks, experts)
        came = [swap_expert(value, 1 << chunks[i][2]) for value, i in zip(outgoing, pair)]
        kept, sends = [], []
        for value, i in zip(came, pair):
            start, width, order = chunks[i]
            total = answered(sides[2 * order], start, width) + value.astype(F32)
            total = total.astype(BF16).reshape(-1, 2, toks, width)
            kept.append((total[:, 0], 2 >> order))
            sends.append(total[:, 1])
        held, held_kept = sends, kept
    finish(held_kept, held, outs, toks, experts)
    return jnp.concatenate(outs, axis=1)


def finish(kept, sends, outs, toks, experts):
    for (mine, mask), outgoing in zip(kept, sends):
        value = mine.astype(F32) + swap_expert(outgoing, mask).astype(F32)
        bit = MOST
        while bit < experts:
            value = value.astype(BF16).reshape(-1, 2, toks, value.shape[-1])
            value = value[:, 0].astype(F32) + swap_expert(value[:, 1], bit).astype(F32)
            bit *= 2
        outs.append(value[0].astype(BF16))


def on_device(tokens, gate_weight, up_weight, down_weight, sketch, clusters, routes, route_weights):
    experts = lax.axis_size("expert")
    position = lax.axis_index("expert").astype(jnp.int32)
    place = position % MOST
    groups = experts // MOST
    half = lax.axis_index("dp").astype(jnp.int32)
    gate_rows = gate_weight[0]
    up_rows = up_weight[0]
    depth, rank = gate_rows.shape[0], sketch.shape[-1]
    rows = depth // 2 // MOST
    toks = tokens.shape[0]
    steps = jnp.arange(2 * MOST, dtype=jnp.int32)
    order = ((steps // MOST) ^ half) * MOST + ((steps % MOST) ^ place)
    meta = jnp.concatenate([order, position[None], clusters])

    down_rows = lax.all_gather(down_weight[0], "dp", axis=0, tiled=True)

    sent_half = swap_dp(sketch_half(meta, gate_rows, up_rows, sketch[0], 1, BF16, rows))
    own_half = sketch_half(meta, gate_rows, up_rows, sketch[0], 0, F32, rows)
    pieces = token_pieces(meta, tokens, routes, route_weights, groups, rows, place)
    plane = [pieces[0]] + [swap_expert(pieces[k], k) for k in range(1, MOST)]
    plane = jnp.concatenate(plane, axis=0)
    spread = [plane] + [swap_expert(plane, step * MOST) for step in range(1, groups)]

    chunks = 2 if rows % 32 == 0 else 1
    chunk = rows // chunks
    group_sums, own_sums = [], []
    for c in range(chunks):
        span = slice(c * chunk, (c + 1) * chunk)
        own = [
            (own_half[k, span] + sent_half[k, span].astype(F32)).astype(BF16) for k in range(MOST)
        ]
        sums, mine = cluster_rows(meta, own)
        group_sums.append((sums, swap_dp(sums)))
        own_sums.append((mine, swap_dp(mine)))

    parts = project(spread, [sums[d] for d in range(2) for sums in group_sums])
    before = ()
    for c in range(chunks):
        before = crossed(meta, *own_sums[c], gate_rows, up_rows, c, chunks, before)
    gram, raw = before
    if lax.axis_size("tensor") > 1:
        gram, raw = lax.psum((gram, raw), "tensor")
        parts = lax.psum(parts.astype(F32), "tensor").astype(BF16)
    gram, raw, parts = lax.optimization_barrier((gram, raw, parts))
    arrived = [parts[0]] + [swap_expert(parts[k], k) for k in range(1, MOST)]
    inverse, coeff = factored(gram, raw)
    other_coeff = swap_dp(coeff)
    shares = jnp.concatenate([value[:, :LANES] for value in spread], axis=0)
    sides = hidden_rows(meta, inverse, coeff, other_coeff, shares, arrived, toks)
    return scattered_answers(sides, down_rows, toks)


def solution(mesh):
    return jax.shard_map(
        on_device,
        mesh=mesh,
        in_specs=(
            P(("expert", "dp"), "tensor"),
            P("expert", "tensor", "dp"),
            P("expert", "tensor", "dp"),
            P("expert", "dp", "tensor"),
            P("expert", None, "dp", None),
            P(),
            P(("expert", "dp"), None),
            P(("expert", "dp"), None),
        ),
        out_specs=P(("expert", "dp"), "tensor"),
        check_vma=False,
    )
```

time: 792 us -> 547 us (0.69)
  waiting for transfers between devices: 407 us -> 232 us
  Pallas kernels: 0 us -> 144 us
  other arithmetic: 140 us -> 11.7 us
  matrix products: 113 us -> 22.5 us
  starting transfers between devices: 13 us -> 96.2 us
  blocking collectives: 41.5 us -> 0 us
  between operations: 47.8 us -> 14.5 us
    reduce_scatter x2 -> x0, waiting for transfers between devices: 319 us -> none  [the longest x1 300 us: on_device(): return lax.psum_scatter(weighted, 'expert', scatter_dimension=0, tiled=True)]
    ppermute x6 -> x51, waiting for transfers between devices: 67.8 us -> 228 us  [the longest x45 228 us: swap_expert(): lax.ppermute(value, 'expert', [(source, source ^ mask) for source in rang...]
    pallas_call x0 -> x14, Pallas kernels: none -> 144 us  [the longest x1 52.5 us: factored(): pl.pallas_call(functools.partial(factor_kernel, min(LANES, rank)), out_sh...]
    another operation x19 -> x0, other arithmetic: 133 us -> none  [the longest x14 87.1 us: on_device(): factor = jnp.linalg.cholesky(gram)]
    ppermute x6 -> x51, starting transfers between devices: 7.11 us -> 87.8 us  [the longest x45 86.6 us: swap_expert(): lax.ppermute(value, 'expert', [(source, source ^ mask) for source in rang...]
    dot_general x10 -> x12, matrix products: 103 us -> 22.5 us  [mul(): return lax.dot_general(a, b, (dims, ((), ())), preferred_element_type=F32)]
    all_gather x1 -> x0, blocking collectives: 41.5 us -> none  [on_device(): all_shares = lax.all_gather(shares, 'expert', axis=0, tiled=True)]
    all_gather x3 -> x0, waiting for transfers between devices: 17.8 us -> none  [the longest x1 17.8 us: on_device(): summed = lax.all_gather(summed_half, 'dp', axis=0, tiled=True)]
  transfers between devices with their start and end apart: 14 -> 56, of which waited for: 8 -> 24; matrix products, arithmetic and copies ran while one was open for 27% -> 7% of each run, Pallas kernels for 0% -> 25%
where the time goes in v3:
time: 547 us; the launch traced here: 538 us
  waiting for transfers between devices  232 us (42%)
  Pallas kernels  144 us (26%)
  starting transfers between devices  96.2 us (18%)
  matrix products  22.5 us (4%)
  local copies, waits for them, and re-layouts  16.7 us (3%)
  between operations  14.5 us (3%)
  other arithmetic  11.7 us (2%)
    ppermute x45, waiting for transfers between devices, swap_expert(): lax.ppermute(value, 'expert', [(source, source ^ mask) for source in rang...  228 us
    ppermute x45, starting transfers between devices, swap_expert(): lax.ppermute(value, 'expert', [(source, source ^ mask) for source in rang...  86.6 us
    pallas_call x1, Pallas kernels, factored(): pl.pallas_call(functools.partial(factor_kernel, min(LANES, rank)), out_sh...  52.5 us
    pallas_call x2, Pallas kernels, crossed(): pl.pallas_call(functools.partial(cross_kernel, bool(before)), grid_spec=p...  26.9 us
    dot_general x12, matrix products, mul(): return lax.dot_general(a, b, (dims, ((), ())), preferred_element_type=F32)  22.5 us
    pallas_call x2, Pallas kernels, sketch_half(): pl.pallas_call(sketch_kernel, grid_spec=pltpu.PrefetchScalarGridSpec(num_...  19.9 us
    pallas_call x1, Pallas kernels, project(): pl.pallas_call(functools.partial(project_kernel, len(sums) // 2), grid=(M...  12.3 us
  transfers between devices with their start and end apart: 56, of which 24 were waited for; matrix products, arithmetic and copies ran while one was open for 7% of the time, Pallas kernels for 25%

profile of v3, /device:TPU:0, one launch (start us, length us, event | category | flops | bytes accessed | tf_op | source)
XLA Modules:
  0.0 538.4 jit_solution(15610515019203438789)
XLA Ops:
  7.8 8.7 %sketch_half.3 = bf16[4,896,512]{2,1,0:T(8,128)(2,1)} custom-call(s32[25]{0:T(128)} %pad_add_fusion.meta, bf16[7168,512]{1,0:T(8,128)(2,1)} %bitcast.269, bf16[7168,512]{1,0:T(8,128)(2,1)} %bitcast.273, bf16[2,512,512]{2,1,0:T(8,128)(2,1)} %bitcast.277), custom_call_target="tpu_custom_call" | custom-call | flops 3758096384 | bytes 7340032 | tf_op jit(solution)/shard_map/sketch_half/pallas_call | solution.py:121
  18.6 2.8 token_pieces.1
  21.3 2.9 collective-permute-start.19
  26.9 11.2 %sketch_half.2 = f32[4,896,512]{2,1,0:T(8,128)} custom-call(s32[25]{0:T(128)} %pad_add_fusion.meta, bf16[7168,512]{1,0:T(8,128)(2,1)} %bitcast.270, bf16[7168,512]{1,0:T(8,128)(2,1)} %bitcast.274, bf16[2,512,512]{2,1,0:T(8,128)(2,1)} %bitcast.278), custom_call_target="tpu_custom_call" | custom-call | flops 3758096384 | bytes 7340032 | tf_op jit(solution)/shard_map/sketch_half/pallas_call | solution.py:121
  38.1 7.4 %fusion.41 = (bf16[448,512]{1,0:T(8,128)(2,1)S(1)}, bf16[448,512]{1,0:T(8,128)(2,1)S(1)}, bf16[448,512]{1,0:T(8,128)(2,1)S(1)}, bf16[448,512]{1,0:T(8,128)(2,1)}...) fusion(f32[4,896,512]{2,1,0:T(8,128)} %sketch_half.2, ...), kind=kLoop, calls=%fused_computation.83 | loop fusion | flops 5505024 | bytes 14680064 | tf_op jit(solution)/shard_map/convert_element_type | solution.py:515
  45.5 1.9 collective-permute-start.1
  49.1 1.9 collective-permute-start.10
  52.6 6.3 %collective-permute-done.1.refs_1_ = bf16[448,512]{1,0:T(8,128)(2,1)S(1)} collective-permute-done((bf16[448,512]{1,0:T(8,128)(2,1)S(1)}, bf16[448,512]{1,0:T(8,128)(2,1)S(1)}, u32[]{:S(2)}, u32[]{:S(2)}) %collective-permute-start.1) | collective-permute-done | bytes 458784 | tf_op jit(solution)/shard_map/ppermute | solution.py:21
  58.9 2.9 collective-permute-start.12
  61.8 9.0 %collective-permute-done.2.refs_2_ = bf16[448,512]{1,0:T(8,128)(2,1)S(1)} collective-permute-done((bf16[448,512]{1,0:T(8,128)(2,1)S(1)}, bf16[448,512]{1,0:T(8,128)(2,1)S(1)}, u32[]{:S(2)}, u32[]{:S(2)}) %collective-permute-start.2) | collective-permute-done | bytes 458784 | tf_op jit(solution)/shard_map/ppermute | solution.py:21
  73.1 2.9 end_sums.2
  76.0 2.4 collective-permute-start.4
  79.9 8.7 %collective-permute-done.11.refs_2_ = bf16[448,512]{1,0:T(8,128)(2,1)S(1)} collective-permute-done((bf16[448,512]{1,0:T(8,128)(2,1)S(1)}, bf16[448,512]{1,0:T(8,128)(2,1)S(1)}, u32[]{:S(2)}, u32[]{:S(2)}) %collective-permute-start.11) | collective-permute-done | bytes 458784 | tf_op jit(solution)/shard_map/ppermute | solution.py:21
  89.6 2.9 end_sums.3
  92.5 3.5 collective-permute-start.13
  98.9 4.5 cluster_sums.2
  104.5 3.9 collective-permute-done.14.refs_5_
  109.1 4.6 cluster_sums.3
  117.7 9.7 %collective-permute-done.15.refs_1_ = bf16[448,512]{1,0:T(8,128)(2,1)S(1)} collective-permute-done((bf16[448,512]{1,0:T(8,128)(2,1)}, bf16[448,512]{1,0:T(8,128)(2,1)S(1)}, u32[]{:S(2)}, u32[]{:S(2)}) %collective-permute-start.15) | collective-permute-done | bytes 458784 | tf_op jit(solution)/shard_map/ppermute | solution.py:21
  127.9 15.0 %collective-permute-done.16.refs_2_ = bf16[448,512]{1,0:T(8,128)(2,1)S(1)} collective-permute-done((bf16[448,512]{1,0:T(8,128)(2,1)}, bf16[448,512]{1,0:T(8,128)(2,1)S(1)}, u32[]{:S(2)}, u32[]{:S(2)}) %collective-permute-start.16) | collective-permute-done | bytes 458784 | tf_op jit(solution)/shard_map/ppermute | solution.py:21
  144.2 1.9 slice_bitcast_fusion.12.refs_0_
  146.2 2.8 own_sums.3.own
  149.0 5.3 collective-permute-done.7.refs_2_
  154.4 2.3 collective-permute-start.24
  156.7 1.8 slice_bitcast_fusion.13.refs_0_
  158.5 2.8 own_sums.2.own
  161.3 37.0 %collective-permute-done.23.refs_2_ = bf16[256,1920]{1,0:T(8,128)(2,1)S(1)} collective-permute-done((bf16[256,1920]{1,0:T(8,128)(2,1)S(1)}, bf16[256,1920]{1,0:T(8,128)(2,1)S(1)}, u32[]{:S(2)}, u32[]{:S(2)}) %collective-permute-start.23) | collective-permute-done | bytes 983072 | tf_op jit(solution)/shard_map/ppermute | solution.py:21
  199.6 12.3 %project.1 = bf16[4,1024,512]{2,1,0:T(8,128)(2,1)} custom-call(bf16[256,1920]{1,0:T(8,128)(2,1)} %copy-done.21, bf16[256,1920]{1,0:T(8,128)(2,1)} %copy-done.20, bf16[256,1920]{1,0:T(8,128)(2,1)} %copy-done.19, bf16[256,1920]{1,0:T(8,128)(2,1)} %copy-done.18, bf16[4,448,512]{2,1,0:T(8,128)(2,1)} %get-tuple-element.50.refs_4_, ...), custom_call_target="tpu_custom_call" | custom-call | flops 7516192768 | bytes 8388608 | tf_op jit(solution)/shard_map/project/pallas_call | solution.py:293
  211.9 13.0 %crossed.2 = (f32[512,512]{1,0:T(8,128)}, f32[2,512,512]{2,1,0:T(8,128)}) custom-call(s32[25]{0:T(128)} %pad_add_fusion.meta, bf16[4,448,512]{2,1,0:T(8,128)(2,1)} %own_sums.3.own, bf16[4,448,512]{2,1,0:T(8,128)(2,1)} %collective-permute-done.18.other, bf16[7168,512]{1,0:T(8,128)(2,1)} %bitcast.271, bf16[7168,512]{1,0:T(8,128)(2,1)} %bitcast.275), custom_call_target="tpu_custom_call" | custom-call | flops 5637144576 | bytes 22020096 | tf_op jit(solution)/shard_map/crossed/pallas_call | solution.py:252
  226.2 14.0 %crossed.3 = (f32[512,512]{1,0:T(8,128)}, f32[2,512,512]{2,1,0:T(8,128)}) custom-call(s32[25]{0:T(128)} %pad_add_fusion.meta, bf16[4,448,512]{2,1,0:T(8,128)(2,1)} %own_sums.2.own, bf16[4,448,512]{2,1,0:T(8,128)(2,1)} %copy-done.1, bf16[7168,512]{1,0:T(8,128)(2,1)} %bitcast.272, bf16[7168,512]{1,0:T(8,128)(2,1)} %bitcast.276, ...), custom_call_target="tpu_custom_call" | custom-call | flops 5637144576 | bytes 22020096 | tf_op jit(solution)/shard_map/crossed/pallas_call | solution.py:252
  240.1 52.5 %factored.1 = (f32[512,512]{1,0:T(8,128)}, bf16[2,512,512]{2,1,0:T(8,128)(2,1)}) custom-call(f32[512,512]{1,0:T(8,128)} %get-tuple-element.62.gram_ref, f32[2,512,512]{2,1,0:T(8,128)} %get-tuple-element.63.raw_ref), custom_call_target="tpu_custom_call" | custom-call | flops 40000000000 | bytes 2097152 | tf_op jit(solution)/shard_map/factored/pallas_call | solution.py:361
  295.2 2.4 collective-permute-start.30
  299.3 20.9 %collective-permute-done.28.refs_1_ = bf16[1024,512]{1,0:T(8,128)(2,1)S(1)} collective-permute-done((bf16[1024,512]{1,0:T(8,128)(2,1)S(1)}, bf16[1024,512]{1,0:T(8,128)(2,1)S(1)}, u32[]{:S(2)}, u32[]{:S(2)}) %collective-permute-start.28) | collective-permute-done | bytes 1048608 | tf_op jit(solution)/shard_map/ppermute | solution.py:21
  320.2 22.4 %collective-permute-done.30.refs_3_ = bf16[1024,512]{1,0:T(8,128)(2,1)S(1)} collective-permute-done((bf16[1024,512]{1,0:T(8,128)(2,1)S(1)}, bf16[1024,512]{1,0:T(8,128)(2,1)S(1)}, u32[]{:S(2)}, u32[]{:S(2)}) %collective-permute-start.30) | collective-permute-done | bytes 1048608 | tf_op jit(solution)/shard_map/ppermute | solution.py:21
  343.5 9.3 %hidden_rows.1 = (bf16[4,128,1024]{2,1,0:T(8,128)(2,1)}, bf16[4,128,1024]{2,1,0:T(8,128)(2,1)}, bf16[4,128,1024]{2,1,0:T(8,128)(2,1)}, bf16[4,128,1024]{2,1,0:T(8,128)(2,1)}) custom-call(s32[25]{0:T(128)} %pad_add_fusion.meta, f32[512,512]{1,0:T(8,128)} %get-tuple-element.64.inverse, bf16[2,512,512]{2,1,0:T(8,128)(2,1)} %get-tuple-element.65.mine, ...), custom_call_target="tpu_custom_call" | custom-call | flops 3758096384 | bytes 8388608 | tf_op jit(solution)/shard_map/hidden_rows/pallas_call | solution.py:409
  352.8 4.1 convolution_convert_fusion
  358.0 4.2 convolution_convert_fusion.3
  362.3 1.7 collective-permute-start.31
  364.0 1.5 convolution_convert_fusion.2
  365.5 1.6 convolution_convert_fusion.1
  367.1 25.8 %collective-permute-done.32 = bf16[512,1536]{1,0:T(8,128)(2,1)S(1)} collective-permute-done((bf16[512,1536]{1,0:T(8,128)(2,1)S(1)}, bf16[512,1536]{1,0:T(8,128)(2,1)S(1)}, u32[]{:S(2)}, u32[]{:S(2)}) %collective-permute-start.32) | collective-permute-done | bytes 1572896 | tf_op jit(solution)/shard_map/ppermute | solution.py:21
  392.9 1.8 fusion.1
  394.7 3.5 collective-permute-done.31
  398.1 1.8 fusion
  406.3 14.4 %collective-permute-done.33 = bf16[4,64,1536]{2,1,0:T(8,128)(2,1)S(1)} collective-permute-done((bf16[4,64,1536]{2,1,0:T(8,128)(2,1)S(1)}, bf16[4,64,1536]{2,1,0:T(8,128)(2,1)S(1)}, u32[]{:S(2)}, u32[]{:S(2)}) %collective-permute-start.33) | collective-permute-done | bytes 786464 | tf_op jit(solution)/shard_map/ppermute | solution.py:21
  420.9 12.9 %collective-permute-start.34 = (bf16[2,64,1536]{2,1,0:T(8,128)(2,1)S(1)}, bf16[2,64,1536]{2,1,0:T(8,128)(2,1)S(1)}, u32[]{:S(2)}, u32[]{:S(2)}) collective-permute-start(bf16[2,64,1536]{2,1,0:T(8,128)(2,1)S(1)} %slice_bitcast_fusion.20), channel_id=1, source_target_pairs={{0,8},{2,10},{4,12},{6,14},{8,0},{10,2},{12,4},{14,6},{16,24},{18,... | collective-permute-start | bytes 1179656 | tf_op jit(solution)/shard_map/ppermute | solution.py:21
  434.2 2.8 collective-permute-start.37
  437.0 6.9 %collective-permute-done.34 = bf16[2,64,1536]{2,1,0:T(8,128)(2,1)S(1)} collective-permute-done((bf16[2,64,1536]{2,1,0:T(8,128)(2,1)S(1)}, bf16[2,64,1536]{2,1,0:T(8,128)(2,1)S(1)}, u32[]{:S(2)}, u32[]{:S(2)}) %collective-permute-start.34) | collective-permute-done | bytes 393248 | tf_op jit(solution)/shard_map/ppermute | solution.py:21
  444.0 4.0 collective-permute-start.35
  448.1 2.6 collective-permute-done.37
  450.8 3.3 collective-permute-start.38
  454.1 1.6 fusion.2
  455.7 1.8 fusion.3
  461.8 13.3 %collective-permute-done.41 = bf16[4,64,1280]{2,1,0:T(8,128)(2,1)S(1)} collective-permute-done((bf16[4,64,1280]{2,1,0:T(8,128)(2,1)S(1)}, bf16[4,64,1280]{2,1,0:T(8,128)(2,1)S(1)}, u32[]{:S(2)}, u32[]{:S(2)}) %collective-permute-start.41) | collective-permute-done | bytes 655392 | tf_op jit(solution)/shard_map/ppermute | solution.py:21
  475.4 7.6 %collective-permute-start.42 = (bf16[2,64,1280]{2,1,0:T(8,128)(2,1)S(1)}, bf16[2,64,1280]{2,1,0:T(8,128)(2,1)S(1)}, u32[]{:S(2)}, u32[]{:S(2)}) collective-permute-start(bf16[2,64,1280]{2,1,0:T(8,128)(2,1)S(1)} %slice_bitcast_fusion.24), channel_id=1, source_target_pairs={{0,8},{2,10},{4,12},{6,14},{8,0},{10,2},{12,4},{14,6},{16,24},{18,... | collective-permute-start | bytes 983048 | tf_op jit(solution)/shard_map/ppermute | solution.py:21
  484.1 3.4 collective-permute-done.47
  490.5 12.1 %collective-permute-start.43 = (bf16[1,64,1280]{2,1,0:T(8,128)(2,1)S(1)}, bf16[1,64,1280]{2,1,0:T(8,128)(2,1)S(1)}, u32[]{:S(2)}, u32[]{:S(2)}) collective-permute-start(bf16[1,64,1280]{2,1,0:T(8,128)(2,1)S(1)} %slice_bitcast_fusion.36), channel_id=1, source_target_pairs={{0,16},{2,18},{4,20},{6,22},{8,24},{10,26},{12,28},{14,30},{16,0},... | collective-permute-start | bytes 491528 | tf_op jit(solution)/shard_map/ppermute | solution.py:21
  502.8 8.4 %collective-permute-done.43 = bf16[1,64,1280]{2,1,0:T(8,128)(2,1)S(1)} collective-permute-done((bf16[1,64,1280]{2,1,0:T(8,128)(2,1)S(1)}, bf16[1,64,1280]{2,1,0:T(8,128)(2,1)S(1)}, u32[]{:S(2)}, u32[]{:S(2)}) %collective-permute-start.43) | collective-permute-done | bytes 163872 | tf_op jit(solution)/shard_map/ppermute | solution.py:21
  511.3 1.7 collective-permute-done.46
  513.4 2.1 collective-permute-start.53
  515.5 5.8 %collective-permute-done.49 = bf16[2,64,768]{2,1,0:T(8,128)(2,1)S(1)} collective-permute-done((bf16[2,64,768]{2,1,0:T(8,128)(2,1)S(1)}, bf16[2,64,768]{2,1,0:T(8,128)(2,1)S(1)}, u32[]{:S(2)}, u32[]{:S(2)}) %collective-permute-start.49) | collective-permute-done | bytes 196640 | tf_op jit(solution)/shard_map/ppermute | solution.py:21
  521.5 2.2 collective-permute-done.53
  524.5 3.4 collective-permute-done.50
  528.0 2.4 collective-permute-done.54
  (202 shorter events, 51.0 us)
Async XLA Ops:
  6.5 346.3 %all-gather.3.cloned.1.call-start = ((), (), s32[]{:S(2)}) async-start(), calls=%async_computation | async-start | bytes 22020096 | tf_op jit(solution)/shard_map/all_gather | solution.py:500
  16.5 21.5 %collective-permute-start = (bf16[4,896,512]{2,1,0:T(8,128)(2,1)}, bf16[4,896,512]{2,1,0:T(8,128)(2,1)}, u32[]{:S(2)}, u32[]{:S(2)}) collective-permute-start(bf16[4,896,512]{2,1,0:T(8,128)(2,1)} %sketch_half.3), channel_id=1, source_target_pairs={{0,1},{1,0},{2,3},{3,2},{4,5},{5,4},{6,7},{7,6},{8,9},{9,8},{10,11... | collective-permute-start | bytes 11010056 | tf_op jit(solution)/shard_map/ppermute | solution.py:26
  21.3 26.1 %collective-permute-start.19 = (bf16[64,1920]{1,0:T(8,128)(2,1)}, bf16[64,1920]{1,0:T(8,128)(2,1)S(1)}, u32[]{:S(2)}, u32[]{:S(2)}) collective-permute-start(bf16[64,1920]{1,0:T(8,128)(2,1)} %get-tuple-element.59), channel_id=1, source_target_pairs={{0,2},{2,0},{4,6},{6,4},{8,10},{10,8},{12,14},{14,12},{16,18},{18,... | collective-permute-start | bytes 737288 | tf_op jit(solution)/shard_map/ppermute | solution.py:21
  24.3 24.8 %collective-permute-start.20 = (bf16[64,1920]{1,0:T(8,128)(2,1)}, bf16[64,1920]{1,0:T(8,128)(2,1)S(1)}, u32[]{:S(2)}, u32[]{:S(2)}) collective-permute-start(bf16[64,1920]{1,0:T(8,128)(2,1)} %get-tuple-element.60), channel_id=1, source_target_pairs={{0,4},{2,6},{4,0},{6,2},{8,12},{10,14},{12,8},{14,10},{16,20},{18,... | collective-permute-start | bytes 737288 | tf_op jit(solution)/shard_map/ppermute | solution.py:21
  25.8 25.2 %collective-permute-start.21 = (bf16[64,1920]{1,0:T(8,128)(2,1)}, bf16[64,1920]{1,0:T(8,128)(2,1)S(1)}, u32[]{:S(2)}, u32[]{:S(2)}) collective-permute-start(bf16[64,1920]{1,0:T(8,128)(2,1)} %get-tuple-element.61), channel_id=1, source_target_pairs={{0,6},{2,4},{4,2},{6,0},{8,14},{10,12},{12,10},{14,8},{16,22},{18,... | collective-permute-start | bytes 737288 | tf_op jit(solution)/shard_map/ppermute | solution.py:21
  45.5 13.4 %collective-permute-start.1 = (bf16[448,512]{1,0:T(8,128)(2,1)S(1)}, bf16[448,512]{1,0:T(8,128)(2,1)S(1)}, u32[]{:S(2)}, u32[]{:S(2)}) collective-permute-start(bf16[448,512]{1,0:T(8,128)(2,1)S(1)} %get-tuple-element.85), channel_id=1, source_target_pairs={{0,2},{2,0},{4,6},{6,4},{8,10},{10,8},{12,14},{14,12},{16,18},{18,... | collective-permute-start | bytes 1376264 | tf_op jit(solution)/shard_map/ppermute | solution.py:21
  47.5 23.4 %collective-permute-start.2 = (bf16[448,512]{1,0:T(8,128)(2,1)S(1)}, bf16[448,512]{1,0:T(8,128)(2,1)S(1)}, u32[]{:S(2)}, u32[]{:S(2)}) collective-permute-start(bf16[448,512]{1,0:T(8,128)(2,1)S(1)} %get-tuple-element.84), channel_id=1, source_target_pairs={{0,4},{2,6},{4,0},{6,2},{8,12},{10,14},{12,8},{14,10},{16,20},{18,... | collective-permute-start | bytes 1376264 | tf_op jit(solution)/shard_map/ppermute | solution.py:21
  49.0 23.3 %collective-permute-start.3 = (bf16[448,512]{1,0:T(8,128)(2,1)S(1)}, bf16[448,512]{1,0:T(8,128)(2,1)S(1)}, u32[]{:S(2)}, u32[]{:S(2)}) collective-permute-start(bf16[448,512]{1,0:T(8,128)(2,1)S(1)} %get-tuple-element.83), channel_id=1, source_target_pairs={{0,6},{2,4},{4,2},{6,0},{8,14},{10,12},{12,10},{14,8},{16,22},{18,... | collective-permute-start | bytes 1376264 | tf_op jit(solution)/shard_map/ppermute | solution.py:21
  49.1 29.6 %collective-permute-start.10 = (bf16[448,512]{1,0:T(8,128)(2,1)S(1)}, bf16[448,512]{1,0:T(8,128)(2,1)S(1)}, u32[]{:S(2)}, u32[]{:S(2)}) collective-permute-start(bf16[448,512]{1,0:T(8,128)(2,1)S(1)} %get-tuple-element.81), channel_id=1, source_target_pairs={{0,2},{2,0},{4,6},{6,4},{8,10},{10,8},{12,14},{14,12},{16,18},{18,... | collective-permute-start | bytes 1376264 | tf_op jit(solution)/shard_map/ppermute | solution.py:21
  51.1 37.6 %collective-permute-start.11 = (bf16[448,512]{1,0:T(8,128)(2,1)S(1)}, bf16[448,512]{1,0:T(8,128)(2,1)S(1)}, u32[]{:S(2)}, u32[]{:S(2)}) collective-permute-start(bf16[448,512]{1,0:T(8,128)(2,1)S(1)} %get-tuple-element.80), channel_id=1, source_target_pairs={{0,4},{2,6},{4,0},{6,2},{8,12},{10,14},{12,8},{14,10},{16,20},{18,... | collective-permute-start | bytes 1376264 | tf_op jit(solution)/shard_map/ppermute | solution.py:21
  58.9 29.7 %collective-permute-start.12 = (bf16[448,512]{1,0:T(8,128)(2,1)S(1)}, bf16[448,512]{1,0:T(8,128)(2,1)S(1)}, u32[]{:S(2)}, u32[]{:S(2)}) collective-permute-start(bf16[448,512]{1,0:T(8,128)(2,1)S(1)} %get-tuple-element.79), channel_id=1, source_target_pairs={{0,6},{2,4},{4,2},{6,0},{8,14},{10,12},{12,10},{14,8},{16,22},{18,... | collective-permute-start | bytes 1376264 | tf_op jit(solution)/shard_map/ppermute | solution.py:21
  61.8 92.5 %copy-start.21 = (bf16[256,1920]{1,0:T(8,128)(2,1)}, bf16[256,1920]{1,0:T(8,128)(2,1)S(1)}, u32[]{:S(2)}) copy-start(bf16[256,1920]{1,0:T(8,128)(2,1)S(1)} %constant_dynamic-update-slice_fusion.refs_0_) | copy-start | bytes 2949124
  70.8 46.4 %collective-permute-start.22 = (bf16[256,1920]{1,0:T(8,128)(2,1)S(1)}, bf16[256,1920]{1,0:T(8,128)(2,1)S(1)}, u32[]{:S(2)}, u32[]{:S(2)}) collective-permute-start(bf16[256,1920]{1,0:T(8,128)(2,1)S(1)} %constant_dynamic-update-slice_fusion.refs_0_), channel_id=1, source_target_pairs={{0,8},{2,10},{4,12},{6,14},{8,0},{10,2},{12,4},{14,6},{16,24},{18,... | collective-permute-start | bytes 2949128 | tf_op jit(solution)/shard_map/ppermute | solution.py:21
  76.0 21.3 %collective-permute-start.4 = (bf16[448,512]{1,0:T(8,128)(2,1)}, bf16[448,512]{1,0:T(8,128)(2,1)S(1)}, u32[]{:S(2)}, u32[]{:S(2)}) collective-permute-start(bf16[448,512]{1,0:T(8,128)(2,1)} %get-tuple-element.42), channel_id=1, source_target_pairs={{0,8},{2,10},{4,12},{6,14},{8,16},{10,18},{12,20},{14,22},{16,24},... | collective-permute-start | bytes 1376264 | tf_op jit(solution)/shard_map/ppermute | solution.py:32
  78.7 18.7 %collective-permute-start.5 = (bf16[448,512]{1,0:T(8,128)(2,1)}, bf16[448,512]{1,0:T(8,128)(2,1)S(1)}, u32[]{:S(2)}, u32[]{:S(2)}) collective-permute-start(bf16[448,512]{1,0:T(8,128)(2,1)} %get-tuple-element.43), channel_id=1, source_target_pairs={{8,0},{10,2},{12,4},{14,6},{16,8},{18,10},{20,12},{22,14},{24,16},... | collective-permute-start | bytes 1376264 | tf_op jit(solution)/shard_map/ppermute | solution.py:32
  92.5 11.9 %collective-permute-start.13 = (bf16[448,512]{1,0:T(8,128)(2,1)}, bf16[448,512]{1,0:T(8,128)(2,1)S(1)}, u32[]{:S(2)}, u32[]{:S(2)}) collective-permute-start(bf16[448,512]{1,0:T(8,128)(2,1)} %get-tuple-element.48), channel_id=1, source_target_pairs={{0,8},{2,10},{4,12},{6,14},{8,16},{10,18},{12,20},{14,22},{16,24},... | collective-permute-start | bytes 1376264 | tf_op jit(solution)/shard_map/ppermute | solution.py:32
  96.0 12.4 %collective-permute-start.14 = (bf16[448,512]{1,0:T(8,128)(2,1)}, bf16[448,512]{1,0:T(8,128)(2,1)S(1)}, u32[]{:S(2)}, u32[]{:S(2)}) collective-permute-start(bf16[448,512]{1,0:T(8,128)(2,1)} %get-tuple-element.49), channel_id=1, source_target_pairs={{8,0},{10,2},{12,4},{14,6},{16,8},{18,10},{20,12},{22,14},{24,16},... | collective-permute-start | bytes 1376264 | tf_op jit(solution)/shard_map/ppermute | solution.py:32
  103.4 24.0 %copy-start.31 = (bf16[448,512]{1,0:T(8,128)(2,1)S(1)}, bf16[448,512]{1,0:T(8,128)(2,1)}, u32[]{:S(2)}) copy-start(bf16[448,512]{1,0:T(8,128)(2,1)} %get-tuple-element.46) | copy-start | bytes 1376260
  103.4 40.8 %copy-start.30 = (bf16[448,512]{1,0:T(8,128)(2,1)S(1)}, bf16[448,512]{1,0:T(8,128)(2,1)}, u32[]{:S(2)}) copy-start(bf16[448,512]{1,0:T(8,128)(2,1)} %get-tuple-element.47) | copy-start | bytes 1376260
  103.4 13.8 %collective-permute-start.6 = (bf16[448,512]{1,0:T(8,128)(2,1)}, bf16[448,512]{1,0:T(8,128)(2,1)S(1)}, u32[]{:S(2)}, u32[]{:S(2)}) collective-permute-start(bf16[448,512]{1,0:T(8,128)(2,1)} %get-tuple-element.45), channel_id=1, source_target_pairs={{0,2},{2,0},{4,6},{6,4},{8,10},{10,8},{12,14},{14,12},{16,18},{18,... | collective-permute-start | bytes 1376264 | tf_op jit(solution)/shard_map/ppermute | solution.py:21
  113.7 13.7 %collective-permute-start.15 = (bf16[448,512]{1,0:T(8,128)(2,1)}, bf16[448,512]{1,0:T(8,128)(2,1)S(1)}, u32[]{:S(2)}, u32[]{:S(2)}) collective-permute-start(bf16[448,512]{1,0:T(8,128)(2,1)} %get-tuple-element.51), channel_id=1, source_target_pairs={{0,2},{2,0},{4,6},{6,4},{8,10},{10,8},{12,14},{14,12},{16,18},{18,... | collective-permute-start | bytes 1376264 | tf_op jit(solution)/shard_map/ppermute | solution.py:21
  115.1 27.8 %collective-permute-start.16 = (bf16[448,512]{1,0:T(8,128)(2,1)}, bf16[448,512]{1,0:T(8,128)(2,1)S(1)}, u32[]{:S(2)}, u32[]{:S(2)}) collective-permute-start(bf16[448,512]{1,0:T(8,128)(2,1)} %get-tuple-element.52), channel_id=1, source_target_pairs={{0,4},{2,6},{4,0},{6,2},{8,12},{10,14},{12,8},{14,10},{16,20},{18,... | collective-permute-start | bytes 1376264 | tf_op jit(solution)/shard_map/ppermute | solution.py:21
  115.7 28.5 %collective-permute-start.17 = (bf16[448,512]{1,0:T(8,128)(2,1)}, bf16[448,512]{1,0:T(8,128)(2,1)S(1)}, u32[]{:S(2)}, u32[]{:S(2)}) collective-permute-start(bf16[448,512]{1,0:T(8,128)(2,1)} %get-tuple-element.53), channel_id=1, source_target_pairs={{0,6},{2,4},{4,2},{6,0},{8,14},{10,12},{12,10},{14,8},{16,22},{18,... | collective-permute-start | bytes 1376264 | tf_op jit(solution)/shard_map/ppermute | solution.py:21
  117.2 81.1 %copy-start.20 = (bf16[256,1920]{1,0:T(8,128)(2,1)}, bf16[256,1920]{1,0:T(8,128)(2,1)S(1)}, u32[]{:S(2)}) copy-start(bf16[256,1920]{1,0:T(8,128)(2,1)S(1)} %collective-permute-done.22.refs_1_) | copy-start | bytes 2949124
  117.2 81.1 %collective-permute-start.25 = (bf16[4,448,512]{2,1,0:T(8,128)(2,1)}, bf16[4,448,512]{2,1,0:T(8,128)(2,1)}, u32[]{:S(2)}, u32[]{:S(2)}) collective-permute-start(bf16[4,448,512]{2,1,0:T(8,128)(2,1)} %get-tuple-element.50.refs_4_), channel_id=1, source_target_pairs={{0,1},{1,0},{2,3},{3,2},{4,5},{5,4},{6,7},{7,6},{8,9},{9,8},{10,11... | collective-permute-start | bytes 5505032 | tf_op jit(solution)/shard_map/ppermute | solution.py:26
  117.2 31.8 %copy-start.8 = (bf16[448,512]{1,0:T(8,128)(2,1)}, bf16[448,512]{1,0:T(8,128)(2,1)S(1)}, u32[]{:S(2)}) copy-start(bf16[448,512]{1,0:T(8,128)(2,1)S(1)} %collective-permute-done.6.refs_1_) | copy-start | bytes 1376260
  117.2 81.1 %collective-permute-start.26 = (bf16[4,448,512]{2,1,0:T(8,128)(2,1)}, bf16[4,448,512]{2,1,0:T(8,128)(2,1)}, u32[]{:S(2)}, u32[]{:S(2)}) collective-permute-start(bf16[4,448,512]{2,1,0:T(8,128)(2,1)} %get-tuple-element.44.refs_5_), channel_id=1, source_target_pairs={{0,1},{1,0},{2,3},{3,2},{4,5},{5,4},{6,7},{7,6},{8,9},{9,8},{10,11... | collective-permute-start | bytes 5505032 | tf_op jit(solution)/shard_map/ppermute | solution.py:26
  127.4 27.0 %collective-permute-start.7 = (bf16[448,512]{1,0:T(8,128)(2,1)S(1)}, bf16[448,512]{1,0:T(8,128)(2,1)S(1)}, u32[]{:S(2)}, u32[]{:S(2)}) collective-permute-start(bf16[448,512]{1,0:T(8,128)(2,1)S(1)} %copy-done.31), channel_id=1, source_target_pairs={{0,4},{2,6},{4,0},{6,2},{8,12},{10,14},{12,8},{14,10},{16,20},{18,... | collective-permute-start | bytes 1376264 | tf_op jit(solution)/shard_map/ppermute | solution.py:21
  142.9 55.4 %collective-permute-start.23 = (bf16[256,1920]{1,0:T(8,128)(2,1)S(1)}, bf16[256,1920]{1,0:T(8,128)(2,1)S(1)}, u32[]{:S(2)}, u32[]{:S(2)}) collective-permute-start(bf16[256,1920]{1,0:T(8,128)(2,1)S(1)} %constant_dynamic-update-slice_fusion.refs_0_), channel_id=1, source_target_pairs={{0,16},{2,18},{4,20},{6,22},{8,24},{10,26},{12,28},{14,30},{16,0},... | collective-permute-start | bytes 2949128 | tf_op jit(solution)/shard_map/ppermute | solution.py:21
  144.2 10.2 %collective-permute-start.8 = (bf16[448,512]{1,0:T(8,128)(2,1)S(1)}, bf16[448,512]{1,0:T(8,128)(2,1)S(1)}, u32[]{:S(2)}, u32[]{:S(2)}) collective-permute-start(bf16[448,512]{1,0:T(8,128)(2,1)S(1)} %copy-done.30), channel_id=1, source_target_pairs={{0,6},{2,4},{4,2},{6,0},{8,14},{10,12},{12,10},{14,8},{16,22},{18,... | collective-permute-start | bytes 1376264 | tf_op jit(solution)/shard_map/ppermute | solution.py:21
  154.4 57.5 %collective-permute-start.18 = (bf16[4,448,512]{2,1,0:T(8,128)(2,1)}, bf16[4,448,512]{2,1,0:T(8,128)(2,1)}, u32[]{:S(2)}, u32[]{:S(2)}) collective-permute-start(bf16[4,448,512]{2,1,0:T(8,128)(2,1)} %own_sums.3.own), channel_id=1, source_target_pairs={{0,1},{1,0},{2,3},{3,2},{4,5},{5,4},{6,7},{7,6},{8,9},{9,8},{10,11... | collective-permute-start | bytes 5505032 | tf_op jit(solution)/shard_map/ppermute | solution.py:26
  154.4 43.9 %collective-permute-start.24 = (bf16[256,1920]{1,0:T(8,128)(2,1)S(1)}, bf16[256,1920]{1,0:T(8,128)(2,1)S(1)}, u32[]{:S(2)}, u32[]{:S(2)}) collective-permute-start(bf16[256,1920]{1,0:T(8,128)(2,1)S(1)} %constant_dynamic-update-slice_fusion.refs_0_), channel_id=1, source_target_pairs={{0,24},{2,26},{4,28},{6,30},{8,16},{10,18},{12,20},{14,22},{16,8},... | collective-permute-start | bytes 2949128 | tf_op jit(solution)/shard_map/ppermute | solution.py:21
  198.3 26.5 %collective-permute-start.9 = (bf16[4,448,512]{2,1,0:T(8,128)(2,1)}, bf16[4,448,512]{2,1,0:T(8,128)(2,1)S(1)}, u32[]{:S(2)}, u32[]{:S(2)}) collective-permute-start(bf16[4,448,512]{2,1,0:T(8,128)(2,1)} %own_sums.2.own), channel_id=1, source_target_pairs={{0,1},{1,0},{2,3},{3,2},{4,5},{5,4},{6,7},{7,6},{8,9},{9,8},{10,11... | collective-permute-start | bytes 5505032 | tf_op jit(solution)/shard_map/ppermute | solution.py:26
  240.1 52.8 %copy-start = (bf16[4,1024,512]{2,1,0:T(8,128)(2,1)S(1)}, bf16[4,1024,512]{2,1,0:T(8,128)(2,1)}, u32[]{:S(2)}) copy-start(bf16[4,1024,512]{2,1,0:T(8,128)(2,1)} %project.1) | copy-start | bytes 12582916
  292.7 6.6 %collective-permute-start.27 = (bf16[2,512,512]{2,1,0:T(8,128)(2,1)}, bf16[2,512,512]{2,1,0:T(8,128)(2,1)S(1)}, u32[]{:S(2)}, u32[]{:S(2)}) collective-permute-start(bf16[2,512,512]{2,1,0:T(8,128)(2,1)} %get-tuple-element.65.mine), channel_id=1, source_target_pairs={{0,1},{1,0},{2,3},{3,2},{4,5},{5,4},{6,7},{7,6},{8,9},{9,8},{10,11... | collective-permute-start | bytes 3145736 | tf_op jit(solution)/shard_map/ppermute | solution.py:26
  294.2 26.0 %collective-permute-start.28 = (bf16[1024,512]{1,0:T(8,128)(2,1)S(1)}, bf16[1024,512]{1,0:T(8,128)(2,1)S(1)}, u32[]{:S(2)}, u32[]{:S(2)}) collective-permute-start(bf16[1024,512]{1,0:T(8,128)(2,1)S(1)} %get-tuple-element.89), channel_id=1, source_target_pairs={{0,2},{2,0},{4,6},{6,4},{8,10},{10,8},{12,14},{14,12},{16,18},{18,... | collective-permute-start | bytes 3145736 | tf_op jit(solution)/shard_map/ppermute | solution.py:21
  294.2 26.0 %collective-permute-start.29 = (bf16[1024,512]{1,0:T(8,128)(2,1)S(1)}, bf16[1024,512]{1,0:T(8,128)(2,1)S(1)}, u32[]{:S(2)}, u32[]{:S(2)}) collective-permute-start(bf16[1024,512]{1,0:T(8,128)(2,1)S(1)} %get-tuple-element.88), channel_id=1, source_target_pairs={{0,4},{2,6},{4,0},{6,2},{8,12},{10,14},{12,8},{14,10},{16,20},{18,... | collective-permute-start | bytes 3145736 | tf_op jit(solution)/shard_map/ppermute | solution.py:21
  295.2 47.3 %collective-permute-start.30 = (bf16[1024,512]{1,0:T(8,128)(2,1)S(1)}, bf16[1024,512]{1,0:T(8,128)(2,1)S(1)}, u32[]{:S(2)}, u32[]{:S(2)}) collective-permute-start(bf16[1024,512]{1,0:T(8,128)(2,1)S(1)} %get-tuple-element.87), channel_id=1, source_target_pairs={{0,6},{2,4},{4,2},{6,0},{8,14},{10,12},{12,10},{14,8},{16,22},{18,... | collective-permute-start | bytes 3145736 | tf_op jit(solution)/shard_map/ppermute | solution.py:21
  299.3 43.3 %copy-start.26 = (bf16[2,512,512]{2,1,0:T(8,128)(2,1)}, bf16[2,512,512]{2,1,0:T(8,128)(2,1)S(1)}, u32[]{:S(2)}) copy-start(bf16[2,512,512]{2,1,0:T(8,128)(2,1)S(1)} %collective-permute-done.27.others) | copy-start | bytes 3145732
  357.0 35.9 %collective-permute-start.32 = (bf16[512,1536]{1,0:T(8,128)(2,1)S(1)}, bf16[512,1536]{1,0:T(8,128)(2,1)S(1)}, u32[]{:S(2)}, u32[]{:S(2)}) collective-permute-start(bf16[512,1536]{1,0:T(8,128)(2,1)S(1)} %convolution_convert_fusion), channel_id=1, source_target_pairs={{0,4},{2,6},{4,0},{6,2},{8,12},{10,14},{12,8},{14,10},{16,20},{18,... | collective-permute-start | bytes 4718600 | tf_op jit(solution)/shard_map/ppermute | solution.py:21
  362.3 35.9 %collective-permute-start.31 = (bf16[512,1536]{1,0:T(8,128)(2,1)S(1)}, bf16[512,1536]{1,0:T(8,128)(2,1)S(1)}, u32[]{:S(2)}, u32[]{:S(2)}) collective-permute-start(bf16[512,1536]{1,0:T(8,128)(2,1)S(1)} %convolution_convert_fusion.3), channel_id=1, source_target_pairs={{0,2},{2,0},{4,6},{6,4},{8,10},{10,8},{12,14},{14,12},{16,18},{18,... | collective-permute-start | bytes 4718600 | tf_op jit(solution)/shard_map/ppermute | solution.py:21
  365.5 27.3 %copy-start.32 = (bf16[4,128,1024]{2,1,0:T(8,128)(2,1)S(1)}, bf16[4,128,1024]{2,1,0:T(8,128)(2,1)}, u32[]{:S(2)}) copy-start(bf16[4,128,1024]{2,1,0:T(8,128)(2,1)} %get-tuple-element.70) | copy-start | bytes 3145732
  400.1 20.5 %collective-permute-start.33 = (bf16[4,64,1536]{2,1,0:T(8,128)(2,1)S(1)}, bf16[4,64,1536]{2,1,0:T(8,128)(2,1)S(1)}, u32[]{:S(2)}, u32[]{:S(2)}) collective-permute-start(bf16[4,64,1536]{2,1,0:T(8,128)(2,1)S(1)} %get-tuple-element.71), channel_id=1, source_target_pairs={{0,4},{2,6},{4,0},{6,2},{8,12},{10,14},{12,8},{14,10},{16,20},{18,... | collective-permute-start | bytes 2359304 | tf_op jit(solution)/shard_map/ppermute | solution.py:21
  403.2 30.7 %collective-permute-start.36 = (bf16[4,64,1536]{2,1,0:T(8,128)(2,1)S(1)}, bf16[4,64,1536]{2,1,0:T(8,128)(2,1)S(1)}, u32[]{:S(2)}, u32[]{:S(2)}) collective-permute-start(bf16[4,64,1536]{2,1,0:T(8,128)(2,1)S(1)} %get-tuple-element.72), channel_id=1, source_target_pairs={{0,2},{2,0},{4,6},{6,4},{8,10},{10,8},{12,14},{14,12},{16,18},{18,... | collective-permute-start | bytes 2359304 | tf_op jit(solution)/shard_map/ppermute | solution.py:21
  404.2 49.8 %collective-permute-start.39 = (bf16[512,1280]{1,0:T(8,128)(2,1)S(1)}, bf16[512,1280]{1,0:T(8,128)(2,1)S(1)}, u32[]{:S(2)}, u32[]{:S(2)}) collective-permute-start(bf16[512,1280]{1,0:T(8,128)(2,1)S(1)} %convolution_convert_fusion.2), channel_id=1, source_target_pairs={{0,2},{2,0},{4,6},{6,4},{8,10},{10,8},{12,14},{14,12},{16,18},{18,... | collective-permute-start | bytes 3932168 | tf_op jit(solution)/shard_map/ppermute | solution.py:21
  405.3 50.4 %collective-permute-start.40 = (bf16[512,1280]{1,0:T(8,128)(2,1)S(1)}, bf16[512,1280]{1,0:T(8,128)(2,1)S(1)}, u32[]{:S(2)}, u32[]{:S(2)}) collective-permute-start(bf16[512,1280]{1,0:T(8,128)(2,1)S(1)} %convolution_convert_fusion.1), channel_id=1, source_target_pairs={{0,4},{2,6},{4,0},{6,2},{8,12},{10,14},{12,8},{14,10},{16,20},{18,... | collective-permute-start | bytes 3932168 | tf_op jit(solution)/shard_map/ppermute | solution.py:21
  420.9 23.0 %collective-permute-start.34 = (bf16[2,64,1536]{2,1,0:T(8,128)(2,1)S(1)}, bf16[2,64,1536]{2,1,0:T(8,128)(2,1)S(1)}, u32[]{:S(2)}, u32[]{:S(2)}) collective-permute-start(bf16[2,64,1536]{2,1,0:T(8,128)(2,1)S(1)} %slice_bitcast_fusion.20), channel_id=1, source_target_pairs={{0,8},{2,10},{4,12},{6,14},{8,0},{10,2},{12,4},{14,6},{16,24},{18,... | collective-permute-start | bytes 1179656 | tf_op jit(solution)/shard_map/ppermute | solution.py:21
  434.2 16.5 %collective-permute-start.37 = (bf16[2,64,1536]{2,1,0:T(8,128)(2,1)S(1)}, bf16[2,64,1536]{2,1,0:T(8,128)(2,1)S(1)}, u32[]{:S(2)}, u32[]{:S(2)}) collective-permute-start(bf16[2,64,1536]{2,1,0:T(8,128)(2,1)S(1)} %slice_bitcast_fusion.18), channel_id=1, source_target_pairs={{0,8},{2,10},{4,12},{6,14},{8,0},{10,2},{12,4},{14,6},{16,24},{18,... | collective-permute-start | bytes 1179656 | tf_op jit(solution)/shard_map/ppermute | solution.py:21
  444.0 16.4 %collective-permute-start.35 = (bf16[1,64,1536]{2,1,0:T(8,128)(2,1)S(1)}, bf16[1,64,1536]{2,1,0:T(8,128)(2,1)S(1)}, u32[]{:S(2)}, u32[]{:S(2)}) collective-permute-start(bf16[1,64,1536]{2,1,0:T(8,128)(2,1)S(1)} %slice_bitcast_fusion.32), channel_id=1, source_target_pairs={{0,16},{2,18},{4,20},{6,22},{8,24},{10,26},{12,28},{14,30},{16,0},... | collective-permute-start | bytes 589832 | tf_op jit(solution)/shard_map/ppermute | solution.py:21
  450.8 11.0 %collective-permute-start.38 = (bf16[1,64,1536]{2,1,0:T(8,128)(2,1)S(1)}, bf16[1,64,1536]{2,1,0:T(8,128)(2,1)S(1)}, u32[]{:S(2)}, u32[]{:S(2)}) collective-permute-start(bf16[1,64,1536]{2,1,0:T(8,128)(2,1)S(1)} %slice_bitcast_fusion.30), channel_id=1, source_target_pairs={{0,16},{2,18},{4,20},{6,22},{8,24},{10,26},{12,28},{14,30},{16,0},... | collective-permute-start | bytes 589832 | tf_op jit(solution)/shard_map/ppermute | solution.py:21
  457.6 17.6 %collective-permute-start.41 = (bf16[4,64,1280]{2,1,0:T(8,128)(2,1)S(1)}, bf16[4,64,1280]{2,1,0:T(8,128)(2,1)S(1)}, u32[]{:S(2)}, u32[]{:S(2)}) collective-permute-start(bf16[4,64,1280]{2,1,0:T(8,128)(2,1)S(1)} %slice_bitcast_fusion.10), channel_id=1, source_target_pairs={{0,4},{2,6},{4,0},{6,2},{8,12},{10,14},{12,8},{14,10},{16,20},{18,... | collective-permute-start | bytes 1966088 | tf_op jit(solution)/shard_map/ppermute | solution.py:21
  458.4 24.6 %collective-permute-start.44 = (bf16[4,64,1280]{2,1,0:T(8,128)(2,1)S(1)}, bf16[4,64,1280]{2,1,0:T(8,128)(2,1)S(1)}, u32[]{:S(2)}, u32[]{:S(2)}) collective-permute-start(bf16[4,64,1280]{2,1,0:T(8,128)(2,1)S(1)} %slice_bitcast_fusion.9), channel_id=1, source_target_pairs={{0,2},{2,0},{4,6},{6,4},{8,10},{10,8},{12,14},{14,12},{16,18},{18,... | collective-permute-start | bytes 1966088 | tf_op jit(solution)/shard_map/ppermute | solution.py:21
  459.3 28.2 %collective-permute-start.47 = (bf16[512,768]{1,0:T(8,128)(2,1)S(1)}, bf16[512,768]{1,0:T(8,128)(2,1)S(1)}, u32[]{:S(2)}, u32[]{:S(2)}) collective-permute-start(bf16[512,768]{1,0:T(8,128)(2,1)S(1)} %convolution_convert_fusion.5), channel_id=1, source_target_pairs={{0,2},{2,0},{4,6},{6,4},{8,10},{10,8},{12,14},{14,12},{16,18},{18,... | collective-permute-start | bytes 2359304 | tf_op jit(solution)/shard_map/ppermute | solution.py:21
  460.4 28.9 %collective-permute-start.51 = (bf16[512,768]{1,0:T(8,128)(2,1)S(1)}, bf16[512,768]{1,0:T(8,128)(2,1)S(1)}, u32[]{:S(2)}, u32[]{:S(2)}) collective-permute-start(bf16[512,768]{1,0:T(8,128)(2,1)S(1)} %convolution_convert_fusion.4), channel_id=1, source_target_pairs={{0,4},{2,6},{4,0},{6,2},{8,12},{10,14},{12,8},{14,10},{16,20},{18,... | collective-permute-start | bytes 2359304 | tf_op jit(solution)/shard_map/ppermute | solution.py:21
  475.4 15.1 %collective-permute-start.42 = (bf16[2,64,1280]{2,1,0:T(8,128)(2,1)S(1)}, bf16[2,64,1280]{2,1,0:T(8,128)(2,1)S(1)}, u32[]{:S(2)}, u32[]{:S(2)}) collective-permute-start(bf16[2,64,1280]{2,1,0:T(8,128)(2,1)S(1)} %slice_bitcast_fusion.24), channel_id=1, source_target_pairs={{0,8},{2,10},{4,12},{6,14},{8,0},{10,2},{12,4},{14,6},{16,24},{18,... | collective-permute-start | bytes 983048 | tf_op jit(solution)/shard_map/ppermute | solution.py:21
  483.2 19.4 %collective-permute-start.45 = (bf16[2,64,1280]{2,1,0:T(8,128)(2,1)S(1)}, bf16[2,64,1280]{2,1,0:T(8,128)(2,1)S(1)}, u32[]{:S(2)}, u32[]{:S(2)}) collective-permute-start(bf16[2,64,1280]{2,1,0:T(8,128)(2,1)S(1)} %slice_bitcast_fusion.22), channel_id=1, source_target_pairs={{0,8},{2,10},{4,12},{6,14},{8,0},{10,2},{12,4},{14,6},{16,24},{18,... | collective-permute-start | bytes 983048 | tf_op jit(solution)/shard_map/ppermute | solution.py:21
  488.5 24.5 %collective-permute-start.48 = (bf16[4,64,768]{2,1,0:T(8,128)(2,1)S(1)}, bf16[4,64,768]{2,1,0:T(8,128)(2,1)S(1)}, u32[]{:S(2)}, u32[]{:S(2)}) collective-permute-start(bf16[4,64,768]{2,1,0:T(8,128)(2,1)S(1)} %slice_bitcast_fusion.16), channel_id=1, source_target_pairs={{0,4},{2,6},{4,0},{6,2},{8,12},{10,14},{12,8},{14,10},{16,20},{18,... | collective-permute-start | bytes 1179656 | tf_op jit(solution)/shard_map/ppermute | solution.py:21
  490.3 23.0 %collective-permute-start.52 = (bf16[4,64,768]{2,1,0:T(8,128)(2,1)S(1)}, bf16[4,64,768]{2,1,0:T(8,128)(2,1)S(1)}, u32[]{:S(2)}, u32[]{:S(2)}) collective-permute-start(bf16[4,64,768]{2,1,0:T(8,128)(2,1)S(1)} %slice_bitcast_fusion.14), channel_id=1, source_target_pairs={{0,2},{2,0},{4,6},{6,4},{8,10},{10,8},{12,14},{14,12},{16,18},{18,... | collective-permute-start | bytes 1179656 | tf_op jit(solution)/shard_map/ppermute | solution.py:21
  490.5 20.7 %collective-permute-start.43 = (bf16[1,64,1280]{2,1,0:T(8,128)(2,1)S(1)}, bf16[1,64,1280]{2,1,0:T(8,128)(2,1)S(1)}, u32[]{:S(2)}, u32[]{:S(2)}) collective-permute-start(bf16[1,64,1280]{2,1,0:T(8,128)(2,1)S(1)} %slice_bitcast_fusion.36), channel_id=1, source_target_pairs={{0,16},{2,18},{4,20},{6,22},{8,24},{10,26},{12,28},{14,30},{16,0},... | collective-permute-start | bytes 491528 | tf_op jit(solution)/shard_map/ppermute | solution.py:21
  502.7 10.3 %collective-permute-start.46 = (bf16[1,64,1280]{2,1,0:T(8,128)(2,1)S(1)}, bf16[1,64,1280]{2,1,0:T(8,128)(2,1)S(1)}, u32[]{:S(2)}, u32[]{:S(2)}) collective-permute-start(bf16[1,64,1280]{2,1,0:T(8,128)(2,1)S(1)} %slice_bitcast_fusion.34), channel_id=1, source_target_pairs={{0,16},{2,18},{4,20},{6,22},{8,24},{10,26},{12,28},{14,30},{16,0},... | collective-permute-start | bytes 491528 | tf_op jit(solution)/shard_map/ppermute | solution.py:21
  513.2 8.1 %collective-permute-start.49 = (bf16[2,64,768]{2,1,0:T(8,128)(2,1)S(1)}, bf16[2,64,768]{2,1,0:T(8,128)(2,1)S(1)}, u32[]{:S(2)}, u32[]{:S(2)}) collective-permute-start(bf16[2,64,768]{2,1,0:T(8,128)(2,1)S(1)} %slice_bitcast_fusion.28), channel_id=1, source_target_pairs={{0,8},{2,10},{4,12},{6,14},{8,0},{10,2},{12,4},{14,6},{16,24},{18,... | collective-permute-start | bytes 589832 | tf_op jit(solution)/shard_map/ppermute | solution.py:21
  513.4 10.3 %collective-permute-start.53 = (bf16[2,64,768]{2,1,0:T(8,128)(2,1)S(1)}, bf16[2,64,768]{2,1,0:T(8,128)(2,1)S(1)}, u32[]{:S(2)}, u32[]{:S(2)}) collective-permute-start(bf16[2,64,768]{2,1,0:T(8,128)(2,1)S(1)} %slice_bitcast_fusion.26), channel_id=1, source_target_pairs={{0,8},{2,10},{4,12},{6,14},{8,0},{10,2},{12,4},{14,6},{16,24},{18,... | collective-permute-start | bytes 589832 | tf_op jit(solution)/shard_map/ppermute | solution.py:21
  521.4 6.6 %collective-permute-start.50 = (bf16[1,64,768]{2,1,0:T(8,128)(2,1)S(1)}, bf16[1,64,768]{2,1,0:T(8,128)(2,1)S(1)}, u32[]{:S(2)}, u32[]{:S(2)}) collective-permute-start(bf16[1,64,768]{2,1,0:T(8,128)(2,1)S(1)} %slice_bitcast_fusion.40), channel_id=1, source_target_pairs={{0,16},{2,18},{4,20},{6,22},{8,24},{10,26},{12,28},{14,30},{16,0},... | collective-permute-start | bytes 294920 | tf_op jit(solution)/shard_map/ppermute | solution.py:21
  523.8 6.6 %collective-permute-start.54 = (bf16[1,64,768]{2,1,0:T(8,128)(2,1)S(1)}, bf16[1,64,768]{2,1,0:T(8,128)(2,1)S(1)}, u32[]{:S(2)}, u32[]{:S(2)}) collective-permute-start(bf16[1,64,768]{2,1,0:T(8,128)(2,1)S(1)} %slice_bitcast_fusion.38), channel_id=1, source_target_pairs={{0,16},{2,18},{4,20},{6,22},{8,24},{10,26},{12,28},{14,30},{16,0},... | collective-permute-start | bytes 294920 | tf_op jit(solution)/shard_map/ppermute | solution.py:21
  (31 other events, 162.9 us)
Sparse Core Ops, SparseCore 0:
  17.1 29.4 all-gather.2

commit v4 on v3

--- a/solution.py
+++ b/solution.py
@@ -111,11 +111,11 @@
 
 
 def sketch_kernel(meta, gate, up, sketch, out):
-    value = mul(gate[...], sketch[0]) + mul(up[...], sketch[1])
-    out[0] = value.astype(out.dtype)
-
-
-def sketch_half(meta, gate, up, sketch, side, dtype, rows):
+    both = jnp.concatenate([gate[...], up[...]], axis=1)
+    out[0] = mul(both, jnp.concatenate([sketch[0], sketch[1]], axis=0)).astype(BF16)
+
+
+def sketch_half(meta, gate, up, sketch, side, rows):
     hid, rank = sketch.shape[1:]
     row_block = pl.BlockSpec((rows, hid), lambda k, meta: (meta[side * MOST + k], 0))
     return pl.pallas_call(
@@ -126,7 +126,7 @@
             in_specs=[row_block, row_block, pl.BlockSpec((2, hid, rank), lambda k, meta: (0, 0, 0))],
             out_specs=pl.BlockSpec((1, rows, rank), lambda k, meta: (k, 0, 0)),
         ),
-        out_shape=jax.ShapeDtypeStruct((MOST, rows, rank), dtype),
+        out_shape=jax.ShapeDtypeStruct((MOST, rows, rank), BF16),
         compiler_params=params(),
         cost_estimate=cost(4 * MOST * rows * hid * rank, 4 * MOST * rows * hid),
         name="sketch_half",
@@ -180,10 +180,9 @@
         refs[MOST][k] = refs[k][...]
 
 
-def cluster_rows(meta, own):
-    shape = own[0].shape
+def cluster_rows(meta, got, riders):
+    shape = got[0].shape
     experts = lax.axis_size("expert")
-    got = [own[0]] + [swap_expert(own[k], k) for k in range(1, MOST)]
     piece = jax.ShapeDtypeStruct(shape, BF16)
     stacked = jax.ShapeDtypeStruct((MOST,) + shape, BF16)
     tail, head = pl.pallas_call(
@@ -196,6 +195,7 @@
     )(meta, *got)
     below = shift_groups(tail, MOST)
     above = shift_groups(head, -MOST)
+    below, above, riders = lax.optimization_barrier((below, above, riders))
     sums, *sends = pl.pallas_call(
         functools.partial(totals_kernel, experts),
         out_shape=[stacked] + [piece] * (MOST - 1),
@@ -213,14 +213,14 @@
         compiler_params=params(),
         name="own_sums",
     )(*back)
-    return sums, mine
-
-
-def cross_kernel(started, meta, own, other, gate, up, *refs):
+    return sums, mine, riders
+
+
+def cross_kernel(started, meta, own, other, gate, gate_other, up, up_other, *refs):
     if started:
-        old_gram, old_raw, gram, raw, current = refs
+        old_gram, old_raw, gram, raw = refs
     else:
-        gram, raw, current = refs
+        gram, raw = refs
     step = pl.program_id(0)
 
     @pl.when(step == 0)
@@ -228,41 +228,29 @@
         gram[...] = old_gram[...] if started else jnp.zeros(gram.shape, F32)
         raw[...] = old_raw[...] if started else jnp.zeros(raw.shape, F32)
 
-    @pl.when(step < MOST)
-    def _():
-        current[...] = own[0]
-
-    @pl.when(step >= MOST)
-    def _():
-        current[...] = other[0]
-
-    rows = current[...]
+    rows = jnp.concatenate([own[0], other[0]], axis=0)
     turned = rows.T
     gram[...] += mul(turned, rows)
-    raw[0] += mul(turned, gate[...])
-    raw[1] += mul(turned, up[...])
+    raw[0] += mul(turned, jnp.concatenate([gate[...], gate_other[...]], axis=0))
+    raw[1] += mul(turned, jnp.concatenate([up[...], up_other[...]], axis=0))
 
 
 def crossed(meta, own, other, gate, up, chunk, chunks, before):
     _, rows, rank = own.shape
     hid = gate.shape[1]
+    sum_block = pl.BlockSpec((1, rows, rank), lambda i, meta: (i, 0, 0))
     row_block = pl.BlockSpec((rows, hid), lambda i, meta: (meta[i] * chunks + chunk, 0))
+    other_block = pl.BlockSpec((rows, hid), lambda i, meta: (meta[MOST + i] * chunks + chunk, 0))
     gram_spec = pl.BlockSpec((rank, rank), lambda i, meta: (0, 0))
     raw_spec = pl.BlockSpec((2, rank, hid), lambda i, meta: (0, 0, 0))
     return pl.pallas_call(
         functools.partial(cross_kernel, bool(before)),
         grid_spec=pltpu.PrefetchScalarGridSpec(
             num_scalar_prefetch=1,
-            grid=(2 * MOST,),
-            in_specs=[
-                pl.BlockSpec((1, rows, rank), lambda i, meta: (jnp.minimum(i, MOST - 1), 0, 0)),
-                pl.BlockSpec((1, rows, rank), lambda i, meta: (jnp.maximum(i - MOST, 0), 0, 0)),
-                row_block,
-                row_block,
-            ]
+            grid=(MOST,),
+            in_specs=[sum_block, sum_block, row_block, other_block, row_block, other_block]
             + ([gram_spec, raw_spec] if before else []),
             out_specs=[gram_spec, raw_spec],
-            scratch_shapes=[pltpu.VMEM((rows, rank), BF16)],
         ),
         out_shape=[
             jax.ShapeDtypeStruct((rank, rank), F32),
@@ -271,45 +259,60 @@
         compiler_params=params(),
         cost_estimate=cost(4 * MOST * rows * rank * (rank + 2 * hid), 8 * MOST * rows * rank * 3),
         name="crossed",
-    )(meta, own, other, gate, up, *before)
-
-
-def project_kernel(chunks, *refs):
-    tokens, refs = refs[: -2 * chunks - 2], refs[-2 * chunks - 2 :]
-    sums, out, basis = refs[: 2 * chunks], refs[-2], refs[-1]
+    )(meta, own, other, gate, gate, up, up, *before)
+
+
+def project_kernel(count, *refs):
+    tokens, sums, out, basis = refs[:count], refs[count:-2], refs[-2], refs[-1]
     rows = sums[0].shape[1]
     for i, ref in enumerate(sums):
         basis[i * rows : (i + 1) * rows, :] = ref[0]
     toks = tokens[0].shape[0]
     for i, ref in enumerate(tokens):
-        out[0, i * toks : (i + 1) * toks] = mul(ref[:, LANES:], basis[...]).astype(BF16)
-
-
-def project(tokens, sums):
+        out[i * toks : (i + 1) * toks, :] = mul(ref[:, LANES:], basis[...]).astype(BF16)
+
+
+def project(tokens, sums, k):
     rank = sums[0].shape[-1]
     toks, width = tokens[0].shape
     depth = width - LANES
     total = len(tokens) * toks
     return pl.pallas_call(
-        functools.partial(project_kernel, len(sums) // 2),
-        grid=(MOST,),
-        in_specs=[pl.BlockSpec((toks, width), lambda k: (0, 0))] * len(tokens)
-        + [pl.BlockSpec((1,) + value.shape[1:], lambda k: (k, 0, 0)) for value in sums],
-        out_specs=pl.BlockSpec((1, total, rank), lambda k: (k, 0, 0)),
-        out_shape=jax.ShapeDtypeStruct((MOST, total, rank), BF16),
+        functools.partial(project_kernel, len(tokens)),
+        grid=(1,),
+        in_specs=[pl.BlockSpec((toks, width), lambda i: (0, 0))] * len(tokens)
+        + [pl.BlockSpec((1,) + value.shape[1:], lambda i: (k, 0, 0)) for value in sums],
+        out_specs=pl.BlockSpec((total, rank), lambda i: (0, 0)),
+        out_shape=jax.ShapeDtypeStruct((total, rank), BF16),
         scratch_shapes=[pltpu.VMEM((depth, rank), BF16)],
         compiler_params=params(),
-        cost_estimate=cost(2 * MOST * total * depth * rank, 4 * MOST * total * rank),
+        cost_estimate=cost(2 * total * depth * rank, 4 * total * rank),
         name="project",
     )(*tokens, *sums)
+
+
+def reciprocal(value):
+    guess = pl.reciprocal(value, approx=True)
+    guess = guess * (2.0 - value * guess)
+    return guess * (2.0 - value * guess)
 
 
 def factor_kernel(tile, gram_ref, raw_ref, inverse_ref, coeff_ref, work_ref):
     rank = gram_ref.shape[0]
     steps = rank // tile
-    work_ref[...] = gram_ref[...]
     row_of = lax.broadcasted_iota(jnp.int32, (tile, tile), 0)
     col_of = lax.broadcasted_iota(jnp.int32, (tile, tile), 1)
+    corners = [
+        jnp.where(row_of == col_of, gram_ref[t * tile : (t + 1) * tile, t * tile : (t + 1) * tile], 0.0)
+        for t in range(steps)
+    ]
+    scale = lax.rsqrt(
+        jnp.concatenate([jnp.sum(c, axis=0, keepdims=True) for c in corners], axis=1)
+    )
+    for t in range(steps):
+        strip = slice(t * tile, (t + 1) * tile)
+        scale_rows = lax.rsqrt(jnp.sum(corners[t], axis=1, keepdims=True))
+        work_ref[strip, :] = gram_ref[strip, :] * scale_rows * scale
     lane = lax.broadcasted_iota(jnp.int32, (8, tile), 1)
     sub = lax.broadcasted_iota(jnp.int32, (8, tile), 0)
     lane_row = lane[:1]
@@ -320,16 +323,26 @@
         strips = [
             work_ref[pl.ds(pl.multiple_of(base + 8 * s, 8), 8), here] for s in range(tile // 8)
         ]
-        for j in range(tile):
+        for j in range(0, tile, 2):
             first, inner = divmod(j, 8)
-            row = strips[first][inner : inner + 1, :]
-            pivot = 1.0 / row[:, j : j + 1]
-            scaled = jnp.where(lane_row == j, 1.0, row) * pivot
+            both = strips[first]
+            row0, row1 = both[inner : inner + 1, :], both[inner + 1 : inner + 2, :]
+            a, b, d = row0[:, j : j + 1], row1[:, j : j + 1], row1[:, j + 1 : j + 2]
+            inverse_a = reciprocal(a)
+            inverse_d = a * reciprocal(a * d - b * b)
+            ratio = b * inverse_a
+            later = jnp.where(lane_row == j, 0.0, row1) - ratio * jnp.where(lane_row == j, 1.0, row0)
+            scaled0 = jnp.where(lane_row == j, 1.0, row0) * inverse_a
+            scaled1 = jnp.where(lane_row == j + 1, 1.0, later) * inverse_d
             for s in range(first, tile // 8):
                 strip = strips[s]
-                column = strip[:, j : j + 1]
-                new = jnp.where(lane == j, 0.0, strip) - column * scaled
-                strips[s] = jnp.where(sub > inner, new, strip) if s == first else new
+                column0 = strip[:, j : j + 1]
+                column1 = strip[:, j + 1 : j + 2] - column0 * ratio
+                new = jnp.where((lane == j) | (lane == j + 1), 0.0, strip)
+                new = new - column0 * jnp.where(lane_row == j + 1, 0.0, scaled0) - column1 * scaled1
+                if s == first:
+                    new = jnp.where(sub > inner + 1, new, jnp.where(sub == inner + 1, later, strip))
+                strips[s] = new
         block = jnp.concatenate(strips, axis=0)
         pivots = jnp.sum(jnp.where(row_of == col_of, block, 0.0), axis=1, keepdims=True)
         unit = jnp.where(row_of == col_of, 1.0, 0.0)
@@ -337,7 +350,7 @@
         work_ref[here, here] = unit
         right = exact(own, work_ref[here, :], ((1,), (0,)))
         columns = lax.broadcasted_iota(jnp.int32, (tile, rank), 1)
-        inverse_ref[here, :] = jnp.where(columns < base + tile, right, 0.0)
+        inverse_ref[here, :] = jnp.where(columns < base + tile, right * scale, 0.0)
         for s in range(steps - 1):
 
             @pl.when(index == s)
@@ -398,6 +411,7 @@
             rows = hidden[k * toks : (k + 1) * toks]
             outs[x][0, y * toks : (y + 1) * toks, block] = rows
             outs[2 + y][0, x * toks : (x + 1) * toks, block] = rows
+        outs[4][0, :, block] = hidden
 
 
 def hidden_rows(meta, inverse, coeff, other_coeff, tokens, arrived, toks):
@@ -417,69 +431,69 @@
             pl.BlockSpec((block, LANES), lambda g: (g, 0)),
         ]
         + [pl.BlockSpec((block, rank), lambda g: (g, 0))] * MOST,
-        out_specs=[pl.BlockSpec((1, block // 2, 2 * hid), lambda g: (g, 0, 0))] * 4,
-        out_shape=[out] * 4,
+        out_specs=[pl.BlockSpec((1, block // 2, 2 * hid), lambda g: (g, 0, 0))] * 4
+        + [pl.BlockSpec((1, block, 2 * hid), lambda g: (g, 0, 0))],
+        out_shape=[out] * 4 + [jax.ShapeDtypeStruct((groups, block, 2 * hid), BF16)],
         compiler_params=params(),
         cost_estimate=cost(groups * block * rank * (6 * rank + 8 * hid), 16 * groups * block * hid),
         name="hidden_rows",
     )(meta, inverse, coeff, other_coeff, tokens, *arrived)
 
 
-def column_chunks(depth):
+def group_masks(experts):
+    masks, mask = [], MOST
+    while mask < experts:
+        masks.insert(0, mask)
+        mask *= 2
+    return masks
+
+
+def column_chunks(depth, bits):
+    near = list(range(bits - 1, 1, -1))
+    orders = [[0, 1] + near, [1, 0] + near, near + [0, 1]]
     units = depth // LANES
-    if units % 2 or units < 6:
-        return [(0, depth, 0)]
-    left = units // 2
-    sizes = [left * 12 // 28, left * 10 // 28]
-    sizes.append(left - sum(sizes))
+    if units % 56:
+        return [(0, depth, orders[0])]
+    sizes = [(13, 0), (13, 1), (10, 2), (10, 0), (10, 1)]
     chunks, start = [], 0
-    for size in sizes:
-        for order in range(2):
-            chunks.append((start, size * LANES, order))
-            start += size * LANES
+    for size, order in sizes:
+        width = size * (units // 56) * LANES
+        chunks.append((start, width, orders[order]))
+        start += width
     return chunks
 
 
 def scattered_answers(sides, down, toks):
-    depth = down.shape[1]
     experts = lax.axis_size("expert")
-    chunks = column_chunks(depth)
+    masks = [1, 2] + group_masks(experts)
+    bits = len(masks)
+    chunks = column_chunks(down.shape[1], bits)
+    groups = experts // MOST
+    halves = {0: sides[0:2], 1: sides[2:4]}
+    if groups > 1:
+        halves[bits - 1] = (sides[4][: groups // 2], sides[4][groups // 2 :])
 
     def answered(rows, start, width):
         return mul(rows.reshape(-1, rows.shape[-1]), down[:, start : start + width])
 
-    first = [answered(sides[2 * order + 1], start, width).astype(BF16) for start, width, order in chunks]
-    pairs = [list(range(i, min(i + 2, len(chunks)))) for i in range(0, len(chunks), 2)]
-    outs = []
-    held = None
-    for pair in pairs:
-        outgoing = [first[i] for i in pair]
-        if held is not None:
-            tied = lax.optimization_barrier(tuple(outgoing) + tuple(held))
-            outgoing, held = list(tied[: len(pair)]), list(tied[len(pair) :])
-            finish(held_kept, held, outs, toks, experts)
-        came = [swap_expert(value, 1 << chunks[i][2]) for value, i in zip(outgoing, pair)]
-        kept, sends = [], []
-        for value, i in zip(came, pair):
-            start, width, order = chunks[i]
-            total = answered(sides[2 * order], start, width) + value.astype(F32)
-            total = total.astype(BF16).reshape(-1, 2, toks, width)
-            kept.append((total[:, 0], 2 >> order))
-            sends.append(total[:, 1])
-        held, held_kept = sends, kept
-    finish(held_kept, held, outs, toks, experts)
-    return jnp.concatenate(outs, axis=1)
-
-
-def finish(kept, sends, outs, toks, experts):
-    for (mine, mask), outgoing in zip(kept, sends):
-        value = mine.astype(F32) + swap_expert(outgoing, mask).astype(F32)
-        bit = MOST
-        while bit < experts:
-            value = value.astype(BF16).reshape(-1, 2, toks, value.shape[-1])
-            value = value[:, 0].astype(F32) + swap_expert(value[:, 1], bit).astype(F32)
-            bit *= 2
-        outs.append(value[0].astype(BF16))
+    first = [
+        swap_expert(answered(halves[order[0]][1], start, width).astype(BF16), masks[order[0]])
+        for start, width, order in chunks
+    ]
+    values = [
+        (answered(halves[order[0]][0], start, width) + came.astype(F32)).astype(BF16)
+        for came, (start, width, order) in zip(first, chunks)
+    ]
+    left = [[bit for bit in range(bits - 1, -1, -1) if bit != order[0]] for _, _, order in chunks]
+    for step in range(1, bits):
+        for i, (_, width, order) in enumerate(chunks):
+            bit = order[step]
+            axis = left[i].index(bit)
+            value = values[i].reshape((2,) * len(left[i]) + (toks, width))
+            kept, out = (lax.index_in_dim(value, side, axis, keepdims=False) for side in (0, 1))
+            values[i] = (kept.astype(F32) + swap_expert(out, masks[bit]).astype(F32)).astype(BF16)
+            left[i].remove(bit)
+    return jnp.concatenate([value.reshape(toks, -1) for value in values], axis=1)
 
 
 def on_device(tokens, gate_weight, up_weight, down_weight, sketch, clusters, routes, route_weights):
@@ -499,38 +513,53 @@
 
     down_rows = lax.all_gather(down_weight[0], "dp", axis=0, tiled=True)
 
-    sent_half = swap_dp(sketch_half(meta, gate_rows, up_rows, sketch[0], 1, BF16, rows))
-    own_half = sketch_half(meta, gate_rows, up_rows, sketch[0], 0, F32, rows)
+    sent_half = swap_dp(sketch_half(meta, gate_rows, up_rows, sketch[0], 1, rows))
+    own_half = sketch_half(meta, gate_rows, up_rows, sketch[0], 0, rows)
     pieces = token_pieces(meta, tokens, routes, route_weights, groups, rows, place)
     plane = [pieces[0]] + [swap_expert(pieces[k], k) for k in range(1, MOST)]
-    plane = jnp.concatenate(plane, axis=0)
-    spread = [plane] + [swap_expert(plane, step * MOST) for step in range(1, groups)]
+    spread = jnp.concatenate(plane, axis=0)
+    spread, own_half = lax.optimization_barrier((spread, own_half))
 
     chunks = 2 if rows % 32 == 0 else 1
     chunk = rows // chunks
-    group_sums, own_sums = [], []
+    got = []
     for c in range(chunks):
         span = slice(c * chunk, (c + 1) * chunk)
         own = [
-            (own_half[k, span] + sent_half[k, span].astype(F32)).astype(BF16) for k in range(MOST)
+            (own_half[k, span].astype(F32) + sent_half[k, span].astype(F32)).astype(BF16)
+            for k in range(MOST)
         ]
-        sums, mine = cluster_rows(meta, own)
+        got.append([own[0]] + [swap_expert(own[k], k) for k in range(1, MOST)])
+    group_sums, own_sums = [], []
+    masks = group_masks(experts)
+    for c in range(chunks):
+        share = masks[c * len(masks) // chunks : (c + 1) * len(masks) // chunks]
+        for mask in share[:-1]:
+            spread = jnp.concatenate([spread, swap_expert(spread, mask)], axis=0)
+        came = swap_expert(spread, share[-1]) if share else spread[:16]
+        if c == 0:
+            sums, mine, came = cluster_rows(meta, got[c], came)
+        else:
+            sums, mine, _ = cluster_rows(meta, got[c], meta)
+        if share:
+            spread = jnp.concatenate([spread, came], axis=0)
         group_sums.append((sums, swap_dp(sums)))
         own_sums.append((mine, swap_dp(mine)))
-
-    parts = project(spread, [sums[d] for d in range(2) for sums in group_sums])
+    halves = [sums[d] for d in range(2) for sums in group_sums]
+    sends = {k: project([spread], halves, k) for k in (3, 1, 2, 0)}
+    parts = [sends[k] for k in range(MOST)]
     before = ()
     for c in range(chunks):
         before = crossed(meta, *own_sums[c], gate_rows, up_rows, c, chunks, before)
     gram, raw = before
     if lax.axis_size("tensor") > 1:
         gram, raw = lax.psum((gram, raw), "tensor")
-        parts = lax.psum(parts.astype(F32), "tensor").astype(BF16)
+        parts = [lax.psum(value.astype(F32), "tensor").astype(BF16) for value in parts]
     gram, raw, parts = lax.optimization_barrier((gram, raw, parts))
     arrived = [parts[0]] + [swap_expert(parts[k], k) for k in range(1, MOST)]
     inverse, coeff = factored(gram, raw)
     other_coeff = swap_dp(coeff)
-    shares = jnp.concatenate([value[:, :LANES] for value in spread], axis=0)
+    shares = spread[:, :LANES]
     sides = hidden_rows(meta, inverse, coeff, other_coeff, shares, arrived, toks)
     return scattered_answers(sides, down_rows, toks)
 

time: 547 us -> 491 us (0.90)
  starting transfers between devices: 96.2 us -> 60 us
  waiting for transfers between devices: 232 us -> 204 us
  Pallas kernels: 144 us -> 153 us
    ppermute x45 -> x40, starting transfers between devices: 86.6 us -> 49.2 us  [swap_expert(): lax.ppermute(value, 'expert', [(source, source ^ mask) for source in rang...]
    ppermute x45 -> x40, waiting for transfers between devices: 228 us -> 203 us  [swap_expert(): lax.ppermute(value, 'expert', [(source, source ^ mask) for source in rang...]
    pallas_call x1 -> x4, Pallas kernels: 12.3 us -> 22.6 us  [project(): pl.pallas_call(functools.partial(project_kernel, len(tokens)), grid=(1,),...]
    unnamed x77 -> x82, local copies, waits for them, and re-layouts: 10.3 us -> 13.5 us
    dot_general x12 -> x10, matrix products: 22.5 us -> 22.5 us  [mul(): return lax.dot_general(a, b, (dims, ((), ())), preferred_element_type=F32)]
  transfers between devices with their start and end apart: 56 -> 51, of which waited for: 24 -> 23; matrix products, arithmetic and copies ran while one was open for 7% -> 8% of each run, Pallas kernels for 25% -> 31%
where the time goes in v4:
time: 491 us; the launch traced here: 486 us
  waiting for transfers between devices  204 us (42%)
  Pallas kernels  153 us (31%)
  starting transfers between devices  60 us (12%)
  matrix products  22.5 us (5%)
  local copies, waits for them, and re-layouts  22.1 us (5%)
  between operations  14.3 us (3%)
  other arithmetic  9.64 us (2%)
    ppermute x40, waiting for transfers between devices, swap_expert(): lax.ppermute(value, 'expert', [(source, source ^ mask) for source in rang...  203 us
    pallas_call x1, Pallas kernels, factored(): pl.pallas_call(functools.partial(factor_kernel, min(LANES, rank)), out_sh...  53.5 us
    ppermute x40, starting transfers between devices, swap_expert(): lax.ppermute(value, 'expert', [(source, source ^ mask) for source in rang...  49.2 us
    pallas_call x2, Pallas kernels, crossed(): pl.pallas_call(functools.partial(cross_kernel, bool(before)), grid_spec=p...  24.8 us
    pallas_call x4, Pallas kernels, project(): pl.pallas_call(functools.partial(project_kernel, len(tokens)), grid=(1,),...  22.6 us
    dot_general x10, matrix products, mul(): return lax.dot_general(a, b, (dims, ((), ())), preferred_element_type=F32)  22.5 us
    pallas_call x2, Pallas kernels, sketch_half(): pl.pallas_call(sketch_kernel, grid_spec=pltpu.PrefetchScalarGridSpec(num_...  18.8 us
    unnamed x82, local copies, waits for them, and re-layouts  13.5 us
  transfers between devices with their start and end apart: 51, of which 23 were waited for; matrix products, arithmetic and copies ran while one was open for 8% of the time, Pallas kernels for 31%

profile of v4, /device:TPU:0, one launch (start us, length us, event | category | flops | bytes accessed | tf_op | source)
XLA Modules:
  0.0 485.6 jit_solution(7449861959065403685)
XLA Ops:
  7.9 8.9 %sketch_half.3 = bf16[4,896,512]{2,1,0:T(8,128)(2,1)} custom-call(s32[25]{0:T(128)} %pad_add_fusion.meta, bf16[7168,512]{1,0:T(8,128)(2,1)} %bitcast.162, bf16[7168,512]{1,0:T(8,128)(2,1)} %bitcast.168, bf16[2,512,512]{2,1,0:T(8,128)(2,1)} %bitcast.174), custom_call_target="tpu_custom_call" | custom-call | flops 3758096384 | bytes 7340032 | tf_op jit(solution)/shard_map/sketch_half/pallas_call | solution.py:121
  18.6 3.0 token_pieces.1
  21.6 2.5 collective-permute-start
  24.1 1.5 collective-permute-start.1
  25.7 9.9 %sketch_half.2 = bf16[4,896,512]{2,1,0:T(8,128)(2,1)} custom-call(s32[25]{0:T(128)} %pad_add_fusion.meta, bf16[7168,512]{1,0:T(8,128)(2,1)} %bitcast.163, bf16[7168,512]{1,0:T(8,128)(2,1)} %bitcast.169, bf16[2,512,512]{2,1,0:T(8,128)(2,1)} %bitcast.175), custom_call_target="tpu_custom_call" | custom-call | flops 3758096384 | bytes 7340032 | tf_op jit(solution)/shard_map/sketch_half/pallas_call | solution.py:121
  35.6 2.2 collective-permute-done.1
  37.9 2.7 collective-permute-start.18
  40.5 5.3 %fusion.38 = (bf16[448,512]{1,0:T(8,128)(2,1)S(1)}, bf16[448,512]{1,0:T(8,128)(2,1)S(1)}, bf16[448,512]{1,0:T(8,128)(2,1)S(1)}, bf16[448,512]{1,0:T(8,128)(2,1)}...) fusion(bf16[4,896,512]{2,1,0:T(8,128)(2,1)} %collective-permute, ...), kind=kLoop, calls=%fused_computation.70 | loop fusion | flops 7340032 | bytes 11010048 | tf_op jit(solution)/shard_map/convert_element_type | solution.py:529
  50.5 8.7 %collective-permute-done.13.refs_1_ = bf16[448,512]{1,0:T(8,128)(2,1)S(1)} collective-permute-done((bf16[448,512]{1,0:T(8,128)(2,1)S(1)}, bf16[448,512]{1,0:T(8,128)(2,1)S(1)}, u32[]{:S(2)}, u32[]{:S(2)}) %collective-permute-start.13) | collective-permute-done | bytes 458784 | tf_op jit(solution)/shard_map/ppermute | solution.py:21
  59.2 1.5 collective-permute-start.5
  60.8 8.4 %collective-permute-done.14.refs_2_ = bf16[448,512]{1,0:T(8,128)(2,1)S(1)} collective-permute-done((bf16[448,512]{1,0:T(8,128)(2,1)S(1)}, bf16[448,512]{1,0:T(8,128)(2,1)S(1)}, u32[]{:S(2)}, u32[]{:S(2)}) %collective-permute-start.14) | collective-permute-done | bytes 458784 | tf_op jit(solution)/shard_map/ppermute | solution.py:21
  71.3 2.9 end_sums.3
  74.2 3.5 collective-permute-start.16
  80.2 7.9 %collective-permute-done.5.refs_2_ = bf16[448,512]{1,0:T(8,128)(2,1)S(1)} collective-permute-done((bf16[448,512]{1,0:T(8,128)(2,1)S(1)}, bf16[448,512]{1,0:T(8,128)(2,1)S(1)}, u32[]{:S(2)}, u32[]{:S(2)}) %collective-permute-start.5) | collective-permute-done | bytes 458784 | tf_op jit(solution)/shard_map/ppermute | solution.py:21
  89.1 2.9 end_sums.2
  92.0 3.5 collective-permute-start.7
  98.6 4.6 cluster_sums.3
  106.6 2.6 collective-permute-start.23
  109.3 1.6 collective-permute-start.21
  111.6 4.6 cluster_sums.2
  116.9 7.8 %collective-permute-done.20.refs_2_ = bf16[448,512]{1,0:T(8,128)(2,1)S(1)} collective-permute-done((bf16[448,512]{1,0:T(8,128)(2,1)}, bf16[448,512]{1,0:T(8,128)(2,1)S(1)}, u32[]{:S(2)}, u32[]{:S(2)}) %collective-permute-start.20) | collective-permute-done | bytes 458784 | tf_op jit(solution)/shard_map/ppermute | solution.py:21
  124.7 1.6 collective-permute-start.11
  126.3 16.9 %collective-permute-done.10.refs_2_ = bf16[448,512]{1,0:T(8,128)(2,1)S(1)} collective-permute-done((bf16[448,512]{1,0:T(8,128)(2,1)}, bf16[448,512]{1,0:T(8,128)(2,1)S(1)}, u32[]{:S(2)}, u32[]{:S(2)}) %collective-permute-start.10) | collective-permute-done | bytes 458784 | tf_op jit(solution)/shard_map/ppermute | solution.py:21
  145.4 2.9 own_sums.3.own
  148.4 1.9 slice_bitcast_fusion.9.refs_0_
  150.3 4.8 collective-permute-done.9.refs_1_
  155.9 2.8 own_sums.2.own
  161.3 1.8 constant_dynamic-update-slice_fusion.refs_0_
  163.2 1.8 copy-done
  165.6 5.6 %project.7 = bf16[1024,512]{1,0:T(8,128)(2,1)} custom-call(bf16[1024,1920]{1,0:T(8,128)(2,1)} %copy-done, bf16[4,448,512]{2,1,0:T(8,128)(2,1)} %get-tuple-element.63.refs_1_, bf16[4,448,512]{2,1,0:T(8,128)(2,1)} %get-tuple-element.54.refs_2_, bf16[4,448,512]{2,1,0:T(8,128)(2,1)} %copy-done.2, bf16[4,448,512]{2,1,0:T(8,128)(2,1)} %collective-permute-done.25.refs_4_), custom_call_target="tpu_custom_call" | custom-call | flops 1879048192 | bytes 2097152 | tf_op jit(solution)/shard_map/project/pallas_call | solution.py:280
  171.2 5.7 %project.6 = bf16[1024,512]{1,0:T(8,128)(2,1)} custom-call(bf16[1024,1920]{1,0:T(8,128)(2,1)} %copy-done, bf16[4,448,512]{2,1,0:T(8,128)(2,1)} %get-tuple-element.63.refs_1_, bf16[4,448,512]{2,1,0:T(8,128)(2,1)} %get-tuple-element.54.refs_2_, bf16[4,448,512]{2,1,0:T(8,128)(2,1)} %copy-done.2, bf16[4,448,512]{2,1,0:T(8,128)(2,1)} %collective-permute-done.25.refs_4_), custom_call_target="tpu_custom_call" | custom-call | flops 1879048192 | bytes 2097152 | tf_op jit(solution)/shard_map/project/pallas_call | solution.py:280
  176.9 5.7 %project.5 = bf16[1024,512]{1,0:T(8,128)(2,1)} custom-call(bf16[1024,1920]{1,0:T(8,128)(2,1)} %copy-done, bf16[4,448,512]{2,1,0:T(8,128)(2,1)} %get-tuple-element.63.refs_1_, bf16[4,448,512]{2,1,0:T(8,128)(2,1)} %get-tuple-element.54.refs_2_, bf16[4,448,512]{2,1,0:T(8,128)(2,1)} %copy-done.2, bf16[4,448,512]{2,1,0:T(8,128)(2,1)} %collective-permute-done.25.refs_4_), custom_call_target="tpu_custom_call" | custom-call | flops 1879048192 | bytes 2097152 | tf_op jit(solution)/shard_map/project/pallas_call | solution.py:280
  182.6 5.6 %project.4.refs_0_ = bf16[1024,512]{1,0:T(8,128)(2,1)} custom-call(bf16[1024,1920]{1,0:T(8,128)(2,1)} %copy-done, bf16[4,448,512]{2,1,0:T(8,128)(2,1)} %get-tuple-element.63.refs_1_, bf16[4,448,512]{2,1,0:T(8,128)(2,1)} %get-tuple-element.54.refs_2_, bf16[4,448,512]{2,1,0:T(8,128)(2,1)} %copy-done.2, bf16[4,448,512]{2,1,0:T(8,128)(2,1)} %collective-permute-done.25.refs_4_), custom_call_target="tpu_custom_call" | custom-call | flops 1879048192 | bytes 2097152 | tf_op jit(solution)/shard_map/project/pallas_call | solution.py:280
  188.2 11.9 %crossed.2 = (f32[512,512]{1,0:T(8,128)}, f32[2,512,512]{2,1,0:T(8,128)}) custom-call(s32[25]{0:T(128)} %pad_add_fusion.meta, bf16[4,448,512]{2,1,0:T(8,128)(2,1)} %own_sums.3.own, bf16[4,448,512]{2,1,0:T(8,128)(2,1)} %collective-permute-done.22.other, bf16[7168,512]{1,0:T(8,128)(2,1)} %bitcast.164, bf16[7168,512]{1,0:T(8,128)(2,1)} %bitcast.165, ...), custom_call_target="tpu_custom_call" | custom-call | flops 5637144576 | bytes 22020096 | tf_op jit(solution)/shard_map/crossed/pallas_call | solution.py:246
  200.1 12.9 %crossed.3 = (f32[512,512]{1,0:T(8,128)}, f32[2,512,512]{2,1,0:T(8,128)}) custom-call(s32[25]{0:T(128)} %pad_add_fusion.meta, bf16[4,448,512]{2,1,0:T(8,128)(2,1)} %own_sums.2.own, bf16[4,448,512]{2,1,0:T(8,128)(2,1)} %collective-permute-done.12.other, bf16[7168,512]{1,0:T(8,128)(2,1)} %bitcast.166, bf16[7168,512]{1,0:T(8,128)(2,1)} %bitcast.167, ...), custom_call_target="tpu_custom_call" | custom-call | flops 5637144576 | bytes 22020096 | tf_op jit(solution)/shard_map/crossed/pallas_call | solution.py:246
  213.0 53.5 %factored.1 = (f32[512,512]{1,0:T(8,128)}, bf16[2,512,512]{2,1,0:T(8,128)(2,1)}) custom-call(f32[512,512]{1,0:T(8,128)} %get-tuple-element.72.gram_ref, f32[2,512,512]{2,1,0:T(8,128)} %get-tuple-element.73.raw_ref), custom_call_target="tpu_custom_call" | custom-call | flops 40000000000 | bytes 2097152 | tf_op jit(solution)/shard_map/factored/pallas_call | solution.py:374
  270.5 1.7 slice.239.tokens
  272.2 20.9 %collective-permute-done.27.refs_1_ = bf16[1024,512]{1,0:T(8,128)(2,1)S(1)} collective-permute-done((bf16[1024,512]{1,0:T(8,128)(2,1)S(1)}, bf16[1024,512]{1,0:T(8,128)(2,1)S(1)}, u32[]{:S(2)}, u32[]{:S(2)}) %collective-permute-start.27) | collective-permute-done | bytes 1048608 | tf_op jit(solution)/shard_map/ppermute | solution.py:21
  293.0 22.4 %collective-permute-done.28.refs_2_ = bf16[1024,512]{1,0:T(8,128)(2,1)S(1)} collective-permute-done((bf16[1024,512]{1,0:T(8,128)(2,1)S(1)}, bf16[1024,512]{1,0:T(8,128)(2,1)S(1)}, u32[]{:S(2)}, u32[]{:S(2)}) %collective-permute-start.28) | collective-permute-done | bytes 1048608 | tf_op jit(solution)/shard_map/ppermute | solution.py:21
  316.8 9.7 %hidden_rows.1 = (bf16[4,128,1024]{2,1,0:T(8,128)(2,1)}, bf16[4,128,1024]{2,1,0:T(8,128)(2,1)}, bf16[4,128,1024]{2,1,0:T(8,128)(2,1)}, bf16[4,128,1024]{2,1,0:T(8,128)(2,1)}, bf16[4,256,1024]{2,1,0:T(8,128)(2,1)}) custom-call(s32[25]{0:T(128)} %pad_add_fusion.meta, f32[512,512]{1,0:T(8,128)} %get-tuple-element.74.inverse, ...), custom_call_target="tpu_custom_call" | custom-call | flops 3758096384 | bytes 8388608 | tf_op jit(solution)/shard_map/hidden_rows/pallas_call | solution.py:423
  326.5 1.8 fusion.53
  328.3 3.7 convolution_convert_fusion
  332.9 3.9 convolution_convert_fusion.1
  337.6 1.6 convolution_convert_fusion.2
  340.4 2.1 fusion.9
  343.4 2.1 fusion.6
  347.0 16.8 %collective-permute-done.46 = bf16[512,1280]{1,0:T(8,128)(2,1)S(1)} collective-permute-done((bf16[512,1280]{1,0:T(8,128)(2,1)S(1)}, bf16[512,1280]{1,0:T(8,128)(2,1)S(1)}, u32[]{:S(2)}, u32[]{:S(2)}) %collective-permute-start.46) | collective-permute-done | bytes 1310752 | tf_op jit(solution)/shard_map/ppermute | solution.py:21
  363.8 1.5 fusion.14
  366.3 2.3 collective-permute-done.42
  368.6 1.6 fusion.13
  371.1 1.6 fusion.12
  374.4 26.0 %collective-permute-done.34 = bf16[512,1664]{1,0:T(8,128)(2,1)S(1)} collective-permute-done((bf16[512,1664]{1,0:T(8,128)(2,1)S(1)}, bf16[512,1664]{1,0:T(8,128)(2,1)S(1)}, u32[]{:S(2)}, u32[]{:S(2)}) %collective-permute-start.34) | collective-permute-done | bytes 1703968 | tf_op jit(solution)/shard_map/ppermute | solution.py:21
  400.3 2.3 add_convert_fusion
  405.1 2.1 add_convert_fusion.1
  408.2 11.0 %collective-permute-done.47 = bf16[2,2,64,1280]{3,2,1,0:T(8,128)(2,1)S(1)} collective-permute-done((bf16[2,2,64,1280]{3,2,1,0:T(8,128)(2,1)S(1)}, bf16[2,2,64,1280]{3,2,1,0:T(8,128)(2,1)S(1)}, u32[]{:S(2)}, u32[]{:S(2)}) %collective-permute-start.47) | collective-permute-done | bytes 655392 | tf_op jit(solution)/shard_map/ppermute | solution.py:21
  422.7 6.3 %collective-permute-done.48 = bf16[2,64,1280]{2,1,0:T(8,128)(2,1)S(1)} collective-permute-done((bf16[2,64,1280]{2,1,0:T(8,128)(2,1)S(1)}, bf16[2,64,1280]{2,1,0:T(8,128)(2,1)S(1)}, u32[]{:S(2)}, u32[]{:S(2)}) %collective-permute-start.48) | collective-permute-done | bytes 327712 | tf_op jit(solution)/shard_map/ppermute | solution.py:21
  429.1 2.7 collective-permute-start.49
  431.8 3.9 collective-permute-done.44
  436.0 5.8 %collective-permute-done.40 = bf16[2,64,1280]{2,1,0:T(8,128)(2,1)S(1)} collective-permute-done((bf16[2,64,1280]{2,1,0:T(8,128)(2,1)S(1)}, bf16[2,64,1280]{2,1,0:T(8,128)(2,1)S(1)}, u32[]{:S(2)}, u32[]{:S(2)}) %collective-permute-start.40) | collective-permute-done | bytes 327712 | tf_op jit(solution)/shard_map/ppermute | solution.py:21
  445.6 12.7 %collective-permute-done.32 = bf16[2,64,1664]{2,1,0:T(8,128)(2,1)S(1)} collective-permute-done((bf16[2,64,1664]{2,1,0:T(8,128)(2,1)S(1)}, bf16[2,64,1664]{2,1,0:T(8,128)(2,1)S(1)}, u32[]{:S(2)}, u32[]{:S(2)}) %collective-permute-start.32) | collective-permute-done | bytes 426016 | tf_op jit(solution)/shard_map/ppermute | solution.py:21
  458.5 5.9 %collective-permute-done.36 = bf16[2,64,1664]{2,1,0:T(8,128)(2,1)S(1)} collective-permute-done((bf16[2,64,1664]{2,1,0:T(8,128)(2,1)S(1)}, bf16[2,64,1664]{2,1,0:T(8,128)(2,1)S(1)}, u32[]{:S(2)}, u32[]{:S(2)}) %collective-permute-start.36) | collective-permute-done | bytes 426016 | tf_op jit(solution)/shard_map/ppermute | solution.py:21
  464.6 2.2 collective-permute-start.37
  466.8 7.3 %collective-permute-done.33 = bf16[64,1664]{1,0:T(8,128)(2,1)S(1)} collective-permute-done((bf16[64,1664]{1,0:T(8,128)(2,1)S(1)}, bf16[64,1664]{1,0:T(8,128)(2,1)S(1)}, u32[]{:S(2)}, u32[]{:S(2)}) %collective-permute-start.33) | collective-permute-done | bytes 213024 | tf_op jit(solution)/shard_map/ppermute | solution.py:21
  474.1 2.6 collective-permute-done.37
  (189 shorter events, 55.1 us)
Async XLA Ops:
  6.5 321.7 %all-gather.3.cloned.1.call-start = ((), (), s32[]{:S(2)}) async-start(), calls=%async_computation | async-start | bytes 22020096 | tf_op jit(solution)/shard_map/all_gather | solution.py:514
  16.8 23.7 %collective-permute-start.3 = (bf16[4,896,512]{2,1,0:T(8,128)(2,1)}, bf16[4,896,512]{2,1,0:T(8,128)(2,1)}, u32[]{:S(2)}, u32[]{:S(2)}) collective-permute-start(bf16[4,896,512]{2,1,0:T(8,128)(2,1)} %sketch_half.3), channel_id=1, source_target_pairs={{0,1},{1,0},{2,3},{3,2},{4,5},{5,4},{6,7},{7,6},{8,9},{9,8},{10,11... | collective-permute-start | bytes 11010056 | tf_op jit(solution)/shard_map/ppermute | solution.py:26
  21.6 14.0 %collective-permute-start = (bf16[64,1920]{1,0:T(8,128)(2,1)}, bf16[64,1920]{1,0:T(8,128)(2,1)S(1)}, u32[]{:S(2)}, u32[]{:S(2)}) collective-permute-start(bf16[64,1920]{1,0:T(8,128)(2,1)} %get-tuple-element.46), channel_id=1, source_target_pairs={{0,2},{2,0},{4,6},{6,4},{8,10},{10,8},{12,14},{14,12},{16,18},{18,... | collective-permute-start | bytes 737288 | tf_op jit(solution)/shard_map/ppermute | solution.py:21
  24.1 13.6 %collective-permute-start.1 = (bf16[64,1920]{1,0:T(8,128)(2,1)}, bf16[64,1920]{1,0:T(8,128)(2,1)S(1)}, u32[]{:S(2)}, u32[]{:S(2)}) collective-permute-start(bf16[64,1920]{1,0:T(8,128)(2,1)} %get-tuple-element.47), channel_id=1, source_target_pairs={{0,4},{2,6},{4,0},{6,2},{8,12},{10,14},{12,8},{14,10},{16,20},{18,... | collective-permute-start | bytes 737288 | tf_op jit(solution)/shard_map/ppermute | solution.py:21
  25.7 12.1 %copy-start.24 = (bf16[64,1920]{1,0:T(8,128)(2,1)S(1)}, bf16[64,1920]{1,0:T(8,128)(2,1)}, u32[]{:S(2)}) copy-start(bf16[64,1920]{1,0:T(8,128)(2,1)} %get-tuple-element.45) | copy-start | bytes 737284
  25.7 12.1 %collective-permute-start.2 = (bf16[64,1920]{1,0:T(8,128)(2,1)}, bf16[64,1920]{1,0:T(8,128)(2,1)S(1)}, u32[]{:S(2)}, u32[]{:S(2)}) collective-permute-start(bf16[64,1920]{1,0:T(8,128)(2,1)} %get-tuple-element.48), channel_id=1, source_target_pairs={{0,6},{2,4},{4,2},{6,0},{8,14},{10,12},{12,10},{14,8},{16,22},{18,... | collective-permute-start | bytes 737288 | tf_op jit(solution)/shard_map/ppermute | solution.py:21
  37.8 67.3 %copy-start.3 = (bf16[256,1920]{1,0:T(8,128)(2,1)}, bf16[256,1920]{1,0:T(8,128)(2,1)S(1)}, u32[]{:S(2)}) copy-start(bf16[256,1920]{1,0:T(8,128)(2,1)S(1)} %pad_maximum_fusion.1) | copy-start | bytes 2949124
  37.9 59.1 %collective-permute-start.18 = (bf16[256,1920]{1,0:T(8,128)(2,1)S(1)}, bf16[256,1920]{1,0:T(8,128)(2,1)S(1)}, u32[]{:S(2)}, u32[]{:S(2)}) collective-permute-start(bf16[256,1920]{1,0:T(8,128)(2,1)S(1)} %pad_maximum_fusion.1), channel_id=1, source_target_pairs={{0,16},{2,18},{4,20},{6,22},{8,24},{10,26},{12,28},{14,30},{16,0},... | collective-permute-start | bytes 2949128 | tf_op jit(solution)/shard_map/ppermute | solution.py:21
  45.8 13.5 %collective-permute-start.13 = (bf16[448,512]{1,0:T(8,128)(2,1)S(1)}, bf16[448,512]{1,0:T(8,128)(2,1)S(1)}, u32[]{:S(2)}, u32[]{:S(2)}) collective-permute-start(bf16[448,512]{1,0:T(8,128)(2,1)S(1)} %get-tuple-element.87), channel_id=1, source_target_pairs={{0,2},{2,0},{4,6},{6,4},{8,10},{10,8},{12,14},{14,12},{16,18},{18,... | collective-permute-start | bytes 1376264 | tf_op jit(solution)/shard_map/ppermute | solution.py:21
  47.0 22.1 %collective-permute-start.14 = (bf16[448,512]{1,0:T(8,128)(2,1)S(1)}, bf16[448,512]{1,0:T(8,128)(2,1)S(1)}, u32[]{:S(2)}, u32[]{:S(2)}) collective-permute-start(bf16[448,512]{1,0:T(8,128)(2,1)S(1)} %get-tuple-element.86), channel_id=1, source_target_pairs={{0,4},{2,6},{4,0},{6,2},{8,12},{10,14},{12,8},{14,10},{16,20},{18,... | collective-permute-start | bytes 1376264 | tf_op jit(solution)/shard_map/ppermute | solution.py:21
  47.8 22.7 %collective-permute-start.15 = (bf16[448,512]{1,0:T(8,128)(2,1)S(1)}, bf16[448,512]{1,0:T(8,128)(2,1)S(1)}, u32[]{:S(2)}, u32[]{:S(2)}) collective-permute-start(bf16[448,512]{1,0:T(8,128)(2,1)S(1)} %get-tuple-element.85), channel_id=1, source_target_pairs={{0,6},{2,4},{4,2},{6,0},{8,14},{10,12},{12,10},{14,8},{16,22},{18,... | collective-permute-start | bytes 1376264 | tf_op jit(solution)/shard_map/ppermute | solution.py:21
  49.3 29.7 %collective-permute-start.4 = (bf16[448,512]{1,0:T(8,128)(2,1)S(1)}, bf16[448,512]{1,0:T(8,128)(2,1)S(1)}, u32[]{:S(2)}, u32[]{:S(2)}) collective-permute-start(bf16[448,512]{1,0:T(8,128)(2,1)S(1)} %get-tuple-element.91), channel_id=1, source_target_pairs={{0,2},{2,0},{4,6},{6,4},{8,10},{10,8},{12,14},{14,12},{16,18},{18,... | collective-permute-start | bytes 1376264 | tf_op jit(solution)/shard_map/ppermute | solution.py:21
  59.2 11.3 %copy-start.8 = (bf16[448,512]{1,0:T(8,128)(2,1)}, bf16[448,512]{1,0:T(8,128)(2,1)S(1)}, u32[]{:S(2)}) copy-start(bf16[448,512]{1,0:T(8,128)(2,1)S(1)} %collective-permute-done.13.refs_1_) | copy-start | bytes 1376260
  59.2 28.9 %collective-permute-start.5 = (bf16[448,512]{1,0:T(8,128)(2,1)S(1)}, bf16[448,512]{1,0:T(8,128)(2,1)S(1)}, u32[]{:S(2)}, u32[]{:S(2)}) collective-permute-start(bf16[448,512]{1,0:T(8,128)(2,1)S(1)} %get-tuple-element.90), channel_id=1, source_target_pairs={{0,4},{2,6},{4,0},{6,2},{8,12},{10,14},{12,8},{14,10},{16,20},{18,... | collective-permute-start | bytes 1376264 | tf_op jit(solution)/shard_map/ppermute | solution.py:21
  69.2 19.0 %collective-permute-start.6 = (bf16[448,512]{1,0:T(8,128)(2,1)S(1)}, bf16[448,512]{1,0:T(8,128)(2,1)S(1)}, u32[]{:S(2)}, u32[]{:S(2)}) collective-permute-start(bf16[448,512]{1,0:T(8,128)(2,1)S(1)} %get-tuple-element.89), channel_id=1, source_target_pairs={{0,6},{2,4},{4,2},{6,0},{8,14},{10,12},{12,10},{14,8},{16,22},{18,... | collective-permute-start | bytes 1376264 | tf_op jit(solution)/shard_map/ppermute | solution.py:21
  74.2 22.8 %collective-permute-start.16 = (bf16[448,512]{1,0:T(8,128)(2,1)}, bf16[448,512]{1,0:T(8,128)(2,1)S(1)}, u32[]{:S(2)}, u32[]{:S(2)}) collective-permute-start(bf16[448,512]{1,0:T(8,128)(2,1)} %get-tuple-element.58), channel_id=1, source_target_pairs={{0,8},{2,10},{4,12},{6,14},{8,16},{10,18},{12,20},{14,22},{16,24},... | collective-permute-start | bytes 1376264 | tf_op jit(solution)/shard_map/ppermute | solution.py:32
  78.9 18.1 %collective-permute-start.17 = (bf16[448,512]{1,0:T(8,128)(2,1)}, bf16[448,512]{1,0:T(8,128)(2,1)S(1)}, u32[]{:S(2)}, u32[]{:S(2)}) collective-permute-start(bf16[448,512]{1,0:T(8,128)(2,1)} %get-tuple-element.59), channel_id=1, source_target_pairs={{8,0},{10,2},{12,4},{14,6},{16,8},{18,10},{20,12},{22,14},{24,16},... | collective-permute-start | bytes 1376264 | tf_op jit(solution)/shard_map/ppermute | solution.py:32
  92.0 17.2 %collective-permute-start.7 = (bf16[448,512]{1,0:T(8,128)(2,1)}, bf16[448,512]{1,0:T(8,128)(2,1)S(1)}, u32[]{:S(2)}, u32[]{:S(2)}) collective-permute-start(bf16[448,512]{1,0:T(8,128)(2,1)} %get-tuple-element.50), channel_id=1, source_target_pairs={{0,8},{2,10},{4,12},{6,14},{8,16},{10,18},{12,20},{14,22},{16,24},... | collective-permute-start | bytes 1376264 | tf_op jit(solution)/shard_map/ppermute | solution.py:32
  95.5 15.3 %collective-permute-start.8 = (bf16[448,512]{1,0:T(8,128)(2,1)}, bf16[448,512]{1,0:T(8,128)(2,1)S(1)}, u32[]{:S(2)}, u32[]{:S(2)}) collective-permute-start(bf16[448,512]{1,0:T(8,128)(2,1)} %get-tuple-element.51), channel_id=1, source_target_pairs={{8,0},{10,2},{12,4},{14,6},{16,8},{18,10},{20,12},{22,14},{24,16},... | collective-permute-start | bytes 1376264 | tf_op jit(solution)/shard_map/ppermute | solution.py:32
  103.2 13.7 %collective-permute-start.19 = (bf16[448,512]{1,0:T(8,128)(2,1)}, bf16[448,512]{1,0:T(8,128)(2,1)S(1)}, u32[]{:S(2)}, u32[]{:S(2)}) collective-permute-start(bf16[448,512]{1,0:T(8,128)(2,1)} %get-tuple-element.64), channel_id=1, source_target_pairs={{0,2},{2,0},{4,6},{6,4},{8,10},{10,8},{12,14},{14,12},{16,18},{18,... | collective-permute-start | bytes 1376264 | tf_op jit(solution)/shard_map/ppermute | solution.py:21
  103.8 20.9 %collective-permute-start.20 = (bf16[448,512]{1,0:T(8,128)(2,1)}, bf16[448,512]{1,0:T(8,128)(2,1)S(1)}, u32[]{:S(2)}, u32[]{:S(2)}) collective-permute-start(bf16[448,512]{1,0:T(8,128)(2,1)} %get-tuple-element.65), channel_id=1, source_target_pairs={{0,4},{2,6},{4,0},{6,2},{8,12},{10,14},{12,8},{14,10},{16,20},{18,... | collective-permute-start | bytes 1376264 | tf_op jit(solution)/shard_map/ppermute | solution.py:21
  106.6 10.3 %copy-start.1 = (bf16[4,448,512]{2,1,0:T(8,128)(2,1)S(1)}, bf16[4,448,512]{2,1,0:T(8,128)(2,1)}, u32[]{:S(2)}) copy-start(bf16[4,448,512]{2,1,0:T(8,128)(2,1)} %get-tuple-element.63.refs_1_) | copy-start | bytes 5505028
  106.6 54.7 %collective-permute-start.23 = (bf16[512,1920]{1,0:T(8,128)(2,1)}, bf16[512,1920]{1,0:T(8,128)(2,1)}, u32[]{:S(2)}, u32[]{:S(2)}) collective-permute-start(bf16[512,1920]{1,0:T(8,128)(2,1)} %pad_maximum_fusion), channel_id=1, source_target_pairs={{0,8},{2,10},{4,12},{6,14},{8,0},{10,2},{12,4},{14,6},{16,24},{18,... | collective-permute-start | bytes 5898248 | tf_op jit(solution)/shard_map/ppermute | solution.py:21
  109.3 15.5 %collective-permute-start.21 = (bf16[448,512]{1,0:T(8,128)(2,1)S(1)}, bf16[448,512]{1,0:T(8,128)(2,1)S(1)}, u32[]{:S(2)}, u32[]{:S(2)}) collective-permute-start(bf16[448,512]{1,0:T(8,128)(2,1)S(1)} %copy-done.34), channel_id=1, source_target_pairs={{0,6},{2,4},{4,2},{6,0},{8,14},{10,12},{12,10},{14,8},{16,22},{18,... | collective-permute-start | bytes 1376264 | tf_op jit(solution)/shard_map/ppermute | solution.py:21
  116.2 27.1 %collective-permute-start.10 = (bf16[448,512]{1,0:T(8,128)(2,1)}, bf16[448,512]{1,0:T(8,128)(2,1)S(1)}, u32[]{:S(2)}, u32[]{:S(2)}) collective-permute-start(bf16[448,512]{1,0:T(8,128)(2,1)} %get-tuple-element.56), channel_id=1, source_target_pairs={{0,4},{2,6},{4,0},{6,2},{8,12},{10,14},{12,8},{14,10},{16,20},{18,... | collective-permute-start | bytes 1376264 | tf_op jit(solution)/shard_map/ppermute | solution.py:21
  116.9 28.5 %copy-start.14 = (bf16[448,512]{1,0:T(8,128)(2,1)}, bf16[448,512]{1,0:T(8,128)(2,1)S(1)}, u32[]{:S(2)}) copy-start(bf16[448,512]{1,0:T(8,128)(2,1)S(1)} %collective-permute-done.19.refs_1_) | copy-start | bytes 1376260
  116.9 46.3 %collective-permute-start.24 = (bf16[4,448,512]{2,1,0:T(8,128)(2,1)S(1)}, bf16[4,448,512]{2,1,0:T(8,128)(2,1)S(1)}, u32[]{:S(2)}, u32[]{:S(2)}) collective-permute-start(bf16[4,448,512]{2,1,0:T(8,128)(2,1)S(1)} %copy-done.1), channel_id=1, source_target_pairs={{0,1},{1,0},{2,3},{3,2},{4,5},{5,4},{6,7},{7,6},{8,9},{9,8},{10,11... | collective-permute-start | bytes 5505032 | tf_op jit(solution)/shard_map/ppermute | solution.py:26
  124.7 20.7 %copy-start.15 = (bf16[448,512]{1,0:T(8,128)(2,1)}, bf16[448,512]{1,0:T(8,128)(2,1)S(1)}, u32[]{:S(2)}) copy-start(bf16[448,512]{1,0:T(8,128)(2,1)S(1)} %collective-permute-done.20.refs_2_) | copy-start | bytes 1376260
  124.7 38.5 %collective-permute-start.25 = (bf16[4,448,512]{2,1,0:T(8,128)(2,1)}, bf16[4,448,512]{2,1,0:T(8,128)(2,1)}, u32[]{:S(2)}, u32[]{:S(2)}) collective-permute-start(bf16[4,448,512]{2,1,0:T(8,128)(2,1)} %get-tuple-element.54.refs_2_), channel_id=1, source_target_pairs={{0,1},{1,0},{2,3},{3,2},{4,5},{5,4},{6,7},{7,6},{8,9},{9,8},{10,11... | collective-permute-start | bytes 5505032 | tf_op jit(solution)/shard_map/ppermute | solution.py:26
  124.7 20.7 %copy-start.16 = (bf16[448,512]{1,0:T(8,128)(2,1)}, bf16[448,512]{1,0:T(8,128)(2,1)S(1)}, u32[]{:S(2)}) copy-start(bf16[448,512]{1,0:T(8,128)(2,1)S(1)} %collective-permute-done.21.refs_3_) | copy-start | bytes 1376260
  124.7 23.6 %collective-permute-start.11 = (bf16[448,512]{1,0:T(8,128)(2,1)}, bf16[448,512]{1,0:T(8,128)(2,1)S(1)}, u32[]{:S(2)}, u32[]{:S(2)}) collective-permute-start(bf16[448,512]{1,0:T(8,128)(2,1)} %get-tuple-element.57), channel_id=1, source_target_pairs={{0,6},{2,4},{4,2},{6,0},{8,14},{10,12},{12,10},{14,8},{16,22},{18,... | collective-permute-start | bytes 1376264 | tf_op jit(solution)/shard_map/ppermute | solution.py:21
  143.2 11.9 %collective-permute-start.9 = (bf16[448,512]{1,0:T(8,128)(2,1)}, bf16[448,512]{1,0:T(8,128)(2,1)S(1)}, u32[]{:S(2)}, u32[]{:S(2)}) collective-permute-start(bf16[448,512]{1,0:T(8,128)(2,1)} %get-tuple-element.55), channel_id=1, source_target_pairs={{0,2},{2,0},{4,6},{6,4},{8,10},{10,8},{12,14},{14,12},{16,18},{18,... | collective-permute-start | bytes 1376264 | tf_op jit(solution)/shard_map/ppermute | solution.py:21
  148.3 39.9 %collective-permute-start.22 = (bf16[4,448,512]{2,1,0:T(8,128)(2,1)}, bf16[4,448,512]{2,1,0:T(8,128)(2,1)}, u32[]{:S(2)}, u32[]{:S(2)}) collective-permute-start(bf16[4,448,512]{2,1,0:T(8,128)(2,1)} %own_sums.3.own), channel_id=1, source_target_pairs={{0,1},{1,0},{2,3},{3,2},{4,5},{5,4},{6,7},{7,6},{8,9},{9,8},{10,11... | collective-permute-start | bytes 5505032 | tf_op jit(solution)/shard_map/ppermute | solution.py:26
  158.7 41.4 %collective-permute-start.12 = (bf16[4,448,512]{2,1,0:T(8,128)(2,1)}, bf16[4,448,512]{2,1,0:T(8,128)(2,1)}, u32[]{:S(2)}, u32[]{:S(2)}) collective-permute-start(bf16[4,448,512]{2,1,0:T(8,128)(2,1)} %own_sums.2.own), channel_id=1, source_target_pairs={{0,1},{1,0},{2,3},{3,2},{4,5},{5,4},{6,7},{7,6},{8,9},{9,8},{10,11... | collective-permute-start | bytes 5505032 | tf_op jit(solution)/shard_map/ppermute | solution.py:26
  213.0 54.0 %copy-start.13 = (bf16[1024,512]{1,0:T(8,128)(2,1)S(1)}, bf16[1024,512]{1,0:T(8,128)(2,1)}, u32[]{:S(2)}) copy-start(bf16[1024,512]{1,0:T(8,128)(2,1)} %project.5) | copy-start | bytes 3145732
  213.0 55.2 %copy-start.12 = (bf16[1024,512]{1,0:T(8,128)(2,1)S(1)}, bf16[1024,512]{1,0:T(8,128)(2,1)}, u32[]{:S(2)}) copy-start(bf16[1024,512]{1,0:T(8,128)(2,1)} %project.6) | copy-start | bytes 3145732
  213.0 56.0 %copy-start.11 = (bf16[1024,512]{1,0:T(8,128)(2,1)S(1)}, bf16[1024,512]{1,0:T(8,128)(2,1)}, u32[]{:S(2)}) copy-start(bf16[1024,512]{1,0:T(8,128)(2,1)} %project.7) | copy-start | bytes 3145732
  266.5 5.7 %collective-permute-start.26 = (bf16[2,512,512]{2,1,0:T(8,128)(2,1)}, bf16[2,512,512]{2,1,0:T(8,128)(2,1)S(1)}, u32[]{:S(2)}, u32[]{:S(2)}) collective-permute-start(bf16[2,512,512]{2,1,0:T(8,128)(2,1)} %get-tuple-element.75.mine), channel_id=1, source_target_pairs={{0,1},{1,0},{2,3},{3,2},{4,5},{5,4},{6,7},{7,6},{8,9},{9,8},{10,11... | collective-permute-start | bytes 3145736 | tf_op jit(solution)/shard_map/ppermute | solution.py:26
  267.0 26.0 %collective-permute-start.27 = (bf16[1024,512]{1,0:T(8,128)(2,1)S(1)}, bf16[1024,512]{1,0:T(8,128)(2,1)S(1)}, u32[]{:S(2)}, u32[]{:S(2)}) collective-permute-start(bf16[1024,512]{1,0:T(8,128)(2,1)S(1)} %copy-done.13), channel_id=1, source_target_pairs={{0,2},{2,0},{4,6},{6,4},{8,10},{10,8},{12,14},{14,12},{16,18},{18,... | collective-permute-start | bytes 3145736 | tf_op jit(solution)/shard_map/ppermute | solution.py:21
  268.2 47.3 %collective-permute-start.28 = (bf16[1024,512]{1,0:T(8,128)(2,1)S(1)}, bf16[1024,512]{1,0:T(8,128)(2,1)S(1)}, u32[]{:S(2)}, u32[]{:S(2)}) collective-permute-start(bf16[1024,512]{1,0:T(8,128)(2,1)S(1)} %copy-done.12), channel_id=1, source_target_pairs={{0,4},{2,6},{4,0},{6,2},{8,12},{10,14},{12,8},{14,10},{16,20},{18,... | collective-permute-start | bytes 3145736 | tf_op jit(solution)/shard_map/ppermute | solution.py:21
  269.0 46.4 %collective-permute-start.29 = (bf16[1024,512]{1,0:T(8,128)(2,1)S(1)}, bf16[1024,512]{1,0:T(8,128)(2,1)S(1)}, u32[]{:S(2)}, u32[]{:S(2)}) collective-permute-start(bf16[1024,512]{1,0:T(8,128)(2,1)S(1)} %copy-done.11), channel_id=1, source_target_pairs={{0,6},{2,4},{4,2},{6,0},{8,14},{10,12},{12,10},{14,8},{16,22},{18,... | collective-permute-start | bytes 3145736 | tf_op jit(solution)/shard_map/ppermute | solution.py:21
  272.2 43.3 %copy-start.30 = (bf16[2,512,512]{2,1,0:T(8,128)(2,1)}, bf16[2,512,512]{2,1,0:T(8,128)(2,1)S(1)}, u32[]{:S(2)}) copy-start(bf16[2,512,512]{2,1,0:T(8,128)(2,1)S(1)} %collective-permute-done.26.others) | copy-start | bytes 3145732
  293.0 22.5 %copy-start.31 = (bf16[1024,512]{1,0:T(8,128)(2,1)}, bf16[1024,512]{1,0:T(8,128)(2,1)S(1)}, u32[]{:S(2)}) copy-start(bf16[1024,512]{1,0:T(8,128)(2,1)S(1)} %collective-permute-done.27.refs_1_) | copy-start | bytes 3145732
  332.0 31.8 %collective-permute-start.46 = (bf16[512,1280]{1,0:T(8,128)(2,1)S(1)}, bf16[512,1280]{1,0:T(8,128)(2,1)S(1)}, u32[]{:S(2)}, u32[]{:S(2)}) collective-permute-start(bf16[512,1280]{1,0:T(8,128)(2,1)S(1)} %convolution_convert_fusion), channel_id=1, source_target_pairs={{0,4},{2,6},{4,0},{6,2},{8,12},{10,14},{12,8},{14,10},{16,20},{18,... | collective-permute-start | bytes 3932168 | tf_op jit(solution)/shard_map/ppermute | solution.py:21
  336.8 31.8 %collective-permute-start.42 = (bf16[512,1280]{1,0:T(8,128)(2,1)S(1)}, bf16[512,1280]{1,0:T(8,128)(2,1)S(1)}, u32[]{:S(2)}, u32[]{:S(2)}) collective-permute-start(bf16[512,1280]{1,0:T(8,128)(2,1)S(1)} %convolution_convert_fusion.1), channel_id=1, source_target_pairs={{0,2},{2,0},{4,6},{6,4},{8,10},{10,8},{12,14},{14,12},{16,18},{18,... | collective-permute-start | bytes 3932168 | tf_op jit(solution)/shard_map/ppermute | solution.py:21
  339.2 32.0 %collective-permute-start.38 = (bf16[512,1280]{1,0:T(8,128)(2,1)S(1)}, bf16[512,1280]{1,0:T(8,128)(2,1)S(1)}, u32[]{:S(2)}, u32[]{:S(2)}) collective-permute-start(bf16[512,1280]{1,0:T(8,128)(2,1)S(1)} %convolution_convert_fusion.2), channel_id=1, source_target_pairs={{0,8},{2,10},{4,12},{6,14},{8,0},{10,2},{12,4},{14,6},{16,24},{18,... | collective-permute-start | bytes 3932168 | tf_op jit(solution)/shard_map/ppermute | solution.py:21
  342.6 21.3 %copy-start.36 = (bf16[4,128,1024]{2,1,0:T(8,128)(2,1)S(1)}, bf16[4,128,1024]{2,1,0:T(8,128)(2,1)}, u32[]{:S(2)}) copy-start(bf16[4,128,1024]{2,1,0:T(8,128)(2,1)} %get-tuple-element.82) | copy-start | bytes 3145732
  342.6 57.8 %collective-permute-start.34 = (bf16[512,1664]{1,0:T(8,128)(2,1)S(1)}, bf16[512,1664]{1,0:T(8,128)(2,1)S(1)}, u32[]{:S(2)}, u32[]{:S(2)}) collective-permute-start(bf16[512,1664]{1,0:T(8,128)(2,1)S(1)} %fusion.9), channel_id=1, source_target_pairs={{0,4},{2,6},{4,0},{6,2},{8,12},{10,14},{12,8},{14,10},{16,20},{18,... | collective-permute-start | bytes 5111816 | tf_op jit(solution)/shard_map/ppermute | solution.py:21
  345.5 59.7 %collective-permute-start.30 = (bf16[512,1664]{1,0:T(8,128)(2,1)S(1)}, bf16[512,1664]{1,0:T(8,128)(2,1)S(1)}, u32[]{:S(2)}, u32[]{:S(2)}) collective-permute-start(bf16[512,1664]{1,0:T(8,128)(2,1)S(1)} %fusion.6), channel_id=1, source_target_pairs={{0,2},{2,0},{4,6},{6,4},{8,10},{10,8},{12,14},{14,12},{16,18},{18,... | collective-permute-start | bytes 5111816 | tf_op jit(solution)/shard_map/ppermute | solution.py:21
  365.4 53.8 %collective-permute-start.47 = (bf16[2,2,64,1280]{3,2,1,0:T(8,128)(2,1)S(1)}, bf16[2,2,64,1280]{3,2,1,0:T(8,128)(2,1)S(1)}, u32[]{:S(2)}, u32[]{:S(2)}) collective-permute-start(bf16[2,2,64,1280]{3,2,1,0:T(8,128)(2,1)S(1)} %slice_bitcast_fusion.4), channel_id=1, source_target_pairs={{0,2},{2,0},{4,6},{6,4},{8,10},{10,8},{12,14},{14,12},{16,18},{18,... | collective-permute-start | bytes 1966088 | tf_op jit(solution)/shard_map/ppermute | solution.py:21
  370.2 50.4 %collective-permute-start.43 = (bf16[2,2,64,1280]{3,2,1,0:T(8,128)(2,1)S(1)}, bf16[2,2,64,1280]{3,2,1,0:T(8,128)(2,1)S(1)}, u32[]{:S(2)}, u32[]{:S(2)}) collective-permute-start(bf16[2,2,64,1280]{3,2,1,0:T(8,128)(2,1)S(1)} %slice_bitcast_fusion.6), channel_id=1, source_target_pairs={{0,4},{2,6},{4,0},{6,2},{8,12},{10,14},{12,8},{14,10},{16,20},{18,... | collective-permute-start | bytes 1966088 | tf_op jit(solution)/shard_map/ppermute | solution.py:21
  372.9 48.9 %collective-permute-start.39 = (bf16[2,2,64,1280]{3,2,0,1:T(8,128)(2,1)S(1)}, bf16[2,2,64,1280]{3,2,0,1:T(8,128)(2,1)S(1)}, u32[]{:S(2)}, u32[]{:S(2)}) collective-permute-start(bf16[2,2,64,1280]{3,2,0,1:T(8,128)(2,1)S(1)} %copy.15), channel_id=1, source_target_pairs={{0,16},{2,18},{4,20},{6,22},{8,24},{10,26},{12,28},{14,30},{16,0},... | collective-permute-start | bytes 1966088 | tf_op jit(solution)/shard_map/ppermute | solution.py:21
  402.7 41.1 %collective-permute-start.35 = (bf16[2,2,64,1664]{3,2,1,0:T(8,128)(2,1)S(1)}, bf16[2,2,64,1664]{3,2,1,0:T(8,128)(2,1)S(1)}, u32[]{:S(2)}, u32[]{:S(2)}) collective-permute-start(bf16[2,2,64,1664]{3,2,1,0:T(8,128)(2,1)S(1)} %slice_bitcast_fusion), channel_id=1, source_target_pairs={{0,2},{2,0},{4,6},{6,4},{8,10},{10,8},{12,14},{14,12},{16,18},{18,... | collective-permute-start | bytes 2555912 | tf_op jit(solution)/shard_map/ppermute | solution.py:21
  407.3 35.6 %collective-permute-start.31 = (bf16[2,2,64,1664]{3,2,1,0:T(8,128)(2,1)S(1)}, bf16[2,2,64,1664]{3,2,1,0:T(8,128)(2,1)S(1)}, u32[]{:S(2)}, u32[]{:S(2)}) collective-permute-start(bf16[2,2,64,1664]{3,2,1,0:T(8,128)(2,1)S(1)} %slice_bitcast_fusion.2), channel_id=1, source_target_pairs={{0,4},{2,6},{4,0},{6,2},{8,12},{10,14},{12,8},{14,10},{16,20},{18,... | collective-permute-start | bytes 2555912 | tf_op jit(solution)/shard_map/ppermute | solution.py:21
  419.4 9.6 %collective-permute-start.48 = (bf16[2,64,1280]{2,1,0:T(8,128)(2,1)S(1)}, bf16[2,64,1280]{2,1,0:T(8,128)(2,1)S(1)}, u32[]{:S(2)}, u32[]{:S(2)}) collective-permute-start(bf16[2,64,1280]{2,1,0:T(8,128)(2,1)S(1)} %slice_bitcast_fusion.14), channel_id=1, source_target_pairs={{0,8},{2,10},{4,12},{6,14},{8,0},{10,2},{12,4},{14,6},{16,24},{18,... | collective-permute-start | bytes 983048 | tf_op jit(solution)/shard_map/ppermute | solution.py:21
  420.8 14.9 %collective-permute-start.44 = (bf16[2,64,1280]{2,1,0:T(8,128)(2,1)S(1)}, bf16[2,64,1280]{2,1,0:T(8,128)(2,1)S(1)}, u32[]{:S(2)}, u32[]{:S(2)}) collective-permute-start(bf16[2,64,1280]{2,1,0:T(8,128)(2,1)S(1)} %slice_bitcast_fusion.16), channel_id=1, source_target_pairs={{0,8},{2,10},{4,12},{6,14},{8,0},{10,2},{12,4},{14,6},{16,24},{18,... | collective-permute-start | bytes 983048 | tf_op jit(solution)/shard_map/ppermute | solution.py:21
  421.9 19.8 %collective-permute-start.40 = (bf16[2,64,1280]{2,1,0:T(8,128)(2,1)S(1)}, bf16[2,64,1280]{2,1,0:T(8,128)(2,1)S(1)}, u32[]{:S(2)}, u32[]{:S(2)}) collective-permute-start(bf16[2,64,1280]{2,1,0:T(8,128)(2,1)S(1)} %slice_bitcast_fusion.18), channel_id=1, source_target_pairs={{0,2},{2,0},{4,6},{6,4},{8,10},{10,8},{12,14},{14,12},{16,18},{18,... | collective-permute-start | bytes 983048 | tf_op jit(solution)/shard_map/ppermute | solution.py:21
  429.1 47.8 %collective-permute-start.49 = (bf16[64,1280]{1,0:T(8,128)(2,1)S(1)}, bf16[64,1280]{1,0:T(8,128)(2,1)S(1)}, u32[]{:S(2)}, u32[]{:S(2)}) collective-permute-start(bf16[64,1280]{1,0:T(8,128)(2,1)S(1)} %slice_bitcast_fusion.24), channel_id=1, source_target_pairs={{0,16},{2,18},{4,20},{6,22},{8,24},{10,26},{12,28},{14,30},{16,0},... | collective-permute-start | bytes 491528 | tf_op jit(solution)/shard_map/ppermute | solution.py:21
  435.8 41.0 %collective-permute-start.45 = (bf16[64,1280]{1,0:T(8,128)(2,1)S(1)}, bf16[64,1280]{1,0:T(8,128)(2,1)S(1)}, u32[]{:S(2)}, u32[]{:S(2)}) collective-permute-start(bf16[64,1280]{1,0:T(8,128)(2,1)S(1)} %slice_bitcast_fusion.26), channel_id=1, source_target_pairs={{0,16},{2,18},{4,20},{6,22},{8,24},{10,26},{12,28},{14,30},{16,0},... | collective-permute-start | bytes 491528 | tf_op jit(solution)/shard_map/ppermute | solution.py:21
  441.8 34.9 %collective-permute-start.41 = (bf16[64,1280]{1,0:T(8,128)(2,1)S(1)}, bf16[64,1280]{1,0:T(8,128)(2,1)S(1)}, u32[]{:S(2)}, u32[]{:S(2)}) collective-permute-start(bf16[64,1280]{1,0:T(8,128)(2,1)S(1)} %slice_bitcast_fusion.28), channel_id=1, source_target_pairs={{0,4},{2,6},{4,0},{6,2},{8,12},{10,14},{12,8},{14,10},{16,20},{18,... | collective-permute-start | bytes 491528 | tf_op jit(solution)/shard_map/ppermute | solution.py:21
  443.2 15.1 %collective-permute-start.32 = (bf16[2,64,1664]{2,1,0:T(8,128)(2,1)S(1)}, bf16[2,64,1664]{2,1,0:T(8,128)(2,1)S(1)}, u32[]{:S(2)}, u32[]{:S(2)}) collective-permute-start(bf16[2,64,1664]{2,1,0:T(8,128)(2,1)S(1)} %slice_bitcast_fusion.12), channel_id=1, source_target_pairs={{0,8},{2,10},{4,12},{6,14},{8,0},{10,2},{12,4},{14,6},{16,24},{18,... | collective-permute-start | bytes 1277960 | tf_op jit(solution)/shard_map/ppermute | solution.py:21
  444.1 20.3 %collective-permute-start.36 = (bf16[2,64,1664]{2,1,0:T(8,128)(2,1)S(1)}, bf16[2,64,1664]{2,1,0:T(8,128)(2,1)S(1)}, u32[]{:S(2)}, u32[]{:S(2)}) collective-permute-start(bf16[2,64,1664]{2,1,0:T(8,128)(2,1)S(1)} %slice_bitcast_fusion.10), channel_id=1, source_target_pairs={{0,8},{2,10},{4,12},{6,14},{8,0},{10,2},{12,4},{14,6},{16,24},{18,... | collective-permute-start | bytes 1277960 | tf_op jit(solution)/shard_map/ppermute | solution.py:21
  458.5 15.6 %collective-permute-start.33 = (bf16[64,1664]{1,0:T(8,128)(2,1)S(1)}, bf16[64,1664]{1,0:T(8,128)(2,1)S(1)}, u32[]{:S(2)}, u32[]{:S(2)}) collective-permute-start(bf16[64,1664]{1,0:T(8,128)(2,1)S(1)} %slice_bitcast_fusion.22), channel_id=1, source_target_pairs={{0,16},{2,18},{4,20},{6,22},{8,24},{10,26},{12,28},{14,30},{16,0},... | collective-permute-start | bytes 638984 | tf_op jit(solution)/shard_map/ppermute | solution.py:21
  464.6 12.2 %collective-permute-start.37 = (bf16[64,1664]{1,0:T(8,128)(2,1)S(1)}, bf16[64,1664]{1,0:T(8,128)(2,1)S(1)}, u32[]{:S(2)}, u32[]{:S(2)}) collective-permute-start(bf16[64,1664]{1,0:T(8,128)(2,1)S(1)} %slice_bitcast_fusion.20), channel_id=1, source_target_pairs={{0,16},{2,18},{4,20},{6,22},{8,24},{10,26},{12,28},{14,30},{16,0},... | collective-permute-start | bytes 638984 | tf_op jit(solution)/shard_map/ppermute | solution.py:21
  (26 other events, 95.0 us)
Sparse Core Ops, SparseCore 0:
  8.9 29.7 all-gather.2

commit v5 on v4

--- a/solution.py
+++ b/solution.py
@@ -180,11 +180,10 @@
         refs[MOST][k] = refs[k][...]
 
 
-def cluster_rows(meta, got, riders):
+def group_sums(meta, got):
     shape = got[0].shape
     experts = lax.axis_size("expert")
     piece = jax.ShapeDtypeStruct(shape, BF16)
-    stacked = jax.ShapeDtypeStruct((MOST,) + shape, BF16)
     tail, head = pl.pallas_call(
         ends_kernel,
         out_shape=[piece, piece],
@@ -195,25 +194,25 @@
     )(meta, *got)
     below = shift_groups(tail, MOST)
     above = shift_groups(head, -MOST)
-    below, above, riders = lax.optimization_barrier((below, above, riders))
-    sums, *sends = pl.pallas_call(
+    return pl.pallas_call(
         functools.partial(totals_kernel, experts),
-        out_shape=[stacked] + [piece] * (MOST - 1),
+        out_shape=[jax.ShapeDtypeStruct((MOST,) + shape, BF16)] + [piece] * (MOST - 1),
         in_specs=[scalars()] + [whole()] * (MOST + 2),
         out_specs=[whole()] * MOST,
         compiler_params=params(),
         name="cluster_sums",
     )(meta, *got, below, above)
-    back = [sums[0]] + [swap_expert(sends[k - 1], k) for k in range(1, MOST)]
-    mine = pl.pallas_call(
+
+
+def stacked(values):
+    return pl.pallas_call(
         stack_kernel,
-        out_shape=stacked,
+        out_shape=jax.ShapeDtypeStruct((MOST,) + values[0].shape, BF16),
         in_specs=[whole()] * MOST,
         out_specs=whole(),
         compiler_params=params(),
         name="own_sums",
-    )(*back)
-    return sums, mine, riders
+    )(*values)
 
 
 def cross_kernel(started, meta, own, other, gate, gate_other, up, up_other, *refs):
@@ -262,33 +261,37 @@
     )(meta, own, other, gate, gate, up, up, *before)
 
 
-def project_kernel(count, *refs):
-    tokens, sums, out, basis = refs[:count], refs[count:-2], refs[-2], refs[-1]
+def project_kernel(count, tokens, *refs):
+    sums, outs, basis = refs[:count], refs[count:-1], refs[-1]
     rows = sums[0].shape[1]
     for i, ref in enumerate(sums):
         basis[i * rows : (i + 1) * rows, :] = ref[0]
-    toks = tokens[0].shape[0]
-    for i, ref in enumerate(tokens):
-        out[i * toks : (i + 1) * toks, :] = mul(ref[:, LANES:], basis[...]).astype(BF16)
-
-
-def project(tokens, sums, k):
+    toks = tokens.shape[0] // MOST
+    for k in range(MOST):
+
+        @pl.when(pl.program_id(0) == k)
+        def _():
+            for i in range(MOST):
+                strip = slice(i * toks, (i + 1) * toks)
+                outs[k][strip, :] = mul(tokens[strip, LANES:], basis[...]).astype(BF16)
+
+
+def project(tokens, sums):
     rank = sums[0].shape[-1]
-    toks, width = tokens[0].shape
+    total, width = tokens.shape
     depth = width - LANES
-    total = len(tokens) * toks
-    return pl.pallas_call(
-        functools.partial(project_kernel, len(tokens)),
-        grid=(1,),
-        in_specs=[pl.BlockSpec((toks, width), lambda i: (0, 0))] * len(tokens)
-        + [pl.BlockSpec((1,) + value.shape[1:], lambda i: (k, 0, 0)) for value in sums],
-        out_specs=pl.BlockSpec((total, rank), lambda i: (0, 0)),
-        out_shape=jax.ShapeDtypeStruct((total, rank), BF16),
+    return pl.pallas_call(
+        functools.partial(project_kernel, len(sums)),
+        grid=(MOST,),
+        in_specs=[pl.BlockSpec((total, width), lambda k: (0, 0))]
+        + [pl.BlockSpec((1,) + value.shape[1:], lambda k: (k, 0, 0)) for value in sums],
+        out_specs=[pl.BlockSpec((total, rank), lambda k: (0, 0))] * MOST,
+        out_shape=[jax.ShapeDtypeStruct((total, rank), BF16)] * MOST,
         scratch_shapes=[pltpu.VMEM((depth, rank), BF16)],
         compiler_params=params(),
-        cost_estimate=cost(2 * total * depth * rank, 4 * total * rank),
+        cost_estimate=cost(2 * MOST * total * depth * rank, 4 * MOST * total * rank),
         name="project",
-    )(*tokens, *sums)
+    )(tokens, *sums)
 
 
 def reciprocal(value):
@@ -297,7 +300,7 @@
     return guess * (2.0 - value * guess)
 
 
-def factor_kernel(tile, gram_ref, raw_ref, inverse_ref, coeff_ref, work_ref):
+def factor_kernel(tile, gram_ref, inverse_ref, work_ref):
     rank = gram_ref.shape[0]
     steps = rank // tile
     row_of = lax.broadcasted_iota(jnp.int32, (tile, tile), 0)
@@ -364,26 +367,39 @@
         return carry
 
     lax.fori_loop(0, steps, step, 0)
-    inverse = inverse_ref[...]
-    for side in range(2):
-        coeff_ref[side] = mul3(inverse, raw_ref[side], ((1,), (0,))).astype(BF16)
-
-
-def factored(gram, raw):
+
+
+def factored(gram):
     rank = gram.shape[0]
     return pl.pallas_call(
         functools.partial(factor_kernel, min(LANES, rank)),
-        out_shape=[
-            jax.ShapeDtypeStruct((rank, rank), F32),
-            jax.ShapeDtypeStruct(raw.shape, BF16),
-        ],
-        in_specs=[whole()] * 2,
-        out_specs=[whole()] * 2,
+        out_shape=jax.ShapeDtypeStruct((rank, rank), F32),
+        in_specs=[whole()],
+        out_specs=whole(),
         scratch_shapes=[pltpu.VMEM((rank, rank), F32)],
         compiler_params=params(),
         cost_estimate=cost(4e10, 8 * rank * rank),
         name="factored",
-    )(gram, raw)
+    )(gram)
+
+
+def coefficient_kernel(inverse, raw, out):
+    out[0] = mul3(inverse[...], raw[0], ((1,), (0,))).astype(BF16)
+
+
+def coefficients(inverse, raw):
+    sides, rank, hid = raw.shape
+    side = pl.BlockSpec((1, rank, hid), lambda i: (i, 0, 0))
+    return pl.pallas_call(
+        coefficient_kernel,
+        grid=(sides,),
+        in_specs=[pl.BlockSpec((rank, rank), lambda i: (0, 0)), side],
+        out_specs=side,
+        out_shape=jax.ShapeDtypeStruct(raw.shape, BF16),
+        compiler_params=params(),
+        cost_estimate=cost(6 * sides * rank * rank * hid, 6 * sides * rank * hid),
+        name="coefficients",
+    )(inverse, raw)
 
 
 def hidden_kernel(toks, groups, meta, inverse, mine, others, tokens, *refs):
@@ -454,7 +470,7 @@
     units = depth // LANES
     if units % 56:
         return [(0, depth, orders[0])]
-    sizes = [(13, 0), (13, 1), (10, 2), (10, 0), (10, 1)]
+    sizes = [(11, 0), (11, 1), (12, 2), (11, 0), (11, 1)]
     chunks, start = [], 0
     for size, order in sizes:
         width = size * (units // 56) * LANES
@@ -530,34 +546,33 @@
             for k in range(MOST)
         ]
         got.append([own[0]] + [swap_expert(own[k], k) for k in range(1, MOST)])
-    group_sums, own_sums = [], []
     masks = group_masks(experts)
+    for mask in masks[:-1]:
+        spread = jnp.concatenate([spread, swap_expert(spread, mask)], axis=0)
+    spread, got[0] = lax.optimization_barrier((spread, got[0]))
+    if masks:
+        spread = jnp.concatenate([spread, swap_expert(spread, masks[-1])], axis=0)
+    sums, other_sums, back = [], [], []
     for c in range(chunks):
-        share = masks[c * len(masks) // chunks : (c + 1) * len(masks) // chunks]
-        for mask in share[:-1]:
-            spread = jnp.concatenate([spread, swap_expert(spread, mask)], axis=0)
-        came = swap_expert(spread, share[-1]) if share else spread[:16]
-        if c == 0:
-            sums, mine, came = cluster_rows(meta, got[c], came)
-        else:
-            sums, mine, _ = cluster_rows(meta, got[c], meta)
-        if share:
-            spread = jnp.concatenate([spread, came], axis=0)
-        group_sums.append((sums, swap_dp(sums)))
-        own_sums.append((mine, swap_dp(mine)))
-    halves = [sums[d] for d in range(2) for sums in group_sums]
-    sends = {k: project([spread], halves, k) for k in (3, 1, 2, 0)}
-    parts = [sends[k] for k in range(MOST)]
+        value, *sends = group_sums(meta, got[c])
+        sums.append(value)
+        other_sums.append(swap_dp(value))
+        back.append([value[0]] + [swap_expert(sends[k - 1], k) for k in range(1, MOST)])
+    parts = project(spread, sums + other_sums)
     before = ()
     for c in range(chunks):
-        before = crossed(meta, *own_sums[c], gate_rows, up_rows, c, chunks, before)
+        if c == chunks - 1:
+            parts, before, back[c] = lax.optimization_barrier((parts, before, back[c]))
+        mine = stacked(back[c])
+        before = crossed(meta, mine, swap_dp(mine), gate_rows, up_rows, c, chunks, before)
     gram, raw = before
     if lax.axis_size("tensor") > 1:
         gram, raw = lax.psum((gram, raw), "tensor")
         parts = [lax.psum(value.astype(F32), "tensor").astype(BF16) for value in parts]
-    gram, raw, parts = lax.optimization_barrier((gram, raw, parts))
     arrived = [parts[0]] + [swap_expert(parts[k], k) for k in range(1, MOST)]
-    inverse, coeff = factored(gram, raw)
+    inverse = factored(gram)
+    inverse, arrived = lax.optimization_barrier((inverse, arrived))
+    coeff = coefficients(inverse, raw)
     other_coeff = swap_dp(coeff)
     shares = spread[:, :LANES]
     sides = hidden_rows(meta, inverse, coeff, other_coeff, shares, arrived, toks)

time: 491 us -> 475 us (0.967)
  waiting for transfers between devices: 204 us -> 189 us
  Pallas kernels: 153 us -> 147 us
    ppermute x40, waiting for transfers between devices: 203 us -> 183 us  [swap_expert(): lax.ppermute(value, 'expert', [(source, source ^ mask) for source in rang...]
    pallas_call x10 -> x8, Pallas kernels: 43.2 us -> 40.1 us  [the longest x1 13.9 us: project(): pl.pallas_call(functools.partial(project_kernel, len(sums)), grid=(MOST,)...]
    unnamed x82 -> x79, local copies, waits for them, and re-layouts: 13.5 us -> 14.9 us
  transfers between devices with their start and end apart: 51 -> 51, of which waited for: 23 -> 21; matrix products, arithmetic and copies ran while one was open for 8% -> 7% of each run, Pallas kernels for 31% -> 30%
where the time goes in v5:
time: 475 us; the launch traced here: 466 us
  waiting for transfers between devices  189 us (40%)
  Pallas kernels  147 us (31%)
  starting transfers between devices  62.6 us (13%)
  matrix products  22.6 us (5%)
  local copies, waits for them, and re-layouts  21.9 us (5%)
  between operations  14.3 us (3%)
  other arithmetic  8.93 us (2%)
    ppermute x40, waiting for transfers between devices, swap_expert(): lax.ppermute(value, 'expert', [(source, source ^ mask) for source in rang...  183 us
    pallas_call x1, Pallas kernels, factored(): pl.pallas_call(functools.partial(factor_kernel, min(LANES, rank)), out_sh...  51.2 us
    ppermute x40, starting transfers between devices, swap_expert(): lax.ppermute(value, 'expert', [(source, source ^ mask) for source in rang...  50.6 us
    pallas_call x2, Pallas kernels, crossed(): pl.pallas_call(functools.partial(cross_kernel, bool(before)), grid_spec=p...  24.3 us
    dot_general x10, matrix products, mul(): return lax.dot_general(a, b, (dims, ((), ())), preferred_element_type=F32)  22.6 us
    pallas_call x2, Pallas kernels, sketch_half(): pl.pallas_call(sketch_kernel, grid_spec=pltpu.PrefetchScalarGridSpec(num_...  19 us
    unnamed x79, local copies, waits for them, and re-layouts  14.9 us
    pallas_call x1, Pallas kernels, project(): pl.pallas_call(functools.partial(project_kernel, len(sums)), grid=(MOST,)...  13.9 us
  transfers between devices with their start and end apart: 51, of which 21 were waited for; matrix products, arithmetic and copies ran while one was open for 7% of the time, Pallas kernels for 30%

profile of v5, /device:TPU:0, one launch (start us, length us, event | category | flops | bytes accessed | tf_op | source)
XLA Modules:
  0.0 466.3 jit_solution(505843567849856606)
XLA Ops:
  7.8 8.7 %sketch_half.3 = bf16[4,896,512]{2,1,0:T(8,128)(2,1)} custom-call(s32[25]{0:T(128)} %pad_add_fusion.meta, bf16[7168,512]{1,0:T(8,128)(2,1)} %bitcast.162, bf16[7168,512]{1,0:T(8,128)(2,1)} %bitcast.168, bf16[2,512,512]{2,1,0:T(8,128)(2,1)} %bitcast.174), custom_call_target="tpu_custom_call" | custom-call | flops 3758096384 | bytes 7340032 | tf_op jit(solution)/shard_map/sketch_half/pallas_call | solution.py:121
  18.6 2.8 token_pieces.1
  21.3 2.9 collective-permute-start
  24.3 1.5 collective-permute-start.1
  25.8 10.3 %sketch_half.2 = bf16[4,896,512]{2,1,0:T(8,128)(2,1)} custom-call(s32[25]{0:T(128)} %pad_add_fusion.meta, bf16[7168,512]{1,0:T(8,128)(2,1)} %bitcast.163, bf16[7168,512]{1,0:T(8,128)(2,1)} %bitcast.169, bf16[2,512,512]{2,1,0:T(8,128)(2,1)} %bitcast.175), custom_call_target="tpu_custom_call" | custom-call | flops 3758096384 | bytes 7340032 | tf_op jit(solution)/shard_map/sketch_half/pallas_call | solution.py:121
  37.3 2.7 collective-permute-start.3
  39.9 5.2 %fusion.32 = (bf16[448,512]{1,0:T(8,128)(2,1)S(1)}, bf16[448,512]{1,0:T(8,128)(2,1)S(1)}, bf16[448,512]{1,0:T(8,128)(2,1)S(1)}, bf16[448,512]{1,0:T(8,128)(2,1)}...) fusion(bf16[4,896,512]{2,1,0:T(8,128)(2,1)} %collective-permute, ...), kind=kLoop, calls=%fused_computation.70 | loop fusion | flops 7340032 | bytes 11010048 | tf_op jit(solution)/shard_map/convert_element_type | solution.py:545
  49.9 31.9 %collective-permute-done.3 = bf16[256,1920]{1,0:T(8,128)(2,1)S(1)} collective-permute-done((bf16[256,1920]{1,0:T(8,128)(2,1)S(1)}, bf16[256,1920]{1,0:T(8,128)(2,1)S(1)}, u32[]{:S(2)}, u32[]{:S(2)}) %collective-permute-start.3) | collective-permute-done | bytes 983072 | tf_op jit(solution)/shard_map/ppermute | solution.py:21
  82.8 1.9 collective-permute-start.13
  85.8 2.9 end_sums.2
  90.0 4.6 collective-permute-start.9
  94.6 8.4 %collective-permute-done.12.refs_2_ = bf16[448,512]{1,0:T(8,128)(2,1)S(1)} collective-permute-done((bf16[448,512]{1,0:T(8,128)(2,1)S(1)}, bf16[448,512]{1,0:T(8,128)(2,1)S(1)}, u32[]{:S(2)}, u32[]{:S(2)}) %collective-permute-start.12) | collective-permute-done | bytes 458784 | tf_op jit(solution)/shard_map/ppermute | solution.py:21
  103.9 2.9 end_sums.3
  106.8 3.7 collective-permute-start.14
  111.8 2.7 collective-permute-start.8
  116.0 4.6 cluster_sums.2
  120.6 1.5 collective-permute-start.18
  122.1 3.9 collective-permute-done.15.refs_5_
  126.8 4.6 cluster_sums.3
  133.0 1.9 collective-permute-start.20
  135.7 18.6 %collective-permute-done.19.refs_2_ = bf16[448,512]{1,0:T(8,128)(2,1)S(1)} collective-permute-done((bf16[448,512]{1,0:T(8,128)(2,1)S(1)}, bf16[448,512]{1,0:T(8,128)(2,1)S(1)}, u32[]{:S(2)}, u32[]{:S(2)}) %collective-permute-start.19) | collective-permute-done | bytes 458784 | tf_op jit(solution)/shard_map/ppermute | solution.py:21
  155.8 2.8 own_sums.2.own
  160.2 1.8 slice_bitcast_fusion.8.refs_0_
  162.0 4.0 collective-permute-done.8
  167.4 1.8 copy-done.8
  169.2 1.9 collective-permute-start.24
  171.1 13.9 %project.1 = (bf16[1024,512]{1,0:T(8,128)(2,1)}, bf16[1024,512]{1,0:T(8,128)(2,1)}, bf16[1024,512]{1,0:T(8,128)(2,1)}, bf16[1024,512]{1,0:T(8,128)(2,1)}) custom-call(bf16[1024,1920]{1,0:T(8,128)(2,1)} %copy-done.8, bf16[4,448,512]{2,1,0:T(8,128)(2,1)} %get-tuple-element.69.refs_0_, bf16[4,448,512]{2,1,0:T(8,128)(2,1)} %get-tuple-element.72.refs_1_, ...), custom_call_target="tpu_custom_call" | custom-call | flops 7516192768 | bytes 8388608 | tf_op jit(solution)/shard_map/project/pallas_call | solution.py:283
  186.3 11.5 %crossed.2 = (f32[512,512]{1,0:T(8,128)}, f32[2,512,512]{2,1,0:T(8,128)}) custom-call(s32[25]{0:T(128)} %pad_add_fusion.meta, bf16[4,448,512]{2,1,0:T(8,128)(2,1)} %own_sums.2.own, bf16[4,448,512]{2,1,0:T(8,128)(2,1)} %copy-done, bf16[7168,512]{1,0:T(8,128)(2,1)} %bitcast.164, bf16[7168,512]{1,0:T(8,128)(2,1)} %bitcast.165, bf16[7168,512]{1,0:T(8,128)(2,1)} %bitcast.170, ...), custom_call_target="tpu_custom_call" | custom-call | flops 5637144576 | bytes 22020096 | tf_op jit(solution)/shard_map/crossed/pallas_call | solution.py:245
  199.0 3.0 own_sums.3.own
  203.6 1.9 collective-permute-start.28
  207.2 12.8 %crossed.3 = (f32[512,512]{1,0:T(8,128)}, f32[2,512,512]{2,1,0:T(8,128)}) custom-call(s32[25]{0:T(128)} %pad_add_fusion.meta, bf16[4,448,512]{2,1,0:T(8,128)(2,1)} %own_sums.3.own, bf16[4,448,512]{2,1,0:T(8,128)(2,1)} %copy-done.1, bf16[7168,512]{1,0:T(8,128)(2,1)} %bitcast.166, bf16[7168,512]{1,0:T(8,128)(2,1)} %bitcast.167, bf16[7168,512]{1,0:T(8,128)(2,1)} %bitcast.172, ...), custom_call_target="tpu_custom_call" | custom-call | flops 5637144576 | bytes 22020096 | tf_op jit(solution)/shard_map/crossed/pallas_call | solution.py:245
  220.1 51.2 %factored.1.inverse = f32[512,512]{1,0:T(8,128)} custom-call(f32[512,512]{1,0:T(8,128)} %get-tuple-element.91.gram_ref), custom_call_target="tpu_custom_call" | custom-call | flops 40000000000 | bytes 2097152 | tf_op jit(solution)/shard_map/factored/pallas_call | solution.py:374
  271.4 5.5 %coefficients.1.mine = bf16[2,512,512]{2,1,0:T(8,128)(2,1)} custom-call(f32[512,512]{1,0:T(8,128)} %factored.1.inverse, f32[2,512,512]{2,1,0:T(8,128)} %get-tuple-element.97.raw), custom_call_target="tpu_custom_call" | custom-call | flops 1610612736 | bytes 3145728 | tf_op jit(solution)/shard_map/coefficients/pallas_call | solution.py:393
  277.1 1.7 slice.239.tokens
  280.8 9.6 %hidden_rows.1 = (bf16[4,128,1024]{2,1,0:T(8,128)(2,1)}, bf16[4,128,1024]{2,1,0:T(8,128)(2,1)}, bf16[4,128,1024]{2,1,0:T(8,128)(2,1)}, bf16[4,128,1024]{2,1,0:T(8,128)(2,1)}, bf16[4,256,1024]{2,1,0:T(8,128)(2,1)}) custom-call(s32[25]{0:T(128)} %pad_add_fusion.meta, f32[512,512]{1,0:T(8,128)} %factored.1.inverse, bf16[2,512,512]{2,1,0:T(8,128)(2,1)} %coefficients.1.mine, ...), custom_call_target="tpu_custom_call" | custom-call | flops 3758096384 | bytes 8388608 | tf_op jit(solution)/shard_map/hidden_rows/pallas_call | solution.py:439
  290.4 1.8 fusion.47
  292.3 4.1 convolution_convert_fusion
  297.5 3.7 convolution_convert_fusion.1
  301.9 1.8 convolution_convert_fusion.2
  303.8 1.8 convolution_convert_fusion.3
  306.8 1.8 convolution_convert_fusion.4
  308.6 1.6 collective-permute-start.30
  310.2 20.7 %collective-permute-done.46 = bf16[512,1408]{1,0:T(8,128)(2,1)S(1)} collective-permute-done((bf16[512,1408]{1,0:T(8,128)(2,1)S(1)}, bf16[512,1408]{1,0:T(8,128)(2,1)S(1)}, u32[]{:S(2)}, u32[]{:S(2)}) %collective-permute-start.46) | collective-permute-done | bytes 1441824 | tf_op jit(solution)/shard_map/ppermute | solution.py:21
  330.9 1.8 fusion.4
  333.4 2.4 collective-permute-done.42
  335.7 1.8 fusion.3
  338.8 23.0 %collective-permute-done.34 = bf16[512,1408]{1,0:T(8,128)(2,1)S(1)} collective-permute-done((bf16[512,1408]{1,0:T(8,128)(2,1)S(1)}, bf16[512,1408]{1,0:T(8,128)(2,1)S(1)}, u32[]{:S(2)}, u32[]{:S(2)}) %collective-permute-start.34) | collective-permute-done | bytes 1441824 | tf_op jit(solution)/shard_map/ppermute | solution.py:21
  361.8 1.8 fusion.2
  364.3 2.4 collective-permute-done.30
  366.6 2.0 fusion.1
  369.9 1.8 fusion
  371.9 3.4 collective-permute-start.39
  375.4 6.7 %collective-permute-done.47 = bf16[2,2,64,1408]{3,2,1,0:T(8,128)(2,1)S(1)} collective-permute-done((bf16[2,2,64,1408]{3,2,1,0:T(8,128)(2,1)S(1)}, bf16[2,2,64,1408]{3,2,1,0:T(8,128)(2,1)S(1)}, u32[]{:S(2)}, u32[]{:S(2)}) %collective-permute-start.47) | collective-permute-done | bytes 720928 | tf_op jit(solution)/shard_map/ppermute | solution.py:21
  382.6 2.1 collective-permute-start.44
  384.7 12.1 %collective-permute-done.35 = bf16[2,2,64,1408]{3,2,1,0:T(8,128)(2,1)S(1)} collective-permute-done((bf16[2,2,64,1408]{3,2,1,0:T(8,128)(2,1)S(1)}, bf16[2,2,64,1408]{3,2,1,0:T(8,128)(2,1)S(1)}, u32[]{:S(2)}, u32[]{:S(2)}) %collective-permute-start.35) | collective-permute-done | bytes 720928 | tf_op jit(solution)/shard_map/ppermute | solution.py:21
  397.3 2.1 collective-permute-start.32
  399.3 7.9 %collective-permute-done.39 = bf16[2,2,64,1536]{3,2,0,1:T(8,128)(2,1)S(1)} collective-permute-done((bf16[2,2,64,1536]{3,2,0,1:T(8,128)(2,1)S(1)}, bf16[2,2,64,1536]{3,2,0,1:T(8,128)(2,1)S(1)}, u32[]{:S(2)}, u32[]{:S(2)}) %collective-permute-start.39) | collective-permute-done | bytes 786464 | tf_op jit(solution)/shard_map/ppermute | solution.py:21
  408.1 2.4 collective-permute-done.48
  410.7 13.3 %collective-permute-done.44 = bf16[2,64,1408]{2,1,0:T(8,128)(2,1)S(1)} collective-permute-done((bf16[2,64,1408]{2,1,0:T(8,128)(2,1)S(1)}, bf16[2,64,1408]{2,1,0:T(8,128)(2,1)S(1)}, u32[]{:S(2)}, u32[]{:S(2)}) %collective-permute-start.44) | collective-permute-done | bytes 360480 | tf_op jit(solution)/shard_map/ppermute | solution.py:21
  424.2 14.7 %collective-permute-done.32 = bf16[2,64,1408]{2,1,0:T(8,128)(2,1)S(1)} collective-permute-done((bf16[2,64,1408]{2,1,0:T(8,128)(2,1)S(1)}, bf16[2,64,1408]{2,1,0:T(8,128)(2,1)S(1)}, u32[]{:S(2)}, u32[]{:S(2)}) %collective-permute-start.32) | collective-permute-done | bytes 360480 | tf_op jit(solution)/shard_map/ppermute | solution.py:21
  439.2 3.0 collective-permute-start.37
  442.2 9.0 %collective-permute-done.33 = bf16[64,1408]{1,0:T(8,128)(2,1)S(1)} collective-permute-done((bf16[64,1408]{1,0:T(8,128)(2,1)S(1)}, bf16[64,1408]{1,0:T(8,128)(2,1)S(1)}, u32[]{:S(2)}, u32[]{:S(2)}) %collective-permute-start.33) | collective-permute-done | bytes 180256 | tf_op jit(solution)/shard_map/ppermute | solution.py:21
  452.5 2.0 collective-permute-done.37
  454.6 2.8 collective-permute-done.41
  (184 shorter events, 44.6 us)
Async XLA Ops:
  6.5 285.7 %all-gather.3.cloned.1.call-start = ((), (), s32[]{:S(2)}) async-start(), calls=%async_computation | async-start | bytes 22020096 | tf_op jit(solution)/shard_map/all_gather | solution.py:530
  16.5 23.4 %collective-permute-start.4 = (bf16[4,896,512]{2,1,0:T(8,128)(2,1)}, bf16[4,896,512]{2,1,0:T(8,128)(2,1)}, u32[]{:S(2)}, u32[]{:S(2)}) collective-permute-start(bf16[4,896,512]{2,1,0:T(8,128)(2,1)} %sketch_half.3), channel_id=1, source_target_pairs={{0,1},{1,0},{2,3},{3,2},{4,5},{5,4},{6,7},{7,6},{8,9},{9,8},{10,11... | collective-permute-start | bytes 11010056 | tf_op jit(solution)/shard_map/ppermute | solution.py:26
  21.3 14.8 %collective-permute-start = (bf16[64,1920]{1,0:T(8,128)(2,1)}, bf16[64,1920]{1,0:T(8,128)(2,1)S(1)}, u32[]{:S(2)}, u32[]{:S(2)}) collective-permute-start(bf16[64,1920]{1,0:T(8,128)(2,1)} %get-tuple-element.57), channel_id=1, source_target_pairs={{0,2},{2,0},{4,6},{6,4},{8,10},{10,8},{12,14},{14,12},{16,18},{18,... | collective-permute-start | bytes 737288 | tf_op jit(solution)/shard_map/ppermute | solution.py:21
  24.3 12.9 %collective-permute-start.1 = (bf16[64,1920]{1,0:T(8,128)(2,1)}, bf16[64,1920]{1,0:T(8,128)(2,1)S(1)}, u32[]{:S(2)}, u32[]{:S(2)}) collective-permute-start(bf16[64,1920]{1,0:T(8,128)(2,1)} %get-tuple-element.58), channel_id=1, source_target_pairs={{0,4},{2,6},{4,0},{6,2},{8,12},{10,14},{12,8},{14,10},{16,20},{18,... | collective-permute-start | bytes 737288 | tf_op jit(solution)/shard_map/ppermute | solution.py:21
  25.8 11.4 %copy-start.19 = (bf16[64,1920]{1,0:T(8,128)(2,1)S(1)}, bf16[64,1920]{1,0:T(8,128)(2,1)}, u32[]{:S(2)}) copy-start(bf16[64,1920]{1,0:T(8,128)(2,1)} %get-tuple-element.56) | copy-start | bytes 737284
  25.8 11.4 %collective-permute-start.2 = (bf16[64,1920]{1,0:T(8,128)(2,1)}, bf16[64,1920]{1,0:T(8,128)(2,1)S(1)}, u32[]{:S(2)}, u32[]{:S(2)}) collective-permute-start(bf16[64,1920]{1,0:T(8,128)(2,1)} %get-tuple-element.59), channel_id=1, source_target_pairs={{0,6},{2,4},{4,2},{6,0},{8,14},{10,12},{12,10},{14,8},{16,22},{18,... | collective-permute-start | bytes 737288 | tf_op jit(solution)/shard_map/ppermute | solution.py:21
  37.3 44.5 %collective-permute-start.3 = (bf16[256,1920]{1,0:T(8,128)(2,1)S(1)}, bf16[256,1920]{1,0:T(8,128)(2,1)S(1)}, u32[]{:S(2)}, u32[]{:S(2)}) collective-permute-start(bf16[256,1920]{1,0:T(8,128)(2,1)S(1)} %pad_maximum_fusion.1), channel_id=1, source_target_pairs={{0,16},{2,18},{4,20},{6,22},{8,24},{10,26},{12,28},{14,30},{16,0},... | collective-permute-start | bytes 2949128 | tf_op jit(solution)/shard_map/ppermute | solution.py:21
  45.1 37.7 %collective-permute-start.5 = (bf16[448,512]{1,0:T(8,128)(2,1)S(1)}, bf16[448,512]{1,0:T(8,128)(2,1)S(1)}, u32[]{:S(2)}, u32[]{:S(2)}) collective-permute-start(bf16[448,512]{1,0:T(8,128)(2,1)S(1)} %get-tuple-element.113), channel_id=1, source_target_pairs={{0,2},{2,0},{4,6},{6,4},{8,10},{10,8},{12,14},{14,12},{16,18},{18,... | collective-permute-start | bytes 1376264 | tf_op jit(solution)/shard_map/ppermute | solution.py:21
  46.4 38.4 %collective-permute-start.6 = (bf16[448,512]{1,0:T(8,128)(2,1)S(1)}, bf16[448,512]{1,0:T(8,128)(2,1)S(1)}, u32[]{:S(2)}, u32[]{:S(2)}) collective-permute-start(bf16[448,512]{1,0:T(8,128)(2,1)S(1)} %get-tuple-element.112), channel_id=1, source_target_pairs={{0,4},{2,6},{4,0},{6,2},{8,12},{10,14},{12,8},{14,10},{16,20},{18,... | collective-permute-start | bytes 1376264 | tf_op jit(solution)/shard_map/ppermute | solution.py:21
  47.4 37.5 %collective-permute-start.7 = (bf16[448,512]{1,0:T(8,128)(2,1)S(1)}, bf16[448,512]{1,0:T(8,128)(2,1)S(1)}, u32[]{:S(2)}, u32[]{:S(2)}) collective-permute-start(bf16[448,512]{1,0:T(8,128)(2,1)S(1)} %get-tuple-element.111), channel_id=1, source_target_pairs={{0,6},{2,4},{4,2},{6,0},{8,14},{10,12},{12,10},{14,8},{16,22},{18,... | collective-permute-start | bytes 1376264 | tf_op jit(solution)/shard_map/ppermute | solution.py:21
  48.6 45.9 %collective-permute-start.11 = (bf16[448,512]{1,0:T(8,128)(2,1)S(1)}, bf16[448,512]{1,0:T(8,128)(2,1)S(1)}, u32[]{:S(2)}, u32[]{:S(2)}) collective-permute-start(bf16[448,512]{1,0:T(8,128)(2,1)S(1)} %get-tuple-element.109), channel_id=1, source_target_pairs={{0,2},{2,0},{4,6},{6,4},{8,10},{10,8},{12,14},{14,12},{16,18},{18,... | collective-permute-start | bytes 1376264 | tf_op jit(solution)/shard_map/ppermute | solution.py:21
  81.7 21.2 %collective-permute-start.12 = (bf16[448,512]{1,0:T(8,128)(2,1)S(1)}, bf16[448,512]{1,0:T(8,128)(2,1)S(1)}, u32[]{:S(2)}, u32[]{:S(2)}) collective-permute-start(bf16[448,512]{1,0:T(8,128)(2,1)S(1)} %get-tuple-element.108), channel_id=1, source_target_pairs={{0,4},{2,6},{4,0},{6,2},{8,12},{10,14},{12,8},{14,10},{16,20},{18,... | collective-permute-start | bytes 1376264 | tf_op jit(solution)/shard_map/ppermute | solution.py:21
  82.8 20.2 %collective-permute-start.13 = (bf16[448,512]{1,0:T(8,128)(2,1)S(1)}, bf16[448,512]{1,0:T(8,128)(2,1)S(1)}, u32[]{:S(2)}, u32[]{:S(2)}) collective-permute-start(bf16[448,512]{1,0:T(8,128)(2,1)S(1)} %get-tuple-element.107), channel_id=1, source_target_pairs={{0,6},{2,4},{4,2},{6,0},{8,14},{10,12},{12,10},{14,8},{16,22},{18,... | collective-permute-start | bytes 1376264 | tf_op jit(solution)/shard_map/ppermute | solution.py:21
  88.7 25.8 %collective-permute-start.10 = (bf16[448,512]{1,0:T(8,128)(2,1)}, bf16[448,512]{1,0:T(8,128)(2,1)S(1)}, u32[]{:S(2)}, u32[]{:S(2)}) collective-permute-start(bf16[448,512]{1,0:T(8,128)(2,1)} %get-tuple-element.68), channel_id=1, source_target_pairs={{8,0},{10,2},{12,4},{14,6},{16,8},{18,10},{20,12},{22,14},{24,16},... | collective-permute-start | bytes 1376264 | tf_op jit(solution)/shard_map/ppermute | solution.py:32
  90.0 24.5 %collective-permute-start.9 = (bf16[448,512]{1,0:T(8,128)(2,1)}, bf16[448,512]{1,0:T(8,128)(2,1)S(1)}, u32[]{:S(2)}, u32[]{:S(2)}) collective-permute-start(bf16[448,512]{1,0:T(8,128)(2,1)} %get-tuple-element.67), channel_id=1, source_target_pairs={{0,8},{2,10},{4,12},{6,14},{8,16},{10,18},{12,20},{14,22},{16,24},... | collective-permute-start | bytes 1376264 | tf_op jit(solution)/shard_map/ppermute | solution.py:32
  94.6 8.4 %copy-start.2 = (bf16[448,512]{1,0:T(8,128)(2,1)}, bf16[448,512]{1,0:T(8,128)(2,1)S(1)}, u32[]{:S(2)}) copy-start(bf16[448,512]{1,0:T(8,128)(2,1)S(1)} %collective-permute-done.11.refs_1_) | copy-start | bytes 1376260
  106.8 15.3 %collective-permute-start.14 = (bf16[448,512]{1,0:T(8,128)(2,1)}, bf16[448,512]{1,0:T(8,128)(2,1)S(1)}, u32[]{:S(2)}, u32[]{:S(2)}) collective-permute-start(bf16[448,512]{1,0:T(8,128)(2,1)} %get-tuple-element.70), channel_id=1, source_target_pairs={{0,8},{2,10},{4,12},{6,14},{8,16},{10,18},{12,20},{14,22},{16,24},... | collective-permute-start | bytes 1376264 | tf_op jit(solution)/shard_map/ppermute | solution.py:32
  110.5 15.6 %collective-permute-start.15 = (bf16[448,512]{1,0:T(8,128)(2,1)}, bf16[448,512]{1,0:T(8,128)(2,1)S(1)}, u32[]{:S(2)}, u32[]{:S(2)}) collective-permute-start(bf16[448,512]{1,0:T(8,128)(2,1)} %get-tuple-element.71), channel_id=1, source_target_pairs={{8,0},{10,2},{12,4},{14,6},{16,8},{18,10},{20,12},{22,14},{24,16},... | collective-permute-start | bytes 1376264 | tf_op jit(solution)/shard_map/ppermute | solution.py:32
  111.8 54.3 %collective-permute-start.8 = (bf16[512,1920]{1,0:T(8,128)(2,1)S(1)}, bf16[512,1920]{1,0:T(8,128)(2,1)S(1)}, u32[]{:S(2)}, u32[]{:S(2)}) collective-permute-start(bf16[512,1920]{1,0:T(8,128)(2,1)S(1)} %pad_maximum_fusion), channel_id=1, source_target_pairs={{0,8},{2,10},{4,12},{6,14},{8,0},{10,2},{12,4},{14,6},{16,24},{18,... | collective-permute-start | bytes 5898248 | tf_op jit(solution)/shard_map/ppermute | solution.py:21
  120.6 10.8 %copy-start.20 = (bf16[4,448,512]{2,1,0:T(8,128)(2,1)S(1)}, bf16[4,448,512]{2,1,0:T(8,128)(2,1)}, u32[]{:S(2)}) copy-start(bf16[4,448,512]{2,1,0:T(8,128)(2,1)} %get-tuple-element.69.refs_0_) | copy-start | bytes 5505028
  120.6 11.4 %copy-start.33 = (bf16[448,512]{1,0:T(8,128)(2,1)S(1)}, bf16[448,512]{1,0:T(8,128)(2,1)}, u32[]{:S(2)}) copy-start(bf16[448,512]{1,0:T(8,128)(2,1)} %get-tuple-element.78) | copy-start | bytes 1376260
  120.6 12.4 %copy-start.32 = (bf16[448,512]{1,0:T(8,128)(2,1)S(1)}, bf16[448,512]{1,0:T(8,128)(2,1)}, u32[]{:S(2)}) copy-start(bf16[448,512]{1,0:T(8,128)(2,1)} %get-tuple-element.79) | copy-start | bytes 1376260
  120.6 12.4 %collective-permute-start.18 = (bf16[448,512]{1,0:T(8,128)(2,1)}, bf16[448,512]{1,0:T(8,128)(2,1)S(1)}, u32[]{:S(2)}, u32[]{:S(2)}) collective-permute-start(bf16[448,512]{1,0:T(8,128)(2,1)} %get-tuple-element.77), channel_id=1, source_target_pairs={{0,2},{2,0},{4,6},{6,4},{8,10},{10,8},{12,14},{14,12},{16,18},{18,... | collective-permute-start | bytes 1376264 | tf_op jit(solution)/shard_map/ppermute | solution.py:21
  131.4 37.8 %collective-permute-start.17 = (bf16[4,448,512]{2,1,0:T(8,128)(2,1)}, bf16[4,448,512]{2,1,0:T(8,128)(2,1)}, u32[]{:S(2)}, u32[]{:S(2)}) collective-permute-start(bf16[4,448,512]{2,1,0:T(8,128)(2,1)} %get-tuple-element.72.refs_1_), channel_id=1, source_target_pairs={{0,1},{1,0},{2,3},{3,2},{4,5},{5,4},{6,7},{7,6},{8,9},{9,8},{10,11... | collective-permute-start | bytes 5505032 | tf_op jit(solution)/shard_map/ppermute | solution.py:26
  131.4 39.7 %collective-permute-start.16 = (bf16[4,448,512]{2,1,0:T(8,128)(2,1)S(1)}, bf16[4,448,512]{2,1,0:T(8,128)(2,1)}, u32[]{:S(2)}, u32[]{:S(2)}) collective-permute-start(bf16[4,448,512]{2,1,0:T(8,128)(2,1)S(1)} %copy-done.20), channel_id=1, source_target_pairs={{0,1},{1,0},{2,3},{3,2},{4,5},{5,4},{6,7},{7,6},{8,9},{9,8},{10,11... | collective-permute-start | bytes 5505032 | tf_op jit(solution)/shard_map/ppermute | solution.py:26
  131.9 22.3 %collective-permute-start.19 = (bf16[448,512]{1,0:T(8,128)(2,1)S(1)}, bf16[448,512]{1,0:T(8,128)(2,1)S(1)}, u32[]{:S(2)}, u32[]{:S(2)}) collective-permute-start(bf16[448,512]{1,0:T(8,128)(2,1)S(1)} %copy-done.33), channel_id=1, source_target_pairs={{0,4},{2,6},{4,0},{6,2},{8,12},{10,14},{12,8},{14,10},{16,20},{18,... | collective-permute-start | bytes 1376264 | tf_op jit(solution)/shard_map/ppermute | solution.py:21
  133.0 21.3 %copy-start.10 = (bf16[448,512]{1,0:T(8,128)(2,1)}, bf16[448,512]{1,0:T(8,128)(2,1)S(1)}, u32[]{:S(2)}) copy-start(bf16[448,512]{1,0:T(8,128)(2,1)S(1)} %collective-permute-done.18.refs_1_) | copy-start | bytes 1376260
  133.0 21.3 %collective-permute-start.20 = (bf16[448,512]{1,0:T(8,128)(2,1)S(1)}, bf16[448,512]{1,0:T(8,128)(2,1)S(1)}, u32[]{:S(2)}, u32[]{:S(2)}) collective-permute-start(bf16[448,512]{1,0:T(8,128)(2,1)S(1)} %copy-done.32), channel_id=1, source_target_pairs={{0,6},{2,4},{4,2},{6,0},{8,14},{10,12},{12,10},{14,8},{16,22},{18,... | collective-permute-start | bytes 1376264 | tf_op jit(solution)/shard_map/ppermute | solution.py:21
  158.6 26.4 %collective-permute-start.21 = (bf16[4,448,512]{2,1,0:T(8,128)(2,1)}, bf16[4,448,512]{2,1,0:T(8,128)(2,1)S(1)}, u32[]{:S(2)}, u32[]{:S(2)}) collective-permute-start(bf16[4,448,512]{2,1,0:T(8,128)(2,1)} %own_sums.2.own), channel_id=1, source_target_pairs={{0,1},{1,0},{2,3},{3,2},{4,5},{5,4},{6,7},{7,6},{8,9},{9,8},{10,11... | collective-permute-start | bytes 5505032 | tf_op jit(solution)/shard_map/ppermute | solution.py:26
  158.7 39.1 %collective-permute-start.22 = (bf16[448,512]{1,0:T(8,128)(2,1)}, bf16[448,512]{1,0:T(8,128)(2,1)S(1)}, u32[]{:S(2)}, u32[]{:S(2)}) collective-permute-start(bf16[448,512]{1,0:T(8,128)(2,1)} %get-tuple-element.82), channel_id=1, source_target_pairs={{0,2},{2,0},{4,6},{6,4},{8,10},{10,8},{12,14},{14,12},{16,18},{18,... | collective-permute-start | bytes 1376264 | tf_op jit(solution)/shard_map/ppermute | solution.py:21
  166.0 31.8 %collective-permute-start.23 = (bf16[448,512]{1,0:T(8,128)(2,1)}, bf16[448,512]{1,0:T(8,128)(2,1)S(1)}, u32[]{:S(2)}, u32[]{:S(2)}) collective-permute-start(bf16[448,512]{1,0:T(8,128)(2,1)} %get-tuple-element.83), channel_id=1, source_target_pairs={{0,4},{2,6},{4,0},{6,2},{8,12},{10,14},{12,8},{14,10},{16,20},{18,... | collective-permute-start | bytes 1376264 | tf_op jit(solution)/shard_map/ppermute | solution.py:21
  169.2 28.6 %collective-permute-start.24 = (bf16[448,512]{1,0:T(8,128)(2,1)}, bf16[448,512]{1,0:T(8,128)(2,1)S(1)}, u32[]{:S(2)}, u32[]{:S(2)}) collective-permute-start(bf16[448,512]{1,0:T(8,128)(2,1)} %get-tuple-element.84), channel_id=1, source_target_pairs={{0,6},{2,4},{4,2},{6,0},{8,14},{10,12},{12,10},{14,8},{16,22},{18,... | collective-permute-start | bytes 1376264 | tf_op jit(solution)/shard_map/ppermute | solution.py:21
  197.8 5.9 %copy-start.25 = (bf16[1024,512]{1,0:T(8,128)(2,1)S(1)}, bf16[1024,512]{1,0:T(8,128)(2,1)}, u32[]{:S(2)}) copy-start(bf16[1024,512]{1,0:T(8,128)(2,1)} %get-tuple-element.95) | copy-start | bytes 3145732
  202.0 4.0 collective-permute-start.25
  202.0 69.3 %collective-permute-start.26 = (bf16[1024,512]{1,0:T(8,128)(2,1)S(1)}, bf16[1024,512]{1,0:T(8,128)(2,1)S(1)}, u32[]{:S(2)}, u32[]{:S(2)}) collective-permute-start(bf16[1024,512]{1,0:T(8,128)(2,1)S(1)} %copy-done.27), channel_id=1, source_target_pairs={{0,2},{2,0},{4,6},{6,4},{8,10},{10,8},{12,14},{14,12},{16,18},{18,... | collective-permute-start | bytes 3145736 | tf_op jit(solution)/shard_map/ppermute | solution.py:21
  202.6 68.7 %collective-permute-start.27 = (bf16[1024,512]{1,0:T(8,128)(2,1)S(1)}, bf16[1024,512]{1,0:T(8,128)(2,1)S(1)}, u32[]{:S(2)}, u32[]{:S(2)}) collective-permute-start(bf16[1024,512]{1,0:T(8,128)(2,1)S(1)} %copy-done.26), channel_id=1, source_target_pairs={{0,4},{2,6},{4,0},{6,2},{8,12},{10,14},{12,8},{14,10},{16,20},{18,... | collective-permute-start | bytes 3145736 | tf_op jit(solution)/shard_map/ppermute | solution.py:21
  203.6 67.7 %collective-permute-start.28 = (bf16[1024,512]{1,0:T(8,128)(2,1)S(1)}, bf16[1024,512]{1,0:T(8,128)(2,1)S(1)}, u32[]{:S(2)}, u32[]{:S(2)}) collective-permute-start(bf16[1024,512]{1,0:T(8,128)(2,1)S(1)} %copy-done.25), channel_id=1, source_target_pairs={{0,6},{2,4},{4,2},{6,0},{8,14},{10,12},{12,10},{14,8},{16,22},{18,... | collective-permute-start | bytes 3145736 | tf_op jit(solution)/shard_map/ppermute | solution.py:21
  271.3 5.5 %copy-start.28 = (bf16[1024,512]{1,0:T(8,128)(2,1)}, bf16[1024,512]{1,0:T(8,128)(2,1)S(1)}, u32[]{:S(2)}) copy-start(bf16[1024,512]{1,0:T(8,128)(2,1)S(1)} %collective-permute-done.26.refs_1_) | copy-start | bytes 3145732
  271.3 5.5 %copy-start.29 = (bf16[1024,512]{1,0:T(8,128)(2,1)}, bf16[1024,512]{1,0:T(8,128)(2,1)S(1)}, u32[]{:S(2)}) copy-start(bf16[1024,512]{1,0:T(8,128)(2,1)S(1)} %collective-permute-done.27.refs_2_) | copy-start | bytes 3145732
  271.4 5.5 %copy-start.30 = (bf16[1024,512]{1,0:T(8,128)(2,1)}, bf16[1024,512]{1,0:T(8,128)(2,1)S(1)}, u32[]{:S(2)}) copy-start(bf16[1024,512]{1,0:T(8,128)(2,1)S(1)} %collective-permute-done.28.refs_3_) | copy-start | bytes 3145732
  276.9 2.9 collective-permute-start.29
  290.4 7.1 %copy-start.36 = (bf16[4,128,1024]{2,1,0:T(8,128)(2,1)S(1)}, bf16[4,128,1024]{2,1,0:T(8,128)(2,1)}, u32[]{:S(2)}) copy-start(bf16[4,128,1024]{2,1,0:T(8,128)(2,1)} %get-tuple-element.103) | copy-start | bytes 3145732
  292.3 9.6 %copy-start.24 = (bf16[1,1024,7168]{2,1,0:T(8,128)(2,1)S(1)}, bf16[1,1024,7168]{2,1,0:T(8,128)(2,1)}, u32[]{:S(2)}) copy-start(bf16[1,1024,7168]{2,1,0:T(8,128)(2,1)} %all-gather.3.cloned.1.call-done) | copy-start | bytes 44040196
  296.4 34.5 %collective-permute-start.46 = (bf16[512,1408]{1,0:T(8,128)(2,1)S(1)}, bf16[512,1408]{1,0:T(8,128)(2,1)S(1)}, u32[]{:S(2)}, u32[]{:S(2)}) collective-permute-start(bf16[512,1408]{1,0:T(8,128)(2,1)S(1)} %convolution_convert_fusion), channel_id=1, source_target_pairs={{0,4},{2,6},{4,0},{6,2},{8,12},{10,14},{12,8},{14,10},{16,20},{18,... | collective-permute-start | bytes 4325384 | tf_op jit(solution)/shard_map/ppermute | solution.py:21
  301.2 34.5 %collective-permute-start.42 = (bf16[512,1408]{1,0:T(8,128)(2,1)S(1)}, bf16[512,1408]{1,0:T(8,128)(2,1)S(1)}, u32[]{:S(2)}, u32[]{:S(2)}) collective-permute-start(bf16[512,1408]{1,0:T(8,128)(2,1)S(1)} %convolution_convert_fusion.1), channel_id=1, source_target_pairs={{0,2},{2,0},{4,6},{6,4},{8,10},{10,8},{12,14},{14,12},{16,18},{18,... | collective-permute-start | bytes 4325384 | tf_op jit(solution)/shard_map/ppermute | solution.py:21
  303.7 66.2 %collective-permute-start.38 = (bf16[512,1536]{1,0:T(8,128)(2,1)S(1)}, bf16[512,1536]{1,0:T(8,128)(2,1)S(1)}, u32[]{:S(2)}, u32[]{:S(2)}) collective-permute-start(bf16[512,1536]{1,0:T(8,128)(2,1)S(1)} %convolution_convert_fusion.2), channel_id=1, source_target_pairs={{0,8},{2,10},{4,12},{6,14},{8,0},{10,2},{12,4},{14,6},{16,24},{18,... | collective-permute-start | bytes 4718600 | tf_op jit(solution)/shard_map/ppermute | solution.py:21
  305.7 25.2 %copy-start.35 = (bf16[4,128,1024]{2,1,0:T(8,128)(2,1)S(1)}, bf16[4,128,1024]{2,1,0:T(8,128)(2,1)}, u32[]{:S(2)}) copy-start(bf16[4,128,1024]{2,1,0:T(8,128)(2,1)} %get-tuple-element.104) | copy-start | bytes 3145732
  305.7 56.1 %collective-permute-start.34 = (bf16[512,1408]{1,0:T(8,128)(2,1)S(1)}, bf16[512,1408]{1,0:T(8,128)(2,1)S(1)}, u32[]{:S(2)}, u32[]{:S(2)}) collective-permute-start(bf16[512,1408]{1,0:T(8,128)(2,1)S(1)} %convolution_convert_fusion.3), channel_id=1, source_target_pairs={{0,4},{2,6},{4,0},{6,2},{8,12},{10,14},{12,8},{14,10},{16,20},{18,... | collective-permute-start | bytes 4325384 | tf_op jit(solution)/shard_map/ppermute | solution.py:21
  308.6 58.0 %collective-permute-start.30 = (bf16[512,1408]{1,0:T(8,128)(2,1)S(1)}, bf16[512,1408]{1,0:T(8,128)(2,1)S(1)}, u32[]{:S(2)}, u32[]{:S(2)}) collective-permute-start(bf16[512,1408]{1,0:T(8,128)(2,1)S(1)} %convolution_convert_fusion.4), channel_id=1, source_target_pairs={{0,2},{2,0},{4,6},{6,4},{8,10},{10,8},{12,14},{14,12},{16,18},{18,... | collective-permute-start | bytes 4325384 | tf_op jit(solution)/shard_map/ppermute | solution.py:21
  332.7 49.3 %collective-permute-start.47 = (bf16[2,2,64,1408]{3,2,1,0:T(8,128)(2,1)S(1)}, bf16[2,2,64,1408]{3,2,1,0:T(8,128)(2,1)S(1)}, u32[]{:S(2)}, u32[]{:S(2)}) collective-permute-start(bf16[2,2,64,1408]{3,2,1,0:T(8,128)(2,1)S(1)} %slice_bitcast_fusion), channel_id=1, source_target_pairs={{0,2},{2,0},{4,6},{6,4},{8,10},{10,8},{12,14},{14,12},{16,18},{18,... | collective-permute-start | bytes 2162696 | tf_op jit(solution)/shard_map/ppermute | solution.py:21
  337.6 44.8 %collective-permute-start.43 = (bf16[2,2,64,1408]{3,2,1,0:T(8,128)(2,1)S(1)}, bf16[2,2,64,1408]{3,2,1,0:T(8,128)(2,1)S(1)}, u32[]{:S(2)}, u32[]{:S(2)}) collective-permute-start(bf16[2,2,64,1408]{3,2,1,0:T(8,128)(2,1)S(1)} %slice_bitcast_fusion.2), channel_id=1, source_target_pairs={{0,4},{2,6},{4,0},{6,2},{8,12},{10,14},{12,8},{14,10},{16,20},{18,... | collective-permute-start | bytes 2162696 | tf_op jit(solution)/shard_map/ppermute | solution.py:21
  363.6 33.1 %collective-permute-start.35 = (bf16[2,2,64,1408]{3,2,1,0:T(8,128)(2,1)S(1)}, bf16[2,2,64,1408]{3,2,1,0:T(8,128)(2,1)S(1)}, u32[]{:S(2)}, u32[]{:S(2)}) collective-permute-start(bf16[2,2,64,1408]{3,2,1,0:T(8,128)(2,1)S(1)} %slice_bitcast_fusion.4), channel_id=1, source_target_pairs={{0,2},{2,0},{4,6},{6,4},{8,10},{10,8},{12,14},{14,12},{16,18},{18,... | collective-permute-start | bytes 2162696 | tf_op jit(solution)/shard_map/ppermute | solution.py:21
  368.7 28.3 %collective-permute-start.31 = (bf16[2,2,64,1408]{3,2,1,0:T(8,128)(2,1)S(1)}, bf16[2,2,64,1408]{3,2,1,0:T(8,128)(2,1)S(1)}, u32[]{:S(2)}, u32[]{:S(2)}) collective-permute-start(bf16[2,2,64,1408]{3,2,1,0:T(8,128)(2,1)S(1)} %slice_bitcast_fusion.6), channel_id=1, source_target_pairs={{0,4},{2,6},{4,0},{6,2},{8,12},{10,14},{12,8},{14,10},{16,20},{18,... | collective-permute-start | bytes 2162696 | tf_op jit(solution)/shard_map/ppermute | solution.py:21
  371.9 35.3 %collective-permute-start.39 = (bf16[2,2,64,1536]{3,2,0,1:T(8,128)(2,1)S(1)}, bf16[2,2,64,1536]{3,2,0,1:T(8,128)(2,1)S(1)}, u32[]{:S(2)}, u32[]{:S(2)}) collective-permute-start(bf16[2,2,64,1536]{3,2,0,1:T(8,128)(2,1)S(1)} %copy.15), channel_id=1, source_target_pairs={{0,16},{2,18},{4,20},{6,22},{8,24},{10,26},{12,28},{14,30},{16,0},... | collective-permute-start | bytes 2359304 | tf_op jit(solution)/shard_map/ppermute | solution.py:21
  382.3 28.2 %collective-permute-start.48 = (bf16[2,64,1408]{2,1,0:T(8,128)(2,1)S(1)}, bf16[2,64,1408]{2,1,0:T(8,128)(2,1)S(1)}, u32[]{:S(2)}, u32[]{:S(2)}) collective-permute-start(bf16[2,64,1408]{2,1,0:T(8,128)(2,1)S(1)} %slice_bitcast_fusion.12), channel_id=1, source_target_pairs={{0,8},{2,10},{4,12},{6,14},{8,0},{10,2},{12,4},{14,6},{16,24},{18,... | collective-permute-start | bytes 1081352 | tf_op jit(solution)/shard_map/ppermute | solution.py:21
  382.6 41.4 %collective-permute-start.44 = (bf16[2,64,1408]{2,1,0:T(8,128)(2,1)S(1)}, bf16[2,64,1408]{2,1,0:T(8,128)(2,1)S(1)}, u32[]{:S(2)}, u32[]{:S(2)}) collective-permute-start(bf16[2,64,1408]{2,1,0:T(8,128)(2,1)S(1)} %slice_bitcast_fusion.14), channel_id=1, source_target_pairs={{0,8},{2,10},{4,12},{6,14},{8,0},{10,2},{12,4},{14,6},{16,24},{18,... | collective-permute-start | bytes 1081352 | tf_op jit(solution)/shard_map/ppermute | solution.py:21
  397.0 42.1 %collective-permute-start.36 = (bf16[2,64,1408]{2,1,0:T(8,128)(2,1)S(1)}, bf16[2,64,1408]{2,1,0:T(8,128)(2,1)S(1)}, u32[]{:S(2)}, u32[]{:S(2)}) collective-permute-start(bf16[2,64,1408]{2,1,0:T(8,128)(2,1)S(1)} %slice_bitcast_fusion.16), channel_id=1, source_target_pairs={{0,8},{2,10},{4,12},{6,14},{8,0},{10,2},{12,4},{14,6},{16,24},{18,... | collective-permute-start | bytes 1081352 | tf_op jit(solution)/shard_map/ppermute | solution.py:21
  397.3 41.6 %collective-permute-start.32 = (bf16[2,64,1408]{2,1,0:T(8,128)(2,1)S(1)}, bf16[2,64,1408]{2,1,0:T(8,128)(2,1)S(1)}, u32[]{:S(2)}, u32[]{:S(2)}) collective-permute-start(bf16[2,64,1408]{2,1,0:T(8,128)(2,1)S(1)} %slice_bitcast_fusion.18), channel_id=1, source_target_pairs={{0,8},{2,10},{4,12},{6,14},{8,0},{10,2},{12,4},{14,6},{16,24},{18,... | collective-permute-start | bytes 1081352 | tf_op jit(solution)/shard_map/ppermute | solution.py:21
  407.5 43.8 %collective-permute-start.40 = (bf16[2,64,1536]{2,1,0:T(8,128)(2,1)S(1)}, bf16[2,64,1536]{2,1,0:T(8,128)(2,1)S(1)}, u32[]{:S(2)}, u32[]{:S(2)}) collective-permute-start(bf16[2,64,1536]{2,1,0:T(8,128)(2,1)S(1)} %slice_bitcast_fusion.10), channel_id=1, source_target_pairs={{0,2},{2,0},{4,6},{6,4},{8,10},{10,8},{12,14},{14,12},{16,18},{18,... | collective-permute-start | bytes 1179656 | tf_op jit(solution)/shard_map/ppermute | solution.py:21
  410.6 47.0 %collective-permute-start.49 = (bf16[64,1408]{1,0:T(8,128)(2,1)S(1)}, bf16[64,1408]{1,0:T(8,128)(2,1)S(1)}, u32[]{:S(2)}, u32[]{:S(2)}) collective-permute-start(bf16[64,1408]{1,0:T(8,128)(2,1)S(1)} %slice_bitcast_fusion.22), channel_id=1, source_target_pairs={{0,16},{2,18},{4,20},{6,22},{8,24},{10,26},{12,28},{14,30},{16,0},... | collective-permute-start | bytes 540680 | tf_op jit(solution)/shard_map/ppermute | solution.py:21
  424.1 33.4 %collective-permute-start.45 = (bf16[64,1408]{1,0:T(8,128)(2,1)S(1)}, bf16[64,1408]{1,0:T(8,128)(2,1)S(1)}, u32[]{:S(2)}, u32[]{:S(2)}) collective-permute-start(bf16[64,1408]{1,0:T(8,128)(2,1)S(1)} %slice_bitcast_fusion.24), channel_id=1, source_target_pairs={{0,16},{2,18},{4,20},{6,22},{8,24},{10,26},{12,28},{14,30},{16,0},... | collective-permute-start | bytes 540680 | tf_op jit(solution)/shard_map/ppermute | solution.py:21
  439.0 12.2 %collective-permute-start.33 = (bf16[64,1408]{1,0:T(8,128)(2,1)S(1)}, bf16[64,1408]{1,0:T(8,128)(2,1)S(1)}, u32[]{:S(2)}, u32[]{:S(2)}) collective-permute-start(bf16[64,1408]{1,0:T(8,128)(2,1)S(1)} %slice_bitcast_fusion.28), channel_id=1, source_target_pairs={{0,16},{2,18},{4,20},{6,22},{8,24},{10,26},{12,28},{14,30},{16,0},... | collective-permute-start | bytes 540680 | tf_op jit(solution)/shard_map/ppermute | solution.py:21
  439.2 15.4 %collective-permute-start.37 = (bf16[64,1408]{1,0:T(8,128)(2,1)S(1)}, bf16[64,1408]{1,0:T(8,128)(2,1)S(1)}, u32[]{:S(2)}, u32[]{:S(2)}) collective-permute-start(bf16[64,1408]{1,0:T(8,128)(2,1)S(1)} %slice_bitcast_fusion.26), channel_id=1, source_target_pairs={{0,16},{2,18},{4,20},{6,22},{8,24},{10,26},{12,28},{14,30},{16,0},... | collective-permute-start | bytes 540680 | tf_op jit(solution)/shard_map/ppermute | solution.py:21
  451.4 6.0 %collective-permute-start.41 = (bf16[64,1536]{1,0:T(8,128)(2,1)S(1)}, bf16[64,1536]{1,0:T(8,128)(2,1)S(1)}, u32[]{:S(2)}, u32[]{:S(2)}) collective-permute-start(bf16[64,1536]{1,0:T(8,128)(2,1)S(1)} %slice_bitcast_fusion.20), channel_id=1, source_target_pairs={{0,4},{2,6},{4,0},{6,2},{8,12},{10,14},{12,8},{14,10},{16,20},{18,... | collective-permute-start | bytes 589832 | tf_op jit(solution)/shard_map/ppermute | solution.py:21
  (25 other events, 40.3 us)
Sparse Core Ops, SparseCore 0:
  17.1 29.4 all-gather.2

commit v6 on v5

--- a/solution.py
+++ b/solution.py
@@ -152,7 +152,7 @@
     head[...] = chosen(values, names, meta[base + first]).astype(BF16)
 
 
-def totals_kernel(experts, meta, *refs):
+def totals_kernel(experts, chunks, meta, *refs):
     values = [ref[...].astype(F32) for ref in refs[:MOST]]
     below, above = (ref[...].astype(F32) for ref in refs[MOST : MOST + 2])
     stacked, sends = refs[MOST + 2], refs[MOST + 3 :]
@@ -172,7 +172,10 @@
         total = total.astype(BF16)
         stacked[k] = total
         if k:
-            sends[k - 1][...] = total
+            for c in range(chunks):
+                part = sends[c * (MOST - 1) + k - 1]
+                rows = part.shape[0]
+                part[...] = total[c * rows : (c + 1) * rows]
 
 
 def stack_kernel(*refs):
@@ -180,10 +183,11 @@
         refs[MOST][k] = refs[k][...]
 
 
-def group_sums(meta, got):
+def group_sums(meta, got, chunks):
     shape = got[0].shape
     experts = lax.axis_size("expert")
     piece = jax.ShapeDtypeStruct(shape, BF16)
+    part = jax.ShapeDtypeStruct((shape[0] // chunks, shape[1]), BF16)
     tail, head = pl.pallas_call(
         ends_kernel,
         out_shape=[piece, piece],
@@ -195,10 +199,10 @@
     below = shift_groups(tail, MOST)
     above = shift_groups(head, -MOST)
     return pl.pallas_call(
-        functools.partial(totals_kernel, experts),
-        out_shape=[jax.ShapeDtypeStruct((MOST,) + shape, BF16)] + [piece] * (MOST - 1),
+        functools.partial(totals_kernel, experts, chunks),
+        out_shape=[jax.ShapeDtypeStruct((MOST,) + shape, BF16)] + [part] * (chunks * (MOST - 1)),
         in_specs=[scalars()] + [whole()] * (MOST + 2),
-        out_specs=[whole()] * MOST,
+        out_specs=[whole()] * (1 + chunks * (MOST - 1)),
         compiler_params=params(),
         name="cluster_sums",
     )(meta, *got, below, above)
@@ -330,19 +334,25 @@
             first, inner = divmod(j, 8)
             both = strips[first]
             row0, row1 = both[inner : inner + 1, :], both[inner + 1 : inner + 2, :]
-            a, b, d = row0[:, j : j + 1], row1[:, j : j + 1], row1[:, j + 1 : j + 2]
+            columns = [
+                [jnp.broadcast_to(strip[:, i : i + 1], strip.shape) for i in (j, j + 1)]
+                for strip in strips[first:]
+            ]
+            column0, column1 = columns[0]
+            a, b = column0[inner : inner + 1, :], column0[inner + 1 : inner + 2, :]
+            d = column1[inner + 1 : inner + 2, :]
             inverse_a = reciprocal(a)
             inverse_d = a * reciprocal(a * d - b * b)
             ratio = b * inverse_a
             later = jnp.where(lane_row == j, 0.0, row1) - ratio * jnp.where(lane_row == j, 1.0, row0)
-            scaled0 = jnp.where(lane_row == j, 1.0, row0) * inverse_a
+            scaled0 = jnp.where(lane_row == j, 1.0, jnp.where(lane_row == j + 1, 0.0, row0)) * inverse_a
             scaled1 = jnp.where(lane_row == j + 1, 1.0, later) * inverse_d
             for s in range(first, tile // 8):
                 strip = strips[s]
-                column0 = strip[:, j : j + 1]
-                column1 = strip[:, j + 1 : j + 2] - column0 * ratio
+                column0, column1 = columns[s - first]
+                column1 = column1 - column0 * ratio
                 new = jnp.where((lane == j) | (lane == j + 1), 0.0, strip)
-                new = new - column0 * jnp.where(lane_row == j + 1, 0.0, scaled0) - column1 * scaled1
+                new = new - column0 * scaled0 - column1 * scaled1
                 if s == first:
                     new = jnp.where(sub > inner + 1, new, jnp.where(sub == inner + 1, later, strip))
                 strips[s] = new
@@ -496,10 +506,15 @@
         swap_expert(answered(halves[order[0]][1], start, width).astype(BF16), masks[order[0]])
         for start, width, order in chunks
     ]
-    values = [
-        (answered(halves[order[0]][0], start, width) + came.astype(F32)).astype(BF16)
-        for came, (start, width, order) in zip(first, chunks)
-    ]
+    def added(i):
+        start, width, order = chunks[i]
+        return (answered(halves[order[0]][0], start, width) + first[i].astype(F32)).astype(BF16)
+
+    values = [None] * len(chunks)
+    if len(chunks) > 2:
+        values[2] = added(2)
+        _, first[0], first[1] = lax.optimization_barrier((values[2], first[0], first[1]))
+    values = [added(i) if value is None else value for i, value in enumerate(values)]
     left = [[bit for bit in range(bits - 1, -1, -1) if bit != order[0]] for _, _, order in chunks]
     for step in range(1, bits):
         for i, (_, width, order) in enumerate(chunks):
@@ -538,33 +553,37 @@
 
     chunks = 2 if rows % 32 == 0 else 1
     chunk = rows // chunks
-    got = []
-    for c in range(chunks):
-        span = slice(c * chunk, (c + 1) * chunk)
-        own = [
-            (own_half[k, span].astype(F32) + sent_half[k, span].astype(F32)).astype(BF16)
-            for k in range(MOST)
-        ]
-        got.append([own[0]] + [swap_expert(own[k], k) for k in range(1, MOST)])
+    own = [(own_half[k].astype(F32) + sent_half[k].astype(F32)).astype(BF16) for k in range(MOST)]
+    got = [own[0]] + [swap_expert(own[k], k) for k in range(1, MOST)]
     masks = group_masks(experts)
     for mask in masks[:-1]:
         spread = jnp.concatenate([spread, swap_expert(spread, mask)], axis=0)
-    spread, got[0] = lax.optimization_barrier((spread, got[0]))
+    spread, got = lax.optimization_barrier((spread, got))
+    sums, *sends = group_sums(meta, got, chunks)
+    other_sums = swap_dp(sums)
+    back = []
+    for c in range(chunks):
+        first = c * (MOST - 1)
+        back.append(
+            [sums[0, c * chunk : (c + 1) * chunk]]
+            + [swap_expert(sends[first + k - 1], k) for k in range(1, MOST)]
+        )
     if masks:
+        spread, sums = lax.optimization_barrier((spread, sums))
         spread = jnp.concatenate([spread, swap_expert(spread, masks[-1])], axis=0)
-    sums, other_sums, back = [], [], []
-    for c in range(chunks):
-        value, *sends = group_sums(meta, got[c])
-        sums.append(value)
-        other_sums.append(swap_dp(value))
-        back.append([value[0]] + [swap_expert(sends[k - 1], k) for k in range(1, MOST)])
-    parts = project(spread, sums + other_sums)
+    other_sums, back[0] = lax.optimization_barrier((other_sums, back[0]))
     before = ()
     for c in range(chunks):
         if c == chunks - 1:
-            parts, before, back[c] = lax.optimization_barrier((parts, before, back[c]))
+            before, back[c] = lax.optimization_barrier((before, back[c]))
         mine = stacked(back[c])
-        before = crossed(meta, mine, swap_dp(mine), gate_rows, up_rows, c, chunks, before)
+        if c == chunks - 1:
+            mine, spread = lax.optimization_barrier((mine, spread))
+        other = swap_dp(mine)
+        if c == chunks - 1:
+            parts = project(spread, [sums, other_sums])
+            parts, gate_rows, other = lax.optimization_barrier((parts, gate_rows, other))
+        before = crossed(meta, mine, other, gate_rows, up_rows, c, chunks, before)
     gram, raw = before
     if lax.axis_size("tensor") > 1:
         gram, raw = lax.psum((gram, raw), "tensor")

time: 475 us -> 437 us (0.920)
  Pallas kernels: 147 us -> 125 us
  starting transfers between devices: 62.6 us -> 46.4 us
  local copies, waits for them, and re-layouts: 21.9 us -> 12.9 us
  waiting for transfers between devices: 189 us -> 194 us
    pallas_call x1, Pallas kernels: 51.2 us -> 33.9 us  [factored(): pl.pallas_call(functools.partial(factor_kernel, min(LANES, rank)), out_sh...]
    ppermute x4 -> x2, waiting for transfers between devices: 3.95 us -> 19.9 us  [shift_groups(): return lax.ppermute(value, 'expert', moves)]
    ppermute x40 -> x37, waiting for transfers between devices: 183 us -> 173 us  [swap_expert(): lax.ppermute(value, 'expert', [(source, source ^ mask) for source in rang...]
    ppermute x40 -> x37, starting transfers between devices: 50.6 us -> 41.1 us  [swap_expert(): lax.ppermute(value, 'expert', [(source, source ^ mask) for source in rang...]
    unnamed x79 -> x58, local copies, waits for them, and re-layouts: 14.9 us -> 8.34 us
    ppermute x4 -> x2, starting transfers between devices: 10.8 us -> 4.82 us  [shift_groups(): return lax.ppermute(value, 'expert', moves)]
  transfers between devices with their start and end apart: 51 -> 45, of which waited for: 21 -> 18; matrix products, arithmetic and copies ran while one was open for 7% -> 8% of each run, Pallas kernels for 30% -> 27%
where the time goes in v6:
time: 437 us; the launch traced here: 429 us
  waiting for transfers between devices  194 us (44%)
  Pallas kernels  125 us (29%)
  starting transfers between devices  46.4 us (11%)
  matrix products  23.2 us (5%)
  between operations  14.2 us (3%)
  other arithmetic  12.9 us (3%)
  local copies, waits for them, and re-layouts  12.9 us (3%)
    ppermute x37, waiting for transfers between devices, swap_expert(): lax.ppermute(value, 'expert', [(source, source ^ mask) for source in rang...  173 us
    ppermute x37, starting transfers between devices, swap_expert(): lax.ppermute(value, 'expert', [(source, source ^ mask) for source in rang...  41.1 us
    pallas_call x1, Pallas kernels, factored(): pl.pallas_call(functools.partial(factor_kernel, min(LANES, rank)), out_sh...  33.9 us
    pallas_call x2, Pallas kernels, crossed(): pl.pallas_call(functools.partial(cross_kernel, bool(before)), grid_spec=p...  24.6 us
    dot_general x10, matrix products, mul(): return lax.dot_general(a, b, (dims, ((), ())), preferred_element_type=F32)  23.2 us
    ppermute x2, waiting for transfers between devices, shift_groups(): return lax.ppermute(value, 'expert', moves)  19.9 us
    pallas_call x2, Pallas kernels, sketch_half(): pl.pallas_call(sketch_kernel, grid_spec=pltpu.PrefetchScalarGridSpec(num_...  17.8 us
    pallas_call x1, Pallas kernels, project(): pl.pallas_call(functools.partial(project_kernel, len(sums)), grid=(MOST,)...  13.5 us
  transfers between devices with their start and end apart: 45, of which 18 were waited for; matrix products, arithmetic and copies ran while one was open for 8% of the time, Pallas kernels for 27%

profile of v6, /device:TPU:0, one launch (start us, length us, event | category | flops | bytes accessed | tf_op | source)
XLA Modules:
  0.0 428.7 jit_solution(4456552956570845090)
XLA Ops:
  6.5 1.3 pad_add_fusion.meta
  7.8 8.9 %sketch_half.3 = bf16[4,896,512]{2,1,0:T(8,128)(2,1)} custom-call(s32[25]{0:T(128)} %pad_add_fusion.meta, bf16[7168,512]{1,0:T(8,128)(2,1)} %bitcast.154, bf16[7168,512]{1,0:T(8,128)(2,1)} %bitcast.160, bf16[2,512,512]{2,1,0:T(8,128)(2,1)} %bitcast.166), custom_call_target="tpu_custom_call" | custom-call | flops 3758096384 | bytes 7340032 | tf_op jit(solution)/shard_map/sketch_half/pallas_call | solution.py:121
  18.6 2.8 token_pieces.1
  21.3 2.5 collective-permute-start
  23.8 1.5 collective-permute-start.1
  25.4 8.8 %sketch_half.2 = bf16[4,896,512]{2,1,0:T(8,128)(2,1)} custom-call(s32[25]{0:T(128)} %pad_add_fusion.meta, bf16[7168,512]{1,0:T(8,128)(2,1)} %bitcast.155, bf16[7168,512]{1,0:T(8,128)(2,1)} %bitcast.161, bf16[2,512,512]{2,1,0:T(8,128)(2,1)} %bitcast.167), custom_call_target="tpu_custom_call" | custom-call | flops 3758096384 | bytes 7340032 | tf_op jit(solution)/shard_map/sketch_half/pallas_call | solution.py:121
  34.2 3.2 collective-permute-done.1
  37.5 2.7 collective-permute-start.3
  40.1 5.7 %fusion.23 = (bf16[896,512]{1,0:T(8,128)(2,1)}, bf16[896,512]{1,0:T(8,128)(2,1)}, bf16[896,512]{1,0:T(8,128)(2,1)}, bf16[896,512]{1,0:T(8,128)(2,1)}) fusion(bf16[4,896,512]{2,1,0:T(8,128)(2,1)} %collective-permute-done.4, bf16[4,896,512]{2,1,0:T(8,128)(2,1)} %sketch_half.2), kind=kLoop, calls=%fused_computation.45 | loop fusion | flops 7340032 | bytes 11010048 | tf_op jit(solution)/shard_map/convert_element_type | solution.py:556
  47.9 1.4 collective-permute-start.7
  49.4 33.4 %collective-permute-done.3 = bf16[256,1920]{1,0:T(8,128)(2,1)} collective-permute-done((bf16[256,1920]{1,0:T(8,128)(2,1)S(1)}, bf16[256,1920]{1,0:T(8,128)(2,1)}, u32[]{:S(2)}, u32[]{:S(2)}) %collective-permute-start.3) | collective-permute-done | bytes 983072 | tf_op jit(solution)/shard_map/ppermute | solution.py:21
  82.8 1.3 pad_maximum_fusion.1
  84.2 4.2 collective-permute-done.6.refs_2_
  89.3 4.3 %end_sums.1 = (bf16[896,512]{1,0:T(8,128)(2,1)}, bf16[896,512]{1,0:T(8,128)(2,1)}) custom-call(s32[25]{0:T(128)} %pad_add_fusion.meta, bf16[896,512]{1,0:T(8,128)(2,1)} %get-tuple-element.72.refs_0_, bf16[896,512]{1,0:T(8,128)(2,1)} %copy-done, bf16[896,512]{1,0:T(8,128)(2,1)} %copy-done.1, bf16[896,512]{1,0:T(8,128)(2,1)} %collective-permute-done.7.refs_3_), custom_call_target="tpu_custom_call" | custom-call | tf_op jit(solution)/shard_map/end_sums/pallas_call | solution.py:191
  93.7 3.5 collective-permute-start.8
  97.2 1.3 collective-permute-start.9
  98.5 15.8 %collective-permute-done.8.refs_4_ = bf16[896,512]{1,0:T(8,128)(2,1)S(1)} collective-permute-done((bf16[896,512]{1,0:T(8,128)(2,1)}, bf16[896,512]{1,0:T(8,128)(2,1)S(1)}, u32[]{:S(2)}, u32[]{:S(2)}) %collective-permute-start.8) | collective-permute-done | bytes 917536 | tf_op jit(solution)/shard_map/ppermute | solution.py:32
  114.3 4.1 collective-permute-done.9.refs_5_
  119.3 7.4 %cluster_sums.1 = (bf16[4,896,512]{2,1,0:T(8,128)(2,1)}, bf16[448,512]{1,0:T(8,128)(2,1)}, bf16[448,512]{1,0:T(8,128)(2,1)}, bf16[448,512]{1,0:T(8,128)(2,1)}, b...) custom-call(s32[25]{0:T(128)} %pad_add_fusion.meta, ...), custom_call_target="tpu_custom_call" | custom-call | tf_op jit(solution)/shard_map/cluster_sums/pallas_call | solution.py:201
  127.0 1.4 collective-permute-start.11
  130.5 2.1 slice_bitcast_fusion.8
  132.6 7.9 %collective-permute-done.11.refs_1_ = bf16[448,512]{1,0:T(8,128)(2,1)S(1)} collective-permute-done((bf16[448,512]{1,0:T(8,128)(2,1)}, bf16[448,512]{1,0:T(8,128)(2,1)S(1)}, u32[]{:S(2)}, u32[]{:S(2)}) %collective-permute-start.11) | collective-permute-done | bytes 458784 | tf_op jit(solution)/shard_map/ppermute | solution.py:21
  140.6 10.2 %collective-permute-done.12.refs_2_ = bf16[448,512]{1,0:T(8,128)(2,1)S(1)} collective-permute-done((bf16[448,512]{1,0:T(8,128)(2,1)}, bf16[448,512]{1,0:T(8,128)(2,1)S(1)}, u32[]{:S(2)}, u32[]{:S(2)}) %collective-permute-start.12) | collective-permute-done | bytes 458784 | tf_op jit(solution)/shard_map/ppermute | solution.py:21
  151.7 2.8 own_sums.2.own
  155.1 1.4 collective-permute-start.16
  156.5 1.5 collective-permute-start.17
  158.0 14.0 %collective-permute-done.18 = bf16[512,1920]{1,0:T(8,128)(2,1)S(1)} collective-permute-done((bf16[512,1920]{1,0:T(8,128)(2,1)S(1)}, bf16[512,1920]{1,0:T(8,128)(2,1)S(1)}, u32[]{:S(2)}, u32[]{:S(2)}) %collective-permute-start.18) | collective-permute-done | bytes 1966112 | tf_op jit(solution)/shard_map/ppermute | solution.py:21
  172.0 2.2 pad_maximum_fusion.tokens
  174.1 1.2 copy-done.4
  175.4 11.7 %crossed.2 = (f32[512,512]{1,0:T(8,128)}, f32[2,512,512]{2,1,0:T(8,128)}) custom-call(s32[25]{0:T(128)} %pad_add_fusion.meta, bf16[4,448,512]{2,1,0:T(8,128)(2,1)} %own_sums.2.own, bf16[4,448,512]{2,1,0:T(8,128)(2,1)} %copy-done.4, bf16[7168,512]{1,0:T(8,128)(2,1)} %bitcast.156, bf16[7168,512]{1,0:T(8,128)(2,1)} %bitcast.157, bf16[7168,512]{1,0:T(8,128)(2,1)} %bitcast.162, ...), custom_call_target="tpu_custom_call" | custom-call | flops 5637144576 | bytes 22020096 | tf_op jit(solution)/shard_map/crossed/pallas_call | solution.py:249
  188.1 2.8 own_sums.3.own
  191.0 13.5 %project.1 = (bf16[1024,512]{1,0:T(8,128)(2,1)}, bf16[1024,512]{1,0:T(8,128)(2,1)}, bf16[1024,512]{1,0:T(8,128)(2,1)}, bf16[1024,512]{1,0:T(8,128)(2,1)}) custom-call(bf16[1024,1920]{1,0:T(8,128)(2,1)} %pad_maximum_fusion.tokens, bf16[4,896,512]{2,1,0:T(8,128)(2,1)} %get-tuple-element.99.refs_0_, bf16[4,896,512]{2,1,0:T(8,128)(2,1)} %collective-permute-done.10.refs_1_), custom_call_target="tpu_custom_call" | custom-call | flops 7516192768 | bytes 8388608 | tf_op jit(solution)/shard_map/project/pallas_call | solution.py:287
  205.1 1.7 collective-permute-start.21
  208.0 12.9 %crossed.3 = (f32[512,512]{1,0:T(8,128)}, f32[2,512,512]{2,1,0:T(8,128)}) custom-call(s32[25]{0:T(128)} %pad_add_fusion.meta, bf16[4,448,512]{2,1,0:T(8,128)(2,1)} %own_sums.3.own, bf16[4,448,512]{2,1,0:T(8,128)(2,1)} %copy-done.3, bf16[7168,512]{1,0:T(8,128)(2,1)} %bitcast.158, bf16[7168,512]{1,0:T(8,128)(2,1)} %bitcast.159, bf16[7168,512]{1,0:T(8,128)(2,1)} %bitcast.164, ...), custom_call_target="tpu_custom_call" | custom-call | flops 5637144576 | bytes 22020096 | tf_op jit(solution)/shard_map/crossed/pallas_call | solution.py:249
  220.9 33.9 %factored.1.inverse = f32[512,512]{1,0:T(8,128)} custom-call(f32[512,512]{1,0:T(8,128)} %get-tuple-element.109.gram_ref), custom_call_target="tpu_custom_call" | custom-call | flops 40000000000 | bytes 2097152 | tf_op jit(solution)/shard_map/factored/pallas_call | solution.py:384
  254.8 5.5 %coefficients.1.mine = bf16[2,512,512]{2,1,0:T(8,128)(2,1)} custom-call(f32[512,512]{1,0:T(8,128)} %factored.1.inverse, f32[2,512,512]{2,1,0:T(8,128)} %get-tuple-element.115.raw), custom_call_target="tpu_custom_call" | custom-call | flops 1610612736 | bytes 3145728 | tf_op jit(solution)/shard_map/coefficients/pallas_call | solution.py:403
  260.4 1.7 slice.161.tokens
  264.3 9.7 %hidden_rows.1 = (bf16[4,128,1024]{2,1,0:T(8,128)(2,1)}, bf16[4,128,1024]{2,1,0:T(8,128)(2,1)}, bf16[4,128,1024]{2,1,0:T(8,128)(2,1)}, bf16[4,128,1024]{2,1,0:T(8,128)(2,1)}, bf16[4,256,1024]{2,1,0:T(8,128)(2,1)}) custom-call(s32[25]{0:T(128)} %pad_add_fusion.meta, f32[512,512]{1,0:T(8,128)} %factored.1.inverse, bf16[2,512,512]{2,1,0:T(8,128)(2,1)} %coefficients.1.mine, ...), custom_call_target="tpu_custom_call" | custom-call | flops 3758096384 | bytes 8388608 | tf_op jit(solution)/shard_map/hidden_rows/pallas_call | solution.py:449
  274.0 4.1 convolution_convert_fusion
  278.8 4.4 %convolution_convert_fusion.1 = bf16[512,1408]{1,0:T(8,128)(2,1)S(1)} fusion(bf16[512,1024]{1,0:T(8,128)(2,1)} %bitcast.196, bf16[1024,7168]{1,0:T(8,128)(2,1)} %bitcast.181), kind=kOutput, calls=%fused_computation.8 | convolution fusion | flops 1477115904 | bytes 5373952 | tf_op jit(solution)/shard_map/dot_general | solution.py:52
  283.2 1.4 collective-permute-start.36
  284.8 1.8 convolution_convert_fusion.4
  287.0 1.8 convolution_convert_fusion.3
  289.9 1.8 convolution_convert_fusion.2
  292.8 19.7 %collective-permute-done.40 = bf16[512,1408]{1,0:T(8,128)(2,1)S(1)} collective-permute-done((bf16[512,1408]{1,0:T(8,128)(2,1)S(1)}, bf16[512,1408]{1,0:T(8,128)(2,1)S(1)}, u32[]{:S(2)}, u32[]{:S(2)}) %collective-permute-start.40) | collective-permute-done | bytes 1441824 | tf_op jit(solution)/shard_map/ppermute | solution.py:21
  312.5 1.8 fusion.4
  315.1 2.6 collective-permute-done.36
  317.7 1.8 fusion.3
  320.7 1.9 collective-permute-done.24
  322.6 1.8 fusion
  324.6 1.7 collective-permute-start.33
  326.3 22.4 %collective-permute-done.25 = bf16[512,1408]{1,0:T(8,128)(2,1)S(1)} collective-permute-done((bf16[512,1408]{1,0:T(8,128)(2,1)S(1)}, bf16[512,1408]{1,0:T(8,128)(2,1)S(1)}, u32[]{:S(2)}, u32[]{:S(2)}) %collective-permute-start.25) | collective-permute-done | bytes 1441824 | tf_op jit(solution)/shard_map/ppermute | solution.py:21
  348.6 2.0 fusion.2
  350.8 1.4 collective-permute-start.30
  352.2 1.8 fusion.1
  355.0 9.1 %collective-permute-done.41 = bf16[2,2,64,1408]{3,2,1,0:T(8,128)(2,1)S(1)} collective-permute-done((bf16[2,2,64,1408]{3,2,1,0:T(8,128)(2,1)S(1)}, bf16[2,2,64,1408]{3,2,1,0:T(8,128)(2,1)S(1)}, u32[]{:S(2)}, u32[]{:S(2)}) %collective-permute-start.41) | collective-permute-done | bytes 720928 | tf_op jit(solution)/shard_map/ppermute | solution.py:21
  365.1 1.5 collective-permute-start.38
  366.7 12.0 %collective-permute-done.30 = bf16[2,2,64,1408]{3,2,1,0:T(8,128)(2,1)S(1)} collective-permute-done((bf16[2,2,64,1408]{3,2,1,0:T(8,128)(2,1)S(1)}, bf16[2,2,64,1408]{3,2,1,0:T(8,128)(2,1)S(1)}, u32[]{:S(2)}, u32[]{:S(2)}) %collective-permute-start.30) | collective-permute-done | bytes 720928 | tf_op jit(solution)/shard_map/ppermute | solution.py:21
  379.5 1.8 collective-permute-start.28
  382.8 1.6 collective-permute-start.43
  384.6 1.4 collective-permute-start.39
  386.0 12.1 %collective-permute-done.31 = bf16[2,64,1408]{2,1,0:T(8,128)(2,1)S(1)} collective-permute-done((bf16[2,64,1408]{2,1,0:T(8,128)(2,1)S(1)}, bf16[2,64,1408]{2,1,0:T(8,128)(2,1)S(1)}, u32[]{:S(2)}, u32[]{:S(2)}) %collective-permute-start.31) | collective-permute-done | bytes 360480 | tf_op jit(solution)/shard_map/ppermute | solution.py:21
  398.3 6.2 %collective-permute-done.28 = bf16[2,64,1408]{2,1,0:T(8,128)(2,1)S(1)} collective-permute-done((bf16[2,64,1408]{2,1,0:T(8,128)(2,1)S(1)}, bf16[2,64,1408]{2,1,0:T(8,128)(2,1)S(1)}, u32[]{:S(2)}, u32[]{:S(2)}) %collective-permute-start.28) | collective-permute-done | bytes 360480 | tf_op jit(solution)/shard_map/ppermute | solution.py:21
  405.8 13.9 %collective-permute-done.29 = bf16[64,1408]{1,0:T(8,128)(2,1)S(1)} collective-permute-done((bf16[64,1408]{1,0:T(8,128)(2,1)S(1)}, bf16[64,1408]{1,0:T(8,128)(2,1)S(1)}, u32[]{:S(2)}, u32[]{:S(2)}) %collective-permute-start.29) | collective-permute-done | bytes 180256 | tf_op jit(solution)/shard_map/ppermute | solution.py:21
  (148 shorter events, 28.2 us)
Async XLA Ops:
  6.5 267.4 %all-gather.3.cloned.1.call-start = ((), (), s32[]{:S(2)}) async-start(), calls=%async_computation | async-start | bytes 22020096 | tf_op jit(solution)/shard_map/all_gather | solution.py:545
  7.8 9.4 %copy-start.15 = (f32[64,8]{0,1:T(8,128)S(1)}, f32[64,8]{0,1:T(8,128)}, u32[]{:S(2)}) copy-start(f32[64,8]{0,1:T(8,128)} %param.15) | copy-start | bytes 6148
  7.8 10.1 %copy-start.16 = (s32[64,8]{0,1:T(8,128)S(1)}, s32[64,8]{0,1:T(8,128)}, u32[]{:S(2)}) copy-start(s32[64,8]{0,1:T(8,128)} %param.14) | copy-start | bytes 6148
  16.8 23.4 %collective-permute-start.4 = (bf16[4,896,512]{2,1,0:T(8,128)(2,1)}, bf16[4,896,512]{2,1,0:T(8,128)(2,1)}, u32[]{:S(2)}, u32[]{:S(2)}) collective-permute-start(bf16[4,896,512]{2,1,0:T(8,128)(2,1)} %sketch_half.3), channel_id=1, source_target_pairs={{0,1},{1,0},{2,3},{3,2},{4,5},{5,4},{6,7},{7,6},{8,9},{9,8},{10,11... | collective-permute-start | bytes 11010056 | tf_op jit(solution)/shard_map/ppermute | solution.py:26
  21.3 12.9 %collective-permute-start = (bf16[64,1920]{1,0:T(8,128)(2,1)}, bf16[64,1920]{1,0:T(8,128)(2,1)S(1)}, u32[]{:S(2)}, u32[]{:S(2)}) collective-permute-start(bf16[64,1920]{1,0:T(8,128)(2,1)} %get-tuple-element.67), channel_id=1, source_target_pairs={{0,2},{2,0},{4,6},{6,4},{8,10},{10,8},{12,14},{14,12},{16,18},{18,... | collective-permute-start | bytes 737288 | tf_op jit(solution)/shard_map/ppermute | solution.py:21
  23.8 13.6 %collective-permute-start.1 = (bf16[64,1920]{1,0:T(8,128)(2,1)}, bf16[64,1920]{1,0:T(8,128)(2,1)S(1)}, u32[]{:S(2)}, u32[]{:S(2)}) collective-permute-start(bf16[64,1920]{1,0:T(8,128)(2,1)} %get-tuple-element.68), channel_id=1, source_target_pairs={{0,4},{2,6},{4,0},{6,2},{8,12},{10,14},{12,8},{14,10},{16,20},{18,... | collective-permute-start | bytes 737288 | tf_op jit(solution)/shard_map/ppermute | solution.py:21
  25.4 12.0 %copy-start.13 = (bf16[64,1920]{1,0:T(8,128)(2,1)S(1)}, bf16[64,1920]{1,0:T(8,128)(2,1)}, u32[]{:S(2)}) copy-start(bf16[64,1920]{1,0:T(8,128)(2,1)} %get-tuple-element.66) | copy-start | bytes 737284
  25.4 12.0 %collective-permute-start.2 = (bf16[64,1920]{1,0:T(8,128)(2,1)}, bf16[64,1920]{1,0:T(8,128)(2,1)S(1)}, u32[]{:S(2)}, u32[]{:S(2)}) collective-permute-start(bf16[64,1920]{1,0:T(8,128)(2,1)} %get-tuple-element.69), channel_id=1, source_target_pairs={{0,6},{2,4},{4,2},{6,0},{8,14},{10,12},{12,10},{14,8},{16,22},{18,... | collective-permute-start | bytes 737288 | tf_op jit(solution)/shard_map/ppermute | solution.py:21
  37.5 45.3 %collective-permute-start.3 = (bf16[256,1920]{1,0:T(8,128)(2,1)S(1)}, bf16[256,1920]{1,0:T(8,128)(2,1)}, u32[]{:S(2)}, u32[]{:S(2)}) collective-permute-start(bf16[256,1920]{1,0:T(8,128)(2,1)S(1)} %pad_maximum_fusion.2), channel_id=1, source_target_pairs={{0,16},{2,18},{4,20},{6,22},{8,24},{10,26},{12,28},{14,30},{16,0},... | collective-permute-start | bytes 2949128 | tf_op jit(solution)/shard_map/ppermute | solution.py:21
  45.9 38.3 %collective-permute-start.5 = (bf16[896,512]{1,0:T(8,128)(2,1)}, bf16[896,512]{1,0:T(8,128)(2,1)S(1)}, u32[]{:S(2)}, u32[]{:S(2)}) collective-permute-start(bf16[896,512]{1,0:T(8,128)(2,1)} %get-tuple-element.129), channel_id=1, source_target_pairs={{0,2},{2,0},{4,6},{6,4},{8,10},{10,8},{12,14},{14,12},{16,18},{18,... | collective-permute-start | bytes 2752520 | tf_op jit(solution)/shard_map/ppermute | solution.py:21
  47.1 41.3 %collective-permute-start.6 = (bf16[896,512]{1,0:T(8,128)(2,1)}, bf16[896,512]{1,0:T(8,128)(2,1)S(1)}, u32[]{:S(2)}, u32[]{:S(2)}) collective-permute-start(bf16[896,512]{1,0:T(8,128)(2,1)} %get-tuple-element.128), channel_id=1, source_target_pairs={{0,4},{2,6},{4,0},{6,2},{8,12},{10,14},{12,8},{14,10},{16,20},{18,... | collective-permute-start | bytes 2752520 | tf_op jit(solution)/shard_map/ppermute | solution.py:21
  47.9 40.5 %collective-permute-start.7 = (bf16[896,512]{1,0:T(8,128)(2,1)}, bf16[896,512]{1,0:T(8,128)(2,1)}, u32[]{:S(2)}, u32[]{:S(2)}) collective-permute-start(bf16[896,512]{1,0:T(8,128)(2,1)} %get-tuple-element.127), channel_id=1, source_target_pairs={{0,6},{2,4},{4,2},{6,0},{8,14},{10,12},{12,10},{14,8},{16,22},{18,... | collective-permute-start | bytes 2752520 | tf_op jit(solution)/shard_map/ppermute | solution.py:21
  84.1 4.3 copy-start
  93.7 20.7 %collective-permute-start.8 = (bf16[896,512]{1,0:T(8,128)(2,1)}, bf16[896,512]{1,0:T(8,128)(2,1)S(1)}, u32[]{:S(2)}, u32[]{:S(2)}) collective-permute-start(bf16[896,512]{1,0:T(8,128)(2,1)} %get-tuple-element.76), channel_id=1, source_target_pairs={{0,8},{2,10},{4,12},{6,14},{8,16},{10,18},{12,20},{14,22},{16,24},... | collective-permute-start | bytes 2752520 | tf_op jit(solution)/shard_map/ppermute | solution.py:32
  97.2 21.2 %collective-permute-start.9 = (bf16[896,512]{1,0:T(8,128)(2,1)}, bf16[896,512]{1,0:T(8,128)(2,1)S(1)}, u32[]{:S(2)}, u32[]{:S(2)}) collective-permute-start(bf16[896,512]{1,0:T(8,128)(2,1)} %get-tuple-element.77), channel_id=1, source_target_pairs={{8,0},{10,2},{12,4},{14,6},{16,8},{18,10},{20,12},{22,14},{24,16},... | collective-permute-start | bytes 2752520 | tf_op jit(solution)/shard_map/ppermute | solution.py:32
  114.3 4.1 copy-start.5
  126.7 24.0 %collective-permute-start.10 = (bf16[4,896,512]{2,1,0:T(8,128)(2,1)}, bf16[4,896,512]{2,1,0:T(8,128)(2,1)}, u32[]{:S(2)}, u32[]{:S(2)}) collective-permute-start(bf16[4,896,512]{2,1,0:T(8,128)(2,1)} %get-tuple-element.99.refs_0_), channel_id=1, source_target_pairs={{0,1},{1,0},{2,3},{3,2},{4,5},{5,4},{6,7},{7,6},{8,9},{9,8},{10,11... | collective-permute-start | bytes 11010056 | tf_op jit(solution)/shard_map/ppermute | solution.py:26
  126.7 45.2 %collective-permute-start.18 = (bf16[512,1920]{1,0:T(8,128)(2,1)S(1)}, bf16[512,1920]{1,0:T(8,128)(2,1)S(1)}, u32[]{:S(2)}, u32[]{:S(2)}) collective-permute-start(bf16[512,1920]{1,0:T(8,128)(2,1)S(1)} %pad_maximum_fusion.1), channel_id=1, source_target_pairs={{0,8},{2,10},{4,12},{6,14},{8,0},{10,2},{12,4},{14,6},{16,24},{18,... | collective-permute-start | bytes 5898248 | tf_op jit(solution)/shard_map/ppermute | solution.py:21
  127.0 13.6 %collective-permute-start.11 = (bf16[448,512]{1,0:T(8,128)(2,1)}, bf16[448,512]{1,0:T(8,128)(2,1)S(1)}, u32[]{:S(2)}, u32[]{:S(2)}) collective-permute-start(bf16[448,512]{1,0:T(8,128)(2,1)} %get-tuple-element.79), channel_id=1, source_target_pairs={{0,2},{2,0},{4,6},{6,4},{8,10},{10,8},{12,14},{14,12},{16,18},{18,... | collective-permute-start | bytes 1376264 | tf_op jit(solution)/shard_map/ppermute | solution.py:21
  128.4 22.4 %collective-permute-start.12 = (bf16[448,512]{1,0:T(8,128)(2,1)}, bf16[448,512]{1,0:T(8,128)(2,1)S(1)}, u32[]{:S(2)}, u32[]{:S(2)}) collective-permute-start(bf16[448,512]{1,0:T(8,128)(2,1)} %get-tuple-element.80), channel_id=1, source_target_pairs={{0,4},{2,6},{4,0},{6,2},{8,12},{10,14},{12,8},{14,10},{16,20},{18,... | collective-permute-start | bytes 1376264 | tf_op jit(solution)/shard_map/ppermute | solution.py:21
  129.4 21.4 %collective-permute-start.13 = (bf16[448,512]{1,0:T(8,128)(2,1)}, bf16[448,512]{1,0:T(8,128)(2,1)S(1)}, u32[]{:S(2)}, u32[]{:S(2)}) collective-permute-start(bf16[448,512]{1,0:T(8,128)(2,1)} %get-tuple-element.81), channel_id=1, source_target_pairs={{0,6},{2,4},{4,2},{6,0},{8,14},{10,12},{12,10},{14,8},{16,22},{18,... | collective-permute-start | bytes 1376264 | tf_op jit(solution)/shard_map/ppermute | solution.py:21
  132.6 22.5 %copy-start.23 = (bf16[448,512]{1,0:T(8,128)(2,1)S(1)}, bf16[448,512]{1,0:T(8,128)(2,1)}, u32[]{:S(2)}) copy-start(bf16[448,512]{1,0:T(8,128)(2,1)} %get-tuple-element.89) | copy-start | bytes 1376260
  132.6 23.9 %copy-start.22 = (bf16[448,512]{1,0:T(8,128)(2,1)S(1)}, bf16[448,512]{1,0:T(8,128)(2,1)}, u32[]{:S(2)}) copy-start(bf16[448,512]{1,0:T(8,128)(2,1)} %get-tuple-element.90) | copy-start | bytes 1376260
  140.6 10.2 %copy-start.10 = (bf16[448,512]{1,0:T(8,128)(2,1)}, bf16[448,512]{1,0:T(8,128)(2,1)S(1)}, u32[]{:S(2)}) copy-start(bf16[448,512]{1,0:T(8,128)(2,1)S(1)} %collective-permute-done.11.refs_1_) | copy-start | bytes 1376260
  154.5 19.6 %collective-permute-start.14 = (bf16[4,448,512]{2,1,0:T(8,128)(2,1)}, bf16[4,448,512]{2,1,0:T(8,128)(2,1)S(1)}, u32[]{:S(2)}, u32[]{:S(2)}) collective-permute-start(bf16[4,448,512]{2,1,0:T(8,128)(2,1)} %own_sums.2.own), channel_id=1, source_target_pairs={{0,1},{1,0},{2,3},{3,2},{4,5},{5,4},{6,7},{7,6},{8,9},{9,8},{10,11... | collective-permute-start | bytes 5505032 | tf_op jit(solution)/shard_map/ppermute | solution.py:26
  154.5 32.6 %collective-permute-start.15 = (bf16[448,512]{1,0:T(8,128)(2,1)}, bf16[448,512]{1,0:T(8,128)(2,1)S(1)}, u32[]{:S(2)}, u32[]{:S(2)}) collective-permute-start(bf16[448,512]{1,0:T(8,128)(2,1)} %get-tuple-element.88), channel_id=1, source_target_pairs={{0,2},{2,0},{4,6},{6,4},{8,10},{10,8},{12,14},{14,12},{16,18},{18,... | collective-permute-start | bytes 1376264 | tf_op jit(solution)/shard_map/ppermute | solution.py:21
  155.1 32.0 %collective-permute-start.16 = (bf16[448,512]{1,0:T(8,128)(2,1)S(1)}, bf16[448,512]{1,0:T(8,128)(2,1)S(1)}, u32[]{:S(2)}, u32[]{:S(2)}) collective-permute-start(bf16[448,512]{1,0:T(8,128)(2,1)S(1)} %copy-done.23), channel_id=1, source_target_pairs={{0,4},{2,6},{4,0},{6,2},{8,12},{10,14},{12,8},{14,10},{16,20},{18,... | collective-permute-start | bytes 1376264 | tf_op jit(solution)/shard_map/ppermute | solution.py:21
  156.5 30.6 %collective-permute-start.17 = (bf16[448,512]{1,0:T(8,128)(2,1)S(1)}, bf16[448,512]{1,0:T(8,128)(2,1)S(1)}, u32[]{:S(2)}, u32[]{:S(2)}) collective-permute-start(bf16[448,512]{1,0:T(8,128)(2,1)S(1)} %copy-done.22), channel_id=1, source_target_pairs={{0,6},{2,4},{4,2},{6,0},{8,14},{10,12},{12,10},{14,8},{16,22},{18,... | collective-permute-start | bytes 1376264 | tf_op jit(solution)/shard_map/ppermute | solution.py:21
  174.1 1.2 copy-start.4
  191.0 13.5 %collective-permute-start.19 = (bf16[4,448,512]{2,1,0:T(8,128)(2,1)}, bf16[4,448,512]{2,1,0:T(8,128)(2,1)S(1)}, u32[]{:S(2)}, u32[]{:S(2)}) collective-permute-start(bf16[4,448,512]{2,1,0:T(8,128)(2,1)} %own_sums.3.own), channel_id=1, source_target_pairs={{0,1},{1,0},{2,3},{3,2},{4,5},{5,4},{6,7},{7,6},{8,9},{9,8},{10,11... | collective-permute-start | bytes 5505032 | tf_op jit(solution)/shard_map/ppermute | solution.py:26
  204.4 3.6 copy-start.3
  204.4 50.3 %collective-permute-start.20 = (bf16[1024,512]{1,0:T(8,128)(2,1)}, bf16[1024,512]{1,0:T(8,128)(2,1)S(1)}, u32[]{:S(2)}, u32[]{:S(2)}) collective-permute-start(bf16[1024,512]{1,0:T(8,128)(2,1)} %get-tuple-element.111), channel_id=1, source_target_pairs={{0,2},{2,0},{4,6},{6,4},{8,10},{10,8},{12,14},{14,12},{16,18},{18,... | collective-permute-start | bytes 3145736 | tf_op jit(solution)/shard_map/ppermute | solution.py:21
  205.1 49.7 %collective-permute-start.21 = (bf16[1024,512]{1,0:T(8,128)(2,1)}, bf16[1024,512]{1,0:T(8,128)(2,1)S(1)}, u32[]{:S(2)}, u32[]{:S(2)}) collective-permute-start(bf16[1024,512]{1,0:T(8,128)(2,1)} %get-tuple-element.112), channel_id=1, source_target_pairs={{0,4},{2,6},{4,0},{6,2},{8,12},{10,14},{12,8},{14,10},{16,20},{18,... | collective-permute-start | bytes 3145736 | tf_op jit(solution)/shard_map/ppermute | solution.py:21
  206.9 47.9 %collective-permute-start.22 = (bf16[1024,512]{1,0:T(8,128)(2,1)}, bf16[1024,512]{1,0:T(8,128)(2,1)S(1)}, u32[]{:S(2)}, u32[]{:S(2)}) collective-permute-start(bf16[1024,512]{1,0:T(8,128)(2,1)} %get-tuple-element.113), channel_id=1, source_target_pairs={{0,6},{2,4},{4,2},{6,0},{8,14},{10,12},{12,10},{14,8},{16,22},{18,... | collective-permute-start | bytes 3145736 | tf_op jit(solution)/shard_map/ppermute | solution.py:21
  254.8 5.5 %copy-start.18 = (bf16[1024,512]{1,0:T(8,128)(2,1)}, bf16[1024,512]{1,0:T(8,128)(2,1)S(1)}, u32[]{:S(2)}) copy-start(bf16[1024,512]{1,0:T(8,128)(2,1)S(1)} %collective-permute-done.20.refs_1_) | copy-start | bytes 3145732
  254.8 5.5 %copy-start.19 = (bf16[1024,512]{1,0:T(8,128)(2,1)}, bf16[1024,512]{1,0:T(8,128)(2,1)S(1)}, u32[]{:S(2)}) copy-start(bf16[1024,512]{1,0:T(8,128)(2,1)S(1)} %collective-permute-done.21.refs_2_) | copy-start | bytes 3145732
  254.8 5.5 %copy-start.20 = (bf16[1024,512]{1,0:T(8,128)(2,1)}, bf16[1024,512]{1,0:T(8,128)(2,1)S(1)}, u32[]{:S(2)}) copy-start(bf16[1024,512]{1,0:T(8,128)(2,1)S(1)} %collective-permute-done.22.refs_3_) | copy-start | bytes 3145732
  260.3 2.9 collective-permute-start.23
  273.9 10.9 %copy-start.17 = (bf16[1,1024,7168]{2,1,0:T(8,128)(2,1)S(1)}, bf16[1,1024,7168]{2,1,0:T(8,128)(2,1)}, u32[]{:S(2)}) copy-start(bf16[1,1024,7168]{2,1,0:T(8,128)(2,1)} %all-gather.3.cloned.1.call-done) | copy-start | bytes 44040196
  278.0 34.5 %collective-permute-start.40 = (bf16[512,1408]{1,0:T(8,128)(2,1)S(1)}, bf16[512,1408]{1,0:T(8,128)(2,1)S(1)}, u32[]{:S(2)}, u32[]{:S(2)}) collective-permute-start(bf16[512,1408]{1,0:T(8,128)(2,1)S(1)} %convolution_convert_fusion), channel_id=1, source_target_pairs={{0,4},{2,6},{4,0},{6,2},{8,12},{10,14},{12,8},{14,10},{16,20},{18,... | collective-permute-start | bytes 4325384 | tf_op jit(solution)/shard_map/ppermute | solution.py:21
  278.8 5.8 %copy-start.2 = (bf16[4,256,1024]{2,1,0:T(8,128)(2,1)S(1)}, bf16[4,256,1024]{2,1,0:T(8,128)(2,1)}, u32[]{:S(2)}) copy-start(bf16[4,256,1024]{2,1,0:T(8,128)(2,1)} %get-tuple-element.121) | copy-start | bytes 6291460
  283.2 34.5 %collective-permute-start.36 = (bf16[512,1408]{1,0:T(8,128)(2,1)S(1)}, bf16[512,1408]{1,0:T(8,128)(2,1)S(1)}, u32[]{:S(2)}, u32[]{:S(2)}) collective-permute-start(bf16[512,1408]{1,0:T(8,128)(2,1)S(1)} %convolution_convert_fusion.1), channel_id=1, source_target_pairs={{0,2},{2,0},{4,6},{6,4},{8,10},{10,8},{12,14},{14,12},{16,18},{18,... | collective-permute-start | bytes 4325384 | tf_op jit(solution)/shard_map/ppermute | solution.py:21
  284.8 2.2 copy-start.27
  286.7 3.2 copy-start.26
  286.7 35.9 %collective-permute-start.24 = (bf16[512,1536]{1,0:T(8,128)(2,1)S(1)}, bf16[512,1536]{1,0:T(8,128)(2,1)S(1)}, u32[]{:S(2)}, u32[]{:S(2)}) collective-permute-start(bf16[512,1536]{1,0:T(8,128)(2,1)S(1)} %convolution_convert_fusion.4), channel_id=1, source_target_pairs={{0,8},{2,10},{4,12},{6,14},{8,0},{10,2},{12,4},{14,6},{16,24},{18,... | collective-permute-start | bytes 4718600 | tf_op jit(solution)/shard_map/ppermute | solution.py:21
  288.9 23.7 %copy-start.25 = (bf16[4,128,1024]{2,1,0:T(8,128)(2,1)S(1)}, bf16[4,128,1024]{2,1,0:T(8,128)(2,1)}, u32[]{:S(2)}) copy-start(bf16[4,128,1024]{2,1,0:T(8,128)(2,1)} %get-tuple-element.125) | copy-start | bytes 3145732
  288.9 59.8 %collective-permute-start.25 = (bf16[512,1408]{1,0:T(8,128)(2,1)S(1)}, bf16[512,1408]{1,0:T(8,128)(2,1)S(1)}, u32[]{:S(2)}, u32[]{:S(2)}) collective-permute-start(bf16[512,1408]{1,0:T(8,128)(2,1)S(1)} %convolution_convert_fusion.3), channel_id=1, source_target_pairs={{0,2},{2,0},{4,6},{6,4},{8,10},{10,8},{12,14},{14,12},{16,18},{18,... | collective-permute-start | bytes 4325384 | tf_op jit(solution)/shard_map/ppermute | solution.py:21
  291.7 57.0 %collective-permute-start.26 = (bf16[512,1408]{1,0:T(8,128)(2,1)S(1)}, bf16[512,1408]{1,0:T(8,128)(2,1)S(1)}, u32[]{:S(2)}, u32[]{:S(2)}) collective-permute-start(bf16[512,1408]{1,0:T(8,128)(2,1)S(1)} %convolution_convert_fusion.2), channel_id=1, source_target_pairs={{0,4},{2,6},{4,0},{6,2},{8,12},{10,14},{12,8},{14,10},{16,20},{18,... | collective-permute-start | bytes 4325384 | tf_op jit(solution)/shard_map/ppermute | solution.py:21
  312.5 5.2 %copy-start.24 = (bf16[4,128,1024]{2,1,0:T(8,128)(2,1)S(1)}, bf16[4,128,1024]{2,1,0:T(8,128)(2,1)}, u32[]{:S(2)}) copy-start(bf16[4,128,1024]{2,1,0:T(8,128)(2,1)} %get-tuple-element.120) | copy-start | bytes 3145732
  314.4 49.7 %collective-permute-start.41 = (bf16[2,2,64,1408]{3,2,1,0:T(8,128)(2,1)S(1)}, bf16[2,2,64,1408]{3,2,1,0:T(8,128)(2,1)S(1)}, u32[]{:S(2)}, u32[]{:S(2)}) collective-permute-start(bf16[2,2,64,1408]{3,2,1,0:T(8,128)(2,1)S(1)} %slice_bitcast_fusion), channel_id=1, source_target_pairs={{0,2},{2,0},{4,6},{6,4},{8,10},{10,8},{12,14},{14,12},{16,18},{18,... | collective-permute-start | bytes 2162696 | tf_op jit(solution)/shard_map/ppermute | solution.py:21
  319.6 45.3 %collective-permute-start.37 = (bf16[2,2,64,1408]{3,2,1,0:T(8,128)(2,1)S(1)}, bf16[2,2,64,1408]{3,2,1,0:T(8,128)(2,1)S(1)}, u32[]{:S(2)}, u32[]{:S(2)}) collective-permute-start(bf16[2,2,64,1408]{3,2,1,0:T(8,128)(2,1)S(1)} %slice_bitcast_fusion.2), channel_id=1, source_target_pairs={{0,4},{2,6},{4,0},{6,2},{8,12},{10,14},{12,8},{14,10},{16,20},{18,... | collective-permute-start | bytes 2162696 | tf_op jit(solution)/shard_map/ppermute | solution.py:21
  324.6 56.7 %collective-permute-start.33 = (bf16[2,2,64,1536]{3,2,0,1:T(8,128)(2,1)S(1)}, bf16[2,2,64,1536]{3,2,0,1:T(8,128)(2,1)S(1)}, u32[]{:S(2)}, u32[]{:S(2)}) collective-permute-start(bf16[2,2,64,1536]{3,2,0,1:T(8,128)(2,1)S(1)} %copy.15), channel_id=1, source_target_pairs={{0,16},{2,18},{4,20},{6,22},{8,24},{10,26},{12,28},{14,30},{16,0},... | collective-permute-start | bytes 2359304 | tf_op jit(solution)/shard_map/ppermute | solution.py:21
  350.8 28.0 %collective-permute-start.30 = (bf16[2,2,64,1408]{3,2,1,0:T(8,128)(2,1)S(1)}, bf16[2,2,64,1408]{3,2,1,0:T(8,128)(2,1)S(1)}, u32[]{:S(2)}, u32[]{:S(2)}) collective-permute-start(bf16[2,2,64,1408]{3,2,1,0:T(8,128)(2,1)S(1)} %slice_bitcast_fusion.4), channel_id=1, source_target_pairs={{0,2},{2,0},{4,6},{6,4},{8,10},{10,8},{12,14},{14,12},{16,18},{18,... | collective-permute-start | bytes 2162696 | tf_op jit(solution)/shard_map/ppermute | solution.py:21
  354.1 25.2 %collective-permute-start.27 = (bf16[2,2,64,1408]{3,2,1,0:T(8,128)(2,1)S(1)}, bf16[2,2,64,1408]{3,2,1,0:T(8,128)(2,1)S(1)}, u32[]{:S(2)}, u32[]{:S(2)}) collective-permute-start(bf16[2,2,64,1408]{3,2,1,0:T(8,128)(2,1)S(1)} %slice_bitcast_fusion.6), channel_id=1, source_target_pairs={{0,4},{2,6},{4,0},{6,2},{8,12},{10,14},{12,8},{14,10},{16,20},{18,... | collective-permute-start | bytes 2162696 | tf_op jit(solution)/shard_map/ppermute | solution.py:21
  364.3 18.4 %collective-permute-start.42 = (bf16[2,64,1408]{2,1,0:T(8,128)(2,1)S(1)}, bf16[2,64,1408]{2,1,0:T(8,128)(2,1)S(1)}, u32[]{:S(2)}, u32[]{:S(2)}) collective-permute-start(bf16[2,64,1408]{2,1,0:T(8,128)(2,1)S(1)} %slice_bitcast_fusion.12), channel_id=1, source_target_pairs={{0,8},{2,10},{4,12},{6,14},{8,0},{10,2},{12,4},{14,6},{16,24},{18,... | collective-permute-start | bytes 1081352 | tf_op jit(solution)/shard_map/ppermute | solution.py:21
  365.1 19.3 %collective-permute-start.38 = (bf16[2,64,1408]{2,1,0:T(8,128)(2,1)S(1)}, bf16[2,64,1408]{2,1,0:T(8,128)(2,1)S(1)}, u32[]{:S(2)}, u32[]{:S(2)}) collective-permute-start(bf16[2,64,1408]{2,1,0:T(8,128)(2,1)S(1)} %slice_bitcast_fusion.14), channel_id=1, source_target_pairs={{0,8},{2,10},{4,12},{6,14},{8,0},{10,2},{12,4},{14,6},{16,24},{18,... | collective-permute-start | bytes 1081352 | tf_op jit(solution)/shard_map/ppermute | solution.py:21
  378.9 19.1 %collective-permute-start.31 = (bf16[2,64,1408]{2,1,0:T(8,128)(2,1)S(1)}, bf16[2,64,1408]{2,1,0:T(8,128)(2,1)S(1)}, u32[]{:S(2)}, u32[]{:S(2)}) collective-permute-start(bf16[2,64,1408]{2,1,0:T(8,128)(2,1)S(1)} %slice_bitcast_fusion.16), channel_id=1, source_target_pairs={{0,8},{2,10},{4,12},{6,14},{8,0},{10,2},{12,4},{14,6},{16,24},{18,... | collective-permute-start | bytes 1081352 | tf_op jit(solution)/shard_map/ppermute | solution.py:21
  379.5 24.9 %collective-permute-start.28 = (bf16[2,64,1408]{2,1,0:T(8,128)(2,1)S(1)}, bf16[2,64,1408]{2,1,0:T(8,128)(2,1)S(1)}, u32[]{:S(2)}, u32[]{:S(2)}) collective-permute-start(bf16[2,64,1408]{2,1,0:T(8,128)(2,1)S(1)} %slice_bitcast_fusion.18), channel_id=1, source_target_pairs={{0,8},{2,10},{4,12},{6,14},{8,0},{10,2},{12,4},{14,6},{16,24},{18,... | collective-permute-start | bytes 1081352 | tf_op jit(solution)/shard_map/ppermute | solution.py:21
  381.6 23.1 %collective-permute-start.34 = (bf16[2,64,1536]{2,1,0:T(8,128)(2,1)S(1)}, bf16[2,64,1536]{2,1,0:T(8,128)(2,1)S(1)}, u32[]{:S(2)}, u32[]{:S(2)}) collective-permute-start(bf16[2,64,1536]{2,1,0:T(8,128)(2,1)S(1)} %slice_bitcast_fusion.10), channel_id=1, source_target_pairs={{0,2},{2,0},{4,6},{6,4},{8,10},{10,8},{12,14},{14,12},{16,18},{18,... | collective-permute-start | bytes 1179656 | tf_op jit(solution)/shard_map/ppermute | solution.py:21
  382.8 37.2 %collective-permute-start.43 = (bf16[64,1408]{1,0:T(8,128)(2,1)S(1)}, bf16[64,1408]{1,0:T(8,128)(2,1)S(1)}, u32[]{:S(2)}, u32[]{:S(2)}) collective-permute-start(bf16[64,1408]{1,0:T(8,128)(2,1)S(1)} %slice_bitcast_fusion.22), channel_id=1, source_target_pairs={{0,16},{2,18},{4,20},{6,22},{8,24},{10,26},{12,28},{14,30},{16,0},... | collective-permute-start | bytes 540680 | tf_op jit(solution)/shard_map/ppermute | solution.py:21
  384.6 35.4 %collective-permute-start.39 = (bf16[64,1408]{1,0:T(8,128)(2,1)S(1)}, bf16[64,1408]{1,0:T(8,128)(2,1)S(1)}, u32[]{:S(2)}, u32[]{:S(2)}) collective-permute-start(bf16[64,1408]{1,0:T(8,128)(2,1)S(1)} %slice_bitcast_fusion.24), channel_id=1, source_target_pairs={{0,16},{2,18},{4,20},{6,22},{8,24},{10,26},{12,28},{14,30},{16,0},... | collective-permute-start | bytes 540680 | tf_op jit(solution)/shard_map/ppermute | solution.py:21
  398.2 21.6 %collective-permute-start.32 = (bf16[64,1408]{1,0:T(8,128)(2,1)S(1)}, bf16[64,1408]{1,0:T(8,128)(2,1)S(1)}, u32[]{:S(2)}, u32[]{:S(2)}) collective-permute-start(bf16[64,1408]{1,0:T(8,128)(2,1)S(1)} %slice_bitcast_fusion.26), channel_id=1, source_target_pairs={{0,16},{2,18},{4,20},{6,22},{8,24},{10,26},{12,28},{14,30},{16,0},... | collective-permute-start | bytes 540680 | tf_op jit(solution)/shard_map/ppermute | solution.py:21
  404.5 15.2 %collective-permute-start.29 = (bf16[64,1408]{1,0:T(8,128)(2,1)S(1)}, bf16[64,1408]{1,0:T(8,128)(2,1)S(1)}, u32[]{:S(2)}, u32[]{:S(2)}) collective-permute-start(bf16[64,1408]{1,0:T(8,128)(2,1)S(1)} %slice_bitcast_fusion.28), channel_id=1, source_target_pairs={{0,16},{2,18},{4,20},{6,22},{8,24},{10,26},{12,28},{14,30},{16,0},... | collective-permute-start | bytes 540680 | tf_op jit(solution)/shard_map/ppermute | solution.py:21
  404.8 15.1 %collective-permute-start.35 = (bf16[64,1536]{1,0:T(8,128)(2,1)S(1)}, bf16[64,1536]{1,0:T(8,128)(2,1)S(1)}, u32[]{:S(2)}, u32[]{:S(2)}) collective-permute-start(bf16[64,1536]{1,0:T(8,128)(2,1)S(1)} %slice_bitcast_fusion.20), channel_id=1, source_target_pairs={{0,4},{2,6},{4,0},{6,2},{8,12},{10,14},{12,8},{14,10},{16,20},{18,... | collective-permute-start | bytes 589832 | tf_op jit(solution)/shard_map/ppermute | solution.py:21
  (9 other events, 8.1 us)
Sparse Core Ops, SparseCore 0:
  49.5 25.3 all-gather.2

commit v7 on v6

--- a/solution.py
+++ b/solution.py
@@ -480,7 +480,7 @@
     units = depth // LANES
     if units % 56:
         return [(0, depth, orders[0])]
-    sizes = [(11, 0), (11, 1), (12, 2), (11, 0), (11, 1)]
+    sizes = [(8, 0), (8, 1)] * 3 + [(8, 2)]
     chunks, start = [], 0
     for size, order in sizes:
         width = size * (units // 56) * LANES
@@ -511,9 +511,9 @@
         return (answered(halves[order[0]][0], start, width) + first[i].astype(F32)).astype(BF16)
 
     values = [None] * len(chunks)
-    if len(chunks) > 2:
-        values[2] = added(2)
-        _, first[0], first[1] = lax.optimization_barrier((values[2], first[0], first[1]))
+    if len(chunks) > 4:
+        values[-1] = added(len(chunks) - 1)
+        _, first[:4] = lax.optimization_barrier((values[-1], first[:4]))
     values = [added(i) if value is None else value for i, value in enumerate(values)]
     left = [[bit for bit in range(bits - 1, -1, -1) if bit != order[0]] for _, _, order in chunks]
     for step in range(1, bits):
@@ -556,22 +556,26 @@
     own = [(own_half[k].astype(F32) + sent_half[k].astype(F32)).astype(BF16) for k in range(MOST)]
     got = [own[0]] + [swap_expert(own[k], k) for k in range(1, MOST)]
     masks = group_masks(experts)
+    came = [swap_expert(spread, masks[-1])] if masks else []
+    first = spread.shape[0]
     for mask in masks[:-1]:
         spread = jnp.concatenate([spread, swap_expert(spread, mask)], axis=0)
-    spread, got = lax.optimization_barrier((spread, got))
+    spread, came, got = lax.optimization_barrier((spread, came, got))
     sums, *sends = group_sums(meta, got, chunks)
     other_sums = swap_dp(sums)
     back = []
     for c in range(chunks):
-        first = c * (MOST - 1)
+        base = c * (MOST - 1)
         back.append(
             [sums[0, c * chunk : (c + 1) * chunk]]
-            + [swap_expert(sends[first + k - 1], k) for k in range(1, MOST)]
+            + [swap_expert(sends[base + k - 1], k) for k in range(1, MOST)]
         )
-    if masks:
+    if len(masks) > 1:
         spread, sums = lax.optimization_barrier((spread, sums))
-        spread = jnp.concatenate([spread, swap_expert(spread, masks[-1])], axis=0)
-    other_sums, back[0] = lax.optimization_barrier((other_sums, back[0]))
+        came.append(swap_expert(spread[first:], masks[-1]))
+    other_sums, back[0][1] = lax.optimization_barrier((other_sums, back[0][1]))
+    came, back[0] = lax.optimization_barrier((came, back[0]))
+    spread = jnp.concatenate([spread] + came, axis=0)
     before = ()
     for c in range(chunks):
         if c == chunks - 1:

time: 437 us -> 456 us (1.043)
  starting transfers between devices: 46.4 us -> 56.4 us
  waiting for transfers between devices: 194 us -> 199 us
    ppermute x37 -> x46, starting transfers between devices: 41.1 us -> 50 us  [swap_expert(): lax.ppermute(value, 'expert', [(source, source ^ mask) for source in rang...]
    ppermute x37 -> x46, waiting for transfers between devices: 173 us -> 181 us  [swap_expert(): lax.ppermute(value, 'expert', [(source, source ^ mask) for source in rang...]
    dot_general x10 -> x14, matrix products: 23.2 us -> 22.6 us  [mul(): return lax.dot_general(a, b, (dims, ((), ())), preferred_element_type=F32)]
  transfers between devices with their start and end apart: 45 -> 54, of which waited for: 18 -> 23; matrix products, arithmetic and copies ran while one was open for 8% -> 8% of each run, Pallas kernels for 27% -> 26%
where the time goes in v7:
time: 456 us; the launch traced here: 448 us
  waiting for transfers between devices  199 us (44%)
  Pallas kernels  125 us (27%)
  starting transfers between devices  56.4 us (12%)
  matrix products  22.6 us (5%)
  other arithmetic  17.2 us (4%)
  between operations  14.4 us (3%)
  local copies, waits for them, and re-layouts  13 us (3%)
    ppermute x46, waiting for transfers between devices, swap_expert(): lax.ppermute(value, 'expert', [(source, source ^ mask) for source in rang...  181 us
    ppermute x46, starting transfers between devices, swap_expert(): lax.ppermute(value, 'expert', [(source, source ^ mask) for source in rang...  50 us
    pallas_call x1, Pallas kernels, factored(): pl.pallas_call(functools.partial(factor_kernel, min(LANES, rank)), out_sh...  34 us
    pallas_call x2, Pallas kernels, crossed(): pl.pallas_call(functools.partial(cross_kernel, bool(before)), grid_spec=p...  24.4 us
    dot_general x14, matrix products, mul(): return lax.dot_general(a, b, (dims, ((), ())), preferred_element_type=F32)  22.6 us
    pallas_call x2, Pallas kernels, sketch_half(): pl.pallas_call(sketch_kernel, grid_spec=pltpu.PrefetchScalarGridSpec(num_...  17.8 us
    ppermute x2, waiting for transfers between devices, shift_groups(): return lax.ppermute(value, 'expert', moves)  16.6 us
    pallas_call x1, Pallas kernels, project(): pl.pallas_call(functools.partial(project_kernel, len(sums)), grid=(MOST,)...  13.5 us
  transfers between devices with their start and end apart: 54, of which 23 were waited for; matrix products, arithmetic and copies ran while one was open for 8% of the time, Pallas kernels for 26%

profile of v7, /device:TPU:0, one launch (start us, length us, event | category | flops | bytes accessed | tf_op | source)
XLA Modules:
  0.0 447.7 jit_solution(6017416066276276919)
XLA Ops:
  7.8 9.0 %sketch_half.3 = bf16[4,896,512]{2,1,0:T(8,128)(2,1)} custom-call(s32[25]{0:T(128)} %pad_add_fusion.meta, bf16[7168,512]{1,0:T(8,128)(2,1)} %bitcast.210, bf16[7168,512]{1,0:T(8,128)(2,1)} %bitcast.216, bf16[2,512,512]{2,1,0:T(8,128)(2,1)} %bitcast.222), custom_call_target="tpu_custom_call" | custom-call | flops 3758096384 | bytes 7340032 | tf_op jit(solution)/shard_map/sketch_half/pallas_call | solution.py:121
  18.6 2.8 token_pieces.1
  21.3 2.5 collective-permute-start
  23.8 1.5 collective-permute-start.1
  25.4 8.9 %sketch_half.2 = bf16[4,896,512]{2,1,0:T(8,128)(2,1)} custom-call(s32[25]{0:T(128)} %pad_add_fusion.meta, bf16[7168,512]{1,0:T(8,128)(2,1)} %bitcast.211, bf16[7168,512]{1,0:T(8,128)(2,1)} %bitcast.217, bf16[2,512,512]{2,1,0:T(8,128)(2,1)} %bitcast.223), custom_call_target="tpu_custom_call" | custom-call | flops 3758096384 | bytes 7340032 | tf_op jit(solution)/shard_map/sketch_half/pallas_call | solution.py:121
  34.2 3.2 collective-permute-done.1
  37.5 2.7 collective-permute-start.3
  40.1 1.6 collective-permute-start.4
  41.7 5.8 %fusion.73 = (bf16[896,512]{1,0:T(8,128)(2,1)}, bf16[896,512]{1,0:T(8,128)(2,1)}, bf16[896,512]{1,0:T(8,128)(2,1)}, bf16[896,512]{1,0:T(8,128)(2,1)}) fusion(bf16[4,896,512]{2,1,0:T(8,128)(2,1)} %collective-permute-done.5, bf16[4,896,512]{2,1,0:T(8,128)(2,1)} %sketch_half.2), kind=kLoop, calls=%fused_computation.66 | loop fusion | flops 7340032 | bytes 11010048 | tf_op jit(solution)/shard_map/convert_element_type | solution.py:556
  49.5 1.4 collective-permute-start.8
  51.0 31.9 %collective-permute-done.3 = bf16[256,1920]{1,0:T(8,128)(2,1)} collective-permute-done((bf16[256,1920]{1,0:T(8,128)(2,1)S(1)}, bf16[256,1920]{1,0:T(8,128)(2,1)}, u32[]{:S(2)}, u32[]{:S(2)}) %collective-permute-start.3) | collective-permute-done | bytes 983072 | tf_op jit(solution)/shard_map/ppermute | solution.py:21
  82.9 1.3 pad_maximum_fusion.1
  84.3 5.5 %collective-permute-done.7.refs_2_ = bf16[896,512]{1,0:T(8,128)(2,1)S(1)} collective-permute-done((bf16[896,512]{1,0:T(8,128)(2,1)}, bf16[896,512]{1,0:T(8,128)(2,1)S(1)}, u32[]{:S(2)}, u32[]{:S(2)}) %collective-permute-start.7) | collective-permute-done | bytes 917536 | tf_op jit(solution)/shard_map/ppermute | solution.py:21
  90.7 4.3 end_sums.1
  95.0 1.3 collective-permute-start.10
  96.3 4.6 %collective-permute-start.9 = (bf16[896,512]{1,0:T(8,128)(2,1)}, bf16[896,512]{1,0:T(8,128)(2,1)S(1)}, u32[]{:S(2)}, u32[]{:S(2)}) collective-permute-start(bf16[896,512]{1,0:T(8,128)(2,1)} %get-tuple-element.84), channel_id=1, source_target_pairs={{0,8},{2,10},{4,12},{6,14},{8,16},{10,18},{12,20},{14,22},{16,24},... | collective-permute-start | bytes 2752520 | tf_op jit(solution)/shard_map/ppermute | solution.py:32
  100.9 15.3 %collective-permute-done.10.refs_5_ = bf16[896,512]{1,0:T(8,128)(2,1)S(1)} collective-permute-done((bf16[896,512]{1,0:T(8,128)(2,1)}, bf16[896,512]{1,0:T(8,128)(2,1)S(1)}, u32[]{:S(2)}, u32[]{:S(2)}) %collective-permute-start.10) | collective-permute-done | bytes 917536 | tf_op jit(solution)/shard_map/ppermute | solution.py:32
  116.2 1.3 collective-permute-done.9.refs_4_
  118.4 7.4 %cluster_sums.1 = (bf16[4,896,512]{2,1,0:T(8,128)(2,1)}, bf16[448,512]{1,0:T(8,128)(2,1)}, bf16[448,512]{1,0:T(8,128)(2,1)}, bf16[448,512]{1,0:T(8,128)(2,1)}, b...) custom-call(s32[25]{0:T(128)} %pad_add_fusion.meta, ...), custom_call_target="tpu_custom_call" | custom-call | tf_op jit(solution)/shard_map/cluster_sums/pallas_call | solution.py:201
  125.9 2.4 collective-permute-start.11
  129.0 1.7 collective-permute-start.14
  131.8 2.2 slice_bitcast_fusion.12
  134.0 7.9 %collective-permute-done.13.refs_1_ = bf16[448,512]{1,0:T(8,128)(2,1)S(1)} collective-permute-done((bf16[448,512]{1,0:T(8,128)(2,1)}, bf16[448,512]{1,0:T(8,128)(2,1)S(1)}, u32[]{:S(2)}, u32[]{:S(2)}) %collective-permute-start.13) | collective-permute-done | bytes 458784 | tf_op jit(solution)/shard_map/ppermute | solution.py:21
  141.9 9.5 %collective-permute-done.14.refs_2_ = bf16[448,512]{1,0:T(8,128)(2,1)S(1)} collective-permute-done((bf16[448,512]{1,0:T(8,128)(2,1)}, bf16[448,512]{1,0:T(8,128)(2,1)S(1)}, u32[]{:S(2)}, u32[]{:S(2)}) %collective-permute-start.14) | collective-permute-done | bytes 458784 | tf_op jit(solution)/shard_map/ppermute | solution.py:21
  152.3 2.8 own_sums.2.own
  155.1 1.3 collective-permute-start.17
  157.2 1.4 collective-permute-start.19
  158.6 6.1 %pad_maximum_fusion.tokens = bf16[1024,1920]{1,0:T(8,128)(2,1)} fusion(bf16[256,1920]{1,0:T(8,128)(2,1)S(1)} %collective-permute-done.11, bf16[256,1920]{1,0:T(8,128)(2,1)} %collective-permute-done.4, bf16[512,1920]{1,0:T(8,128)(2,1)S(1)} %pad_maximum_fusion.1), kind=kLoop, calls=%fused_computation | loop fusion | flops 11796480 | bytes 7864320 | tf_op jit(solution)/shard_map/concatenate | solution.py:578
  166.0 11.5 %crossed.2 = (f32[512,512]{1,0:T(8,128)}, f32[2,512,512]{2,1,0:T(8,128)}) custom-call(s32[25]{0:T(128)} %pad_add_fusion.meta, bf16[4,448,512]{2,1,0:T(8,128)(2,1)} %own_sums.2.own, bf16[4,448,512]{2,1,0:T(8,128)(2,1)} %copy-done.4, bf16[7168,512]{1,0:T(8,128)(2,1)} %bitcast.212, bf16[7168,512]{1,0:T(8,128)(2,1)} %bitcast.213, bf16[7168,512]{1,0:T(8,128)(2,1)} %bitcast.218, ...), custom_call_target="tpu_custom_call" | custom-call | flops 5637144576 | bytes 22020096 | tf_op jit(solution)/shard_map/crossed/pallas_call | solution.py:249
  177.5 1.6 collective-permute-done.19.refs_3_
  179.9 2.8 own_sums.3.own
  182.7 13.5 %project.1 = (bf16[1024,512]{1,0:T(8,128)(2,1)}, bf16[1024,512]{1,0:T(8,128)(2,1)}, bf16[1024,512]{1,0:T(8,128)(2,1)}, bf16[1024,512]{1,0:T(8,128)(2,1)}) custom-call(bf16[1024,1920]{1,0:T(8,128)(2,1)} %pad_maximum_fusion.tokens, bf16[4,896,512]{2,1,0:T(8,128)(2,1)} %get-tuple-element.109.refs_0_, bf16[4,896,512]{2,1,0:T(8,128)(2,1)} %copy-done.18), custom_call_target="tpu_custom_call" | custom-call | flops 7516192768 | bytes 8388608 | tf_op jit(solution)/shard_map/project/pallas_call | solution.py:287
  197.0 1.7 collective-permute-start.22
  199.7 12.9 %crossed.3 = (f32[512,512]{1,0:T(8,128)}, f32[2,512,512]{2,1,0:T(8,128)}) custom-call(s32[25]{0:T(128)} %pad_add_fusion.meta, bf16[4,448,512]{2,1,0:T(8,128)(2,1)} %own_sums.3.own, bf16[4,448,512]{2,1,0:T(8,128)(2,1)} %copy-done.3, bf16[7168,512]{1,0:T(8,128)(2,1)} %bitcast.214, bf16[7168,512]{1,0:T(8,128)(2,1)} %bitcast.215, bf16[7168,512]{1,0:T(8,128)(2,1)} %bitcast.220, ...), custom_call_target="tpu_custom_call" | custom-call | flops 5637144576 | bytes 22020096 | tf_op jit(solution)/shard_map/crossed/pallas_call | solution.py:249
  212.7 34.0 %factored.1.inverse = f32[512,512]{1,0:T(8,128)} custom-call(f32[512,512]{1,0:T(8,128)} %get-tuple-element.119.gram_ref), custom_call_target="tpu_custom_call" | custom-call | flops 40000000000 | bytes 2097152 | tf_op jit(solution)/shard_map/factored/pallas_call | solution.py:384
  246.7 5.5 %coefficients.1.mine = bf16[2,512,512]{2,1,0:T(8,128)(2,1)} custom-call(f32[512,512]{1,0:T(8,128)} %factored.1.inverse, f32[2,512,512]{2,1,0:T(8,128)} %get-tuple-element.125.raw), custom_call_target="tpu_custom_call" | custom-call | flops 1610612736 | bytes 3145728 | tf_op jit(solution)/shard_map/coefficients/pallas_call | solution.py:403
  252.3 1.7 slice.209.tokens
  256.2 9.7 %hidden_rows.1 = (bf16[4,128,1024]{2,1,0:T(8,128)(2,1)}, bf16[4,128,1024]{2,1,0:T(8,128)(2,1)}, bf16[4,128,1024]{2,1,0:T(8,128)(2,1)}, bf16[4,128,1024]{2,1,0:T(8,128)(2,1)}, bf16[4,256,1024]{2,1,0:T(8,128)(2,1)}) custom-call(s32[25]{0:T(128)} %pad_add_fusion.meta, f32[512,512]{1,0:T(8,128)} %factored.1.inverse, bf16[2,512,512]{2,1,0:T(8,128)(2,1)} %coefficients.1.mine, ...), custom_call_target="tpu_custom_call" | custom-call | flops 3758096384 | bytes 8388608 | tf_op jit(solution)/shard_map/hidden_rows/pallas_call | solution.py:449
  265.9 3.3 fusion.43
  269.2 3.9 fusion.28
  277.6 1.5 collective-permute-start.42
  284.6 15.6 %collective-permute-done.25 = bf16[512,1024]{1,0:T(8,128)(2,1)S(1)} collective-permute-done((bf16[512,1024]{1,0:T(8,128)(2,1)S(1)}, bf16[512,1024]{1,0:T(8,128)(2,1)S(1)}, u32[]{:S(2)}, u32[]{:S(2)}) %collective-permute-start.25) | collective-permute-done | bytes 1048608 | tf_op jit(solution)/shard_map/ppermute | solution.py:21
  302.7 1.3 collective-permute-start.29
  307.9 18.2 %collective-permute-done.26 = bf16[512,1024]{1,0:T(8,128)(2,1)S(1)} collective-permute-done((bf16[512,1024]{1,0:T(8,128)(2,1)S(1)}, bf16[512,1024]{1,0:T(8,128)(2,1)S(1)}, u32[]{:S(2)}, u32[]{:S(2)}) %collective-permute-start.26) | collective-permute-done | bytes 1048608 | tf_op jit(solution)/shard_map/ppermute | solution.py:21
  326.1 1.5 collective-permute-start.47
  327.9 20.6 %collective-permute-done.28 = bf16[512,1024]{1,0:T(8,128)(2,1)S(1)} collective-permute-done((bf16[512,1024]{1,0:T(8,128)(2,1)S(1)}, bf16[512,1024]{1,0:T(8,128)(2,1)S(1)}, u32[]{:S(2)}, u32[]{:S(2)}) %collective-permute-start.28) | collective-permute-done | bytes 1048608 | tf_op jit(solution)/shard_map/ppermute | solution.py:21
  349.9 1.6 collective-permute-start.39
  351.5 1.5 add_convert_fusion.3
  354.7 1.3 add_convert_fusion.5
  356.0 1.4 collective-permute-start.33
  357.6 2.2 collective-permute-done.47
  362.2 8.9 %collective-permute-done.39 = bf16[2,2,64,1024]{3,2,1,0:T(8,128)(2,1)S(1)} collective-permute-done((bf16[2,2,64,1024]{3,2,1,0:T(8,128)(2,1)S(1)}, bf16[2,2,64,1024]{3,2,1,0:T(8,128)(2,1)S(1)}, u32[]{:S(2)}, u32[]{:S(2)}) %collective-permute-start.39) | collective-permute-done | bytes 524320 | tf_op jit(solution)/shard_map/ppermute | solution.py:21
  371.0 1.6 collective-permute-start.48
  373.6 8.7 %collective-permute-done.33 = bf16[2,2,64,1024]{3,2,1,0:T(8,128)(2,1)S(1)} collective-permute-done((bf16[2,2,64,1024]{3,2,1,0:T(8,128)(2,1)S(1)}, bf16[2,2,64,1024]{3,2,1,0:T(8,128)(2,1)S(1)}, u32[]{:S(2)}, u32[]{:S(2)}) %collective-permute-start.33) | collective-permute-done | bytes 524320 | tf_op jit(solution)/shard_map/ppermute | solution.py:21
  382.3 1.6 collective-permute-start.40
  384.8 1.6 collective-permute-done.51
  386.5 1.6 collective-permute-start.34
  390.0 2.9 collective-permute-done.40
  393.1 8.3 %collective-permute-done.37 = bf16[2,64,1024]{2,1,0:T(8,128)(2,1)S(1)} collective-permute-done((bf16[2,64,1024]{2,1,0:T(8,128)(2,1)S(1)}, bf16[2,64,1024]{2,1,0:T(8,128)(2,1)S(1)}, u32[]{:S(2)}, u32[]{:S(2)}) %collective-permute-start.37) | collective-permute-done | bytes 262176 | tf_op jit(solution)/shard_map/ppermute | solution.py:21
  401.4 9.0 %collective-permute-done.31 = bf16[2,64,1024]{2,1,0:T(8,128)(2,1)S(1)} collective-permute-done((bf16[2,64,1024]{2,1,0:T(8,128)(2,1)S(1)}, bf16[2,64,1024]{2,1,0:T(8,128)(2,1)S(1)}, u32[]{:S(2)}, u32[]{:S(2)}) %collective-permute-start.31) | collective-permute-done | bytes 262176 | tf_op jit(solution)/shard_map/ppermute | solution.py:21
  410.7 2.8 collective-permute-start.32
  413.7 8.6 %collective-permute-done.32 = bf16[64,1024]{1,0:T(8,128)(2,1)S(1)} collective-permute-done((bf16[64,1024]{1,0:T(8,128)(2,1)S(1)}, bf16[64,1024]{1,0:T(8,128)(2,1)S(1)}, u32[]{:S(2)}, u32[]{:S(2)}) %collective-permute-start.32) | collective-permute-done | bytes 131104 | tf_op jit(solution)/shard_map/ppermute | solution.py:21
  422.3 7.5 %collective-permute-done.35 = bf16[64,1024]{1,0:T(8,128)(2,1)S(1)} collective-permute-done((bf16[64,1024]{1,0:T(8,128)(2,1)S(1)}, bf16[64,1024]{1,0:T(8,128)(2,1)S(1)}, u32[]{:S(2)}, u32[]{:S(2)}) %collective-permute-start.35) | collective-permute-done | bytes 131104 | tf_op jit(solution)/shard_map/ppermute | solution.py:21
  429.8 9.0 %collective-permute-done.38 = bf16[64,1024]{1,0:T(8,128)(2,1)S(1)} collective-permute-done((bf16[64,1024]{1,0:T(8,128)(2,1)S(1)}, bf16[64,1024]{1,0:T(8,128)(2,1)S(1)}, u32[]{:S(2)}, u32[]{:S(2)}) %collective-permute-start.38) | collective-permute-done | bytes 131104 | tf_op jit(solution)/shard_map/ppermute | solution.py:21
  (187 shorter events, 45.0 us)
Async XLA Ops:
  6.5 259.3 %all-gather.3.cloned.1.call-start = ((), (), s32[]{:S(2)}) async-start(), calls=%async_computation | async-start | bytes 22020096 | tf_op jit(solution)/shard_map/all_gather | solution.py:545
  7.8 9.4 %copy-start.15 = (f32[64,8]{0,1:T(8,128)S(1)}, f32[64,8]{0,1:T(8,128)}, u32[]{:S(2)}) copy-start(f32[64,8]{0,1:T(8,128)} %param.15) | copy-start | bytes 6148
  7.8 10.1 %copy-start.16 = (s32[64,8]{0,1:T(8,128)S(1)}, s32[64,8]{0,1:T(8,128)}, u32[]{:S(2)}) copy-start(s32[64,8]{0,1:T(8,128)} %param.14) | copy-start | bytes 6148
  16.7 25.0 %collective-permute-start.5 = (bf16[4,896,512]{2,1,0:T(8,128)(2,1)}, bf16[4,896,512]{2,1,0:T(8,128)(2,1)}, u32[]{:S(2)}, u32[]{:S(2)}) collective-permute-start(bf16[4,896,512]{2,1,0:T(8,128)(2,1)} %sketch_half.3), channel_id=1, source_target_pairs={{0,1},{1,0},{2,3},{3,2},{4,5},{5,4},{6,7},{7,6},{8,9},{9,8},{10,11... | collective-permute-start | bytes 11010056 | tf_op jit(solution)/shard_map/ppermute | solution.py:26
  21.3 12.9 %collective-permute-start = (bf16[64,1920]{1,0:T(8,128)(2,1)}, bf16[64,1920]{1,0:T(8,128)(2,1)S(1)}, u32[]{:S(2)}, u32[]{:S(2)}) collective-permute-start(bf16[64,1920]{1,0:T(8,128)(2,1)} %get-tuple-element.73), channel_id=1, source_target_pairs={{0,2},{2,0},{4,6},{6,4},{8,10},{10,8},{12,14},{14,12},{16,18},{18,... | collective-permute-start | bytes 737288 | tf_op jit(solution)/shard_map/ppermute | solution.py:21
  23.8 13.6 %collective-permute-start.1 = (bf16[64,1920]{1,0:T(8,128)(2,1)}, bf16[64,1920]{1,0:T(8,128)(2,1)S(1)}, u32[]{:S(2)}, u32[]{:S(2)}) collective-permute-start(bf16[64,1920]{1,0:T(8,128)(2,1)} %get-tuple-element.74), channel_id=1, source_target_pairs={{0,4},{2,6},{4,0},{6,2},{8,12},{10,14},{12,8},{14,10},{16,20},{18,... | collective-permute-start | bytes 737288 | tf_op jit(solution)/shard_map/ppermute | solution.py:21
  25.4 12.0 %copy-start.13 = (bf16[64,1920]{1,0:T(8,128)(2,1)S(1)}, bf16[64,1920]{1,0:T(8,128)(2,1)}, u32[]{:S(2)}) copy-start(bf16[64,1920]{1,0:T(8,128)(2,1)} %get-tuple-element.72) | copy-start | bytes 737284
  25.4 12.0 %collective-permute-start.2 = (bf16[64,1920]{1,0:T(8,128)(2,1)}, bf16[64,1920]{1,0:T(8,128)(2,1)S(1)}, u32[]{:S(2)}, u32[]{:S(2)}) collective-permute-start(bf16[64,1920]{1,0:T(8,128)(2,1)} %get-tuple-element.75), channel_id=1, source_target_pairs={{0,6},{2,4},{4,2},{6,0},{8,14},{10,12},{12,10},{14,8},{16,22},{18,... | collective-permute-start | bytes 737288 | tf_op jit(solution)/shard_map/ppermute | solution.py:21
  37.5 45.4 %collective-permute-start.3 = (bf16[256,1920]{1,0:T(8,128)(2,1)S(1)}, bf16[256,1920]{1,0:T(8,128)(2,1)}, u32[]{:S(2)}, u32[]{:S(2)}) collective-permute-start(bf16[256,1920]{1,0:T(8,128)(2,1)S(1)} %pad_maximum_fusion.2), channel_id=1, source_target_pairs={{0,16},{2,18},{4,20},{6,22},{8,24},{10,26},{12,28},{14,30},{16,0},... | collective-permute-start | bytes 2949128 | tf_op jit(solution)/shard_map/ppermute | solution.py:21
  40.1 44.1 %collective-permute-start.4 = (bf16[256,1920]{1,0:T(8,128)(2,1)S(1)}, bf16[256,1920]{1,0:T(8,128)(2,1)}, u32[]{:S(2)}, u32[]{:S(2)}) collective-permute-start(bf16[256,1920]{1,0:T(8,128)(2,1)S(1)} %pad_maximum_fusion.2), channel_id=1, source_target_pairs={{0,8},{2,10},{4,12},{6,14},{8,0},{10,2},{12,4},{14,6},{16,24},{18,... | collective-permute-start | bytes 2949128 | tf_op jit(solution)/shard_map/ppermute | solution.py:21
  47.5 36.8 %collective-permute-start.6 = (bf16[896,512]{1,0:T(8,128)(2,1)}, bf16[896,512]{1,0:T(8,128)(2,1)S(1)}, u32[]{:S(2)}, u32[]{:S(2)}) collective-permute-start(bf16[896,512]{1,0:T(8,128)(2,1)} %get-tuple-element.141), channel_id=1, source_target_pairs={{0,2},{2,0},{4,6},{6,4},{8,10},{10,8},{12,14},{14,12},{16,18},{18,... | collective-permute-start | bytes 2752520 | tf_op jit(solution)/shard_map/ppermute | solution.py:21
  48.7 41.0 %collective-permute-start.7 = (bf16[896,512]{1,0:T(8,128)(2,1)}, bf16[896,512]{1,0:T(8,128)(2,1)S(1)}, u32[]{:S(2)}, u32[]{:S(2)}) collective-permute-start(bf16[896,512]{1,0:T(8,128)(2,1)} %get-tuple-element.140), channel_id=1, source_target_pairs={{0,4},{2,6},{4,0},{6,2},{8,12},{10,14},{12,8},{14,10},{16,20},{18,... | collective-permute-start | bytes 2752520 | tf_op jit(solution)/shard_map/ppermute | solution.py:21
  49.5 40.2 %collective-permute-start.8 = (bf16[896,512]{1,0:T(8,128)(2,1)}, bf16[896,512]{1,0:T(8,128)(2,1)}, u32[]{:S(2)}, u32[]{:S(2)}) collective-permute-start(bf16[896,512]{1,0:T(8,128)(2,1)} %get-tuple-element.139), channel_id=1, source_target_pairs={{0,6},{2,4},{4,2},{6,0},{8,14},{10,12},{12,10},{14,8},{16,22},{18,... | collective-permute-start | bytes 2752520 | tf_op jit(solution)/shard_map/ppermute | solution.py:21
  95.0 21.2 %collective-permute-start.10 = (bf16[896,512]{1,0:T(8,128)(2,1)}, bf16[896,512]{1,0:T(8,128)(2,1)S(1)}, u32[]{:S(2)}, u32[]{:S(2)}) collective-permute-start(bf16[896,512]{1,0:T(8,128)(2,1)} %get-tuple-element.85), channel_id=1, source_target_pairs={{8,0},{10,2},{12,4},{14,6},{16,8},{18,10},{20,12},{22,14},{24,16},... | collective-permute-start | bytes 2752520 | tf_op jit(solution)/shard_map/ppermute | solution.py:32
  96.3 21.2 %collective-permute-start.9 = (bf16[896,512]{1,0:T(8,128)(2,1)}, bf16[896,512]{1,0:T(8,128)(2,1)S(1)}, u32[]{:S(2)}, u32[]{:S(2)}) collective-permute-start(bf16[896,512]{1,0:T(8,128)(2,1)} %get-tuple-element.84), channel_id=1, source_target_pairs={{0,8},{2,10},{4,12},{6,14},{8,16},{10,18},{12,20},{14,22},{16,24},... | collective-permute-start | bytes 2752520 | tf_op jit(solution)/shard_map/ppermute | solution.py:32
  125.8 16.1 %collective-permute-start.12 = (bf16[4,896,512]{2,1,0:T(8,128)(2,1)}, bf16[4,896,512]{2,1,0:T(8,128)(2,1)S(1)}, u32[]{:S(2)}, u32[]{:S(2)}) collective-permute-start(bf16[4,896,512]{2,1,0:T(8,128)(2,1)} %get-tuple-element.109.refs_0_), channel_id=1, source_target_pairs={{0,1},{1,0},{2,3},{3,2},{4,5},{5,4},{6,7},{7,6},{8,9},{9,8},{10,11... | collective-permute-start | bytes 11010056 | tf_op jit(solution)/shard_map/ppermute | solution.py:26
  125.9 25.5 %collective-permute-start.11 = (bf16[256,1920]{1,0:T(8,128)(2,1)S(1)}, bf16[256,1920]{1,0:T(8,128)(2,1)S(1)}, u32[]{:S(2)}, u32[]{:S(2)}) collective-permute-start(bf16[256,1920]{1,0:T(8,128)(2,1)S(1)} %slice.206), channel_id=1, source_target_pairs={{0,8},{2,10},{4,12},{6,14},{8,0},{10,2},{12,4},{14,6},{16,24},{18,... | collective-permute-start | bytes 2949128 | tf_op jit(solution)/shard_map/ppermute | solution.py:21
  128.3 13.6 %collective-permute-start.13 = (bf16[448,512]{1,0:T(8,128)(2,1)}, bf16[448,512]{1,0:T(8,128)(2,1)S(1)}, u32[]{:S(2)}, u32[]{:S(2)}) collective-permute-start(bf16[448,512]{1,0:T(8,128)(2,1)} %get-tuple-element.88), channel_id=1, source_target_pairs={{0,2},{2,0},{4,6},{6,4},{8,10},{10,8},{12,14},{14,12},{16,18},{18,... | collective-permute-start | bytes 1376264 | tf_op jit(solution)/shard_map/ppermute | solution.py:21
  129.0 22.4 %collective-permute-start.14 = (bf16[448,512]{1,0:T(8,128)(2,1)}, bf16[448,512]{1,0:T(8,128)(2,1)S(1)}, u32[]{:S(2)}, u32[]{:S(2)}) collective-permute-start(bf16[448,512]{1,0:T(8,128)(2,1)} %get-tuple-element.90), channel_id=1, source_target_pairs={{0,4},{2,6},{4,0},{6,2},{8,12},{10,14},{12,8},{14,10},{16,20},{18,... | collective-permute-start | bytes 1376264 | tf_op jit(solution)/shard_map/ppermute | solution.py:21
  130.7 20.7 %collective-permute-start.15 = (bf16[448,512]{1,0:T(8,128)(2,1)}, bf16[448,512]{1,0:T(8,128)(2,1)S(1)}, u32[]{:S(2)}, u32[]{:S(2)}) collective-permute-start(bf16[448,512]{1,0:T(8,128)(2,1)} %get-tuple-element.91), channel_id=1, source_target_pairs={{0,6},{2,4},{4,2},{6,0},{8,14},{10,12},{12,10},{14,8},{16,22},{18,... | collective-permute-start | bytes 1376264 | tf_op jit(solution)/shard_map/ppermute | solution.py:21
  134.0 21.2 %copy-start.25 = (bf16[448,512]{1,0:T(8,128)(2,1)S(1)}, bf16[448,512]{1,0:T(8,128)(2,1)}, u32[]{:S(2)}) copy-start(bf16[448,512]{1,0:T(8,128)(2,1)} %get-tuple-element.98) | copy-start | bytes 1376260
  134.0 22.5 %copy-start.24 = (bf16[448,512]{1,0:T(8,128)(2,1)S(1)}, bf16[448,512]{1,0:T(8,128)(2,1)}, u32[]{:S(2)}) copy-start(bf16[448,512]{1,0:T(8,128)(2,1)} %get-tuple-element.99) | copy-start | bytes 1376260
  134.0 23.3 %copy-start.23 = (bf16[448,512]{1,0:T(8,128)(2,1)S(1)}, bf16[448,512]{1,0:T(8,128)(2,1)}, u32[]{:S(2)}) copy-start(bf16[448,512]{1,0:T(8,128)(2,1)} %get-tuple-element.100) | copy-start | bytes 1376260
  141.9 9.5 %copy-start.9 = (bf16[448,512]{1,0:T(8,128)(2,1)}, bf16[448,512]{1,0:T(8,128)(2,1)S(1)}, u32[]{:S(2)}) copy-start(bf16[448,512]{1,0:T(8,128)(2,1)S(1)} %collective-permute-done.13.refs_1_) | copy-start | bytes 1376260
  141.9 9.5 %copy-start.18 = (bf16[4,896,512]{2,1,0:T(8,128)(2,1)}, bf16[4,896,512]{2,1,0:T(8,128)(2,1)S(1)}, u32[]{:S(2)}) copy-start(bf16[4,896,512]{2,1,0:T(8,128)(2,1)S(1)} %collective-permute-done.12.refs_1_) | copy-start | bytes 11010052
  155.1 9.6 %collective-permute-start.16 = (bf16[4,448,512]{2,1,0:T(8,128)(2,1)}, bf16[4,448,512]{2,1,0:T(8,128)(2,1)S(1)}, u32[]{:S(2)}, u32[]{:S(2)}) collective-permute-start(bf16[4,448,512]{2,1,0:T(8,128)(2,1)} %own_sums.2.own), channel_id=1, source_target_pairs={{0,1},{1,0},{2,3},{3,2},{4,5},{5,4},{6,7},{7,6},{8,9},{9,8},{10,11... | collective-permute-start | bytes 5505032 | tf_op jit(solution)/shard_map/ppermute | solution.py:26
  155.1 22.3 %collective-permute-start.17 = (bf16[448,512]{1,0:T(8,128)(2,1)S(1)}, bf16[448,512]{1,0:T(8,128)(2,1)S(1)}, u32[]{:S(2)}, u32[]{:S(2)}) collective-permute-start(bf16[448,512]{1,0:T(8,128)(2,1)S(1)} %copy-done.25), channel_id=1, source_target_pairs={{0,2},{2,0},{4,6},{6,4},{8,10},{10,8},{12,14},{14,12},{16,18},{18,... | collective-permute-start | bytes 1376264 | tf_op jit(solution)/shard_map/ppermute | solution.py:21
  156.4 21.0 %collective-permute-start.18 = (bf16[448,512]{1,0:T(8,128)(2,1)S(1)}, bf16[448,512]{1,0:T(8,128)(2,1)S(1)}, u32[]{:S(2)}, u32[]{:S(2)}) collective-permute-start(bf16[448,512]{1,0:T(8,128)(2,1)S(1)} %copy-done.24), channel_id=1, source_target_pairs={{0,4},{2,6},{4,0},{6,2},{8,12},{10,14},{12,8},{14,10},{16,20},{18,... | collective-permute-start | bytes 1376264 | tf_op jit(solution)/shard_map/ppermute | solution.py:21
  157.2 21.8 %collective-permute-start.19 = (bf16[448,512]{1,0:T(8,128)(2,1)S(1)}, bf16[448,512]{1,0:T(8,128)(2,1)S(1)}, u32[]{:S(2)}, u32[]{:S(2)}) collective-permute-start(bf16[448,512]{1,0:T(8,128)(2,1)S(1)} %copy-done.23), channel_id=1, source_target_pairs={{0,6},{2,4},{4,2},{6,0},{8,14},{10,12},{12,10},{14,8},{16,22},{18,... | collective-permute-start | bytes 1376264 | tf_op jit(solution)/shard_map/ppermute | solution.py:21
  182.7 13.5 %collective-permute-start.20 = (bf16[4,448,512]{2,1,0:T(8,128)(2,1)}, bf16[4,448,512]{2,1,0:T(8,128)(2,1)S(1)}, u32[]{:S(2)}, u32[]{:S(2)}) collective-permute-start(bf16[4,448,512]{2,1,0:T(8,128)(2,1)} %own_sums.3.own), channel_id=1, source_target_pairs={{0,1},{1,0},{2,3},{3,2},{4,5},{5,4},{6,7},{7,6},{8,9},{9,8},{10,11... | collective-permute-start | bytes 5505032 | tf_op jit(solution)/shard_map/ppermute | solution.py:26
  196.2 50.5 %collective-permute-start.21 = (bf16[1024,512]{1,0:T(8,128)(2,1)}, bf16[1024,512]{1,0:T(8,128)(2,1)S(1)}, u32[]{:S(2)}, u32[]{:S(2)}) collective-permute-start(bf16[1024,512]{1,0:T(8,128)(2,1)} %get-tuple-element.121), channel_id=1, source_target_pairs={{0,2},{2,0},{4,6},{6,4},{8,10},{10,8},{12,14},{14,12},{16,18},{18,... | collective-permute-start | bytes 3145736 | tf_op jit(solution)/shard_map/ppermute | solution.py:21
  197.0 49.7 %collective-permute-start.22 = (bf16[1024,512]{1,0:T(8,128)(2,1)}, bf16[1024,512]{1,0:T(8,128)(2,1)S(1)}, u32[]{:S(2)}, u32[]{:S(2)}) collective-permute-start(bf16[1024,512]{1,0:T(8,128)(2,1)} %get-tuple-element.122), channel_id=1, source_target_pairs={{0,4},{2,6},{4,0},{6,2},{8,12},{10,14},{12,8},{14,10},{16,20},{18,... | collective-permute-start | bytes 3145736 | tf_op jit(solution)/shard_map/ppermute | solution.py:21
  198.7 48.0 %collective-permute-start.23 = (bf16[1024,512]{1,0:T(8,128)(2,1)}, bf16[1024,512]{1,0:T(8,128)(2,1)S(1)}, u32[]{:S(2)}, u32[]{:S(2)}) collective-permute-start(bf16[1024,512]{1,0:T(8,128)(2,1)} %get-tuple-element.123), channel_id=1, source_target_pairs={{0,6},{2,4},{4,2},{6,0},{8,14},{10,12},{12,10},{14,8},{16,22},{18,... | collective-permute-start | bytes 3145736 | tf_op jit(solution)/shard_map/ppermute | solution.py:21
  246.7 5.5 %copy-start.19 = (bf16[1024,512]{1,0:T(8,128)(2,1)}, bf16[1024,512]{1,0:T(8,128)(2,1)S(1)}, u32[]{:S(2)}) copy-start(bf16[1024,512]{1,0:T(8,128)(2,1)S(1)} %collective-permute-done.21.refs_1_) | copy-start | bytes 3145732
  252.3 2.9 collective-permute-start.24
  265.9 7.7 %copy-start.17 = (bf16[1,1024,7168]{2,1,0:T(8,128)(2,1)S(1)}, bf16[1,1024,7168]{2,1,0:T(8,128)(2,1)}, u32[]{:S(2)}) copy-start(bf16[1,1024,7168]{2,1,0:T(8,128)(2,1)} %all-gather.3.cloned.1.call-done) | copy-start | bytes 44040196
  274.9 25.3 %collective-permute-start.25 = (bf16[512,1024]{1,0:T(8,128)(2,1)S(1)}, bf16[512,1024]{1,0:T(8,128)(2,1)S(1)}, u32[]{:S(2)}, u32[]{:S(2)}) collective-permute-start(bf16[512,1024]{1,0:T(8,128)(2,1)S(1)} %fusion.31), channel_id=1, source_target_pairs={{0,8},{2,10},{4,12},{6,14},{8,0},{10,2},{12,4},{14,6},{16,24},{18,... | collective-permute-start | bytes 3145736 | tf_op jit(solution)/shard_map/ppermute | solution.py:21
  276.6 26.1 %collective-permute-start.46 = (bf16[512,1024]{1,0:T(8,128)(2,1)S(1)}, bf16[512,1024]{1,0:T(8,128)(2,1)S(1)}, u32[]{:S(2)}, u32[]{:S(2)}) collective-permute-start(bf16[512,1024]{1,0:T(8,128)(2,1)S(1)} %fusion.46), channel_id=1, source_target_pairs={{0,4},{2,6},{4,0},{6,2},{8,12},{10,14},{12,8},{14,10},{16,20},{18,... | collective-permute-start | bytes 3145736 | tf_op jit(solution)/shard_map/ppermute | solution.py:21
  277.6 27.9 %collective-permute-start.42 = (bf16[512,1024]{1,0:T(8,128)(2,1)S(1)}, bf16[512,1024]{1,0:T(8,128)(2,1)S(1)}, u32[]{:S(2)}, u32[]{:S(2)}) collective-permute-start(bf16[512,1024]{1,0:T(8,128)(2,1)S(1)} %fusion.43), channel_id=1, source_target_pairs={{0,2},{2,0},{4,6},{6,4},{8,10},{10,8},{12,14},{14,12},{16,18},{18,... | collective-permute-start | bytes 3145736 | tf_op jit(solution)/shard_map/ppermute | solution.py:21
  279.1 47.0 %collective-permute-start.26 = (bf16[512,1024]{1,0:T(8,128)(2,1)S(1)}, bf16[512,1024]{1,0:T(8,128)(2,1)S(1)}, u32[]{:S(2)}, u32[]{:S(2)}) collective-permute-start(bf16[512,1024]{1,0:T(8,128)(2,1)S(1)} %fusion.28), channel_id=1, source_target_pairs={{0,2},{2,0},{4,6},{6,4},{8,10},{10,8},{12,14},{14,12},{16,18},{18,... | collective-permute-start | bytes 3145736 | tf_op jit(solution)/shard_map/ppermute | solution.py:21
  280.9 46.8 %collective-permute-start.27 = (bf16[512,1024]{1,0:T(8,128)(2,1)S(1)}, bf16[512,1024]{1,0:T(8,128)(2,1)S(1)}, u32[]{:S(2)}, u32[]{:S(2)}) collective-permute-start(bf16[512,1024]{1,0:T(8,128)(2,1)S(1)} %fusion.34), channel_id=1, source_target_pairs={{0,4},{2,6},{4,0},{6,2},{8,12},{10,14},{12,8},{14,10},{16,20},{18,... | collective-permute-start | bytes 3145736 | tf_op jit(solution)/shard_map/ppermute | solution.py:21
  300.1 48.4 %collective-permute-start.28 = (bf16[512,1024]{1,0:T(8,128)(2,1)S(1)}, bf16[512,1024]{1,0:T(8,128)(2,1)S(1)}, u32[]{:S(2)}, u32[]{:S(2)}) collective-permute-start(bf16[512,1024]{1,0:T(8,128)(2,1)S(1)} %fusion.37), channel_id=1, source_target_pairs={{0,2},{2,0},{4,6},{6,4},{8,10},{10,8},{12,14},{14,12},{16,18},{18,... | collective-permute-start | bytes 3145736 | tf_op jit(solution)/shard_map/ppermute | solution.py:21
  302.7 45.9 %collective-permute-start.29 = (bf16[512,1024]{1,0:T(8,128)(2,1)S(1)}, bf16[512,1024]{1,0:T(8,128)(2,1)S(1)}, u32[]{:S(2)}, u32[]{:S(2)}) collective-permute-start(bf16[512,1024]{1,0:T(8,128)(2,1)S(1)} %fusion.40), channel_id=1, source_target_pairs={{0,4},{2,6},{4,0},{6,2},{8,12},{10,14},{12,8},{14,10},{16,20},{18,... | collective-permute-start | bytes 3145736 | tf_op jit(solution)/shard_map/ppermute | solution.py:21
  305.4 50.6 %collective-permute-start.50 = (bf16[2,2,64,1024]{3,2,0,1:T(8,128)(2,1)S(1)}, bf16[2,2,64,1024]{3,2,0,1:T(8,128)(2,1)S(1)}, u32[]{:S(2)}, u32[]{:S(2)}) collective-permute-start(bf16[2,2,64,1024]{3,2,0,1:T(8,128)(2,1)S(1)} %copy.23), channel_id=1, source_target_pairs={{0,16},{2,18},{4,20},{6,22},{8,24},{10,26},{12,28},{14,30},{16,0},... | collective-permute-start | bytes 1572872 | tf_op jit(solution)/shard_map/ppermute | solution.py:21
  326.1 33.7 %collective-permute-start.47 = (bf16[2,2,64,1024]{3,2,1,0:T(8,128)(2,1)S(1)}, bf16[2,2,64,1024]{3,2,1,0:T(8,128)(2,1)S(1)}, u32[]{:S(2)}, u32[]{:S(2)}) collective-permute-start(bf16[2,2,64,1024]{3,2,1,0:T(8,128)(2,1)S(1)} %slice_bitcast_fusion), channel_id=1, source_target_pairs={{0,2},{2,0},{4,6},{6,4},{8,10},{10,8},{12,14},{14,12},{16,18},{18,... | collective-permute-start | bytes 1572872 | tf_op jit(solution)/shard_map/ppermute | solution.py:21
  327.7 33.5 %collective-permute-start.43 = (bf16[2,2,64,1024]{3,2,1,0:T(8,128)(2,1)S(1)}, bf16[2,2,64,1024]{3,2,1,0:T(8,128)(2,1)S(1)}, u32[]{:S(2)}, u32[]{:S(2)}) collective-permute-start(bf16[2,2,64,1024]{3,2,1,0:T(8,128)(2,1)S(1)} %slice_bitcast_fusion.2), channel_id=1, source_target_pairs={{0,4},{2,6},{4,0},{6,2},{8,12},{10,14},{12,8},{14,10},{16,20},{18,... | collective-permute-start | bytes 1572872 | tf_op jit(solution)/shard_map/ppermute | solution.py:21
  349.9 21.2 %collective-permute-start.39 = (bf16[2,2,64,1024]{3,2,1,0:T(8,128)(2,1)S(1)}, bf16[2,2,64,1024]{3,2,1,0:T(8,128)(2,1)S(1)}, u32[]{:S(2)}, u32[]{:S(2)}) collective-permute-start(bf16[2,2,64,1024]{3,2,1,0:T(8,128)(2,1)S(1)} %slice_bitcast_fusion.4), channel_id=1, source_target_pairs={{0,2},{2,0},{4,6},{6,4},{8,10},{10,8},{12,14},{14,12},{16,18},{18,... | collective-permute-start | bytes 1572872 | tf_op jit(solution)/shard_map/ppermute | solution.py:21
  353.1 19.8 %collective-permute-start.36 = (bf16[2,2,64,1024]{3,2,1,0:T(8,128)(2,1)S(1)}, bf16[2,2,64,1024]{3,2,1,0:T(8,128)(2,1)S(1)}, u32[]{:S(2)}, u32[]{:S(2)}) collective-permute-start(bf16[2,2,64,1024]{3,2,1,0:T(8,128)(2,1)S(1)} %slice_bitcast_fusion.6), channel_id=1, source_target_pairs={{0,4},{2,6},{4,0},{6,2},{8,12},{10,14},{12,8},{14,10},{16,20},{18,... | collective-permute-start | bytes 1572872 | tf_op jit(solution)/shard_map/ppermute | solution.py:21
  356.0 26.2 %collective-permute-start.33 = (bf16[2,2,64,1024]{3,2,1,0:T(8,128)(2,1)S(1)}, bf16[2,2,64,1024]{3,2,1,0:T(8,128)(2,1)S(1)}, u32[]{:S(2)}, u32[]{:S(2)}) collective-permute-start(bf16[2,2,64,1024]{3,2,1,0:T(8,128)(2,1)S(1)} %slice_bitcast_fusion.8), channel_id=1, source_target_pairs={{0,2},{2,0},{4,6},{6,4},{8,10},{10,8},{12,14},{14,12},{16,18},{18,... | collective-permute-start | bytes 1572872 | tf_op jit(solution)/shard_map/ppermute | solution.py:21
  359.8 24.2 %collective-permute-start.30 = (bf16[2,2,64,1024]{3,2,1,0:T(8,128)(2,1)S(1)}, bf16[2,2,64,1024]{3,2,1,0:T(8,128)(2,1)S(1)}, u32[]{:S(2)}, u32[]{:S(2)}) collective-permute-start(bf16[2,2,64,1024]{3,2,1,0:T(8,128)(2,1)S(1)} %slice_bitcast_fusion.10), channel_id=1, source_target_pairs={{0,4},{2,6},{4,0},{6,2},{8,12},{10,14},{12,8},{14,10},{16,20},{18,... | collective-permute-start | bytes 1572872 | tf_op jit(solution)/shard_map/ppermute | solution.py:21
  361.1 25.4 %collective-permute-start.51 = (bf16[2,64,1024]{2,1,0:T(8,128)(2,1)S(1)}, bf16[2,64,1024]{2,1,0:T(8,128)(2,1)S(1)}, u32[]{:S(2)}, u32[]{:S(2)}) collective-permute-start(bf16[2,64,1024]{2,1,0:T(8,128)(2,1)S(1)} %slice_bitcast_fusion.14), channel_id=1, source_target_pairs={{0,2},{2,0},{4,6},{6,4},{8,10},{10,8},{12,14},{14,12},{16,18},{18,... | collective-permute-start | bytes 786440 | tf_op jit(solution)/shard_map/ppermute | solution.py:21
  371.0 17.1 %collective-permute-start.48 = (bf16[2,64,1024]{2,1,0:T(8,128)(2,1)S(1)}, bf16[2,64,1024]{2,1,0:T(8,128)(2,1)S(1)}, u32[]{:S(2)}, u32[]{:S(2)}) collective-permute-start(bf16[2,64,1024]{2,1,0:T(8,128)(2,1)S(1)} %slice_bitcast_fusion.16), channel_id=1, source_target_pairs={{0,8},{2,10},{4,12},{6,14},{8,0},{10,2},{12,4},{14,6},{16,24},{18,... | collective-permute-start | bytes 786440 | tf_op jit(solution)/shard_map/ppermute | solution.py:21
  372.8 15.9 %collective-permute-start.44 = (bf16[2,64,1024]{2,1,0:T(8,128)(2,1)S(1)}, bf16[2,64,1024]{2,1,0:T(8,128)(2,1)S(1)}, u32[]{:S(2)}, u32[]{:S(2)}) collective-permute-start(bf16[2,64,1024]{2,1,0:T(8,128)(2,1)S(1)} %slice_bitcast_fusion.18), channel_id=1, source_target_pairs={{0,8},{2,10},{4,12},{6,14},{8,0},{10,2},{12,4},{14,6},{16,24},{18,... | collective-permute-start | bytes 786440 | tf_op jit(solution)/shard_map/ppermute | solution.py:21
  382.3 10.6 %collective-permute-start.40 = (bf16[2,64,1024]{2,1,0:T(8,128)(2,1)S(1)}, bf16[2,64,1024]{2,1,0:T(8,128)(2,1)S(1)}, u32[]{:S(2)}, u32[]{:S(2)}) collective-permute-start(bf16[2,64,1024]{2,1,0:T(8,128)(2,1)S(1)} %slice_bitcast_fusion.20), channel_id=1, source_target_pairs={{0,8},{2,10},{4,12},{6,14},{8,0},{10,2},{12,4},{14,6},{16,24},{18,... | collective-permute-start | bytes 786440 | tf_op jit(solution)/shard_map/ppermute | solution.py:21
  384.1 17.3 %collective-permute-start.37 = (bf16[2,64,1024]{2,1,0:T(8,128)(2,1)S(1)}, bf16[2,64,1024]{2,1,0:T(8,128)(2,1)S(1)}, u32[]{:S(2)}, u32[]{:S(2)}) collective-permute-start(bf16[2,64,1024]{2,1,0:T(8,128)(2,1)S(1)} %slice_bitcast_fusion.22), channel_id=1, source_target_pairs={{0,8},{2,10},{4,12},{6,14},{8,0},{10,2},{12,4},{14,6},{16,24},{18,... | collective-permute-start | bytes 786440 | tf_op jit(solution)/shard_map/ppermute | solution.py:21
  386.5 24.3 %collective-permute-start.34 = (bf16[2,64,1024]{2,1,0:T(8,128)(2,1)S(1)}, bf16[2,64,1024]{2,1,0:T(8,128)(2,1)S(1)}, u32[]{:S(2)}, u32[]{:S(2)}) collective-permute-start(bf16[2,64,1024]{2,1,0:T(8,128)(2,1)S(1)} %slice_bitcast_fusion.24), channel_id=1, source_target_pairs={{0,8},{2,10},{4,12},{6,14},{8,0},{10,2},{12,4},{14,6},{16,24},{18,... | collective-permute-start | bytes 786440 | tf_op jit(solution)/shard_map/ppermute | solution.py:21
  388.1 22.3 %collective-permute-start.31 = (bf16[2,64,1024]{2,1,0:T(8,128)(2,1)S(1)}, bf16[2,64,1024]{2,1,0:T(8,128)(2,1)S(1)}, u32[]{:S(2)}, u32[]{:S(2)}) collective-permute-start(bf16[2,64,1024]{2,1,0:T(8,128)(2,1)S(1)} %slice_bitcast_fusion.26), channel_id=1, source_target_pairs={{0,8},{2,10},{4,12},{6,14},{8,0},{10,2},{12,4},{14,6},{16,24},{18,... | collective-permute-start | bytes 786440 | tf_op jit(solution)/shard_map/ppermute | solution.py:21
  388.8 50.2 %collective-permute-start.52 = (bf16[64,1024]{1,0:T(8,128)(2,1)S(1)}, bf16[64,1024]{1,0:T(8,128)(2,1)S(1)}, u32[]{:S(2)}, u32[]{:S(2)}) collective-permute-start(bf16[64,1024]{1,0:T(8,128)(2,1)S(1)} %slice_bitcast_fusion.28), channel_id=1, source_target_pairs={{0,4},{2,6},{4,0},{6,2},{8,12},{10,14},{12,8},{14,10},{16,20},{18,... | collective-permute-start | bytes 393224 | tf_op jit(solution)/shard_map/ppermute | solution.py:21
  392.9 46.0 %collective-permute-start.49 = (bf16[64,1024]{1,0:T(8,128)(2,1)S(1)}, bf16[64,1024]{1,0:T(8,128)(2,1)S(1)}, u32[]{:S(2)}, u32[]{:S(2)}) collective-permute-start(bf16[64,1024]{1,0:T(8,128)(2,1)S(1)} %slice_bitcast_fusion.30), channel_id=1, source_target_pairs={{0,16},{2,18},{4,20},{6,22},{8,24},{10,26},{12,28},{14,30},{16,0},... | collective-permute-start | bytes 393224 | tf_op jit(solution)/shard_map/ppermute | solution.py:21
  401.4 37.5 %collective-permute-start.45 = (bf16[64,1024]{1,0:T(8,128)(2,1)S(1)}, bf16[64,1024]{1,0:T(8,128)(2,1)S(1)}, u32[]{:S(2)}, u32[]{:S(2)}) collective-permute-start(bf16[64,1024]{1,0:T(8,128)(2,1)S(1)} %slice_bitcast_fusion.32), channel_id=1, source_target_pairs={{0,16},{2,18},{4,20},{6,22},{8,24},{10,26},{12,28},{14,30},{16,0},... | collective-permute-start | bytes 393224 | tf_op jit(solution)/shard_map/ppermute | solution.py:21
  410.5 28.4 %collective-permute-start.41 = (bf16[64,1024]{1,0:T(8,128)(2,1)S(1)}, bf16[64,1024]{1,0:T(8,128)(2,1)S(1)}, u32[]{:S(2)}, u32[]{:S(2)}) collective-permute-start(bf16[64,1024]{1,0:T(8,128)(2,1)S(1)} %slice_bitcast_fusion.34), channel_id=1, source_target_pairs={{0,16},{2,18},{4,20},{6,22},{8,24},{10,26},{12,28},{14,30},{16,0},... | collective-permute-start | bytes 393224 | tf_op jit(solution)/shard_map/ppermute | solution.py:21
  410.7 11.5 %collective-permute-start.32 = (bf16[64,1024]{1,0:T(8,128)(2,1)S(1)}, bf16[64,1024]{1,0:T(8,128)(2,1)S(1)}, u32[]{:S(2)}, u32[]{:S(2)}) collective-permute-start(bf16[64,1024]{1,0:T(8,128)(2,1)S(1)} %slice_bitcast_fusion.40), channel_id=1, source_target_pairs={{0,16},{2,18},{4,20},{6,22},{8,24},{10,26},{12,28},{14,30},{16,0},... | collective-permute-start | bytes 393224 | tf_op jit(solution)/shard_map/ppermute | solution.py:21
  422.2 7.5 %collective-permute-start.35 = (bf16[64,1024]{1,0:T(8,128)(2,1)S(1)}, bf16[64,1024]{1,0:T(8,128)(2,1)S(1)}, u32[]{:S(2)}, u32[]{:S(2)}) collective-permute-start(bf16[64,1024]{1,0:T(8,128)(2,1)S(1)} %slice_bitcast_fusion.38), channel_id=1, source_target_pairs={{0,16},{2,18},{4,20},{6,22},{8,24},{10,26},{12,28},{14,30},{16,0},... | collective-permute-start | bytes 393224 | tf_op jit(solution)/shard_map/ppermute | solution.py:21
  429.7 9.1 %collective-permute-start.38 = (bf16[64,1024]{1,0:T(8,128)(2,1)S(1)}, bf16[64,1024]{1,0:T(8,128)(2,1)S(1)}, u32[]{:S(2)}, u32[]{:S(2)}) collective-permute-start(bf16[64,1024]{1,0:T(8,128)(2,1)S(1)} %slice_bitcast_fusion.36), channel_id=1, source_target_pairs={{0,16},{2,18},{4,20},{6,22},{8,24},{10,26},{12,28},{14,30},{16,0},... | collective-permute-start | bytes 393224 | tf_op jit(solution)/shard_map/ppermute | solution.py:21
  (20 other events, 47.6 us)
Sparse Core Ops, SparseCore 0:
  51.1 24.3 all-gather.2
